TPU v7x, 32 devices: a whole 2x2x4 slice. The times are simulated.
32 devices in a mesh: seq: 4 (over y, x), grp: 8 (over z, core).
Axes of the slice: x: 2, y: 2, z: 4, core: 2. Of those that a mesh axis runs over, the one named last changes fastest.
Arguments:
- layer_in: bfloat16 [8, 768, 2048], P('seq', 'grp'), may hold values from -6 to 6
- gain_one: bfloat16 [2048], P(('seq', 'grp')), may hold values from 0.5 to 1.5
- w_branch: bfloat16 [2048, 2816], P('seq', 'grp'), may hold values from -0.125 to 0.125
- w_rec: bfloat16 [2048, 2816], P('seq', 'grp'), may hold values from -0.125 to 0.125
- conv_w: bfloat16 [16, 4, 176], P('grp', None, 'seq'), may hold values from -3 to 3
- conv_b: bfloat16 [16, 176], P('grp', 'seq'), may hold values from -3 to 3
- gate_a_w: bfloat16 [16, 176, 176], P('grp', 'seq'), may hold values from -0.4375 to 0.4375
- gate_a_b: bfloat16 [16, 176], P('grp', 'seq'), may hold values from -4 to 4
- gate_x_w: bfloat16 [16, 176, 176], P('grp', 'seq'), may hold values from -0.4375 to 0.4375
- gate_x_b: bfloat16 [16, 176], P('grp', 'seq'), may hold values from -4 to 4
- decay_logit: bfloat16 [16, 176], P('grp', 'seq'), may hold values from 5 to 12
- w_out: bfloat16 [2816, 2048], P('grp', 'seq'), may hold values from -0.3125 to 0.3125
- gain_two: bfloat16 [2048], P(('seq', 'grp')), may hold values from 0.5 to 1.5
- mlp_gate: bfloat16 [2048, 6144], P('seq', 'grp'), may hold values from -0.125 to 0.125
- mlp_up: bfloat16 [2048, 6144], P('seq', 'grp'), may hold values from -0.125 to 0.125
- mlp_down: bfloat16 [6144, 2048], P('grp', 'seq'), may hold values from -0.15625 to 0.15625
- out_grad: bfloat16 [8, 768, 2048], P('seq', 'grp'), may hold values from -6 to 6
Outputs:
- layer_out: bfloat16 [8, 768, 2048], P('seq', 'grp')
- grad_x: float32 [8, 768, 2048], P('seq', 'grp')
- grad_gain_one: float32 [2048], P(('seq', 'grp'))
- grad_w_branch: float32 [2048, 2816], P('seq', 'grp')
- grad_w_rec: float32 [2048, 2816], P('seq', 'grp')
- grad_conv_w: float32 [16, 4, 176], P('grp', None, 'seq')
- grad_conv_b: float32 [16, 176], P('grp', 'seq')
- grad_gate_a_w: float32 [16, 176, 176], P('grp', 'seq')
- grad_gate_a_b: float32 [16, 176], P('grp', 'seq')
- grad_gate_x_w: float32 [16, 176, 176], P('grp', 'seq')
- grad_gate_x_b: float32 [16, 176], P('grp', 'seq')
- grad_decay_logit: float32 [16, 176], P('grp', 'seq')
- grad_w_out: float32 [2816, 2048], P('grp', 'seq')
- grad_gain_two: float32 [2048], P(('seq', 'grp'))
- grad_mlp_gate: float32 [2048, 6144], P('seq', 'grp')
- grad_mlp_up: float32 [2048, 6144], P('seq', 'grp')
- grad_mlp_down: float32 [6144, 2048], P('grp', 'seq')
All inputs are finite; a program needn't handle non-finite values.
Results may differ from a plain program's by a relative error of at most 0.013.
Values may be sent and summed in bfloat16 or wider, within the bound.
A program may use at most 512 MiB of HBM per device.

v0:
```python
import jax
import jax.numpy as jnp
from jax import lax
from jax.sharding import PartitionSpec as P

epsilon = 1e-06


def matmul(left, right):
    return jnp.dot(left, right, preferred_element_type=jnp.float32)


def matmul_tn(left, right):
    return lax.dot_general(
        left, right, (((0,), (0,)), ((), ())), preferred_element_type=jnp.float32
    )


def matmul_nt(left, right):
    return lax.dot_general(
        left, right, (((1,), (1,)), ((), ())), preferred_element_type=jnp.float32
    )


def combine(earlier, latter):
    return (earlier[0] * latter[0], latter[0] * earlier[1] + latter[1])


def run_scan(decay_rate, drive_term):
    return lax.associative_scan(combine, (decay_rate, drive_term), axis=1)[1]


def norm_back(grad_normed, normal_part, inverse, gain):
    scaled = grad_normed * gain
    return inverse * (scaled - normal_part * jnp.mean(scaled * normal_part, axis=-1, keepdims=True))


def gather_rows(weights):
    return (
        lax.all_gather(weights[0], "seq", axis=0, tiled=True),
        lax.all_gather(weights[1], "seq", axis=0, tiled=True),
        lax.all_gather(weights[2], "seq", axis=1, tiled=True),
    )


def gather_cols(weights):
    return (
        lax.all_gather(weights[0], "grp", axis=1, tiled=True),
        lax.all_gather(weights[1], "grp", axis=1, tiled=True),
        lax.all_gather(weights[2], "grp", axis=0, tiled=True),
    )


def sum_cols(grads):
    return (
        lax.psum_scatter(grads[0], "grp", scatter_dimension=1, tiled=True),
        lax.psum_scatter(grads[1], "grp", scatter_dimension=1, tiled=True),
        lax.psum_scatter(grads[2], "grp", scatter_dimension=0, tiled=True),
    )


def sum_rows(grads):
    return (
        lax.psum_scatter(grads[0], "seq", scatter_dimension=0, tiled=True),
        lax.psum_scatter(grads[1], "seq", scatter_dimension=0, tiled=True),
        lax.psum_scatter(grads[2], "seq", scatter_dimension=1, tiled=True),
    )


def to_heads(values):
    return lax.all_to_all(values, "grp", split_axis=2, concat_axis=1, tiled=True)


def to_positions(values):
    return lax.all_to_all(values, "grp", split_axis=1, concat_axis=2, tiled=True)


def per_device(
    layer_in,
    gain_one,
    w_branch,
    w_rec,
    conv_w,
    conv_b,
    gate_a_w,
    gate_a_b,
    gate_x_w,
    gate_x_b,
    decay_logit,
    w_out,
    gain_two,
    mlp_gate,
    mlp_up,
    mlp_down,
    out_grad,
):
    seqs_here, positions, model_width = layer_in.shape
    tokens_here = seqs_here * positions
    gains = (
        lax.all_gather(gain_one, ("seq", "grp"), axis=0, tiled=True),
        lax.all_gather(gain_two, ("seq", "grp"), axis=0, tiled=True),
    )
    gain_first = gains[0].astype(jnp.float32)
    gain_second = gains[1].astype(jnp.float32)
    mixer_set = gather_rows((w_branch, w_rec, w_out))
    mlp_set = gather_rows((mlp_gate, mlp_up, mlp_down))
    mixer_set = gather_cols(mixer_set)
    mlp_set = gather_cols(mlp_set)
    branch_w, rec_w, out_w = mixer_set
    gate_w, up_w, down_w = mlp_set
    rec_params = (
        lax.all_gather(conv_w, "seq", axis=2, tiled=True),
        lax.all_gather(conv_b, "seq", axis=1, tiled=True),
        lax.all_gather(gate_a_w, "seq", axis=1, tiled=True),
        lax.all_gather(gate_a_b, "seq", axis=1, tiled=True),
        lax.all_gather(gate_x_w, "seq", axis=1, tiled=True),
        lax.all_gather(gate_x_b, "seq", axis=1, tiled=True),
        lax.all_gather(decay_logit, "seq", axis=1, tiled=True),
    )
    taps_full, taps_bias, weight_a, bias_a, weight_x, bias_x, logit_full = rec_params
    heads_here, tap_count, head_dim = taps_full.shape
    channels = heads_here * head_dim
    inputs = layer_in.reshape(tokens_here, model_width).astype(jnp.float32)
    inverse_one = lax.rsqrt(jnp.mean(inputs * inputs, axis=-1, keepdims=True) + epsilon)
    normal_one = inputs * inverse_one
    normed_one = (normal_one * gain_first).astype(jnp.bfloat16)
    gelu_branch, branch_pull = jax.vjp(jax.nn.gelu, matmul(normed_one, branch_w))
    feed = matmul(normed_one, rec_w).astype(jnp.bfloat16).reshape(seqs_here, positions, -1)
    channel_feed = to_heads(feed)
    seq_len = channel_feed.shape[1]
    feed_float = channel_feed.astype(jnp.float32)
    kernel = jnp.transpose(taps_full, (1, 0, 2)).reshape(tap_count, channels).astype(jnp.float32)
    padded = jnp.pad(feed_float, ((0, 0), (tap_count - 1, 0), (0, 0)))
    conv_sum = jnp.zeros((seqs_here, seq_len, channels), jnp.float32) + taps_bias.reshape(
        channels
    ).astype(jnp.float32)
    for offset in range(tap_count):
        start = tap_count - 1 - offset
        conv_sum = conv_sum + kernel[offset] * padded[:, start : start + seq_len]
    conv_low = conv_sum.astype(jnp.bfloat16)
    conv_heads = conv_low.reshape(seqs_here, seq_len, heads_here, head_dim)
    pre_a = jnp.einsum(
        "slhi,hij->slhj", conv_heads, weight_a, preferred_element_type=jnp.float32
    ).reshape(seqs_here, seq_len, channels)
    pre_x = jnp.einsum(
        "slhi,hij->slhj", conv_heads, weight_x, preferred_element_type=jnp.float32
    ).reshape(seqs_here, seq_len, channels)
    rate_gate = jax.nn.sigmoid(pre_a + bias_a.reshape(channels).astype(jnp.float32))
    input_gate = jax.nn.sigmoid(pre_x + bias_x.reshape(channels).astype(jnp.float32))
    logit_float = logit_full.reshape(channels).astype(jnp.float32)
    softness = jax.nn.softplus(-logit_float)
    log_decay = -8.0 * rate_gate * softness
    decay_rate = jnp.exp(log_decay)
    input_scale = jnp.sqrt(-jnp.expm1(2.0 * log_decay))
    conv_float = conv_low.astype(jnp.float32)
    states = run_scan(decay_rate, input_scale * input_gate * conv_float)
    state_low = states.astype(jnp.bfloat16)
    state_float = to_positions(state_low).reshape(tokens_here, -1).astype(jnp.float32)
    mixed_low = (gelu_branch * state_float).astype(jnp.bfloat16)
    residual = inputs + matmul(mixed_low, out_w)
    inverse_two = lax.rsqrt(jnp.mean(residual * residual, axis=-1, keepdims=True) + epsilon)
    normal_two = residual * inverse_two
    normed_two = (normal_two * gain_second).astype(jnp.bfloat16)
    up_proj = matmul(normed_two, up_w)
    gate_act, gate_pull = jax.vjp(jax.nn.gelu, matmul(normed_two, gate_w))
    hidden_low = (gate_act * up_proj).astype(jnp.bfloat16)
    down_term = matmul(hidden_low, down_w)
    layer_sum = residual + down_term
    layer_out = layer_sum.astype(jnp.bfloat16).reshape(layer_in.shape)
    grad_output = out_grad.reshape(tokens_here, model_width)
    grad_down = matmul_tn(hidden_low, grad_output)
    grad_hidden = matmul_nt(grad_output, down_w)
    grad_gate = gate_pull(grad_hidden * up_proj)[0].astype(jnp.bfloat16)
    grad_up = (grad_hidden * gate_act).astype(jnp.bfloat16)
    normed_two_term = matmul_nt(grad_gate, gate_w) + matmul_nt(grad_up, up_w)
    mlp_grads = (matmul_tn(normed_two, grad_gate), matmul_tn(normed_two, grad_up), grad_down)
    mlp_grads = sum_cols(mlp_grads)
    mlp_grads = sum_rows(mlp_grads)
    gain_two_local = jnp.sum(normed_two_term * normal_two, axis=0)
    grad_residual = grad_output.astype(jnp.float32) + norm_back(
        normed_two_term, normal_two, inverse_two, gain_second
    )
    residual_low = grad_residual.astype(jnp.bfloat16)
    out_weight_grad = matmul_tn(mixed_low, residual_low)
    grad_mixed = matmul_nt(residual_low, out_w)
    grad_state = (grad_mixed * gelu_branch).astype(jnp.bfloat16)
    grad_branch = branch_pull(grad_mixed * state_float)[0].astype(jnp.bfloat16)
    channel_grad = to_heads(grad_state.reshape(seqs_here, positions, -1)).astype(jnp.float32)
    next_decay = jnp.concatenate([decay_rate[:, 1:], jnp.zeros_like(decay_rate[:, :1])], axis=1)
    carried = jnp.flip(run_scan(jnp.flip(next_decay, 1), jnp.flip(channel_grad, 1)), 1)
    previous = jnp.concatenate([jnp.zeros_like(states[:, :1]), states[:, :-1]], axis=1)
    grad_scale = carried * input_gate * conv_float
    grad_log = carried * previous * decay_rate - grad_scale * decay_rate * decay_rate / input_scale
    grad_logit = 8.0 * jax.nn.sigmoid(-logit_float) * jnp.sum(grad_log * rate_gate, axis=(0, 1))
    grad_pre_a = -8.0 * softness * grad_log * rate_gate * (1.0 - rate_gate)
    grad_pre_x = carried * input_scale * conv_float * input_gate * (1.0 - input_gate)
    low_a = grad_pre_a.astype(jnp.bfloat16).reshape(seqs_here, seq_len, heads_here, head_dim)
    low_x = grad_pre_x.astype(jnp.bfloat16).reshape(seqs_here, seq_len, heads_here, head_dim)
    grad_weight_a = jnp.einsum(
        "slhi,slhj->hij", conv_heads, low_a, preferred_element_type=jnp.float32
    )
    grad_weight_x = jnp.einsum(
        "slhi,slhj->hij", conv_heads, low_x, preferred_element_type=jnp.float32
    )
    back_gates = jnp.einsum(
        "slhj,hij->slhi", low_a, weight_a, preferred_element_type=jnp.float32
    ) + jnp.einsum("slhj,hij->slhi", low_x, weight_x, preferred_element_type=jnp.float32)
    grad_conv = carried * input_scale * input_gate + back_gates.reshape(
        seqs_here, seq_len, channels
    )
    tap_grads = []
    for offset in range(tap_count):
        start = tap_count - 1 - offset
        tap_grads.append(jnp.sum(grad_conv * padded[:, start : start + seq_len], axis=(0, 1)))
    grad_taps = jnp.transpose(
        jnp.stack(tap_grads, axis=0).reshape(tap_count, heads_here, head_dim), (1, 0, 2)
    )
    grad_padded = jnp.pad(grad_conv, ((0, 0), (0, tap_count - 1), (0, 0)))
    grad_feed = jnp.zeros((seqs_here, seq_len, channels), jnp.float32)
    for offset in range(tap_count):
        grad_feed = grad_feed + kernel[offset] * grad_padded[:, offset : offset + seq_len]
    feed_grad_low = grad_feed.astype(jnp.bfloat16)
    rec_parts = (
        lax.psum_scatter(grad_taps, "seq", scatter_dimension=2, tiled=True),
        lax.psum_scatter(
            jnp.sum(grad_conv, axis=(0, 1)).reshape(heads_here, head_dim),
            "seq",
            scatter_dimension=1,
            tiled=True,
        ),
        lax.psum_scatter(grad_weight_a, "seq", scatter_dimension=1, tiled=True),
        lax.psum_scatter(
            jnp.sum(grad_pre_a, axis=(0, 1)).reshape(heads_here, head_dim),
            "seq",
            scatter_dimension=1,
            tiled=True,
        ),
        lax.psum_scatter(grad_weight_x, "seq", scatter_dimension=1, tiled=True),
        lax.psum_scatter(
            jnp.sum(grad_pre_x, axis=(0, 1)).reshape(heads_here, head_dim),
            "seq",
            scatter_dimension=1,
            tiled=True,
        ),
        lax.psum_scatter(
            grad_logit.reshape(heads_here, head_dim), "seq", scatter_dimension=1, tiled=True
        ),
    )
    feed_rows = to_positions(feed_grad_low).reshape(tokens_here, -1)
    normed_one_term = matmul_nt(grad_branch, branch_w) + matmul_nt(feed_rows, rec_w)
    mixer_grads = (
        matmul_tn(normed_one, grad_branch),
        matmul_tn(normed_one, feed_rows),
        out_weight_grad,
    )
    mixer_grads = sum_cols(mixer_grads)
    mixer_grads = sum_rows(mixer_grads)
    gain_one_local = jnp.sum(normed_one_term * normal_one, axis=0)
    grad_input = grad_residual + norm_back(normed_one_term, normal_one, inverse_one, gain_first)
    gain_parts = (
        lax.psum_scatter(gain_one_local, ("seq", "grp"), scatter_dimension=0, tiled=True),
        lax.psum_scatter(gain_two_local, ("seq", "grp"), scatter_dimension=0, tiled=True),
    )
    return (
        layer_out,
        grad_input.reshape(layer_in.shape),
        gain_parts[0],
        mixer_grads[0],
        mixer_grads[1],
        rec_parts[0],
        rec_parts[1],
        rec_parts[2],
        rec_parts[3],
        rec_parts[4],
        rec_parts[5],
        rec_parts[6],
        mixer_grads[2],
        gain_parts[1],
        mlp_grads[0],
        mlp_grads[1],
        mlp_grads[2],
    )


def solution(mesh):
    placed = (
        P("seq", "grp", None),
        P(("seq", "grp")),
        P("seq", "grp"),
        P("seq", "grp"),
        P("grp", None, "seq"),
        P("grp", "seq"),
        P("grp", "seq", None),
        P("grp", "seq"),
        P("grp", "seq", None),
        P("grp", "seq"),
        P("grp", "seq"),
        P("grp", "seq"),
        P(("seq", "grp")),
        P("seq", "grp"),
        P("seq", "grp"),
        P("grp", "seq"),
        P("seq", "grp", None),
    )
    return jax.shard_map(
        per_device,
        mesh=mesh,
        in_specs=placed,
        out_specs=(
            P("seq", "grp", None),
            P("seq", "grp", None),
            P(("seq", "grp")),
            P("seq", "grp"),
            P("seq", "grp"),
            P("grp", None, "seq"),
            P("grp", "seq"),
            P("grp", "seq", None),
            P("grp", "seq"),
            P("grp", "seq", None),
            P("grp", "seq"),
            P("grp", "seq"),
            P("grp", "seq"),
            P(("seq", "grp")),
            P("seq", "grp"),
            P("seq", "grp"),
            P("grp", "seq"),
        ),
        check_vma=False,
    )
```

profile of v0, /device:TPU:0, one launch (start us, length us, event | category | flops | bytes accessed | tf_op | source)
XLA Modules:
  0.0 3948.6 jit_solution(10119081302056198352)
XLA Ops:
  11.2 31.1 all-gather.21.cloned.1.call-done
  42.4 31.5 all-gather.17.cloned.1.call-done
  74.0 31.5 all-gather.25.cloned.1.call-done
  105.6 45.6 %all-gather.33.cloned.1.call-done = bf16[2048,768]{1,0:T(8,128)(2,1)} async-done(((bf16[512,768]{1,0:T(8,128)(2,1)}), bf16[2048,768]{1,0:T(8,128)(2,1)}) %all-gather.33.cloned.1.call-update) | async-done | bytes 3145744 | tf_op jit(solution)/shard_map/all_gather | solution.py:41
  151.3 45.6 %all-gather.29.cloned.1.call-done = bf16[2048,768]{1,0:T(8,128)(2,1)} async-done(((bf16[512,768]{1,0:T(8,128)(2,1)}), bf16[2048,768]{1,0:T(8,128)(2,1)}) %all-gather.29.cloned.1.call-update) | async-done | bytes 3145744 | tf_op jit(solution)/shard_map/all_gather | solution.py:40
  197.1 45.4 %all-gather.37.cloned.1.call-done = bf16[768,2048]{1,0:T(8,128)(2,1)} async-done(((bf16[768,512]{1,0:T(8,128)(2,1)}), bf16[768,2048]{1,0:T(8,128)(2,1)}) %all-gather.37.cloned.1.call-update) | async-done | bytes 3145744 | tf_op jit(solution)/shard_map/all_gather | solution.py:42
  243.8 47.1 %all-reduce.54 = (bf16[2048]{0:T(1024)(128)(2,1)S(1)}, bf16[2048]{0:T(1024)(128)(2,1)S(1)}) all-reduce(bf16[2048]{0:T(1024)(128)(2,1)S(1)} %dynamic-update-slice, bf16[2048]{0:T(1024)(128)(2,1)S(1)} %dynamic-update-slice.1), channel_id=1, replica_groups=mesh['seq'=4,'grp'=8] {'seq','grp'}, use_global_device_ids=true, to_apply=%add.40 | all-reduce | flops 4096 | bytes 16384
  292.9 60.3 %all-gather.23.cloned.1.call-done = bf16[2048,2816]{0,1:T(8,128)(2,1)} async-done(((bf16[2048,352]{0,1:T(8,128)(2,1)}), bf16[2048,2816]{0,1:T(8,128)(2,1)}) %all-gather.23.cloned.1.call-update) | async-done | bytes 11534352 | tf_op jit(solution)/shard_map/all_gather | solution.py:49
  409.2 9.8 all_gather.70
  427.7 14.6 all-to-all-done
  532.4 61.1 %all-to-all-done.1 = bf16[2,768,352]{2,0,1:T(2,128)(2,1)S(1)} async-done(((bf16[2,768,352]{2,0,1:T(2,128)(2,1)}), bf16[2,768,352]{2,0,1:T(2,128)(2,1)S(1)}, u32[]{:S(2)}, u32[]{:S(2)}) %all-to-all-start.1) | async-done | bytes 1081376 | tf_op jit(solution)/shard_map/all_to_all | solution.py:75
  597.1 11.1 multiply_convert_fusion.3
  608.2 16.7 all-gather.27.cloned.1.call-done
  632.3 212.2 %all-gather.35.cloned.1.call-done = bf16[2048,6144]{1,0:T(8,128)(2,1)} async-done(((bf16[2048,768]{1,0:T(8,128)(2,1)}), bf16[2048,6144]{1,0:T(8,128)(2,1)}) %all-gather.35.cloned.1.call-update) | async-done | bytes 25165840 | tf_op jit(solution)/shard_map/all_gather | solution.py:49
  844.5 14.6 fusion.78
  859.1 205.1 %all-gather.31.cloned.1.call-done = bf16[2048,6144]{1,0:T(8,128)(2,1)} async-done(((bf16[2048,768]{1,0:T(8,128)(2,1)}), bf16[2048,6144]{1,0:T(8,128)(2,1)}) %all-gather.31.cloned.1.call-update) | async-done | bytes 25165840 | tf_op jit(solution)/shard_map/all_gather | solution.py:48
  1064.2 14.8 fusion.77
  1079.0 204.7 %all-gather.39.cloned.1.call-done = bf16[6144,2048]{1,0:T(8,128)(2,1)} async-done(((bf16[768,2048]{1,0:T(8,128)(2,1)}), bf16[6144,2048]{1,0:T(8,128)(2,1)}) %all-gather.39.cloned.1.call-update) | async-done | bytes 25165840 | tf_op jit(solution)/shard_map/all_gather | solution.py:50
  1283.8 19.4 multiply_convert_fusion
  1303.2 14.7 fusion.79
  1317.9 15.8 multiply_reduce_fusion.5
  1335.9 9.4 fusion.30
  1345.4 11.7 multiply_convert_fusion.2
  1358.1 9.7 fusion.81
  1394.5 10.2 slice.574
  1404.7 9.8 slice.576
  1417.8 16.2 all-to-all-done.2
  1453.8 9.9 slice.578
  1503.3 18.9 rev.6
  1522.2 9.4 fusion.57
  1559.7 47.4 %all-to-all-done.3 = bf16[2,768,352]{2,0,1:T(2,128)(2,1)S(1)} async-done(((bf16[2,768,352]{2,0,1:T(2,128)(2,1)}), bf16[2,768,352]{2,0,1:T(2,128)(2,1)S(1)}, u32[]{:S(2)}, u32[]{:S(2)}) %all-to-all-start.3) | async-done | bytes 1081376 | tf_op jit(solution)/shard_map/all_to_all | solution.py:75
  1611.1 10.9 fusion.82
  1623.1 22.5 fusion.84
  1645.7 21.6 fusion.83
  1668.4 21.7 fusion.85
  1696.2 158.2 %reduce-scatter.18.cloned.1.call-done = f32[2048,352]{0,1:T(8,128)} async-done(((f32[2048,2816]{0,1:T(8,128)}), f32[2048,352]{0,1:T(8,128)}) %reduce-scatter.18.cloned.1.call-update) | async-done | bytes 2883600 | tf_op jit(solution)/shard_map/reduce_scatter | solution.py:56
  1854.5 228.0 %reduce-scatter.22.cloned.1.call-done = f32[2048,352]{0,1:T(8,128)} async-done(((f32[2048,2816]{0,1:T(8,128)}), f32[2048,352]{0,1:T(8,128)}) %reduce-scatter.22.cloned.1.call-update) | async-done | bytes 2883600 | tf_op jit(solution)/shard_map/reduce_scatter | solution.py:57
  2082.5 483.7 %reduce-scatter.34.cloned.1.call-done = f32[2048,768]{1,0:T(8,128)} async-done(((f32[2048,6144]{1,0:T(8,128)}), f32[2048,768]{1,0:T(8,128)}) %reduce-scatter.34.cloned.1.call-update) | async-done | bytes 6291472 | tf_op jit(solution)/shard_map/reduce_scatter | solution.py:57
  2566.3 483.8 %reduce-scatter.30.cloned.1.call-done = f32[2048,768]{1,0:T(8,128)} async-done(((f32[2048,6144]{1,0:T(8,128)}), f32[2048,768]{1,0:T(8,128)}) %reduce-scatter.30.cloned.1.call-update) | async-done | bytes 6291472 | tf_op jit(solution)/shard_map/reduce_scatter | solution.py:56
  3050.4 483.4 %reduce-scatter.38.cloned.1.call-done = f32[768,2048]{1,0:T(8,128)} async-done(((f32[6144,2048]{1,0:T(8,128)}), f32[768,2048]{1,0:T(8,128)}) %reduce-scatter.38.cloned.1.call-update) | async-done | bytes 6291472 | tf_op jit(solution)/shard_map/reduce_scatter | solution.py:58
  3543.8 12.1 fusion.7
  3556.6 16.0 all-reduce.52
  3594.2 39.8 %all-reduce.51 = (f32[2048]{0:T(1024)S(1)}, f32[2048]{0:T(1024)S(1)}) all-reduce(f32[2048]{0:T(1024)S(1)} %get-tuple-element.77, f32[2048]{0:T(1024)S(1)} %copy-done.65), channel_id=2, replica_groups=mesh['seq'=4,'grp'=8] {'seq','grp'}, use_global_device_ids=true, to_apply=%region_5.6.clone | all-reduce | flops 4096 | bytes 32768
  3638.1 36.9 reduce-scatter.20.cloned.1.call-done
  3675.0 45.4 %reduce-scatter.24.cloned.1.call-done = f32[512,352]{0,1:T(8,128)} async-done(((f32[2048,352]{0,1:T(8,128)}), f32[512,352]{0,1:T(8,128)}) %reduce-scatter.24.cloned.1.call-update) | async-done | bytes 720912 | tf_op jit(solution)/shard_map/reduce_scatter | solution.py:65
  3720.4 73.8 %reduce-scatter.36.cloned.1.call-done = f32[512,768]{1,0:T(8,128)} async-done(((f32[2048,768]{1,0:T(8,128)}), f32[512,768]{1,0:T(8,128)}) %reduce-scatter.36.cloned.1.call-update) | async-done | bytes 1572880 | tf_op jit(solution)/shard_map/reduce_scatter | solution.py:65
  3794.2 73.6 %reduce-scatter.32.cloned.1.call-done = f32[512,768]{1,0:T(8,128)} async-done(((f32[2048,768]{1,0:T(8,128)}), f32[512,768]{1,0:T(8,128)}) %reduce-scatter.32.cloned.1.call-update) | async-done | bytes 1572880 | tf_op jit(solution)/shard_map/reduce_scatter | solution.py:64
  3867.8 73.8 %reduce-scatter.40.cloned.1.call-done = f32[768,512]{1,0:T(8,128)} async-done(((f32[768,2048]{1,0:T(8,128)}), f32[768,512]{1,0:T(8,128)}) %reduce-scatter.40.cloned.1.call-update) | async-done | bytes 1572880 | tf_op jit(solution)/shard_map/reduce_scatter | solution.py:66
  (541 shorter events, 340.5 us)
Async XLA Ops:
  7.2 35.1 all-gather.21.cloned.1.call-start
  7.9 66.0 %all-gather.17.cloned.1.call-start = ((), (), s32[]{:S(2)}) async-start(), calls=%async_computation.16 | async-start | bytes 1802240 | tf_op jit(solution)/shard_map/all_gather | solution.py:40
  8.7 96.9 %all-gather.25.cloned.1.call-start = ((), (), s32[]{:S(2)}) async-start(), calls=%async_computation.20 | async-start | bytes 1802240 | tf_op jit(solution)/shard_map/all_gather | solution.py:42
  9.4 141.9 %all-gather.33.cloned.1.call-start = ((), (), s32[]{:S(2)}) async-start(), calls=%async_computation.24 | async-start | bytes 3932160 | tf_op jit(solution)/shard_map/all_gather | solution.py:41
  10.0 187.0 %all-gather.29.cloned.1.call-start = ((), (), s32[]{:S(2)}) async-start(), calls=%async_computation.22 | async-start | bytes 3932160 | tf_op jit(solution)/shard_map/all_gather | solution.py:40
  10.6 231.9 %all-gather.37.cloned.1.call-start = ((), (), s32[]{:S(2)}) async-start(), calls=%async_computation.26 | async-start | bytes 3932160 | tf_op jit(solution)/shard_map/all_gather | solution.py:42
  11.1 342.1 %all-gather.23.cloned.1.call-start = ((), (), s32[]{:S(2)}) async-start(), calls=%async_computation.19 | async-start | bytes 12976128 | tf_op jit(solution)/shard_map/all_gather | solution.py:49
  42.4 554.8 %all-gather.19.cloned.1.call-start = ((), (), s32[]{:S(2)}) async-start(), calls=%async_computation.17 | async-start | bytes 12976128 | tf_op jit(solution)/shard_map/all_gather | solution.py:48
  74.0 550.9 %all-gather.27.cloned.1.call-start = ((), (), s32[]{:S(2)}) async-start(), calls=%async_computation.21 | async-start | bytes 12976128 | tf_op jit(solution)/shard_map/all_gather | solution.py:50
  105.6 738.9 %all-gather.35.cloned.1.call-start = ((), (), s32[]{:S(2)}) async-start(), calls=%async_computation.25 | async-start | bytes 28311552 | tf_op jit(solution)/shard_map/all_gather | solution.py:49
  151.3 912.9 %all-gather.31.cloned.1.call-start = ((), (), s32[]{:S(2)}) async-start(), calls=%async_computation.23 | async-start | bytes 28311552 | tf_op jit(solution)/shard_map/all_gather | solution.py:48
  197.0 45.6 %copy-start.11 = (bf16[2,96,2048]{2,1,0:T(8,128)(2,1)S(1)}, bf16[2,96,2048]{2,1,0:T(8,128)(2,1)}, u32[]{:S(2)}) copy-start(bf16[2,96,2048]{2,1,0:T(8,128)(2,1)} %param.17) | copy-start | bytes 2359300
  197.0 46.4 %copy-start.74 = (bf16[64]{0:T(256)(128)(2,1)S(1)}, bf16[64]{0:T(256)(128)(2,1)}, u32[]{:S(2)}) copy-start(bf16[64]{0:T(256)(128)(2,1)} %param.18) | copy-start | bytes 388
  197.0 46.6 %copy-start.75 = (bf16[64]{0:T(256)(128)(2,1)S(1)}, bf16[64]{0:T(256)(128)(2,1)}, u32[]{:S(2)}) copy-start(bf16[64]{0:T(256)(128)(2,1)} %param.29) | copy-start | bytes 388
  197.0 1086.8 %all-gather.39.cloned.1.call-start = ((), (), s32[]{:S(2)}) async-start(), calls=%async_computation.27 | async-start | bytes 28311552 | tf_op jit(solution)/shard_map/all_gather | solution.py:50
  242.9 110.4 %copy-start.61 = (f32[192]{0:T(256)}, f32[192]{0:T(256)S(1)}, u32[]{:S(2)}) copy-start(f32[192]{0:T(256)S(1)} %rsqrt.21) | copy-start | bytes 2308
  292.9 68.6 %copy-start.28 = (bf16[192,2048]{1,0:T(8,128)(2,1)}, bf16[192,2048]{1,0:T(8,128)(2,1)S(1)}, u32[]{:S(2)}) copy-start(bf16[192,2048]{1,0:T(8,128)(2,1)S(1)} %get-tuple-element.113) | copy-start | bytes 2359300
  364.5 44.7 %copy-start.55 = (bf16[2,44,176]{2,0,1:T(2,128)(2,1)S(1)}, bf16[2,44,176]{2,0,1:T(2,128)(2,1)}, u32[]{:S(2)}) copy-start(bf16[2,44,176]{2,0,1:T(2,128)(2,1)} %param.23) | copy-start | bytes 92932
  364.5 54.5 %copy-start.56 = (bf16[2,44,176]{2,0,1:T(2,128)(2,1)S(1)}, bf16[2,44,176]{2,0,1:T(2,128)(2,1)}, u32[]{:S(2)}) copy-start(bf16[2,44,176]{2,0,1:T(2,128)(2,1)} %param.25) | copy-start | bytes 92932
  364.5 77.7 %all-to-all-start = ((bf16[2,96,2816]{1,0,2:T(2,128)(2,1)}), bf16[2,96,2816]{1,0,2:T(2,128)(2,1)S(1)}, u32[]{:S(2)}, u32[]{:S(2)}) async-start(bf16[2,96,2816]{1,0,2:T(2,128)(2,1)} %copy.171), calls=%async_computation | async-start | bytes 2883584 | tf_op jit(solution)/shard_map/all_to_all | solution.py:71
  376.3 88.8 %copy-start.59 = (f32[352]{0:T(512)}, f32[352]{0:T(512)S(1)}, u32[]{:S(2)}) copy-start(f32[352]{0:T(512)S(1)} %reshape.228) | copy-start | bytes 4228
  384.3 80.7 %copy-start.43 = (f32[352]{0:T(512)}, f32[352]{0:T(512)S(1)}, u32[]{:S(2)}) copy-start(f32[352]{0:T(512)S(1)} %reshape.230) | copy-start | bytes 4228
  391.5 73.6 %copy-start.57 = (f32[352]{0:T(512)}, f32[352]{0:T(512)S(1)}, u32[]{:S(2)}) copy-start(f32[352]{0:T(512)S(1)} %reshape.231) | copy-start | bytes 4228
  408.6 56.5 %copy-start.45 = (f32[352]{0:T(512)}, f32[352]{0:T(512)S(1)}, u32[]{:S(2)}) copy-start(f32[352]{0:T(512)S(1)} %mul.540) | copy-start | bytes 4228
  408.8 56.3 %copy-start.47 = (f32[352]{0:T(512)}, f32[352]{0:T(512)S(1)}, u32[]{:S(2)}) copy-start(f32[352]{0:T(512)S(1)} %mul.549) | copy-start | bytes 4228
  409.0 56.1 %copy-start.49 = (f32[352]{0:T(512)}, f32[352]{0:T(512)S(1)}, u32[]{:S(2)}) copy-start(f32[352]{0:T(512)S(1)} %mul.546) | copy-start | bytes 4228
  409.2 55.9 %copy-start.51 = (f32[352]{0:T(512)}, f32[352]{0:T(512)S(1)}, u32[]{:S(2)}) copy-start(f32[352]{0:T(512)S(1)} %mul.543) | copy-start | bytes 4228
  528.8 64.7 %all-to-all-start.1 = ((bf16[2,768,352]{2,0,1:T(2,128)(2,1)}), bf16[2,768,352]{2,0,1:T(2,128)(2,1)S(1)}, u32[]{:S(2)}, u32[]{:S(2)}) async-start(bf16[2,768,352]{2,0,1:T(2,128)(2,1)} %copy.189), calls=%async_computation.1 | async-start | bytes 2359296 | tf_op jit(solution)/shard_map/all_to_all | solution.py:75
  532.3 1163.3 %reduce-scatter.26.cloned.1.call-start = ((), (), s32[]{:S(2)}) async-start(), calls=%async_computation.32 | async-start | bytes 25952256 | tf_op jit(solution)/shard_map/reduce_scatter | solution.py:58
  632.1 701.7 %copy-start.17 = (f32[192,2048]{1,0:T(8,128)}, f32[192,2048]{1,0:T(8,128)S(1)}, u32[]{:S(2)}) copy-start(f32[192,2048]{1,0:T(8,128)S(1)} %get-tuple-element.153) | copy-start | bytes 4718596
  632.3 431.9 %copy-start.15 = (bf16[192,2048]{1,0:T(8,128)(2,1)}, bf16[192,2048]{1,0:T(8,128)(2,1)S(1)}, u32[]{:S(2)}) copy-start(bf16[192,2048]{1,0:T(8,128)(2,1)S(1)} %multiply_convert_fusion.5) | copy-start | bytes 2359300
  859.1 424.7 %copy-start.31 = (bf16[2,96,2048]{2,1,0:T(8,128)(2,1)S(1)}, bf16[2,96,2048]{2,1,0:T(8,128)(2,1)}, u32[]{:S(2)}) copy-start(bf16[2,96,2048]{2,1,0:T(8,128)(2,1)} %param.33) | copy-start | bytes 2359300
  1345.4 509.1 %reduce-scatter.18.cloned.1.call-start = ((), (), s32[]{:S(2)}) async-start(), calls=%async_computation.28 | async-start | bytes 25952256 | tf_op jit(solution)/shard_map/reduce_scatter | solution.py:56
  1370.8 63.2 %all-to-all-start.2 = ((bf16[2,96,2816]{1,0,2:T(2,128)(2,1)}), bf16[2,96,2816]{1,0,2:T(2,128)(2,1)}, u32[]{:S(2)}, u32[]{:S(2)}) async-start(bf16[2,96,2816]{1,0,2:T(2,128)(2,1)} %copy.192), calls=%async_computation.2 | async-start | bytes 2883584 | tf_op jit(solution)/shard_map/all_to_all | solution.py:71
  1555.0 52.2 %all-to-all-start.3 = ((bf16[2,768,352]{2,0,1:T(2,128)(2,1)}), bf16[2,768,352]{2,0,1:T(2,128)(2,1)S(1)}, u32[]{:S(2)}, u32[]{:S(2)}) async-start(bf16[2,768,352]{2,0,1:T(2,128)(2,1)} %copy.203), calls=%async_computation.3 | async-start | bytes 2359296 | tf_op jit(solution)/shard_map/all_to_all | solution.py:75
  1558.5 523.9 %reduce-scatter.22.cloned.1.call-start = ((), (), s32[]{:S(2)}) async-start(), calls=%async_computation.30 | async-start | bytes 25952256 | tf_op jit(solution)/shard_map/reduce_scatter | solution.py:57
  1622.0 944.2 %reduce-scatter.34.cloned.1.call-start = ((), (), s32[]{:S(2)}) async-start(), calls=%async_computation.36 | async-start | bytes 56623104 | tf_op jit(solution)/shard_map/reduce_scatter | solution.py:57
  1645.7 1404.4 %reduce-scatter.30.cloned.1.call-start = ((), (), s32[]{:S(2)}) async-start(), calls=%async_computation.34 | async-start | bytes 56623104 | tf_op jit(solution)/shard_map/reduce_scatter | solution.py:56
  1667.3 1866.5 %reduce-scatter.38.cloned.1.call-start = ((), (), s32[]{:S(2)}) async-start(), calls=%async_computation.38 | async-start | bytes 56623104 | tf_op jit(solution)/shard_map/reduce_scatter | solution.py:58
  1690.1 1893.4 %all-reduce.57.cloned.1.call-start = ((), (), s32[]{:S(2)}) async-start(), calls=%async_computation.40 | async-start | bytes 1441792
  1695.6 1942.6 %reduce-scatter.28.cloned.1.call-start = ((), (), s32[]{:S(2)}) async-start(), calls=%async_computation.33 | async-start | bytes 3604480 | tf_op jit(solution)/shard_map/reduce_scatter | solution.py:66
  1696.1 1978.8 %reduce-scatter.20.cloned.1.call-start = ((), (), s32[]{:S(2)}) async-start(), calls=%async_computation.29 | async-start | bytes 3604480 | tf_op jit(solution)/shard_map/reduce_scatter | solution.py:64
  1854.4 1865.9 %reduce-scatter.24.cloned.1.call-start = ((), (), s32[]{:S(2)}) async-start(), calls=%async_computation.31 | async-start | bytes 3604480 | tf_op jit(solution)/shard_map/reduce_scatter | solution.py:65
  2082.5 1711.7 %reduce-scatter.36.cloned.1.call-start = ((), (), s32[]{:S(2)}) async-start(), calls=%async_computation.37 | async-start | bytes 7864320 | tf_op jit(solution)/shard_map/reduce_scatter | solution.py:65
  2566.2 1301.6 %reduce-scatter.32.cloned.1.call-start = ((), (), s32[]{:S(2)}) async-start(), calls=%async_computation.35 | async-start | bytes 7864320 | tf_op jit(solution)/shard_map/reduce_scatter | solution.py:64
  3050.1 891.5 %reduce-scatter.40.cloned.1.call-start = ((), (), s32[]{:S(2)}) async-start(), calls=%async_computation.39 | async-start | bytes 7864320 | tf_op jit(solution)/shard_map/reduce_scatter | solution.py:66
  3543.8 41.3 %copy-start.26 = (bf16[192,2816]{1,0:T(8,128)(2,1)S(1)}, bf16[192,2816]{1,0:T(8,128)(2,1)}, u32[]{:S(2)}) copy-start(bf16[192,2816]{1,0:T(8,128)(2,1)} %copy-done.25) | copy-start | bytes 3244036
  3585.1 50.0 %copy-start.10 = (f32[192,2048]{1,0:T(8,128)S(1)}, f32[192,2048]{1,0:T(8,128)}, u32[]{:S(2)}) copy-start(f32[192,2048]{1,0:T(8,128)} %copy-done.9) | copy-start | bytes 4718596
  (58 other events, 545.1 us)
Sparse Core Ops, SparseCore 0:
  9.8 32.4 all-gather.20
  44.1 29.7 all-gather.16
  75.8 29.7 all-gather.24
  107.2 43.9 all-gather.32
  152.9 43.9 all-gather.28
  198.6 43.8 all-gather.36
  244.1 109.0 all-gather.22
  354.9 136.9 all-gather.18
  493.6 131.2 all-gather.26
  626.4 218.0 all-gather.34
  846.1 218.0 all-gather.30
  1065.7 218.0 all-gather.38
  1345.5 267.7 reduce-scatter.25
  1615.5 238.8 reduce-scatter.17
  1856.6 225.7 reduce-scatter.21
  2084.7 481.4 reduce-scatter.33
  2568.6 481.4 reduce-scatter.29
  3052.3 481.4 reduce-scatter.37
  3537.1 46.3 all-reduce.56
  3587.0 42.5 reduce-scatter.27
  3633.1 41.8 reduce-scatter.19
  3678.6 41.7 reduce-scatter.23
  3723.9 70.2 reduce-scatter.35
  3797.6 70.1 reduce-scatter.31
  3871.4 70.1 reduce-scatter.39
where the time goes:
time: 3960 us; the launch traced here: 3950 us
  waiting for transfers between devices  3220 us (81%)
  matrix products  249 us (6%)
  local copies, waits for them, and re-layouts  225 us (6%)
  blocking collectives  159 us (4%)
  other arithmetic  57.1 us (1%)
    reduce_scatter x2, waiting for transfers between devices, sum_cols(): lax.psum_scatter(grads[1], 'grp', scatter_dimension=1, tiled=True)  712 us
    reduce_scatter x2, waiting for transfers between devices, sum_cols(): lax.psum_scatter(grads[0], 'grp', scatter_dimension=1, tiled=True)  642 us
    reduce_scatter x2, waiting for transfers between devices, sum_cols(): lax.psum_scatter(grads[2], 'grp', scatter_dimension=0, tiled=True)  483 us
    all_gather x2, waiting for transfers between devices, gather_cols(): lax.all_gather(weights[1], 'grp', axis=1, tiled=True)  273 us
    all_gather x2, waiting for transfers between devices, gather_cols(): lax.all_gather(weights[2], 'grp', axis=0, tiled=True)  221 us
    all_gather x2, waiting for transfers between devices, gather_cols(): lax.all_gather(weights[0], 'grp', axis=1, tiled=True)  205 us
    reduce_scatter x2, waiting for transfers between devices, sum_rows(): lax.psum_scatter(grads[1], 'seq', scatter_dimension=0, tiled=True)  119 us
    slice x118, local copies, waits for them, and re-layouts, run_scan(): return lax.associative_scan(combine, (decay_rate, drive_term), axis=1)[1]  118 us
  transfers between devices with their start and end apart: 29, of which 26 were waited for; matrix products, arithmetic and copies ran while one was open for 12% of the time, Pallas kernels for 0%

commit v1 on v0

--- a/solution.py
+++ b/solution.py
@@ -43,36 +43,29 @@
     )
 
 
-def gather_cols(weights):
+def gather_tokens(values):
+    return jnp.stack(
+        [lax.all_gather(values[s], "grp", axis=0, tiled=True) for s in range(values.shape[0])]
+    ).reshape(-1, values.shape[-1])
+
+
+def scatter_tokens(values, seqs_here):
+    parts = values.astype(jnp.bfloat16).reshape(seqs_here, -1, values.shape[-1])
+    return jnp.concatenate(
+        [
+            lax.psum_scatter(parts[s], "grp", scatter_dimension=0, tiled=True)
+            for s in range(seqs_here)
+        ]
+    ).astype(jnp.float32)
+
+
+def sum_rows(grads):
+    low = [grad.astype(jnp.bfloat16) for grad in grads]
     return (
-        lax.all_gather(weights[0], "grp", axis=1, tiled=True),
-        lax.all_gather(weights[1], "grp", axis=1, tiled=True),
-        lax.all_gather(weights[2], "grp", axis=0, tiled=True),
-    )
-
-
-def sum_cols(grads):
-    return (
-        lax.psum_scatter(grads[0], "grp", scatter_dimension=1, tiled=True),
-        lax.psum_scatter(grads[1], "grp", scatter_dimension=1, tiled=True),
-        lax.psum_scatter(grads[2], "grp", scatter_dimension=0, tiled=True),
-    )
-
-
-def sum_rows(grads):
-    return (
-        lax.psum_scatter(grads[0], "seq", scatter_dimension=0, tiled=True),
-        lax.psum_scatter(grads[1], "seq", scatter_dimension=0, tiled=True),
-        lax.psum_scatter(grads[2], "seq", scatter_dimension=1, tiled=True),
-    )
-
-
-def to_heads(values):
-    return lax.all_to_all(values, "grp", split_axis=2, concat_axis=1, tiled=True)
-
-
-def to_positions(values):
-    return lax.all_to_all(values, "grp", split_axis=1, concat_axis=2, tiled=True)
+        lax.psum_scatter(low[0], "seq", scatter_dimension=0, tiled=True).astype(jnp.float32),
+        lax.psum_scatter(low[1], "seq", scatter_dimension=0, tiled=True).astype(jnp.float32),
+        lax.psum_scatter(low[2], "seq", scatter_dimension=1, tiled=True).astype(jnp.float32),
+    )
 
 
 def per_device(
@@ -104,8 +97,6 @@
     gain_second = gains[1].astype(jnp.float32)
     mixer_set = gather_rows((w_branch, w_rec, w_out))
     mlp_set = gather_rows((mlp_gate, mlp_up, mlp_down))
-    mixer_set = gather_cols(mixer_set)
-    mlp_set = gather_cols(mlp_set)
     branch_w, rec_w, out_w = mixer_set
     gate_w, up_w, down_w = mlp_set
     rec_params = (
@@ -123,10 +114,10 @@
     inputs = layer_in.reshape(tokens_here, model_width).astype(jnp.float32)
     inverse_one = lax.rsqrt(jnp.mean(inputs * inputs, axis=-1, keepdims=True) + epsilon)
     normal_one = inputs * inverse_one
-    normed_one = (normal_one * gain_first).astype(jnp.bfloat16)
+    normed_own = (normal_one * gain_first).astype(jnp.bfloat16)
+    normed_one = gather_tokens(normed_own.reshape(layer_in.shape))
     gelu_branch, branch_pull = jax.vjp(jax.nn.gelu, matmul(normed_one, branch_w))
-    feed = matmul(normed_one, rec_w).astype(jnp.bfloat16).reshape(seqs_here, positions, -1)
-    channel_feed = to_heads(feed)
+    channel_feed = matmul(normed_one, rec_w).astype(jnp.bfloat16).reshape(seqs_here, -1, channels)
     seq_len = channel_feed.shape[1]
     feed_float = channel_feed.astype(jnp.float32)
     kernel = jnp.transpose(taps_full, (1, 0, 2)).reshape(tap_count, channels).astype(jnp.float32)
@@ -155,37 +146,41 @@
     conv_float = conv_low.astype(jnp.float32)
     states = run_scan(decay_rate, input_scale * input_gate * conv_float)
     state_low = states.astype(jnp.bfloat16)
-    state_float = to_positions(state_low).reshape(tokens_here, -1).astype(jnp.float32)
+    state_float = state_low.reshape(-1, channels).astype(jnp.float32)
     mixed_low = (gelu_branch * state_float).astype(jnp.bfloat16)
-    residual = inputs + matmul(mixed_low, out_w)
+    residual = inputs + scatter_tokens(matmul(mixed_low, out_w), seqs_here)
     inverse_two = lax.rsqrt(jnp.mean(residual * residual, axis=-1, keepdims=True) + epsilon)
     normal_two = residual * inverse_two
-    normed_two = (normal_two * gain_second).astype(jnp.bfloat16)
+    normed_two_own = (normal_two * gain_second).astype(jnp.bfloat16)
+    normed_two = gather_tokens(normed_two_own.reshape(layer_in.shape))
     up_proj = matmul(normed_two, up_w)
     gate_act, gate_pull = jax.vjp(jax.nn.gelu, matmul(normed_two, gate_w))
     hidden_low = (gate_act * up_proj).astype(jnp.bfloat16)
-    down_term = matmul(hidden_low, down_w)
+    down_term = scatter_tokens(matmul(hidden_low, down_w), seqs_here)
     layer_sum = residual + down_term
     layer_out = layer_sum.astype(jnp.bfloat16).reshape(layer_in.shape)
-    grad_output = out_grad.reshape(tokens_here, model_width)
+    grad_output = gather_tokens(out_grad)
     grad_down = matmul_tn(hidden_low, grad_output)
     grad_hidden = matmul_nt(grad_output, down_w)
     grad_gate = gate_pull(grad_hidden * up_proj)[0].astype(jnp.bfloat16)
     grad_up = (grad_hidden * gate_act).astype(jnp.bfloat16)
-    normed_two_term = matmul_nt(grad_gate, gate_w) + matmul_nt(grad_up, up_w)
+    normed_two_term = scatter_tokens(
+        matmul_nt(grad_gate, gate_w) + matmul_nt(grad_up, up_w), seqs_here
+    )
     mlp_grads = (matmul_tn(normed_two, grad_gate), matmul_tn(normed_two, grad_up), grad_down)
-    mlp_grads = sum_cols(mlp_grads)
     mlp_grads = sum_rows(mlp_grads)
     gain_two_local = jnp.sum(normed_two_term * normal_two, axis=0)
-    grad_residual = grad_output.astype(jnp.float32) + norm_back(
+    grad_own = out_grad.reshape(tokens_here, model_width).astype(jnp.float32)
+    grad_residual = grad_own + norm_back(
         normed_two_term, normal_two, inverse_two, gain_second
     )
-    residual_low = grad_residual.astype(jnp.bfloat16)
+    residual_own = grad_residual.astype(jnp.bfloat16)
+    residual_low = gather_tokens(residual_own.reshape(layer_in.shape))
     out_weight_grad = matmul_tn(mixed_low, residual_low)
     grad_mixed = matmul_nt(residual_low, out_w)
     grad_state = (grad_mixed * gelu_branch).astype(jnp.bfloat16)
     grad_branch = branch_pull(grad_mixed * state_float)[0].astype(jnp.bfloat16)
-    channel_grad = to_heads(grad_state.reshape(seqs_here, positions, -1)).astype(jnp.float32)
+    channel_grad = grad_state.reshape(seqs_here, seq_len, channels).astype(jnp.float32)
     next_decay = jnp.concatenate([decay_rate[:, 1:], jnp.zeros_like(decay_rate[:, :1])], axis=1)
     carried = jnp.flip(run_scan(jnp.flip(next_decay, 1), jnp.flip(channel_grad, 1)), 1)
     previous = jnp.concatenate([jnp.zeros_like(states[:, :1]), states[:, :-1]], axis=1)
@@ -246,14 +241,15 @@
             grad_logit.reshape(heads_here, head_dim), "seq", scatter_dimension=1, tiled=True
         ),
     )
-    feed_rows = to_positions(feed_grad_low).reshape(tokens_here, -1)
-    normed_one_term = matmul_nt(grad_branch, branch_w) + matmul_nt(feed_rows, rec_w)
+    feed_rows = feed_grad_low.reshape(-1, channels)
+    normed_one_term = scatter_tokens(
+        matmul_nt(grad_branch, branch_w) + matmul_nt(feed_rows, rec_w), seqs_here
+    )
     mixer_grads = (
         matmul_tn(normed_one, grad_branch),
         matmul_tn(normed_one, feed_rows),
         out_weight_grad,
     )
-    mixer_grads = sum_cols(mixer_grads)
     mixer_grads = sum_rows(mixer_grads)
     gain_one_local = jnp.sum(normed_one_term * normal_one, axis=0)
     grad_input = grad_residual + norm_back(normed_one_term, normal_one, inverse_one, gain_first)

time: 3960 us -> 2270 us (0.57)
  waiting for transfers between devices: 3220 us -> 627 us
  local copies, waits for them, and re-layouts: 225 us -> 1120 us
  other arithmetic: 57.1 us -> 184 us
  matrix products: 249 us -> 146 us
    reduce_scatter x12 -> x14, waiting for transfers between devices: 2140 us -> 293 us  [the longest x8 242 us: scatter_tokens(): lax.psum_scatter(parts[s], 'grp', scatter_dimension=0, tiled=True)]
    pad x34, local copies, waits for them, and re-layouts: 14.9 us -> 861 us  [run_scan(): return lax.associative_scan(combine, (decay_rate, drive_term), axis=1)[1]]
    all_gather x6 -> x8, waiting for transfers between devices: 699 us -> 190 us  [gather_tokens(): lax.all_gather(values[s], 'grp', axis=0, tiled=True)]
    all_to_all x4 -> x0, waiting for transfers between devices: 139 us -> none  [the longest x2 109 us: to_positions(): lax.all_to_all(values, 'grp', split_axis=1, concat_axis=2, tiled=True)]
    dot_general x6, matrix products: 95.7 us -> 44.7 us  [matmul_tn(): lax.dot_general(left, right, (((0,), (0,)), ((), ())), preferred_element_...]
    all_gather x2, waiting for transfers between devices: 77 us -> 36 us  [gather_rows(): lax.all_gather(weights[2], 'seq', axis=1, tiled=True)]
    all_gather x2, waiting for transfers between devices: 77.2 us -> 36.4 us  [gather_rows(): lax.all_gather(weights[0], 'seq', axis=0, tiled=True)]
    slice x118 -> x21, local copies, waits for them, and re-layouts: 118 us -> 147 us  [run_scan(): return lax.associative_scan(combine, (decay_rate, drive_term), axis=1)[1]]
  transfers between devices with their start and end apart: 29 -> 29, of which waited for: 26 -> 18; matrix products, arithmetic and copies ran while one was open for 12% -> 61% of each run, Pallas kernels for 0% -> 0%
where the time goes in v1:
time: 2270 us; the launch traced here: 2240 us
  local copies, waits for them, and re-layouts  1120 us (49%)
  waiting for transfers between devices  627 us (28%)
  other arithmetic  184 us (8%)
  blocking collectives  152 us (7%)
  matrix products  146 us (6%)
    pad x34, local copies, waits for them, and re-layouts, run_scan(): return lax.associative_scan(combine, (decay_rate, drive_term), axis=1)[1]  861 us
    reduce_scatter x8, waiting for transfers between devices, scatter_tokens(): lax.psum_scatter(parts[s], 'grp', scatter_dimension=0, tiled=True)  242 us
    all_gather x8, waiting for transfers between devices, gather_tokens(): lax.all_gather(values[s], 'grp', axis=0, tiled=True)  190 us
    slice x21, local copies, waits for them, and re-layouts, run_scan(): return lax.associative_scan(combine, (decay_rate, drive_term), axis=1)[1]  147 us
    unnamed x3, blocking collectives  96.3 us
    all_gather x2, waiting for transfers between devices, gather_rows(): lax.all_gather(weights[1], 'seq', axis=0, tiled=True)  63 us
    dot_general x6, matrix products, matmul(): return jnp.dot(left, right, preferred_element_type=jnp.float32)  46 us
    dot_general x6, matrix products, matmul_nt(): lax.dot_general(left, right, (((1,), (1,)), ((), ())), preferred_element_...  45.5 us
  transfers between devices with their start and end apart: 29, of which 18 were waited for; matrix products, arithmetic and copies ran while one was open for 61% of the time, Pallas kernels for 0%

profile of v1, /device:TPU:0, one launch (start us, length us, event | category | flops | bytes accessed | tf_op | source)
XLA Modules:
  0.0 2242.4 jit_solution(16605442712456042050)
XLA Ops:
  10.9 42.1 %all-reduce.54 = (bf16[2048]{0:T(1024)(128)(2,1)}, bf16[2048]{0:T(1024)(128)(2,1)S(1)}) all-reduce(bf16[2048]{0:T(1024)(128)(2,1)S(1)} %dynamic-update-slice.1, bf16[2048]{0:T(1024)(128)(2,1)S(1)} %dynamic-update-slice), channel_id=1, replica_groups=mesh['seq'=4,'grp'=8] {'seq','grp'}, use_global_device_ids=true, to_apply=%add.41 | all-reduce | flops 4096 | bytes 16384
  58.1 8.9 all-gather.2
  90.3 8.4 all_gather.74
  106.5 8.8 all_gather.79
  116.7 16.6 all-gather.23.cloned.1.call-done
  139.3 24.5 %all-gather.27.cloned.1.call-done = bf16[2048,352]{0,1:T(8,128)(2,1)} async-done(((bf16[512,352]{0,1:T(8,128)(2,1)}), bf16[2048,352]{0,1:T(8,128)(2,1)}) %all-gather.27.cloned.1.call-update) | async-done | bytes 1441808 | tf_op jit(solution)/shard_map/all_gather | solution.py:41
  207.6 11.5 convert_multiply_fusion.2
  251.9 11.5 pad.130
  267.6 21.8 pad.132
  293.9 42.6 %pad.134 = f32[2,192,352]{2,0,1:T(2,128)} pad(f32[2,96,352]{2,0,1:T(2,128)} %add.459, f32[]{:T(128)} %constant.12.clone.1), padding=0_0_0x1_0_1x0_0_0 | pad | bytes 811012 | tf_op jit(solution)/shard_map/pad | solution.py:30
  340.6 57.6 %pad.135 = f32[2,384,352]{2,0,1:T(2,128)} pad(f32[2,192,352]{2,0,1:T(2,128)S(1)} %pad_maximum_fusion.8, f32[]{:T(128)} %constant.12.clone.1), padding=0_0_0x0_1_1x0_0_0 | pad | bytes 1622020 | tf_op jit(solution)/shard_map/pad | solution.py:30
  398.2 57.6 %pad.136 = f32[2,384,352]{2,0,1:T(2,128)} pad(f32[2,192,352]{2,0,1:T(2,128)S(1)} %copy-done.34, f32[]{:T(128)} %constant.12.clone.1), padding=0_0_0x1_0_1x0_0_0 | pad | bytes 1622020 | tf_op jit(solution)/shard_map/pad | solution.py:30
  463.0 165.9 %pad.137 = f32[2,768,352]{2,0,1:T(2,128)} pad(f32[2,384,352]{2,0,1:T(2,128)} %pad_maximum_fusion.4, f32[]{:T(128)} %constant.12.clone.1), padding=0_0_0x0_1_1x0_0_0 | pad | bytes 3244036 | tf_op jit(solution)/shard_map/pad | solution.py:30
  628.9 166.0 %pad.138 = f32[2,768,352]{2,0,1:T(2,128)} pad(f32[2,384,352]{2,0,1:T(2,128)} %add.463, f32[]{:T(128)} %constant.12.clone.1), padding=0_0_0x1_0_1x0_0_0 | pad | bytes 3244036 | tf_op jit(solution)/shard_map/pad | solution.py:30
  808.5 8.4 multiply_convert_fusion.3
  829.2 36.5 %reduce-scatter.20.cloned.1.call-done = bf16[96,2048]{1,0:T(8,128)(2,1)} async-done(((bf16[768,2048]{1,0:T(8,128)(2,1)}), bf16[96,2048]{1,0:T(8,128)(2,1)}) %reduce-scatter.20.cloned.1.call-update) | async-done | bytes 393232 | tf_op jit(solution)/shard_map/reduce_scatter | solution.py:56
  865.7 41.7 %reduce-scatter.22.cloned.1.call-done = bf16[96,2048]{1,0:T(8,128)(2,1)} async-done(((bf16[768,2048]{1,0:T(8,128)(2,1)}), bf16[96,2048]{1,0:T(8,128)(2,1)}) %reduce-scatter.22.cloned.1.call-update) | async-done | bytes 393232 | tf_op jit(solution)/shard_map/reduce_scatter | solution.py:56
  915.3 31.7 %all-gather.45.cloned.1.call-done = bf16[1,768,2048]{2,1,0:T(8,128)(2,1)} async-done(((bf16[1,96,2048]{2,1,0:T(8,128)(2,1)}), bf16[1,768,2048]{2,1,0:T(8,128)(2,1)}) %all-gather.45.cloned.1.call-update) | async-done | bytes 3145744 | tf_op jit(solution)/shard_map/all_gather | solution.py:48
  947.0 39.4 %all-gather.47.cloned.1.call-done = bf16[1,768,2048]{2,1,0:T(8,128)(2,1)} async-done(((bf16[1,96,2048]{2,1,0:T(8,128)(2,1)}), bf16[1,768,2048]{2,1,0:T(8,128)(2,1)}) %all-gather.47.cloned.1.call-update) | async-done | bytes 3145744 | tf_op jit(solution)/shard_map/all_gather | solution.py:48
  992.5 33.2 %all-gather.31.cloned.1.call-done = bf16[768,2048]{1,0:T(8,128)(2,1)} async-done(((bf16[96,2048]{1,0:T(8,128)(2,1)}), bf16[768,2048]{1,0:T(8,128)(2,1)}) %all-gather.31.cloned.1.call-update) | async-done | bytes 3145744 | tf_op jit(solution)/shard_map/all_gather | solution.py:48
  1025.7 39.4 %all-gather.33.cloned.1.call-done = bf16[768,2048]{1,0:T(8,128)(2,1)} async-done(((bf16[96,2048]{1,0:T(8,128)(2,1)}), bf16[768,2048]{1,0:T(8,128)(2,1)}) %all-gather.33.cloned.1.call-update) | async-done | bytes 3145744 | tf_op jit(solution)/shard_map/all_gather | solution.py:48
  1071.2 38.5 %all-gather.37.cloned.1.call-done = bf16[2048,768]{1,0:T(8,128)(2,1)} async-done(((bf16[512,768]{1,0:T(8,128)(2,1)}), bf16[2048,768]{1,0:T(8,128)(2,1)}) %all-gather.37.cloned.1.call-update) | async-done | bytes 3145744 | tf_op jit(solution)/shard_map/all_gather | solution.py:41
  1109.7 9.4 fusion.80
  1119.1 36.4 %all-gather.35.cloned.1.call-done = bf16[2048,768]{1,0:T(8,128)(2,1)} async-done(((bf16[512,768]{1,0:T(8,128)(2,1)}), bf16[2048,768]{1,0:T(8,128)(2,1)}) %all-gather.35.cloned.1.call-update) | async-done | bytes 3145744 | tf_op jit(solution)/shard_map/all_gather | solution.py:40
  1155.5 9.5 fusion.79
  1165.0 36.0 %all-gather.39.cloned.1.call-done = bf16[768,2048]{1,0:T(8,128)(2,1)} async-done(((bf16[768,512]{1,0:T(8,128)(2,1)}), bf16[768,2048]{1,0:T(8,128)(2,1)}) %all-gather.39.cloned.1.call-update) | async-done | bytes 3145744 | tf_op jit(solution)/shard_map/all_gather | solution.py:42
  1201.1 14.4 multiply_convert_fusion
  1223.6 8.5 add_convert_fusion.1
  1235.9 39.9 %reduce-scatter.28.cloned.1.call-done = bf16[96,2048]{1,0:T(8,128)(2,1)} async-done(((bf16[768,2048]{1,0:T(8,128)(2,1)}), bf16[96,2048]{1,0:T(8,128)(2,1)}) %reduce-scatter.28.cloned.1.call-update) | async-done | bytes 393232 | tf_op jit(solution)/shard_map/reduce_scatter | solution.py:56
  1275.8 41.6 %reduce-scatter.30.cloned.1.call-done = bf16[96,2048]{1,0:T(8,128)(2,1)} async-done(((bf16[768,2048]{1,0:T(8,128)(2,1)}), bf16[96,2048]{1,0:T(8,128)(2,1)}) %reduce-scatter.30.cloned.1.call-update) | async-done | bytes 393232 | tf_op jit(solution)/shard_map/reduce_scatter | solution.py:56
  1325.8 9.2 convolution_convert_fusion.2
  1335.0 9.2 convolution_convert_fusion.3
  1344.3 9.3 convolution_convert_fusion.4
  1372.2 29.8 %all-gather.43.cloned.1.call-done = bf16[768,2048]{1,0:T(8,128)(2,1)} async-done(((bf16[96,2048]{1,0:T(8,128)(2,1)}), bf16[768,2048]{1,0:T(8,128)(2,1)}) %all-gather.43.cloned.1.call-update) | async-done | bytes 3145744 | tf_op jit(solution)/shard_map/all_gather | solution.py:48
  1414.9 44.4 %slice.655 = f32[2,384,352]{1,0,2:T(2,128)} slice(f32[2,768,352]{1,0,2:T(2,128)S(1)} %reshape.361), slice={[0:2:1], [0:767:2], [0:352:1]} | slice | bytes 2162688 | tf_op jit(solution)/shard_map/slice | solution.py:30
  1459.3 44.6 %slice.653 = f32[2,384,352]{1,0,2:T(2,128)} slice(f32[2,768,352]{1,0,2:T(2,128)S(1)} %reshape.361), slice={[0:2:1], [1:768:2], [0:352:1]} | slice | bytes 2162688 | tf_op jit(solution)/shard_map/slice | solution.py:30
  1544.5 44.5 %slice.721 = f32[2,383,352]{1,0,2:T(2,128)} slice(f32[2,768,352]{1,0,2:T(2,128)S(1)} %reshape.361), slice={[0:2:1], [1:766:2], [0:352:1]} | slice | bytes 2157056 | tf_op jit(solution)/shard_map/slice | solution.py:30
  1612.2 67.1 %pad.154 = f32[2,384,352]{2,0,1:T(2,128)S(1)} pad(f32[2,192,352]{2,0,1:T(2,128)} %add.497, f32[]{:T(128)} %constant.12.clone.1), padding=0_0_0x1_0_1x0_0_0 | pad | bytes 1622020 | tf_op jit(solution)/shard_map/pad | solution.py:30
  1682.7 116.4 %pad.155 = f32[2,768,352]{2,0,1:T(2,128)} pad(f32[2,384,352]{2,0,1:T(2,128)S(1)} %pad_maximum_fusion.5, f32[]{:T(128)} %constant.12.clone.1), padding=0_0_0x0_1_1x0_0_0 | pad | bytes 3244036 | tf_op jit(solution)/shard_map/pad | solution.py:30
  1799.2 116.4 %pad.156 = f32[2,768,352]{2,0,1:T(2,128)} pad(f32[2,384,352]{2,0,1:T(2,128)S(1)} %copy-done.26, f32[]{:T(128)} %constant.12.clone.1), padding=0_0_0x1_0_1x0_0_0 | pad | bytes 3244036 | tf_op jit(solution)/shard_map/pad | solution.py:30
  1920.1 18.3 fusion.67
  1981.4 13.8 multiply_reduce_fusion.4
  2030.4 16.2 all-reduce.52
  2052.1 19.8 reduce-scatter.36.cloned.1.call-done
  2073.9 31.2 %reduce-scatter.38.cloned.1.call-done = bf16[512,352]{0,1:T(8,128)(2,1)} async-done(((bf16[2048,352]{0,1:T(8,128)(2,1)}), bf16[512,352]{0,1:T(8,128)(2,1)}) %reduce-scatter.38.cloned.1.call-update) | async-done | bytes 360464 | tf_op jit(solution)/shard_map/reduce_scatter | solution.py:66
  2107.1 40.7 %reduce-scatter.32.cloned.1.call-done = bf16[96,2048]{1,0:T(8,128)(2,1)} async-done(((bf16[768,2048]{1,0:T(8,128)(2,1)}), bf16[96,2048]{1,0:T(8,128)(2,1)}) %reduce-scatter.32.cloned.1.call-update) | async-done | bytes 393232 | tf_op jit(solution)/shard_map/reduce_scatter | solution.py:56
  2147.8 41.6 %reduce-scatter.34.cloned.1.call-done = bf16[96,2048]{1,0:T(8,128)(2,1)} async-done(((bf16[768,2048]{1,0:T(8,128)(2,1)}), bf16[96,2048]{1,0:T(8,128)(2,1)}) %reduce-scatter.34.cloned.1.call-update) | async-done | bytes 393232 | tf_op jit(solution)/shard_map/reduce_scatter | solution.py:56
  2192.1 38.0 %all-reduce.51 = (f32[2048]{0:T(1024)S(1)}, f32[2048]{0:T(1024)S(1)}) all-reduce(f32[2048]{0:T(1024)S(1)} %get-tuple-element.58, f32[2048]{0:T(1024)S(1)} %get-tuple-element.55), channel_id=12, replica_groups=mesh['seq'=4,'grp'=8] {'seq','grp'}, use_global_device_ids=true, to_apply=%region_13.14.clone | all-reduce | flops 4096 | bytes 32768
  (510 shorter events, 407.1 us)
Async XLA Ops:
  7.2 109.5 %all-gather.21.cloned.1.call-start = ((), (), s32[]{:S(2)}) async-start(), calls=%async_computation.14 | async-start | bytes 3538944 | tf_op jit(solution)/shard_map/all_gather | solution.py:48
  55.4 77.9 %all-gather.23.cloned.1.call-start = ((), (), s32[]{:S(2)}) async-start(), calls=%async_computation.15 | async-start | bytes 3538944 | tf_op jit(solution)/shard_map/all_gather | solution.py:48
  56.2 107.6 %all-gather.27.cloned.1.call-start = ((), (), s32[]{:S(2)}) async-start(), calls=%async_computation.17 | async-start | bytes 1802240 | tf_op jit(solution)/shard_map/all_gather | solution.py:41
  56.9 751.5 %all-gather.25.cloned.1.call-start = ((), (), s32[]{:S(2)}) async-start(), calls=%async_computation.16 | async-start | bytes 1802240 | tf_op jit(solution)/shard_map/all_gather | solution.py:40
  57.5 759.4 %all-gather.29.cloned.1.call-start = ((), (), s32[]{:S(2)}) async-start(), calls=%async_computation.18 | async-start | bytes 1802240 | tf_op jit(solution)/shard_map/all_gather | solution.py:42
  58.1 807.6 %reduce-scatter.20.cloned.1.call-start = ((), (), s32[]{:S(2)}) async-start(), calls=%async_computation.19 | async-start | bytes 3538944 | tf_op jit(solution)/shard_map/reduce_scatter | solution.py:56
  67.2 140.2 %copy-start.72 = (f32[352]{0:T(512)}, f32[352]{0:T(512)S(1)}, u32[]{:S(2)}) copy-start(f32[352]{0:T(512)S(1)} %reshape.352) | copy-start | bytes 4228
  90.2 117.3 %copy-start.60 = (f32[352]{0:T(512)}, f32[352]{0:T(512)S(1)}, u32[]{:S(2)}) copy-start(f32[352]{0:T(512)S(1)} %fusion.65) | copy-start | bytes 4228
  116.1 91.4 %copy-start.62 = (f32[352]{0:T(512)}, f32[352]{0:T(512)S(1)}, u32[]{:S(2)}) copy-start(f32[352]{0:T(512)S(1)} %mul.569) | copy-start | bytes 4228
  116.3 91.2 %copy-start.64 = (f32[352]{0:T(512)}, f32[352]{0:T(512)S(1)}, u32[]{:S(2)}) copy-start(f32[352]{0:T(512)S(1)} %mul.578) | copy-start | bytes 4228
  116.5 91.0 %copy-start.66 = (f32[352]{0:T(512)}, f32[352]{0:T(512)S(1)}, u32[]{:S(2)}) copy-start(f32[352]{0:T(512)S(1)} %mul.575) | copy-start | bytes 4228
  116.7 90.8 %copy-start.68 = (f32[352]{0:T(512)}, f32[352]{0:T(512)S(1)}, u32[]{:S(2)}) copy-start(f32[352]{0:T(512)S(1)} %mul.572) | copy-start | bytes 4228
  825.3 82.2 %reduce-scatter.22.cloned.1.call-start = ((), (), s32[]{:S(2)}) async-start(), calls=%async_computation.20 | async-start | bytes 3538944 | tf_op jit(solution)/shard_map/reduce_scatter | solution.py:56
  826.0 121.0 %all-gather.45.cloned.1.call-start = ((), (), s32[]{:S(2)}) async-start(), calls=%async_computation.40 | async-start | bytes 3538944 | tf_op jit(solution)/shard_map/all_gather | solution.py:48
  828.2 158.2 %all-gather.47.cloned.1.call-start = ((), (), s32[]{:S(2)}) async-start(), calls=%async_computation.41 | async-start | bytes 3538944 | tf_op jit(solution)/shard_map/all_gather | solution.py:48
  829.0 196.7 %all-gather.31.cloned.1.call-start = ((), (), s32[]{:S(2)}) async-start(), calls=%async_computation.21 | async-start | bytes 3538944 | tf_op jit(solution)/shard_map/all_gather | solution.py:48
  912.6 152.5 %all-gather.33.cloned.1.call-start = ((), (), s32[]{:S(2)}) async-start(), calls=%async_computation.22 | async-start | bytes 3538944 | tf_op jit(solution)/shard_map/all_gather | solution.py:48
  913.4 196.3 %all-gather.37.cloned.1.call-start = ((), (), s32[]{:S(2)}) async-start(), calls=%async_computation.24 | async-start | bytes 3932160 | tf_op jit(solution)/shard_map/all_gather | solution.py:41
  913.9 241.6 %all-gather.35.cloned.1.call-start = ((), (), s32[]{:S(2)}) async-start(), calls=%async_computation.23 | async-start | bytes 3932160 | tf_op jit(solution)/shard_map/all_gather | solution.py:40
  914.7 286.4 %all-gather.39.cloned.1.call-start = ((), (), s32[]{:S(2)}) async-start(), calls=%async_computation.25 | async-start | bytes 3932160 | tf_op jit(solution)/shard_map/all_gather | solution.py:42
  915.3 360.5 %reduce-scatter.28.cloned.1.call-start = ((), (), s32[]{:S(2)}) async-start(), calls=%async_computation.28 | async-start | bytes 3538944 | tf_op jit(solution)/shard_map/reduce_scatter | solution.py:56
  1235.3 82.1 %reduce-scatter.30.cloned.1.call-start = ((), (), s32[]{:S(2)}) async-start(), calls=%async_computation.29 | async-start | bytes 3538944 | tf_op jit(solution)/shard_map/reduce_scatter | solution.py:56
  1235.9 136.3 %all-gather.41.cloned.1.call-start = ((), (), s32[]{:S(2)}) async-start(), calls=%async_computation.30 | async-start | bytes 3538944 | tf_op jit(solution)/shard_map/all_gather | solution.py:48
  1325.2 76.8 %all-gather.43.cloned.1.call-start = ((), (), s32[]{:S(2)}) async-start(), calls=%async_computation.31 | async-start | bytes 3538944 | tf_op jit(solution)/shard_map/all_gather | solution.py:48
  1325.8 694.6 %reduce-scatter.46.cloned.1.call-start = ((), (), s32[]{:S(2)}) async-start(), calls=%async_computation.39 | async-start | bytes 3932160 | tf_op jit(solution)/shard_map/reduce_scatter | solution.py:67
  1335.0 687.8 %reduce-scatter.44.cloned.1.call-start = ((), (), s32[]{:S(2)}) async-start(), calls=%async_computation.38 | async-start | bytes 3932160 | tf_op jit(solution)/shard_map/reduce_scatter | solution.py:66
  1344.2 681.0 %reduce-scatter.42.cloned.1.call-start = ((), (), s32[]{:S(2)}) async-start(), calls=%async_computation.37 | async-start | bytes 3932160 | tf_op jit(solution)/shard_map/reduce_scatter | solution.py:65
  1353.6 674.0 %reduce-scatter.24.cloned.1.call-start = ((), (), s32[]{:S(2)}) async-start(), calls=%async_computation.26 | async-start | bytes 3538944 | tf_op jit(solution)/shard_map/reduce_scatter | solution.py:56
  1364.7 662.9 %reduce-scatter.26.cloned.1.call-start = ((), (), s32[]{:S(2)}) async-start(), calls=%async_computation.27 | async-start | bytes 3538944 | tf_op jit(solution)/shard_map/reduce_scatter | solution.py:56
  1372.1 676.5 %all-reduce.57.cloned.1.call-start = ((), (), s32[]{:S(2)}) async-start(), calls=%async_computation.42 | async-start | bytes 1441792
  1682.7 116.5 %copy-start.26 = (f32[2,384,352]{2,0,1:T(2,128)S(1)}, f32[2,384,352]{2,0,1:T(2,128)}, u32[]{:S(2)}) copy-start(f32[2,384,352]{2,0,1:T(2,128)} %add.499) | copy-start | bytes 3244036
  1682.7 236.6 %copy-start.61 = (f32[352]{0:T(512)S(1)}, f32[352]{0:T(512)}, u32[]{:S(2)}) copy-start(f32[352]{0:T(512)} %copy-done.60) | copy-start | bytes 4228
  1682.7 236.6 %copy-start.63 = (f32[352]{0:T(512)S(1)}, f32[352]{0:T(512)}, u32[]{:S(2)}) copy-start(f32[352]{0:T(512)} %copy-done.62) | copy-start | bytes 4228
  1682.7 236.6 %copy-start.65 = (f32[352]{0:T(512)S(1)}, f32[352]{0:T(512)}, u32[]{:S(2)}) copy-start(f32[352]{0:T(512)} %copy-done.64) | copy-start | bytes 4228
  1682.7 236.6 %copy-start.67 = (f32[352]{0:T(512)S(1)}, f32[352]{0:T(512)}, u32[]{:S(2)}) copy-start(f32[352]{0:T(512)} %copy-done.66) | copy-start | bytes 4228
  1682.7 236.6 %copy-start.69 = (f32[352]{0:T(512)S(1)}, f32[352]{0:T(512)}, u32[]{:S(2)}) copy-start(f32[352]{0:T(512)} %copy-done.68) | copy-start | bytes 4228
  1799.2 120.2 %copy-start.73 = (f32[352]{0:T(512)S(1)}, f32[352]{0:T(512)}, u32[]{:S(2)}) copy-start(f32[352]{0:T(512)} %copy-done.72) | copy-start | bytes 4228
  1958.4 91.8 %reduce-scatter.40.cloned.1.call-start = ((), (), s32[]{:S(2)}) async-start(), calls=%async_computation.36 | async-start | bytes 1802240 | tf_op jit(solution)/shard_map/reduce_scatter | solution.py:67
  1965.1 106.9 %reduce-scatter.36.cloned.1.call-start = ((), (), s32[]{:S(2)}) async-start(), calls=%async_computation.34 | async-start | bytes 1802240 | tf_op jit(solution)/shard_map/reduce_scatter | solution.py:65
  1981.4 123.8 %reduce-scatter.38.cloned.1.call-start = ((), (), s32[]{:S(2)}) async-start(), calls=%async_computation.35 | async-start | bytes 1802240 | tf_op jit(solution)/shard_map/reduce_scatter | solution.py:66
  2002.5 145.4 %reduce-scatter.32.cloned.1.call-start = ((), (), s32[]{:S(2)}) async-start(), calls=%async_computation.32 | async-start | bytes 3538944 | tf_op jit(solution)/shard_map/reduce_scatter | solution.py:56
  2018.2 171.3 %reduce-scatter.34.cloned.1.call-start = ((), (), s32[]{:S(2)}) async-start(), calls=%async_computation.33 | async-start | bytes 3538944 | tf_op jit(solution)/shard_map/reduce_scatter | solution.py:56
  2050.2 141.3 %copy-start.55 = (f32[2048]{0:T(1024)S(1)}, f32[2048]{0:T(1024)}, u32[]{:S(2)}) copy-start(f32[2048]{0:T(1024)} %copy-done.54) | copy-start | bytes 24580
  2050.2 141.3 %copy-start.76 = (f32[2,96]{1,0:T(2,128)S(1)}, f32[2,96]{1,0:T(2,128)}, u32[]{:S(2)}) copy-start(f32[2,96]{1,0:T(2,128)} %copy-done.75) | copy-start | bytes 2308
  2073.9 157.3 %copy-start.11 = (f32[192,2048]{1,0:T(8,128)S(1)}, f32[192,2048]{1,0:T(8,128)}, u32[]{:S(2)}) copy-start(f32[192,2048]{1,0:T(8,128)} %copy-done.9) | copy-start | bytes 4718596
  2073.9 157.3 %copy-start.23 = (bf16[2,96,2048]{2,1,0:T(8,128)(2,1)S(1)}, bf16[2,96,2048]{2,1,0:T(8,128)(2,1)}, u32[]{:S(2)}) copy-start(bf16[2,96,2048]{2,1,0:T(8,128)(2,1)} %param.33) | copy-start | bytes 2359300
  2073.9 157.3 %copy-start.78 = (f32[2,96]{1,0:T(2,128)S(1)}, f32[2,96]{1,0:T(2,128)}, u32[]{:S(2)}) copy-start(f32[2,96]{1,0:T(2,128)} %copy-done.77) | copy-start | bytes 2308
  2073.9 157.3 %copy-start.84 = (f32[2,96]{1,0:T(2,128)S(1)}, f32[2,96]{1,0:T(2,128)}, u32[]{:S(2)}) copy-start(f32[2,96]{1,0:T(2,128)} %broadcast_multiply_fusion.1) | copy-start | bytes 2308
  (79 other events, 895.7 us)
Sparse Core Ops, SparseCore 0:
  55.5 38.3 all-gather.20
  96.1 37.1 all-gather.22
  135.2 28.5 all-gather.26
  165.5 29.7 all-gather.24
  196.9 29.7 all-gather.28
  825.4 40.2 reduce-scatter.19
  868.0 39.3 reduce-scatter.21
  909.6 37.3 all-gather.44
  949.3 37.1 all-gather.46
  988.5 37.1 all-gather.30
  1027.9 37.1 all-gather.32
  1066.8 42.8 all-gather.36
  1111.5 43.9 all-gather.34
  1157.2 43.8 all-gather.38
  1235.4 40.3 reduce-scatter.27
  1277.9 39.4 reduce-scatter.29
  1325.3 37.3 all-gather.40
  1364.8 37.1 all-gather.42
  1404.9 42.8 reduce-scatter.45
  1450.6 43.9 reduce-scatter.43
  1497.6 43.9 reduce-scatter.41
  1543.8 40.3 reduce-scatter.23
  1586.5 39.4 reduce-scatter.25
  1958.5 46.9 all-reduce.56
  2008.7 30.2 reduce-scatter.39
  2041.8 30.1 reduce-scatter.35
  2075.1 30.0 reduce-scatter.37
  2107.5 40.3 reduce-scatter.31
  2150.1 39.2 reduce-scatter.33

commit v2 on v1

v2 whole, which is shorter than its diff:
```python
import math

import jax
import jax.numpy as jnp
from jax import lax
from jax.experimental import pallas as pl
from jax.experimental.pallas import tpu as pltpu
from jax.sharding import PartitionSpec as P

epsilon = 1e-06
gelu_slope = math.sqrt(2.0 / math.pi)
gelu_cubic = 0.044715


def matmul(left, right):
    return jnp.dot(left, right, preferred_element_type=jnp.float32)


def matmul_tn(left, right):
    return lax.dot_general(
        left, right, (((0,), (0,)), ((), ())), preferred_element_type=jnp.float32
    )


def matmul_nt(left, right):
    return lax.dot_general(
        left, right, (((1,), (1,)), ((), ())), preferred_element_type=jnp.float32
    )


def norm_back(grad_normed, normal_part, inverse, gain):
    scaled = grad_normed * gain
    return inverse * (scaled - normal_part * jnp.mean(scaled * normal_part, axis=-1, keepdims=True))


def gather_rows(weights):
    return (
        lax.all_gather(weights[0], "seq", axis=0, tiled=True),
        lax.all_gather(weights[1], "seq", axis=0, tiled=True),
        lax.all_gather(weights[2], "seq", axis=1, tiled=True),
    )


def gather_tokens(values):
    return jnp.stack(
        [lax.all_gather(values[s], "grp", axis=0, tiled=True) for s in range(values.shape[0])]
    ).reshape(-1, values.shape[-1])


def scatter_tokens(values, seqs_here):
    parts = values.astype(jnp.bfloat16).reshape(seqs_here, -1, values.shape[-1])
    return jnp.concatenate(
        [
            lax.psum_scatter(parts[s], "grp", scatter_dimension=0, tiled=True)
            for s in range(seqs_here)
        ]
    ).astype(jnp.float32)


def sum_rows(grads):
    low = [grad.astype(jnp.bfloat16) for grad in grads]
    return (
        lax.psum_scatter(low[0], "seq", scatter_dimension=0, tiled=True).astype(jnp.float32),
        lax.psum_scatter(low[1], "seq", scatter_dimension=0, tiled=True).astype(jnp.float32),
        lax.psum_scatter(low[2], "seq", scatter_dimension=1, tiled=True).astype(jnp.float32),
    )


def head_diagonal(blocks):
    heads, head_dim, _ = blocks.shape
    rows = []
    for h in range(heads):
        row = [jnp.zeros((head_dim, head_dim), blocks.dtype)] * heads
        row[h] = blocks[h]
        rows.append(jnp.concatenate(row, axis=1))
    return jnp.concatenate(rows, axis=0)


def diagonal_heads(square, heads):
    head_dim = square.shape[0] // heads
    return jnp.stack(
        [
            square[h * head_dim : (h + 1) * head_dim, h * head_dim : (h + 1) * head_dim]
            for h in range(heads)
        ]
    )


def pick_rows(seq_len):
    for rows in (128, 96, 64, 32, 16):
        if seq_len % rows == 0:
            return rows
    return seq_len


def gelu_parts(x):
    cubic = gelu_slope * (x + gelu_cubic * x * x * x)
    bend = jnp.tanh(cubic)
    gate = 0.5 * (1.0 + bend)
    slope = gate + 0.5 * x * (1.0 - bend * bend) * gelu_slope * (1.0 + 3.0 * gelu_cubic * x * x)
    return x * gate, slope


def minus_expm1(x):
    series = 1.0 + x * (1.0 / 9.0)
    for k in (8, 7, 6, 5, 4, 3, 2):
        series = 1.0 + x * (1.0 / k) * series
    return jnp.where(x > -0.4, -x * series, 1.0 - jnp.exp(x))


def shift_down(values, by, fill):
    rows = values.shape[0]
    if by % 8 == 0:
        return jnp.concatenate([jnp.full((by, values.shape[1]), fill), values[: rows - by]], axis=0)
    index = lax.broadcasted_iota(jnp.int32, values.shape, 0)
    return jnp.where(index >= by, pltpu.roll(values, by, 0), fill)


def shift_up(values, by, fill):
    rows = values.shape[0]
    if by % 8 == 0:
        return jnp.concatenate([values[by:], jnp.full((by, values.shape[1]), fill)], axis=0)
    index = lax.broadcasted_iota(jnp.int32, values.shape, 0)
    return jnp.where(index < rows - by, pltpu.roll(values, rows - by, 0), fill)


def scan_block(decay, drive, shift):
    by = 1
    while by < decay.shape[0]:
        drive = drive + decay * shift(drive, by, 0.0)
        decay = decay * shift(decay, by, 1.0)
        by *= 2
    return decay, drive


def decay_parts(rate, softness):
    log_decay = -8.0 * rate * softness
    return jnp.exp(log_decay), jnp.sqrt(minus_expm1(2.0 * log_decay))


def rec_forward_body(
    feed_ref, branch_ref, vectors_ref, softness_ref, gate_a_ref, gate_x_ref,
    conv_ref, rate_ref, input_ref, state_ref, mixed_ref, window, carry,
):
    seqs, rows, _ = feed_ref.shape

    @pl.when(pl.program_id(0) == 0)
    def _():
        window[...] = jnp.zeros_like(window)
        carry[...] = jnp.zeros_like(carry)

    softness = softness_ref[...]
    for s in range(seqs):
        window[s, pl.ds(8, rows), :] = feed_ref[s].astype(jnp.float32)
        conv = vectors_ref[4:5, :] + vectors_ref[0:1, :] * window[s, pl.ds(8, rows), :]
        for k in range(1, 4):
            conv = conv + vectors_ref[k : k + 1, :] * window[s, pl.ds(8 - k, rows), :]
        window[s, pl.ds(0, 8), :] = window[s, pl.ds(rows, 8), :]
        conv_low = conv.astype(jnp.bfloat16)
        conv_ref[s] = conv_low
        rate = jax.nn.sigmoid(matmul(conv_low, gate_a_ref[...]) + vectors_ref[5:6, :])
        gate = jax.nn.sigmoid(matmul(conv_low, gate_x_ref[...]) + vectors_ref[6:7, :])
        rate_ref[s] = rate
        input_ref[s] = gate
        decay, scale = decay_parts(rate, softness)
        total, state = scan_block(decay, scale * gate * conv_low.astype(jnp.float32), shift_down)
        state = state + total * carry[s, 0:1, :]
        carry[s, 0:1, :] = state[rows - 1 : rows, :]
        state_ref[s] = state
        gelu_branch = gelu_parts(branch_ref[s])[0]
        mixed_ref[s] = (gelu_branch * state.astype(jnp.bfloat16).astype(jnp.float32)).astype(
            jnp.bfloat16
        )


def rec_backward_body(
    grad_mixed_ref, branch_ref, feed_ref, feed_before_ref, conv_ref, rate_ref, input_ref,
    state_ref, state_before_ref, vectors_ref, softness_ref, gate_a_ref, gate_x_ref,
    grad_branch_ref, grad_feed_ref, grad_a_ref, grad_x_ref, sums_ref, window, later, carry,
):
    seqs, rows, channels = feed_ref.shape
    step = pl.program_id(0)
    first_block = step == pl.num_programs(0) - 1
    before = feed_before_ref.shape[1]

    @pl.when(step == 0)
    def _():
        later[...] = jnp.zeros_like(later)
        carry[...] = jnp.zeros_like(carry)
        grad_a_ref[...] = jnp.zeros_like(grad_a_ref)
        grad_x_ref[...] = jnp.zeros_like(grad_x_ref)
        sums_ref[...] = jnp.zeros_like(sums_ref)

    softness = softness_ref[...]
    keep = jnp.where(first_block, 0.0, 1.0)
    for s in range(seqs):
        gelu_branch, slope = gelu_parts(branch_ref[s])
        grad_mixed = grad_mixed_ref[s]
        state = state_ref[s]
        state_low = state.astype(jnp.bfloat16).astype(jnp.float32)
        grad_state = (grad_mixed * gelu_branch).astype(jnp.bfloat16).astype(jnp.float32)
        grad_branch_ref[s] = (slope * grad_mixed * state_low).astype(jnp.bfloat16)
        rate = rate_ref[s]
        gate = input_ref[s]
        decay, scale = decay_parts(rate, softness)
        total, carried = scan_block(shift_up(decay, 1, 1.0), grad_state, shift_up)
        carried = carried + total * carry[s, 0:1, :]
        carry[s, 0:1, :] = decay[0:1, :] * carried[0:1, :]
        index = lax.broadcasted_iota(jnp.int32, state.shape, 0)
        last = state_before_ref[s][7:8, :] * keep
        previous = jnp.where(index >= 1, pltpu.roll(state, 1, 0), last)
        conv_low = conv_ref[s]
        conv = conv_low.astype(jnp.float32)
        grad_log = carried * previous * decay - carried * gate * conv * decay * decay / scale
        log_rate = grad_log * rate
        pre_a = -8.0 * softness * log_rate * (1.0 - rate)
        pre_x = carried * scale * conv * gate * (1.0 - gate)
        low_a = pre_a.astype(jnp.bfloat16)
        low_x = pre_x.astype(jnp.bfloat16)
        grad_a_ref[...] += matmul_tn(conv_low, low_a)
        grad_x_ref[...] += matmul_tn(conv_low, low_x)
        grad_conv = (
            carried * scale * gate
            + matmul_nt(low_a, gate_a_ref[...])
            + matmul_nt(low_x, gate_x_ref[...])
        )
        window[s, pl.ds(0, 8), :] = feed_before_ref[s].astype(jnp.float32)[before - 8 :, :] * keep
        window[s, pl.ds(8, rows), :] = feed_ref[s].astype(jnp.float32)
        later[s, pl.ds(rows, 8), :] = later[s, pl.ds(0, 8), :]
        later[s, pl.ds(0, rows), :] = grad_conv
        grad_feed = vectors_ref[0:1, :] * grad_conv
        sums_ref[0:1, :] += jnp.sum(grad_conv * window[s, pl.ds(8, rows), :], axis=0, keepdims=True)
        for k in range(1, 4):
            grad_feed = grad_feed + vectors_ref[k : k + 1, :] * later[s, pl.ds(k, rows), :]
            sums_ref[k : k + 1, :] += jnp.sum(
                grad_conv * window[s, pl.ds(8 - k, rows), :], axis=0, keepdims=True
            )
        grad_feed_ref[s] = grad_feed.astype(jnp.bfloat16)
        sums_ref[4:5, :] += jnp.sum(grad_conv, axis=0, keepdims=True)
        sums_ref[5:6, :] += jnp.sum(pre_a, axis=0, keepdims=True)
        sums_ref[6:7, :] += jnp.sum(pre_x, axis=0, keepdims=True)
        sums_ref[7:8, :] += jnp.sum(log_rate, axis=0, keepdims=True)


def whole(shape):
    return pl.BlockSpec(shape, lambda i: (0,) * len(shape))


def rec_forward(feed, branch, vectors, softness, gate_a, gate_x):
    seqs, seq_len, channels = feed.shape
    rows = pick_rows(seq_len)
    block = pl.BlockSpec((seqs, rows, channels), lambda i: (0, i, 0))
    full = jax.ShapeDtypeStruct(feed.shape, jnp.float32)
    low = jax.ShapeDtypeStruct(feed.shape, jnp.bfloat16)
    return pl.pallas_call(
        rec_forward_body,
        grid=(seq_len // rows,),
        in_specs=[block, block]
        + [whole(v.shape) for v in (vectors, softness, gate_a, gate_x)],
        out_specs=[block] * 5,
        out_shape=[low, full, full, full, low],
        scratch_shapes=[
            pltpu.VMEM((seqs, rows + 8, channels), jnp.float32),
            pltpu.VMEM((seqs, 8, channels), jnp.float32),
        ],
        compiler_params=pltpu.CompilerParams(vmem_limit_bytes=40 << 20),
        name="rec_forward",
    )(feed, branch, vectors, softness, gate_a, gate_x)


def rec_backward(grad_mixed, branch, feed, conv, rate, gate, state, vectors, softness, gate_a, gate_x):
    seqs, seq_len, channels = feed.shape
    rows = pick_rows(seq_len)
    blocks = seq_len // rows
    block = pl.BlockSpec((seqs, rows, channels), lambda i: (0, blocks - 1 - i, 0))

    def ahead(by):
        return pl.BlockSpec(
            (seqs, by, channels),
            lambda i: (0, jnp.maximum((blocks - 1 - i) * (rows // by) - 1, 0), 0),
        )

    low = jax.ShapeDtypeStruct(feed.shape, jnp.bfloat16)
    square = jax.ShapeDtypeStruct((channels, channels), jnp.float32)
    return pl.pallas_call(
        rec_backward_body,
        grid=(blocks,),
        in_specs=[block, block, block, ahead(16), block, block, block, block, ahead(8)]
        + [whole(v.shape) for v in (vectors, softness, gate_a, gate_x)],
        out_specs=[block, block, whole((channels, channels)), whole((channels, channels)), whole((8, channels))],
        out_shape=[low, low, square, square, jax.ShapeDtypeStruct((8, channels), jnp.float32)],
        scratch_shapes=[
            pltpu.VMEM((seqs, rows + 8, channels), jnp.float32),
            pltpu.VMEM((seqs, rows + 8, channels), jnp.float32),
            pltpu.VMEM((seqs, 8, channels), jnp.float32),
        ],
        compiler_params=pltpu.CompilerParams(vmem_limit_bytes=40 << 20),
        name="rec_backward",
    )(grad_mixed, branch, feed, feed, conv, rate, gate, state, state, vectors, softness, gate_a, gate_x)


def per_device(
    layer_in, gain_one, w_branch, w_rec, conv_w, conv_b, gate_a_w, gate_a_b, gate_x_w, gate_x_b,
    decay_logit, w_out, gain_two, mlp_gate, mlp_up, mlp_down, out_grad,
):
    seqs_here, positions, model_width = layer_in.shape
    tokens_here = seqs_here * positions
    heads_here, tap_count, part_dim = conv_w.shape
    seq_devices = lax.axis_size("seq")
    head_dim = part_dim * seq_devices
    channels = heads_here * head_dim
    f32 = jnp.float32

    own_gains = lax.all_gather(jnp.stack([gain_one, gain_two]), "grp", axis=1, tiled=True)
    own_params = jnp.concatenate(
        [jnp.transpose(conv_w, (0, 2, 1))]
        + [v[:, :, None] for v in (conv_b, gate_a_b, gate_x_b, decay_logit)]
        + [gate_a_w, gate_x_w],
        axis=2,
    )
    packed = jnp.concatenate([own_gains.reshape(-1), own_params.reshape(-1)])
    packed = lax.all_gather(packed, "seq", axis=0).reshape(seq_devices, -1)
    gains = packed[:, : own_gains.size].reshape(seq_devices, 2, -1)
    gains = jnp.transpose(gains, (1, 0, 2)).reshape(2, model_width).astype(f32)
    params = packed[:, own_gains.size :].reshape(seq_devices, heads_here, part_dim, -1)
    params = jnp.transpose(params, (1, 0, 2, 3)).reshape(heads_here, head_dim, -1)
    vectors = params[:, :, : tap_count + 4].reshape(channels, -1).T.astype(f32)
    diag_a = head_diagonal(params[:, :, tap_count + 4 : tap_count + 4 + head_dim])
    diag_x = head_diagonal(params[:, :, tap_count + 4 + head_dim :])
    logit = vectors[tap_count + 3 :]
    softness = jax.nn.softplus(-logit)

    branch_w, rec_w, out_w = gather_rows((w_branch, w_rec, w_out))
    gate_w, up_w, down_w = gather_rows((mlp_gate, mlp_up, mlp_down))

    inputs = layer_in.reshape(tokens_here, model_width).astype(f32)
    inverse_one = lax.rsqrt(jnp.mean(inputs * inputs, axis=-1, keepdims=True) + epsilon)
    normal_one = inputs * inverse_one
    normed_own = (normal_one * gains[0]).astype(jnp.bfloat16)
    normed_one = gather_tokens(normed_own.reshape(layer_in.shape))
    branch_pre = matmul(normed_one, branch_w).reshape(seqs_here, -1, channels)
    feed = matmul(normed_one, rec_w).astype(jnp.bfloat16).reshape(seqs_here, -1, channels)
    conv, rate, gate, state, mixed = rec_forward(feed, branch_pre, vectors, softness, diag_a, diag_x)
    mixed = mixed.reshape(-1, channels)
    residual = inputs + scatter_tokens(matmul(mixed, out_w), seqs_here)
    inverse_two = lax.rsqrt(jnp.mean(residual * residual, axis=-1, keepdims=True) + epsilon)
    normal_two = residual * inverse_two
    normed_two_own = (normal_two * gains[1]).astype(jnp.bfloat16)
    normed_two = gather_tokens(normed_two_own.reshape(layer_in.shape))
    up_proj = matmul(normed_two, up_w)
    gate_act, gate_pull = jax.vjp(jax.nn.gelu, matmul(normed_two, gate_w))
    hidden = (gate_act * up_proj).astype(jnp.bfloat16)
    layer_sum = residual + scatter_tokens(matmul(hidden, down_w), seqs_here)
    layer_out = layer_sum.astype(jnp.bfloat16).reshape(layer_in.shape)

    grad_output = gather_tokens(out_grad)
    grad_down = matmul_tn(hidden, grad_output)
    grad_hidden = matmul_nt(grad_output, down_w)
    grad_gate = gate_pull(grad_hidden * up_proj)[0].astype(jnp.bfloat16)
    grad_up = (grad_hidden * gate_act).astype(jnp.bfloat16)
    normed_two_term = scatter_tokens(
        matmul_nt(grad_gate, gate_w) + matmul_nt(grad_up, up_w), seqs_here
    )
    mlp_grads = sum_rows((matmul_tn(normed_two, grad_gate), matmul_tn(normed_two, grad_up), grad_down))
    gain_two_local = jnp.sum(normed_two_term * normal_two, axis=0)
    grad_residual = out_grad.reshape(tokens_here, model_width).astype(f32) + norm_back(
        normed_two_term, normal_two, inverse_two, gains[1]
    )
    residual_low = gather_tokens(grad_residual.astype(jnp.bfloat16).reshape(layer_in.shape))
    out_weight_grad = matmul_tn(mixed, residual_low)
    grad_mixed = matmul_nt(residual_low, out_w).reshape(seqs_here, -1, channels)
    grad_branch, grad_feed, square_a, square_x, sums = rec_backward(
        grad_mixed, branch_pre, feed, conv, rate, gate, state, vectors, softness, diag_a, diag_x
    )
    grad_branch = grad_branch.reshape(-1, channels)
    grad_feed = grad_feed.reshape(-1, channels)
    vector_grads = jnp.concatenate(
        [sums[: tap_count + 3], 8.0 * jax.nn.sigmoid(-logit) * sums[tap_count + 3 :]]
    )
    rec_grads = jnp.concatenate(
        [
            vector_grads.T.reshape(heads_here, head_dim, -1),
            diagonal_heads(square_a, heads_here),
            diagonal_heads(square_x, heads_here),
        ],
        axis=2,
    )
    rec_grads = lax.psum_scatter(rec_grads, "seq", scatter_dimension=1, tiled=True)
    normed_one_term = scatter_tokens(
        matmul_nt(grad_branch, branch_w) + matmul_nt(grad_feed, rec_w), seqs_here
    )
    mixer_grads = sum_rows(
        (matmul_tn(normed_one, grad_branch), matmul_tn(normed_one, grad_feed), out_weight_grad)
    )
    gain_one_local = jnp.sum(normed_one_term * normal_one, axis=0)
    grad_input = grad_residual + norm_back(normed_one_term, normal_one, inverse_one, gains[0])
    gain_grads = lax.psum_scatter(
        jnp.stack([gain_one_local, gain_two_local]), "seq", scatter_dimension=1, tiled=True
    )
    gain_grads = lax.psum_scatter(gain_grads, "grp", scatter_dimension=1, tiled=True)
    at = tap_count + 4
    return (
        layer_out,
        grad_input.reshape(layer_in.shape),
        gain_grads[0],
        mixer_grads[0],
        mixer_grads[1],
        jnp.transpose(rec_grads[:, :, :tap_count], (0, 2, 1)),
        rec_grads[:, :, tap_count],
        rec_grads[:, :, at : at + head_dim],
        rec_grads[:, :, tap_count + 1],
        rec_grads[:, :, at + head_dim :],
        rec_grads[:, :, tap_count + 2],
        rec_grads[:, :, tap_count + 3],
        mixer_grads[2],
        gain_grads[1],
        mlp_grads[0],
        mlp_grads[1],
        mlp_grads[2],
    )


def solution(mesh):
    placed = (
        P("seq", "grp", None),
        P(("seq", "grp")),
        P("seq", "grp"),
        P("seq", "grp"),
        P("grp", None, "seq"),
        P("grp", "seq"),
        P("grp", "seq", None),
        P("grp", "seq"),
        P("grp", "seq", None),
        P("grp", "seq"),
        P("grp", "seq"),
        P("grp", "seq"),
        P(("seq", "grp")),
        P("seq", "grp"),
        P("seq", "grp"),
        P("grp", "seq"),
        P("seq", "grp", None),
    )
    return jax.shard_map(
        per_device,
        mesh=mesh,
        in_specs=placed,
        out_specs=(
            P("seq", "grp", None),
            P("seq", "grp", None),
            P(("seq", "grp")),
            P("seq", "grp"),
            P("seq", "grp"),
            P("grp", None, "seq"),
            P("grp", "seq"),
            P("grp", "seq", None),
            P("grp", "seq"),
            P("grp", "seq", None),
            P("grp", "seq"),
            P("grp", "seq"),
            P("grp", "seq"),
            P(("seq", "grp")),
            P("seq", "grp"),
            P("seq", "grp"),
            P("grp", "seq"),
        ),
        check_vma=False,
    )
```

time: 2270 us -> 1370 us (0.60); the launches traced: 2240 us -> 1370 us
  local copies, waits for them, and re-layouts: 1120 us -> 61 us
  waiting for transfers between devices: 627 us -> 1050 us
  blocking collectives: 152 us -> 13.4 us
  other arithmetic: 184 us -> 56 us
  Pallas kernels: 0 us -> 32.2 us
    pad x34 -> x0, local copies, waits for them, and re-layouts: 861 us -> none  [run_scan(): return lax.associative_scan(combine, (decay_rate, drive_term), axis=1)[1]]
    unnamed x30 -> x36, waiting for transfers between devices: 8.21 us -> 149 us
    slice x27 -> x11, local copies, waits for them, and re-layouts: 149 us -> 8.48 us  [the longest x2 1.98 us: per_device(): rec_grads[:, :, tap_count + 3]]
    unnamed x3 -> x0, blocking collectives: 96.3 us -> none
    reduce_scatter x8, waiting for transfers between devices: 242 us -> 325 us  [scatter_tokens(): lax.psum_scatter(parts[s], 'grp', scatter_dimension=0, tiled=True)]
    all_gather x8, waiting for transfers between devices: 190 us -> 249 us  [gather_tokens(): lax.all_gather(values[s], 'grp', axis=0, tiled=True)]
    reduce_scatter x2, waiting for transfers between devices: 19.8 us -> 75.8 us  [sum_rows(): lax.psum_scatter(low[0], 'seq', scatter_dimension=0, tiled=True)]
    add x38 -> x1, other arithmetic: 50.3 us -> 4.42 us  [per_device(): grad_residual + norm_back(normed_one_term, normal_one, inverse_one, gains...]
  transfers between devices with their start and end apart: 29 -> 32, of which waited for: 18 -> 30; matrix products, arithmetic and copies ran while one was open for 61% -> 13% of each run, Pallas kernels for 0% -> 2%
where the time goes in v2:
time: 1370 us
  waiting for transfers between devices  1050 us (77%)
  matrix products  138 us (10%)
  local copies, waits for them, and re-layouts  61 us (4%)
  other arithmetic  56 us (4%)
  Pallas kernels  32.2 us (2%)
  between operations  16.6 us (1%)
    reduce_scatter x8, waiting for transfers between devices, scatter_tokens(): lax.psum_scatter(parts[s], 'grp', scatter_dimension=0, tiled=True)  325 us
    all_gather x8, waiting for transfers between devices, gather_tokens(): lax.all_gather(values[s], 'grp', axis=0, tiled=True)  249 us
    unnamed x36, waiting for transfers between devices  149 us
    reduce_scatter x2, waiting for transfers between devices, sum_rows(): lax.psum_scatter(low[0], 'seq', scatter_dimension=0, tiled=True)  75.8 us
    all_gather x2, waiting for transfers between devices, gather_rows(): lax.all_gather(weights[1], 'seq', axis=0, tiled=True)  63.3 us
    all_gather x2, waiting for transfers between devices, gather_rows(): lax.all_gather(weights[0], 'seq', axis=0, tiled=True)  61 us
    reduce_scatter x2, waiting for transfers between devices, sum_rows(): lax.psum_scatter(low[1], 'seq', scatter_dimension=0, tiled=True)  53.4 us
    dot_general x6, matrix products, matmul_tn(): lax.dot_general(left, right, (((0,), (0,)), ((), ())), preferred_element_...  47.2 us
  transfers between devices with their start and end apart: 32, of which 30 were waited for; matrix products, arithmetic and copies ran while one was open for 13% of the time, Pallas kernels for 2%

profile of v2, /device:TPU:0, one launch (start us, length us, event | category | flops | bytes accessed | tf_op | source)
XLA Modules:
  0.0 1365.3 jit_solution(12580571815210976090)
XLA Ops:
  8.0 13.4 all-gather.3
  32.7 39.1 %all-reduce.9.cloned.1.call-done = bf16[130816]{0:T(1024)(128)(2,1)} async-done(((bf16[130816]{0:T(1024)(128)(2,1)}), bf16[130816]{0:T(1024)(128)(2,1)}) %all-reduce.9.cloned.1.call-update) | async-done | bytes 261648
  81.4 32.0 %all-gather.19.cloned.1.call-done = bf16[768,2048]{1,0:T(8,128)(2,1)} async-done(((bf16[96,2048]{1,0:T(8,128)(2,1)}), bf16[768,2048]{1,0:T(8,128)(2,1)}) %all-gather.19.cloned.1.call-update) | async-done | bytes 3145744 | tf_op jit(solution)/shard_map/all_gather | solution.py:46
  113.4 39.5 %all-gather.21.cloned.1.call-done = bf16[768,2048]{1,0:T(8,128)(2,1)} async-done(((bf16[96,2048]{1,0:T(8,128)(2,1)}), bf16[768,2048]{1,0:T(8,128)(2,1)}) %all-gather.21.cloned.1.call-update) | async-done | bytes 3145744 | tf_op jit(solution)/shard_map/all_gather | solution.py:46
  152.9 6.0 pad_maximum_fusion
  159.0 24.4 %all-gather.23.cloned.1.call-done = bf16[2048,352]{0,1:T(8,128)(2,1)} async-done(((bf16[512,352]{0,1:T(8,128)(2,1)}), bf16[2048,352]{0,1:T(8,128)(2,1)}) %all-gather.23.cloned.1.call-update) | async-done | bytes 1441808 | tf_op jit(solution)/shard_map/all_gather | solution.py:39
  189.9 25.0 %all-gather.25.cloned.1.call-done = bf16[2048,352]{0,1:T(8,128)(2,1)} async-done(((bf16[512,352]{0,1:T(8,128)(2,1)}), bf16[2048,352]{0,1:T(8,128)(2,1)}) %all-gather.25.cloned.1.call-update) | async-done | bytes 1441808 | tf_op jit(solution)/shard_map/all_gather | solution.py:38
  221.0 11.8 rec_forward.1
  239.0 7.5 all-gather.27.cloned.1.call-done
  258.6 37.0 %reduce-scatter.21.cloned.1.call-done = bf16[96,2048]{1,0:T(8,128)(2,1)} async-done(((bf16[768,2048]{1,0:T(8,128)(2,1)}), bf16[96,2048]{1,0:T(8,128)(2,1)}) %reduce-scatter.21.cloned.1.call-update) | async-done | bytes 393232 | tf_op jit(solution)/shard_map/reduce_scatter | solution.py:54
  295.6 41.9 %reduce-scatter.23.cloned.1.call-done = bf16[96,2048]{1,0:T(8,128)(2,1)} async-done(((bf16[768,2048]{1,0:T(8,128)(2,1)}), bf16[96,2048]{1,0:T(8,128)(2,1)}) %reduce-scatter.23.cloned.1.call-update) | async-done | bytes 393232 | tf_op jit(solution)/shard_map/reduce_scatter | solution.py:54
  348.4 28.7 %all-gather.43.cloned.1.call-done = bf16[1,768,2048]{2,1,0:T(8,128)(2,1)} async-done(((bf16[1,96,2048]{2,1,0:T(8,128)(2,1)}), bf16[1,768,2048]{2,1,0:T(8,128)(2,1)}) %all-gather.43.cloned.1.call-update) | async-done | bytes 3145744 | tf_op jit(solution)/shard_map/all_gather | solution.py:46
  377.2 39.3 %all-gather.45.cloned.1.call-done = bf16[1,768,2048]{2,1,0:T(8,128)(2,1)} async-done(((bf16[1,96,2048]{2,1,0:T(8,128)(2,1)}), bf16[1,768,2048]{2,1,0:T(8,128)(2,1)}) %all-gather.45.cloned.1.call-update) | async-done | bytes 3145744 | tf_op jit(solution)/shard_map/all_gather | solution.py:46
  416.5 6.1 pad_maximum_fusion.2
  422.6 33.4 %all-gather.29.cloned.1.call-done = bf16[768,2048]{1,0:T(8,128)(2,1)} async-done(((bf16[96,2048]{1,0:T(8,128)(2,1)}), bf16[768,2048]{1,0:T(8,128)(2,1)}) %all-gather.29.cloned.1.call-update) | async-done | bytes 3145744 | tf_op jit(solution)/shard_map/all_gather | solution.py:46
  456.0 39.3 %all-gather.31.cloned.1.call-done = bf16[768,2048]{1,0:T(8,128)(2,1)} async-done(((bf16[96,2048]{1,0:T(8,128)(2,1)}), bf16[768,2048]{1,0:T(8,128)(2,1)}) %all-gather.31.cloned.1.call-update) | async-done | bytes 3145744 | tf_op jit(solution)/shard_map/all_gather | solution.py:46
  501.3 38.9 %all-gather.35.cloned.1.call-done = bf16[2048,768]{1,0:T(8,128)(2,1)} async-done(((bf16[512,768]{1,0:T(8,128)(2,1)}), bf16[2048,768]{1,0:T(8,128)(2,1)}) %all-gather.35.cloned.1.call-update) | async-done | bytes 3145744 | tf_op jit(solution)/shard_map/all_gather | solution.py:39
  540.2 9.9 fusion.50
  550.1 35.9 %all-gather.33.cloned.1.call-done = bf16[2048,768]{1,0:T(8,128)(2,1)} async-done(((bf16[512,768]{1,0:T(8,128)(2,1)}), bf16[2048,768]{1,0:T(8,128)(2,1)}) %all-gather.33.cloned.1.call-update) | async-done | bytes 3145744 | tf_op jit(solution)/shard_map/all_gather | solution.py:38
  586.1 9.5 fusion.49
  595.5 36.2 %all-gather.37.cloned.1.call-done = bf16[768,2048]{1,0:T(8,128)(2,1)} async-done(((bf16[768,512]{1,0:T(8,128)(2,1)}), bf16[768,2048]{1,0:T(8,128)(2,1)}) %all-gather.37.cloned.1.call-update) | async-done | bytes 3145744 | tf_op jit(solution)/shard_map/all_gather | solution.py:40
  631.7 14.4 %multiply_convert_fusion = (bf16[1536,768]{1,0:T(8,128)(2,1)S(1)}, bf16[1536,768]{1,0:T(8,128)(2,1)S(1)}, bf16[1536,768]{1,0:T(8,128)(2,1)}) fusion(f32[1536,768]{1,0:T(8,128)} %fusion.49, f32[1536,768]{1,0:T(8,128)} %fusion.50, bf16[1536,2048]{1,0:T(8,128)(2,1)} %bitcast.166, bf16[768,2048]{1,0:T(8,128)(2,1)} %all-gather.37.cloned.1.call-done), kind=kOutput, calls=%fused_computation.17 | convolution fusion | flops 4862509056 | bytes 25952256 | tf_op jit(solution)/shard_map/dot_general | solution.py:26
  646.2 8.1 fusion.51
  654.3 8.4 add_convert_fusion.1
  666.6 39.9 %reduce-scatter.29.cloned.1.call-done = bf16[96,2048]{1,0:T(8,128)(2,1)} async-done(((bf16[768,2048]{1,0:T(8,128)(2,1)}), bf16[96,2048]{1,0:T(8,128)(2,1)}) %reduce-scatter.29.cloned.1.call-update) | async-done | bytes 393232 | tf_op jit(solution)/shard_map/reduce_scatter | solution.py:54
  706.5 41.7 %reduce-scatter.31.cloned.1.call-done = bf16[96,2048]{1,0:T(8,128)(2,1)} async-done(((bf16[768,2048]{1,0:T(8,128)(2,1)}), bf16[96,2048]{1,0:T(8,128)(2,1)}) %reduce-scatter.31.cloned.1.call-update) | async-done | bytes 393232 | tf_op jit(solution)/shard_map/reduce_scatter | solution.py:54
  758.7 9.2 convolution_convert_fusion.2
  767.9 9.2 convolution_convert_fusion.3
  777.2 9.3 convolution_convert_fusion.4
  786.6 7.7 convolution_convert_fusion
  798.2 36.7 %all-gather.41.cloned.1.call-done = bf16[768,2048]{1,0:T(8,128)(2,1)} async-done(((bf16[96,2048]{1,0:T(8,128)(2,1)}), bf16[768,2048]{1,0:T(8,128)(2,1)}) %all-gather.41.cloned.1.call-update) | async-done | bytes 3145744 | tf_op jit(solution)/shard_map/all_gather | solution.py:46
  835.0 6.1 fusion.8.grad_mixed_ref
  841.1 20.4 %rec_backward.1 = (bf16[2,768,352]{2,1,0:T(8,128)(2,1)S(1)}, bf16[2,768,352]{2,1,0:T(8,128)(2,1)S(1)}, f32[352,352]{1,0:T(8,128)S(1)}, f32[352,352]{1,0:T(8,128)S(1)}, f32[8,352]{1,0:T(8,128)S(1)}) custom-call(f32[2,768,352]{2,1,0:T(8,128)S(1)} %fusion.8.grad_mixed_ref, f32[2,768,352]{2,1,0:T(8,128)S(1)} %fusion.27.branch_ref, ...), custom_call_target="tpu_custom_call" | custom-call | tf_op jit(solution)/shard_map/rec_backward/pallas_call | solution.py:285
  869.1 6.5 fusion.10
  876.0 6.6 fusion.11
  882.6 6.5 fusion.12
  906.1 22.0 %reduce-scatter.45.cloned.1.call-done = bf16[512,768]{1,0:T(8,128)(2,1)} async-done(((bf16[2048,768]{1,0:T(8,128)(2,1)}), bf16[512,768]{1,0:T(8,128)(2,1)}) %reduce-scatter.45.cloned.1.call-update) | async-done | bytes 786448 | tf_op jit(solution)/shard_map/reduce_scatter | solution.py:64
  930.5 44.9 %reduce-scatter.43.cloned.1.call-done = bf16[512,768]{1,0:T(8,128)(2,1)} async-done(((bf16[2048,768]{1,0:T(8,128)(2,1)}), bf16[512,768]{1,0:T(8,128)(2,1)}) %reduce-scatter.43.cloned.1.call-update) | async-done | bytes 786448 | tf_op jit(solution)/shard_map/reduce_scatter | solution.py:63
  977.8 40.4 %reduce-scatter.25.cloned.1.call-done = bf16[96,2048]{1,0:T(8,128)(2,1)} async-done(((bf16[768,2048]{1,0:T(8,128)(2,1)}), bf16[96,2048]{1,0:T(8,128)(2,1)}) %reduce-scatter.25.cloned.1.call-update) | async-done | bytes 393232 | tf_op jit(solution)/shard_map/reduce_scatter | solution.py:54
  1018.2 41.7 %reduce-scatter.27.cloned.1.call-done = bf16[96,2048]{1,0:T(8,128)(2,1)} async-done(((bf16[768,2048]{1,0:T(8,128)(2,1)}), bf16[96,2048]{1,0:T(8,128)(2,1)}) %reduce-scatter.27.cloned.1.call-update) | async-done | bytes 393232 | tf_op jit(solution)/shard_map/reduce_scatter | solution.py:54
  1062.0 46.6 %all-reduce.11.cloned.1.call-done = f32[2,176,360]{2,0,1:T(2,128)} async-done(((f32[2,176,360]{2,0,1:T(2,128)}), f32[2,176,360]{2,0,1:T(2,128)}) %all-reduce.11.cloned.1.call-update) | async-done | bytes 506896
  1115.8 26.0 %reduce-scatter.41.cloned.1.call-done = bf16[352,512]{1,0:T(8,128)(2,1)} async-done(((bf16[352,2048]{1,0:T(8,128)(2,1)}), bf16[352,512]{1,0:T(8,128)(2,1)}) %reduce-scatter.41.cloned.1.call-update) | async-done | bytes 360464 | tf_op jit(solution)/shard_map/reduce_scatter | solution.py:65
  1143.8 31.0 %reduce-scatter.37.cloned.1.call-done = bf16[512,352]{0,1:T(8,128)(2,1)} async-done(((bf16[2048,352]{0,1:T(8,128)(2,1)}), bf16[512,352]{0,1:T(8,128)(2,1)}) %reduce-scatter.37.cloned.1.call-update) | async-done | bytes 360464 | tf_op jit(solution)/shard_map/reduce_scatter | solution.py:63
  1176.7 31.4 %reduce-scatter.39.cloned.1.call-done = bf16[512,352]{0,1:T(8,128)(2,1)} async-done(((bf16[2048,352]{0,1:T(8,128)(2,1)}), bf16[512,352]{0,1:T(8,128)(2,1)}) %reduce-scatter.39.cloned.1.call-update) | async-done | bytes 360464 | tf_op jit(solution)/shard_map/reduce_scatter | solution.py:64
  1210.1 40.7 %reduce-scatter.33.cloned.1.call-done = bf16[96,2048]{1,0:T(8,128)(2,1)} async-done(((bf16[768,2048]{1,0:T(8,128)(2,1)}), bf16[96,2048]{1,0:T(8,128)(2,1)}) %reduce-scatter.33.cloned.1.call-update) | async-done | bytes 393232 | tf_op jit(solution)/shard_map/reduce_scatter | solution.py:54
  1250.8 41.7 %reduce-scatter.35.cloned.1.call-done = bf16[96,2048]{1,0:T(8,128)(2,1)} async-done(((bf16[768,2048]{1,0:T(8,128)(2,1)}), bf16[96,2048]{1,0:T(8,128)(2,1)}) %reduce-scatter.35.cloned.1.call-update) | async-done | bytes 393232 | tf_op jit(solution)/shard_map/reduce_scatter | solution.py:54
  1296.6 26.9 %reduce-scatter.49.cloned.1.call-done = f32[512,2]{1,0:T(8,128)} async-done(((f32[2048,2]{1,0:T(8,128)}), f32[512,2]{1,0:T(8,128)}) %reduce-scatter.49.cloned.1.call-update) | async-done | bytes 4112
  1328.0 28.3 %reduce-scatter.51.cloned.1.call-done = f32[64,2]{1,0:T(8,128)} async-done(((f32[512,2]{1,0:T(8,128)}), f32[64,2]{1,0:T(8,128)}) %reduce-scatter.51.cloned.1.call-update) | async-done | bytes 528
  (237 shorter events, 141.5 us)
Async XLA Ops:
  7.2 66.5 %copy-start.18 = (bf16[2,96,2048]{2,1,0:T(8,128)(2,1)S(1)}, bf16[2,96,2048]{2,1,0:T(8,128)(2,1)}, u32[]{:S(2)}) copy-start(bf16[2,96,2048]{2,1,0:T(8,128)(2,1)} %param.17) | copy-start | bytes 2359300
  7.2 64.6 %all-reduce.9.cloned.1.call-start = ((), (), s32[]{:S(2)}) async-start(), calls=%async_computation.44 | async-start | bytes 524288
  30.7 82.7 %all-gather.19.cloned.1.call-start = ((), (), s32[]{:S(2)}) async-start(), calls=%async_computation.16 | async-start | bytes 3538944 | tf_op jit(solution)/shard_map/all_gather | solution.py:46
  75.0 77.9 %all-gather.21.cloned.1.call-start = ((), (), s32[]{:S(2)}) async-start(), calls=%async_computation.17 | async-start | bytes 3538944 | tf_op jit(solution)/shard_map/all_gather | solution.py:46
  75.7 107.7 %all-gather.23.cloned.1.call-start = ((), (), s32[]{:S(2)}) async-start(), calls=%async_computation.18 | async-start | bytes 1802240 | tf_op jit(solution)/shard_map/all_gather | solution.py:39
  76.3 138.7 %all-gather.25.cloned.1.call-start = ((), (), s32[]{:S(2)}) async-start(), calls=%async_computation.19 | async-start | bytes 1802240 | tf_op jit(solution)/shard_map/all_gather | solution.py:38
  76.9 169.7 %all-gather.27.cloned.1.call-start = ((), (), s32[]{:S(2)}) async-start(), calls=%async_computation.20 | async-start | bytes 1802240 | tf_op jit(solution)/shard_map/all_gather | solution.py:40
  77.4 218.1 %reduce-scatter.21.cloned.1.call-start = ((), (), s32[]{:S(2)}) async-start(), calls=%async_computation.21 | async-start | bytes 3538944 | tf_op jit(solution)/shard_map/reduce_scatter | solution.py:54
  255.0 82.4 %reduce-scatter.23.cloned.1.call-start = ((), (), s32[]{:S(2)}) async-start(), calls=%async_computation.22 | async-start | bytes 3538944 | tf_op jit(solution)/shard_map/reduce_scatter | solution.py:54
  255.8 121.4 %all-gather.43.cloned.1.call-start = ((), (), s32[]{:S(2)}) async-start(), calls=%async_computation.42 | async-start | bytes 3538944 | tf_op jit(solution)/shard_map/all_gather | solution.py:46
  257.9 158.6 %all-gather.45.cloned.1.call-start = ((), (), s32[]{:S(2)}) async-start(), calls=%async_computation.43 | async-start | bytes 3538944 | tf_op jit(solution)/shard_map/all_gather | solution.py:46
  258.5 197.5 %all-gather.29.cloned.1.call-start = ((), (), s32[]{:S(2)}) async-start(), calls=%async_computation.23 | async-start | bytes 3538944 | tf_op jit(solution)/shard_map/all_gather | solution.py:46
  345.9 149.4 %all-gather.31.cloned.1.call-start = ((), (), s32[]{:S(2)}) async-start(), calls=%async_computation.24 | async-start | bytes 3538944 | tf_op jit(solution)/shard_map/all_gather | solution.py:46
  346.5 193.7 %all-gather.35.cloned.1.call-start = ((), (), s32[]{:S(2)}) async-start(), calls=%async_computation.26 | async-start | bytes 3932160 | tf_op jit(solution)/shard_map/all_gather | solution.py:39
  347.2 238.8 %all-gather.33.cloned.1.call-start = ((), (), s32[]{:S(2)}) async-start(), calls=%async_computation.25 | async-start | bytes 3932160 | tf_op jit(solution)/shard_map/all_gather | solution.py:38
  347.8 283.9 %all-gather.37.cloned.1.call-start = ((), (), s32[]{:S(2)}) async-start(), calls=%async_computation.27 | async-start | bytes 3932160 | tf_op jit(solution)/shard_map/all_gather | solution.py:40
  348.4 358.1 %reduce-scatter.29.cloned.1.call-start = ((), (), s32[]{:S(2)}) async-start(), calls=%async_computation.30 | async-start | bytes 3538944 | tf_op jit(solution)/shard_map/reduce_scatter | solution.py:54
  631.7 14.4 %copy-start.36 = (bf16[2048,768]{1,0:T(8,128)(2,1)S(1)}, bf16[2048,768]{1,0:T(8,128)(2,1)}, u32[]{:S(2)}) copy-start(bf16[2048,768]{1,0:T(8,128)(2,1)} %all-gather.33.cloned.1.call-done) | copy-start | bytes 9437188
  646.2 8.1 copy-start.37
  646.2 8.1 copy-start.38
  646.2 8.1 copy-start.35
  666.0 82.2 %reduce-scatter.31.cloned.1.call-start = ((), (), s32[]{:S(2)}) async-start(), calls=%async_computation.31 | async-start | bytes 3538944 | tf_op jit(solution)/shard_map/reduce_scatter | solution.py:54
  666.6 131.6 %all-gather.39.cloned.1.call-start = ((), (), s32[]{:S(2)}) async-start(), calls=%async_computation.32 | async-start | bytes 3538944 | tf_op jit(solution)/shard_map/all_gather | solution.py:46
  757.9 77.1 %all-gather.41.cloned.1.call-start = ((), (), s32[]{:S(2)}) async-start(), calls=%async_computation.33 | async-start | bytes 3538944 | tf_op jit(solution)/shard_map/all_gather | solution.py:46
  758.6 145.0 %reduce-scatter.47.cloned.1.call-start = ((), (), s32[]{:S(2)}) async-start(), calls=%async_computation.41 | async-start | bytes 3932160 | tf_op jit(solution)/shard_map/reduce_scatter | solution.py:65
  767.9 160.3 %reduce-scatter.45.cloned.1.call-start = ((), (), s32[]{:S(2)}) async-start(), calls=%async_computation.40 | async-start | bytes 3932160 | tf_op jit(solution)/shard_map/reduce_scatter | solution.py:64
  777.1 198.2 %reduce-scatter.43.cloned.1.call-start = ((), (), s32[]{:S(2)}) async-start(), calls=%async_computation.39 | async-start | bytes 3932160 | tf_op jit(solution)/shard_map/reduce_scatter | solution.py:63
  786.6 231.6 %reduce-scatter.25.cloned.1.call-start = ((), (), s32[]{:S(2)}) async-start(), calls=%async_computation.28 | async-start | bytes 3538944 | tf_op jit(solution)/shard_map/reduce_scatter | solution.py:54
  797.6 262.3 %reduce-scatter.27.cloned.1.call-start = ((), (), s32[]{:S(2)}) async-start(), calls=%async_computation.29 | async-start | bytes 3538944 | tf_op jit(solution)/shard_map/reduce_scatter | solution.py:54
  798.1 310.4 %all-reduce.11.cloned.1.call-start = ((), (), s32[]{:S(2)}) async-start(), calls=%async_computation.47 | async-start | bytes 1081344
  869.1 6.9 copy-start.11
  869.1 272.8 %reduce-scatter.41.cloned.1.call-start = ((), (), s32[]{:S(2)}) async-start(), calls=%async_computation.38 | async-start | bytes 1802240 | tf_op jit(solution)/shard_map/reduce_scatter | solution.py:65
  875.7 299.1 %reduce-scatter.37.cloned.1.call-start = ((), (), s32[]{:S(2)}) async-start(), calls=%async_computation.36 | async-start | bytes 1802240 | tf_op jit(solution)/shard_map/reduce_scatter | solution.py:63
  876.0 6.7 copy-start.2
  882.6 325.6 %reduce-scatter.39.cloned.1.call-start = ((), (), s32[]{:S(2)}) async-start(), calls=%async_computation.37 | async-start | bytes 1802240 | tf_op jit(solution)/shard_map/reduce_scatter | solution.py:64
  889.1 361.7 %reduce-scatter.33.cloned.1.call-start = ((), (), s32[]{:S(2)}) async-start(), calls=%async_computation.34 | async-start | bytes 3538944 | tf_op jit(solution)/shard_map/reduce_scatter | solution.py:54
  902.3 390.1 %reduce-scatter.35.cloned.1.call-start = ((), (), s32[]{:S(2)}) async-start(), calls=%async_computation.35 | async-start | bytes 3538944 | tf_op jit(solution)/shard_map/reduce_scatter | solution.py:54
  902.9 420.5 %reduce-scatter.49.cloned.1.call-start = ((), (), s32[]{:S(2)}) async-start(), calls=%async_computation.45 | async-start | bytes 1310720
  1062.0 232.6 %copy-start.19 = (bf16[2,96,2048]{2,1,0:T(8,128)(2,1)S(1)}, bf16[2,96,2048]{2,1,0:T(8,128)(2,1)}, u32[]{:S(2)}) copy-start(bf16[2,96,2048]{2,1,0:T(8,128)(2,1)} %param.17) | copy-start | bytes 2359300
  1062.0 232.6 %copy-start.29 = (f32[1,4,512]{2,0,1:T(1,128)S(1)}, f32[1,4,512]{2,0,1:T(1,128)}, u32[]{:S(2)}) copy-start(f32[1,4,512]{2,0,1:T(1,128)} %copy-done.28) | copy-start | bytes 24580
  1062.0 232.6 %copy-start.32 = (f32[2,96]{1,0:T(2,128)S(1)}, f32[2,96]{1,0:T(2,128)}, u32[]{:S(2)}) copy-start(f32[2,96]{1,0:T(2,128)} %copy-done.31) | copy-start | bytes 2308
  1115.8 179.3 %copy-start.30 = (f32[2048]{0:T(1024)S(1)}, f32[2048]{0:T(1024)}, u32[]{:S(2)}) copy-start(f32[2048]{0:T(1024)} %get-tuple-element.105) | copy-start | bytes 24580
  1176.7 146.8 %copy-start.22 = (f32[192,2048]{1,0:T(8,128)S(1)}, f32[192,2048]{1,0:T(8,128)}, u32[]{:S(2)}) copy-start(f32[192,2048]{1,0:T(8,128)} %copy-done.20) | copy-start | bytes 4718596
  1176.7 146.8 %copy-start.24 = (bf16[2,96,2048]{2,1,0:T(8,128)(2,1)S(1)}, bf16[2,96,2048]{2,1,0:T(8,128)(2,1)}, u32[]{:S(2)}) copy-start(bf16[2,96,2048]{2,1,0:T(8,128)(2,1)} %param.33) | copy-start | bytes 2359300
  1176.7 146.8 %copy-start.27 = (f32[1,4,512]{2,0,1:T(1,128)S(1)}, f32[1,4,512]{2,0,1:T(1,128)}, u32[]{:S(2)}) copy-start(f32[1,4,512]{2,0,1:T(1,128)} %get-tuple-element.147) | copy-start | bytes 24580
  1176.7 146.8 %copy-start.33 = (f32[2,96]{1,0:T(2,128)S(1)}, f32[2,96]{1,0:T(2,128)}, u32[]{:S(2)}) copy-start(f32[2,96]{1,0:T(2,128)} %add_rsqrt_fusion) | copy-start | bytes 2308
  1176.7 146.8 %copy-start.34 = (f32[2,96]{1,0:T(2,128)S(1)}, f32[2,96]{1,0:T(2,128)}, u32[]{:S(2)}) copy-start(f32[2,96]{1,0:T(2,128)} %broadcast_multiply_fusion.1) | copy-start | bytes 2308
  1296.5 59.7 %reduce-scatter.51.cloned.1.call-start = ((), (), s32[]{:S(2)}) async-start(), calls=%async_computation.46 | async-start | bytes 294912
  (23 other events, 59.5 us)
Sparse Core Ops, SparseCore 0:
  30.8 41.0 all-reduce.8
  75.1 38.2 all-gather.18
  115.7 37.1 all-gather.20
  154.7 28.5 all-gather.22
  185.2 29.7 all-gather.24
  216.8 29.7 all-gather.26
  255.2 40.3 reduce-scatter.20
  298.0 39.4 reduce-scatter.22
  339.7 37.3 all-gather.42
  379.3 37.1 all-gather.44
  418.8 37.1 all-gather.28
  458.2 37.1 all-gather.30
  497.3 42.8 all-gather.34
  542.0 43.9 all-gather.32
  587.9 43.8 all-gather.36
  666.1 40.3 reduce-scatter.28
  708.7 39.3 reduce-scatter.30
  758.0 37.4 all-gather.38
  797.8 37.1 all-gather.40
  838.1 42.8 reduce-scatter.46
  884.2 43.9 reduce-scatter.44
  931.4 43.9 reduce-scatter.42
  977.8 40.3 reduce-scatter.24
  1020.4 39.3 reduce-scatter.26
  1063.8 44.7 all-reduce.10
  1111.6 30.2 reduce-scatter.40
  1144.7 30.0 reduce-scatter.36
  1178.0 30.1 reduce-scatter.38
  1210.5 40.2 reduce-scatter.32
  1253.0 39.4 reduce-scatter.34
  1296.6 26.7 reduce-scatter.48
  1325.8 30.3 reduce-scatter.50

commit v3 on v2

--- a/solution.py
+++ b/solution.py
@@ -10,6 +10,7 @@
 epsilon = 1e-06
 gelu_slope = math.sqrt(2.0 / math.pi)
 gelu_cubic = 0.044715
+MESH = pl.DeviceIdType.MESH
 
 
 def matmul(left, right):
@@ -39,22 +40,6 @@
         lax.all_gather(weights[1], "seq", axis=0, tiled=True),
         lax.all_gather(weights[2], "seq", axis=1, tiled=True),
     )
-
-
-def gather_tokens(values):
-    return jnp.stack(
-        [lax.all_gather(values[s], "grp", axis=0, tiled=True) for s in range(values.shape[0])]
-    ).reshape(-1, values.shape[-1])
-
-
-def scatter_tokens(values, seqs_here):
-    parts = values.astype(jnp.bfloat16).reshape(seqs_here, -1, values.shape[-1])
-    return jnp.concatenate(
-        [
-            lax.psum_scatter(parts[s], "grp", scatter_dimension=0, tiled=True)
-            for s in range(seqs_here)
-        ]
-    ).astype(jnp.float32)
 
 
 def sum_rows(grads):
@@ -64,6 +49,12 @@
         lax.psum_scatter(low[1], "seq", scatter_dimension=0, tiled=True).astype(jnp.float32),
         lax.psum_scatter(low[2], "seq", scatter_dimension=1, tiled=True).astype(jnp.float32),
     )
+
+
+def padded_rows(values):
+    flat = values.reshape(values.shape[0], -1)
+    flat = jnp.pad(flat, ((0, 0), (0, -flat.shape[1] % 1024)))
+    return flat.reshape(values.shape[0], -1, 128)
 
 
 def head_diagonal(blocks):
@@ -299,81 +290,722 @@
     )(grad_mixed, branch, feed, feed, conv, rate, gate, state, state, vectors, softness, gate_a, gate_x)
 
 
+def line_place():
+    return lax.axis_size("grp") // 2, lax.axis_index("grp") // 2, lax.axis_index("grp") % 2
+
+
+def greet_line():
+    chips, chip, core = line_place()
+    barrier = pltpu.get_barrier_semaphore()
+
+    def signal(place):
+        pl.semaphore_signal(barrier, inc=1, device_id={"grp": place}, device_id_type=MESH)
+
+    signal(chip * 2 + 1 - core)
+
+    @pl.when(chip > 0)
+    def _():
+        signal(chip * 2 + core - 2)
+
+    @pl.when(chip < chips - 1)
+    def _():
+        signal(chip * 2 + core + 2)
+
+    ends = (chip == 0).astype(jnp.int32) + (chip == chips - 1).astype(jnp.int32)
+    pl.semaphore_wait(barrier, 3 - ends)
+
+
+def greet_axes(axes):
+    barrier = pltpu.get_barrier_semaphore()
+    for axis in axes:
+        size = lax.axis_size(axis)
+        for k in range(1, size):
+            pl.semaphore_signal(
+                barrier,
+                inc=1,
+                device_id={axis: lax.rem(lax.axis_index(axis) + k, size)},
+                device_id_type=MESH,
+            )
+    pl.semaphore_wait(barrier, sum(lax.axis_size(axis) - 1 for axis in axes))
+
+
+class Gather:
+    def __init__(self, sources, outs, rows, send_sem, recv_sem, own_sem):
+        self.chips, self.chip, self.core = line_place()
+        self.me = self.chip * 2 + self.core
+        self.sources, self.outs, self.rows = sources, outs, rows
+        self.send_sem, self.recv_sem, self.own_sem = send_sem, recv_sem, own_sem
+
+    def slot(self, p, origin):
+        return self.outs[p].at[pl.ds(pl.multiple_of(origin * self.rows, self.rows), self.rows), :]
+
+    def copy(self, p, source, origin, target, way):
+        return pltpu.make_async_remote_copy(
+            src_ref=source,
+            dst_ref=self.slot(p, origin),
+            send_sem=self.send_sem.at[way, p, origin],
+            recv_sem=self.recv_sem.at[p, origin],
+            device_id={"grp": target},
+            device_id_type=MESH,
+        )
+
+    def to_right(self, p, source, origin):
+        return self.copy(p, source, origin, self.me + 2, 0)
+
+    def to_left(self, p, source, origin):
+        return self.copy(p, source, origin, self.me - 2, 1)
+
+    def to_partner(self, p, source, origin):
+        return self.copy(p, source, origin, self.chip * 2 + 1 - self.core, 2)
+
+    def own(self, p):
+        return pltpu.make_async_copy(self.sources[p], self.slot(p, self.me), self.own_sem.at[p])
+
+    def start(self, p):
+        source = self.sources[p]
+
+        @pl.when(self.chip < self.chips - 1)
+        def _():
+            self.to_right(p, source, self.me).start()
+
+        @pl.when(self.chip > 0)
+        def _():
+            self.to_left(p, source, self.me).start()
+
+        self.to_partner(p, source, self.me).start()
+        self.own(p).start()
+
+    def hop(self, p, h):
+        left_origin = self.me - 2 - 2 * h
+        right_origin = self.me + 2 + 2 * h
+
+        @pl.when(self.chip - 1 - h >= 0)
+        def _():
+            here = self.slot(p, left_origin)
+            self.to_right(p, here, left_origin).wait_recv()
+
+            @pl.when(self.chip < self.chips - 1)
+            def _():
+                self.to_right(p, here, left_origin).start()
+
+            self.to_partner(p, here, left_origin).start()
+
+        @pl.when(self.chip + 1 + h <= self.chips - 1)
+        def _():
+            here = self.slot(p, right_origin)
+            self.to_left(p, here, right_origin).wait_recv()
+
+            @pl.when(self.chip > 0)
+            def _():
+                self.to_left(p, here, right_origin).start()
+
+            self.to_partner(p, here, right_origin).start()
+
+    def finish(self, p):
+        for c in range(self.chips):
+            origin = c * 2 + 1 - self.core
+            self.to_partner(p, self.slot(p, origin), origin).wait_recv()
+        self.own(p).wait()
+        for c in range(self.chips):
+            origin = c * 2 + self.core
+            here = self.slot(p, origin)
+            self.to_partner(p, here, origin).wait_send()
+
+            @pl.when((c <= self.chip) & (self.chip < self.chips - 1))
+            def _():
+                self.to_right(p, here, origin).wait_send()
+
+            @pl.when((c >= self.chip) & (self.chip > 0))
+            def _():
+                self.to_left(p, here, origin).wait_send()
+
+
+def gather_sems(pieces):
+    n = lax.axis_size("grp")
+    return [
+        pltpu.SemaphoreType.DMA((3, pieces, n)),
+        pltpu.SemaphoreType.DMA((pieces, n)),
+        pltpu.SemaphoreType.DMA((pieces,)),
+    ]
+
+
+class Scatter:
+    def __init__(self, rows, part, out, swap_in, line_in, send_sem, recv_sem):
+        self.chips, self.chip, self.core = line_place()
+        self.me = self.chip * 2 + self.core
+        self.rows, self.part, self.out = rows, part, out
+        self.swap_in, self.line_in = swap_in, line_in
+        self.send_sem, self.recv_sem = send_sem, recv_sem
+
+    def copy(self, dest, place, way, slot, p):
+        return pltpu.make_async_remote_copy(
+            src_ref=self.out.at[p, slot],
+            dst_ref=dest,
+            send_sem=self.send_sem.at[way, p, slot],
+            recv_sem=self.recv_sem.at[way, p, slot],
+            device_id={"grp": place},
+            device_id_type=MESH,
+        )
+
+    def swap(self, p, c):
+        return self.copy(self.swap_in.at[p, c], self.chip * 2 + 1 - self.core, 0, c, p)
+
+    def right(self, p, c):
+        return self.copy(self.line_in.at[p, c], self.me + 2, 1, c, p)
+
+    def left(self, p, c):
+        slot = jnp.where(c == self.chip - 1, self.chips, c)
+        return self.copy(self.line_in.at[p, slot], self.me - 2, 2, c, p)
+
+    def from_right(self, p, c):
+        slot = jnp.where(c == self.chip, self.chips, c)
+        return self.copy(self.line_in.at[p, slot], self.me + 2, 2, c, p)
+
+    def fill(self, p, s, lefts, rights, transposed, width=512):
+        def rows_of(ref, core):
+            at = [pl.multiple_of((c * 2 + core) * self.rows, self.rows) for c in range(self.chips)]
+            return jnp.concatenate([ref[s, pl.ds(a, self.rows), :] for a in at], axis=0)
+
+        def product(core, store):
+            chosen = [rows_of(ref, core) for ref in lefts]
+
+            @pl.loop(0, self.out.shape[-1] // width)
+            def _(j):
+                columns = pl.ds(pl.multiple_of(j * width, width), width)
+                total = None
+                for left, right in zip(chosen, rights):
+                    term = matmul_nt(left, right[columns, :]) if transposed else matmul(left, right[:, columns])
+                    total = term if total is None else total + term
+                for c in range(self.chips):
+                    store(c, columns, total[c * self.rows : (c + 1) * self.rows])
+
+        def to_out(c, columns, value):
+            self.out[p, c, :, columns] = value.astype(jnp.bfloat16)
+
+        def to_part(c, columns, value):
+            self.part[p, c, :, columns] = value
+
+        product(1 - self.core, to_out)
+        for c in range(self.chips):
+            self.swap(p, c).start()
+        product(self.core, to_part)
+
+    def own(self, p, c):
+        self.swap(p, c).wait_recv()
+        return self.part[p, c] + self.swap_in[p, c].astype(jnp.float32)
+
+    def hop(self, p, h):
+        c = self.chips - 1 - h
+
+        @pl.when(c > self.chip)
+        def _():
+            self.swap(p, c).wait_send()
+
+            @pl.when(self.chip == 0)
+            def _():
+                self.out[p, c] = self.own(p, c).astype(jnp.bfloat16)
+
+            @pl.when(self.chip > 0)
+            def _():
+                total = self.own(p, c)
+                self.right(p, c).wait_recv()
+                self.out[p, c] = (total + self.line_in[p, c].astype(jnp.float32)).astype(jnp.bfloat16)
+
+            self.right(p, c).start()
+
+        @pl.when(h < self.chip)
+        def _():
+            self.swap(p, h).wait_send()
+
+            @pl.when(self.chip == self.chips - 1)
+            def _():
+                self.out[p, h] = self.own(p, h).astype(jnp.bfloat16)
+
+            @pl.when(self.chip < self.chips - 1)
+            def _():
+                total = self.own(p, h)
+                self.from_right(p, h).wait_recv()
+                self.out[p, h] = (total + self.line_in[p, h].astype(jnp.float32)).astype(jnp.bfloat16)
+
+            self.left(p, h).start()
+
+    def result(self, p):
+        chip = self.chip
+        self.part[p, chip] = self.own(p, chip)
+
+        @pl.when(chip > 0)
+        def _():
+            self.right(p, chip).wait_recv()
+            self.part[p, chip] += self.line_in[p, chip].astype(jnp.float32)
+
+        @pl.when(chip < self.chips - 1)
+        def _():
+            self.from_right(p, chip).wait_recv()
+            self.part[p, chip] += self.line_in[p, self.chips].astype(jnp.float32)
+
+        return self.part.at[p, chip]
+
+    def finish(self, p):
+        self.swap(p, self.chip).wait_send()
+        for c in range(self.chips):
+
+            @pl.when(c > self.chip)
+            def _():
+                self.right(p, c).wait_send()
+
+            @pl.when(c < self.chip)
+            def _():
+                self.left(p, c).wait_send()
+
+
+def scatter_scratch(pieces, rows, width):
+    chips = lax.axis_size("grp") // 2
+    return [
+        pltpu.VMEM((pieces, chips, rows, width), jnp.float32),
+        pltpu.VMEM((pieces, chips, rows, width), jnp.bfloat16),
+        pltpu.VMEM((pieces, chips, rows, width), jnp.bfloat16),
+        pltpu.VMEM((pieces, chips + 1, rows, width), jnp.bfloat16),
+        pltpu.SemaphoreType.DMA((3, pieces, chips)),
+        pltpu.SemaphoreType.DMA((3, pieces, chips)),
+    ]
+
+
+in_vmem = pl.BlockSpec(memory_space=pltpu.VMEM)
+in_hbm = pl.BlockSpec(memory_space=pl.ANY)
+
+
+def call(body, name, number, inputs, in_specs, outs, out_specs, scratch, us):
+    return pl.pallas_call(
+        body,
+        in_specs=in_specs,
+        out_specs=out_specs,
+        out_shape=outs,
+        scratch_shapes=scratch,
+        name=name,
+        cost_estimate=pl.CostEstimate(
+            flops=us * 1000000000, bytes_accessed=us * 3000000, transcendentals=0
+        ),
+        compiler_params=pltpu.CompilerParams(
+            collective_id=number, has_side_effects=True, vmem_limit_bytes=60 << 20
+        ),
+    )(*inputs)
+
+
+def views(ref):
+    return [ref.at[s] for s in range(ref.shape[0])]
+
+
+def first_body(seqs, x_ref, pack_ref, *refs):
+    full_ref, params_ref, gains_ref = refs[:3]
+    small_send, small_recv, gain_send, gain_recv = refs[6:]
+    greet_axes(("seq", "grp"))
+    gather = Gather(views(x_ref), views(full_ref), x_ref.shape[1], *refs[3:6])
+    for s in range(seqs):
+        gather.start(s)
+    size, me = lax.axis_size("seq"), lax.axis_index("seq")
+
+    def small(k, owner):
+        return pltpu.make_async_remote_copy(
+            src_ref=pack_ref,
+            dst_ref=params_ref.at[owner],
+            send_sem=small_send.at[k],
+            recv_sem=small_recv.at[k],
+            device_id={"seq": lax.rem(me + k, size)},
+            device_id_type=MESH,
+        )
+
+    for k in range(1, size):
+        small(k, me).start()
+    params_ref[me] = pack_ref[...]
+    for k in range(1, size):
+        small(k, lax.rem(me - k + size, size)).wait_recv()
+    n, place = lax.axis_size("grp"), lax.axis_index("grp")
+    for owner in range(size):
+        gains_ref[place, owner] = params_ref[owner, pl.ds(pack_ref.shape[0] - 8, 8), :]
+
+    def gain(k, owner):
+        return pltpu.make_async_remote_copy(
+            src_ref=gains_ref.at[place],
+            dst_ref=gains_ref.at[owner],
+            send_sem=gain_send.at[k],
+            recv_sem=gain_recv.at[k],
+            device_id={"grp": lax.rem(place + k, n)},
+            device_id_type=MESH,
+        )
+
+    for k in range(1, n):
+        gain(k, place).start()
+    for h in range(gather.chips - 1):
+        for s in range(seqs):
+            gather.hop(s, h)
+    for k in range(1, n):
+        gain(k, lax.rem(place - k + n, n)).wait_recv()
+    for k in range(1, size):
+        small(k, me).wait_send()
+    for k in range(1, n):
+        gain(k, place).wait_send()
+    for s in range(seqs):
+        gather.finish(s)
+
+
+def gather_first(layer_in, pack):
+    seqs, rows, width = layer_in.shape
+    n, size = lax.axis_size("grp"), lax.axis_size("seq")
+    full = jax.ShapeDtypeStruct((seqs, n * rows, width), jnp.bfloat16)
+    return call(
+        lambda *refs: first_body(seqs, *refs), "gather_first", 1,
+        (layer_in, pack), [in_hbm, in_vmem],
+        [
+            full,
+            jax.ShapeDtypeStruct((size,) + pack.shape, jnp.float32),
+            jax.ShapeDtypeStruct((n, size, 8, 128), jnp.float32),
+        ],
+        [in_hbm] + [in_vmem] * 2,
+        gather_sems(seqs)
+        + [pltpu.SemaphoreType.DMA((size,))] * 2
+        + [pltpu.SemaphoreType.DMA((n,))] * 2,
+        70,
+    )
+
+
+def mean_of(values):
+    return jnp.mean(values, axis=-1, keepdims=True)
+
+
+def mixer_out_body(seqs, mixed_ref, out_w_ref, x_ref, grad_ref, gain_ref, *refs):
+    residual_ref, normed_ref, grads_ref, low_ref = refs[:4]
+    greet_line()
+    rows = x_ref.shape[1]
+    gather = Gather(
+        views(low_ref) + views(grad_ref), views(normed_ref) + views(grads_ref), rows, *refs[4:7]
+    )
+    scatter = Scatter(rows, *refs[7:])
+    hops = range(gather.chips - 1)
+    for s in range(seqs):
+        scatter.fill(s, s, [mixed_ref], [out_w_ref], False)
+        if s == 0:
+            gather.start(seqs)
+    for s in range(seqs):
+        for h in hops:
+            scatter.hop(s, h)
+            if s == 0:
+                gather.hop(seqs, h)
+            else:
+                gather.hop(s - 1, h)
+        residual = x_ref[s].astype(jnp.float32) + scatter.result(s)[...]
+        residual_ref[s] = residual
+        normal = residual * lax.rsqrt(mean_of(residual * residual) + epsilon)
+        low_ref[s] = (normal * gain_ref[...]).astype(jnp.bfloat16)
+        gather.start(s)
+    for s in range(1, seqs):
+        gather.start(seqs + s)
+    for h in hops:
+        gather.hop(seqs - 1, h)
+        for s in range(1, seqs):
+            gather.hop(seqs + s, h)
+    for s in range(seqs):
+        scatter.finish(s)
+        gather.finish(s)
+        gather.finish(seqs + s)
+
+
+def mixer_out(mixed, out_w, layer_in, out_grad, gain):
+    seqs, rows, width = layer_in.shape
+    full = jax.ShapeDtypeStruct((seqs, lax.axis_size("grp") * rows, width), jnp.bfloat16)
+    return call(
+        lambda *refs: mixer_out_body(seqs, *refs), "mixer_out", 2,
+        (mixed, out_w, layer_in, out_grad, gain), [in_vmem] * 3 + [in_hbm] + [in_vmem],
+        [jax.ShapeDtypeStruct(layer_in.shape, jnp.float32), full, full],
+        [in_vmem] + [in_hbm] * 2,
+        [pltpu.VMEM(layer_in.shape, jnp.bfloat16)]
+        + gather_sems(2 * seqs)
+        + scatter_scratch(seqs, rows, width),
+        130,
+    )
+
+
+def mlp_back_body(seqs, gate_ref, up_ref, gate_w_ref, up_w_ref, residual_ref, grad_ref, gain_ref, *refs):
+    grad_residual_ref, gain_grad_ref, full_ref, low_ref = refs[:4]
+    greet_line()
+    rows = grad_ref.shape[1]
+    gather = Gather(views(low_ref), views(full_ref), rows, *refs[4:7])
+    scatter = Scatter(rows, *refs[7:])
+    hops = range(gather.chips - 1)
+    for s in range(seqs):
+        scatter.fill(s, s, [gate_ref, up_ref], [gate_w_ref, up_w_ref], True)
+    gain_grad_ref[...] = jnp.zeros_like(gain_grad_ref)
+    for s in range(seqs):
+        for h in hops:
+            scatter.hop(s, h)
+            if s:
+                gather.hop(s - 1, h)
+        term = scatter.result(s)[...]
+        residual = residual_ref[s]
+        inverse = lax.rsqrt(mean_of(residual * residual) + epsilon)
+        normal = residual * inverse
+        gain_grad_ref[0:1, :] += jnp.sum(term * normal, axis=0, keepdims=True)
+        grad = grad_ref[s].astype(jnp.float32) + norm_back(term, normal, inverse, gain_ref[...])
+        grad_residual_ref[s] = grad
+        low_ref[s] = grad.astype(jnp.bfloat16)
+        gather.start(s)
+    for h in hops:
+        gather.hop(seqs - 1, h)
+    for s in range(seqs):
+        scatter.finish(s)
+        gather.finish(s)
+
+
+def mlp_back(grad_gate, grad_up, gate_w, up_w, residual, out_grad, gain):
+    seqs, rows, width = residual.shape
+    full = jax.ShapeDtypeStruct((seqs, lax.axis_size("grp") * rows, width), jnp.bfloat16)
+    return call(
+        lambda *refs: mlp_back_body(seqs, *refs), "mlp_back", 3,
+        (grad_gate, grad_up, gate_w, up_w, residual, out_grad, gain), [in_vmem] * 7,
+        [
+            jax.ShapeDtypeStruct(residual.shape, jnp.float32),
+            jax.ShapeDtypeStruct((8, width), jnp.float32),
+            full,
+        ],
+        [in_vmem] * 2 + [in_hbm],
+        [pltpu.VMEM(residual.shape, jnp.bfloat16)] + gather_sems(seqs) + scatter_scratch(seqs, rows, width),
+        110,
+    )
+
+
+class Exchange:
+    def __init__(self, axis, source, slots, send_sem, recv_sem):
+        self.axis, self.source, self.slots = axis, source, slots
+        self.size, self.me = lax.axis_size(axis), lax.axis_index(axis)
+        self.send_sem, self.recv_sem = send_sem, recv_sem
+
+    def copy(self, k, owner):
+        peer = lax.rem(self.me + k, self.size)
+        return pltpu.make_async_remote_copy(
+            src_ref=self.source(peer),
+            dst_ref=self.slots.at[owner],
+            send_sem=self.send_sem.at[k],
+            recv_sem=self.recv_sem.at[k],
+            device_id={self.axis: peer},
+            device_id_type=MESH,
+        )
+
+    def start(self):
+        for k in range(1, self.size):
+            self.copy(k, self.me).start()
+
+    def finish(self):
+        for k in range(1, self.size):
+            self.copy(k, lax.rem(self.me - k + self.size, self.size)).wait_recv()
+        for k in range(1, self.size):
+            self.copy(k, self.me).wait_send()
+
+    def total(self):
+        total = self.slots[0]
+        for k in range(1, self.size):
+            total = total + self.slots[k]
+        return total
+
+
+def out_body(seqs, hidden_ref, down_w_ref, residual_ref, layer_out_ref, scatter, first):
+    def fill(s):
+        scatter.fill(first + s, s, [hidden_ref], [down_w_ref], False)
+
+    def store(s):
+        layer_out_ref[s] = (residual_ref[s] + scatter.result(first + s)[...]).astype(jnp.bfloat16)
+
+    return fill, store
+
+
+def last_body(
+    seqs, with_out, branch_ref, feed_ref, branch_w_ref, rec_w_ref, x_ref, grad_ref, gain_ref, gain_two_ref, rec_ref, *refs
+):
+    if with_out:
+        hidden_ref, down_w_ref, residual_ref = refs[:3]
+        refs = refs[3:]
+    grad_x_ref, rec_sum_ref, gain_sum_ref = refs[:3]
+    refs = refs[3:]
+    if with_out:
+        layer_out_ref = refs[0]
+        refs = refs[1:]
+    rec_slots, gain_local, gain_part, gain_slots, part_slots = refs[:5]
+    rec_sems, gain_sems, part_sems = refs[5:7], refs[7:9], refs[9:11]
+    greet_axes(("seq", "grp"))
+    rows = x_ref.shape[1]
+    scatter = Scatter(rows, *refs[11:])
+    rec = Exchange("seq", lambda peer: rec_ref.at[peer], rec_slots, *rec_sems)
+    rec.start()
+    rec_slots[rec.me] = rec_ref[rec.me]
+    fills = [lambda s=s: scatter.fill(s, s, [branch_ref, feed_ref], [branch_w_ref, rec_w_ref], True) for s in range(seqs)]
+    stores = []
+    if with_out:
+        fill, store = out_body(seqs, hidden_ref, down_w_ref, residual_ref, layer_out_ref, scatter, seqs)
+        fills += [lambda s=s: fill(s) for s in range(seqs)]
+        stores = [lambda s=s: store(s) for s in range(seqs)]
+    gain_local[...] = jnp.zeros_like(gain_local)
+    gain_local[1:2, :] = gain_two_ref[0:1, :]
+
+    def finish_grad(s):
+        term = scatter.result(s)[...]
+        inputs = x_ref[s].astype(jnp.float32)
+        inverse = lax.rsqrt(mean_of(inputs * inputs) + epsilon)
+        normal = inputs * inverse
+        gain_local[0:1, :] += jnp.sum(term * normal, axis=0, keepdims=True)
+        grad_x_ref[s] = grad_ref[s] + norm_back(term, normal, inverse, gain_ref[...])
+
+    stores = [lambda s=s: finish_grad(s) for s in range(seqs)] + stores
+    ahead = seqs
+    for p in range(min(ahead, len(fills))):
+        fills[p]()
+    for p in range(len(fills)):
+        for h in range(scatter.chips - 1):
+            scatter.hop(p, h)
+        if p + ahead < len(fills):
+            fills[p + ahead]()
+        stores[p]()
+        if p == seqs - 1:
+            part = gain_part.shape[1]
+
+            def lanes(owner):
+                return gain_local.at[:, pl.ds(pl.multiple_of(owner * part, part), part)]
+
+            across = Exchange("seq", lanes, gain_slots, *gain_sems)
+            across.start()
+            gain_slots[across.me] = lanes(across.me)[...]
+    across.finish()
+    gain_part[...] = across.total()
+    along = Exchange("grp", lambda peer: gain_part, part_slots, *part_sems)
+    along.start()
+    part_slots[along.me] = gain_part[...]
+    rec.finish()
+    rec_sum_ref[...] = rec.total()
+    along.finish()
+    gain_sum_ref[...] = along.total()
+    for p in range(len(fills)):
+        scatter.finish(p)
+
+
+def last(grad_branch, grad_feed, branch_w, rec_w, layer_in, grad_residual, gain, gain_two_grad, rec_blocks, out_inputs):
+    seqs, rows, width = layer_in.shape
+    size, n = lax.axis_size("seq"), lax.axis_size("grp")
+    f32 = jnp.float32
+    inputs = (grad_branch, grad_feed, branch_w, rec_w, layer_in, grad_residual, gain, gain_two_grad, rec_blocks)
+    inputs = inputs + tuple(out_inputs)
+    outs = [
+        jax.ShapeDtypeStruct(layer_in.shape, f32),
+        jax.ShapeDtypeStruct(rec_blocks.shape[1:], f32),
+        jax.ShapeDtypeStruct((8, width // size), f32),
+    ]
+    if out_inputs:
+        outs.append(jax.ShapeDtypeStruct(layer_in.shape, jnp.bfloat16))
+    return call(
+        lambda *refs: last_body(seqs, bool(out_inputs), *refs), "last", 4,
+        inputs, [in_vmem] * len(inputs), outs, [in_vmem] * len(outs),
+        [
+            pltpu.VMEM(rec_blocks.shape, f32),
+            pltpu.VMEM((8, width), f32),
+            pltpu.VMEM((8, width // size), f32),
+            pltpu.VMEM((size, 8, width // size), f32),
+            pltpu.VMEM((n, 8, width // size), f32),
+        ]
+        + [pltpu.SemaphoreType.DMA((size,))] * 4
+        + [pltpu.SemaphoreType.DMA((n,))] * 2
+        + scatter_scratch(seqs * (2 if out_inputs else 1), rows, width),
+        110,
+    )
+
+
+def out_only_body(seqs, hidden_ref, down_w_ref, residual_ref, layer_out_ref, *scratch):
+    greet_line()
+    scatter = Scatter(residual_ref.shape[1], *scratch)
+    fill, store = out_body(seqs, hidden_ref, down_w_ref, residual_ref, layer_out_ref, scatter, 0)
+    for s in range(seqs):
+        fill(s)
+    for s in range(seqs):
+        for h in range(scatter.chips - 1):
+            scatter.hop(s, h)
+        store(s)
+    for s in range(seqs):
+        scatter.finish(s)
+
+
+def out_only(hidden, down_w, residual):
+    seqs, rows, width = residual.shape
+    return call(
+        lambda *refs: out_only_body(seqs, *refs), "layer_out", 5,
+        (hidden, down_w, residual), [in_vmem] * 3,
+        [jax.ShapeDtypeStruct(residual.shape, jnp.bfloat16)], [in_vmem],
+        scatter_scratch(seqs, rows, width), 60,
+    )[0]
+
+
 def per_device(
     layer_in, gain_one, w_branch, w_rec, conv_w, conv_b, gate_a_w, gate_a_b, gate_x_w, gate_x_b,
     decay_logit, w_out, gain_two, mlp_gate, mlp_up, mlp_down, out_grad,
 ):
     seqs_here, positions, model_width = layer_in.shape
-    tokens_here = seqs_here * positions
     heads_here, tap_count, part_dim = conv_w.shape
-    seq_devices = lax.axis_size("seq")
+    seq_devices, grp_devices = lax.axis_size("seq"), lax.axis_size("grp")
     head_dim = part_dim * seq_devices
     channels = heads_here * head_dim
     f32 = jnp.float32
 
-    own_gains = lax.all_gather(jnp.stack([gain_one, gain_two]), "grp", axis=1, tiled=True)
     own_params = jnp.concatenate(
         [jnp.transpose(conv_w, (0, 2, 1))]
         + [v[:, :, None] for v in (conv_b, gate_a_b, gate_x_b, decay_logit)]
         + [gate_a_w, gate_x_w],
         axis=2,
-    )
-    packed = jnp.concatenate([own_gains.reshape(-1), own_params.reshape(-1)])
-    packed = lax.all_gather(packed, "seq", axis=0).reshape(seq_devices, -1)
-    gains = packed[:, : own_gains.size].reshape(seq_devices, 2, -1)
-    gains = jnp.transpose(gains, (1, 0, 2)).reshape(2, model_width).astype(f32)
-    params = packed[:, own_gains.size :].reshape(seq_devices, heads_here, part_dim, -1)
+    ).astype(f32)
+    own_gains = jnp.concatenate([gain_one, gain_two]).astype(f32)
+    pack = jnp.concatenate(
+        [padded_rows(own_params.reshape(1, -1))[0], padded_rows(own_gains.reshape(1, -1))[0]]
+    )
+    x_full, params, gains = gather_first(layer_in, pack)
+    branch_w, rec_w, out_w = gather_rows((w_branch, w_rec, w_out))
+    gate_w, up_w, down_w = gather_rows((mlp_gate, mlp_up, mlp_down))
+
+    gains = gains.reshape(grp_devices, seq_devices, -1)[:, :, : own_gains.size]
+    gains = jnp.transpose(gains.reshape(grp_devices, seq_devices, 2, -1), (2, 1, 0, 3)).reshape(2, 1, -1)
+    params = params.reshape(seq_devices, -1)[:, : own_params.size]
+    params = params.reshape((seq_devices,) + own_params.shape)
     params = jnp.transpose(params, (1, 0, 2, 3)).reshape(heads_here, head_dim, -1)
-    vectors = params[:, :, : tap_count + 4].reshape(channels, -1).T.astype(f32)
-    diag_a = head_diagonal(params[:, :, tap_count + 4 : tap_count + 4 + head_dim])
-    diag_x = head_diagonal(params[:, :, tap_count + 4 + head_dim :])
+    vectors = params[:, :, : tap_count + 4].reshape(channels, -1).T
+    at = tap_count + 4
+    diag_a = head_diagonal(params[:, :, at : at + head_dim].astype(jnp.bfloat16))
+    diag_x = head_diagonal(params[:, :, at + head_dim :].astype(jnp.bfloat16))
     logit = vectors[tap_count + 3 :]
     softness = jax.nn.softplus(-logit)
 
-    branch_w, rec_w, out_w = gather_rows((w_branch, w_rec, w_out))
-    gate_w, up_w, down_w = gather_rows((mlp_gate, mlp_up, mlp_down))
-
-    inputs = layer_in.reshape(tokens_here, model_width).astype(f32)
-    inverse_one = lax.rsqrt(jnp.mean(inputs * inputs, axis=-1, keepdims=True) + epsilon)
-    normal_one = inputs * inverse_one
-    normed_own = (normal_one * gains[0]).astype(jnp.bfloat16)
-    normed_one = gather_tokens(normed_own.reshape(layer_in.shape))
+    inputs = x_full.astype(f32)
+    normal_one = inputs * lax.rsqrt(mean_of(inputs * inputs) + epsilon)
+    normed_one = (normal_one * gains[0]).astype(jnp.bfloat16).reshape(-1, model_width)
     branch_pre = matmul(normed_one, branch_w).reshape(seqs_here, -1, channels)
     feed = matmul(normed_one, rec_w).astype(jnp.bfloat16).reshape(seqs_here, -1, channels)
     conv, rate, gate, state, mixed = rec_forward(feed, branch_pre, vectors, softness, diag_a, diag_x)
+    residual, normed_two, grad_output = mixer_out(mixed, out_w, layer_in, out_grad, gains[1])
     mixed = mixed.reshape(-1, channels)
-    residual = inputs + scatter_tokens(matmul(mixed, out_w), seqs_here)
-    inverse_two = lax.rsqrt(jnp.mean(residual * residual, axis=-1, keepdims=True) + epsilon)
-    normal_two = residual * inverse_two
-    normed_two_own = (normal_two * gains[1]).astype(jnp.bfloat16)
-    normed_two = gather_tokens(normed_two_own.reshape(layer_in.shape))
+    normed_two = normed_two.reshape(-1, model_width)
+    grad_output = grad_output.reshape(-1, model_width)
     up_proj = matmul(normed_two, up_w)
     gate_act, gate_pull = jax.vjp(jax.nn.gelu, matmul(normed_two, gate_w))
     hidden = (gate_act * up_proj).astype(jnp.bfloat16)
-    layer_sum = residual + scatter_tokens(matmul(hidden, down_w), seqs_here)
-    layer_out = layer_sum.astype(jnp.bfloat16).reshape(layer_in.shape)
-
-    grad_output = gather_tokens(out_grad)
     grad_down = matmul_tn(hidden, grad_output)
     grad_hidden = matmul_nt(grad_output, down_w)
     grad_gate = gate_pull(grad_hidden * up_proj)[0].astype(jnp.bfloat16)
     grad_up = (grad_hidden * gate_act).astype(jnp.bfloat16)
-    normed_two_term = scatter_tokens(
-        matmul_nt(grad_gate, gate_w) + matmul_nt(grad_up, up_w), seqs_here
-    )
     mlp_grads = sum_rows((matmul_tn(normed_two, grad_gate), matmul_tn(normed_two, grad_up), grad_down))
-    gain_two_local = jnp.sum(normed_two_term * normal_two, axis=0)
-    grad_residual = out_grad.reshape(tokens_here, model_width).astype(f32) + norm_back(
-        normed_two_term, normal_two, inverse_two, gains[1]
-    )
-    residual_low = gather_tokens(grad_residual.astype(jnp.bfloat16).reshape(layer_in.shape))
+
+    def by_seq(values):
+        return values.reshape(seqs_here, -1, values.shape[-1])
+
+    grad_residual, gain_two_grad, residual_low = mlp_back(
+        by_seq(grad_gate), by_seq(grad_up), gate_w, up_w, residual, out_grad, gains[1]
+    )
+    residual_low = residual_low.reshape(-1, model_width)
     out_weight_grad = matmul_tn(mixed, residual_low)
-    grad_mixed = matmul_nt(residual_low, out_w).reshape(seqs_here, -1, channels)
+    grad_mixed = by_seq(matmul_nt(residual_low, out_w))
     grad_branch, grad_feed, square_a, square_x, sums = rec_backward(
         grad_mixed, branch_pre, feed, conv, rate, gate, state, vectors, softness, diag_a, diag_x
     )
-    grad_branch = grad_branch.reshape(-1, channels)
-    grad_feed = grad_feed.reshape(-1, channels)
     vector_grads = jnp.concatenate(
         [sums[: tap_count + 3], 8.0 * jax.nn.sigmoid(-logit) * sums[tap_count + 3 :]]
     )
@@ -385,33 +1017,40 @@
         ],
         axis=2,
     )
-    rec_grads = lax.psum_scatter(rec_grads, "seq", scatter_dimension=1, tiled=True)
-    normed_one_term = scatter_tokens(
-        matmul_nt(grad_branch, branch_w) + matmul_nt(grad_feed, rec_w), seqs_here
-    )
+    rec_grads = rec_grads.reshape(heads_here, seq_devices, part_dim, -1)
+    rec_blocks = padded_rows(jnp.transpose(rec_grads, (1, 0, 2, 3)))
     mixer_grads = sum_rows(
-        (matmul_tn(normed_one, grad_branch), matmul_tn(normed_one, grad_feed), out_weight_grad)
-    )
-    gain_one_local = jnp.sum(normed_one_term * normal_one, axis=0)
-    grad_input = grad_residual + norm_back(normed_one_term, normal_one, inverse_one, gains[0])
-    gain_grads = lax.psum_scatter(
-        jnp.stack([gain_one_local, gain_two_local]), "seq", scatter_dimension=1, tiled=True
-    )
-    gain_grads = lax.psum_scatter(gain_grads, "grp", scatter_dimension=1, tiled=True)
-    at = tap_count + 4
+        (
+            matmul_tn(normed_one, grad_branch.reshape(-1, channels)),
+            matmul_tn(normed_one, grad_feed.reshape(-1, channels)),
+            out_weight_grad,
+        )
+    )
+    last_inputs = (
+        grad_branch, grad_feed, branch_w, rec_w, layer_in, grad_residual, gains[0], gain_two_grad, rec_blocks
+    )
+    out_inputs = (by_seq(hidden), down_w, residual)
+    if grp_devices > 8:
+        layer_out = out_only(*out_inputs)
+        grad_x, rec_sum, gain_sum = last(*last_inputs, ())
+    else:
+        grad_x, rec_sum, gain_sum, layer_out = last(*last_inputs, out_inputs)
+    rec_sum = rec_sum.reshape(-1)[: own_params.size].reshape(own_params.shape)
+    own_part = gain_one.shape[0]
+    gain_grads = lax.dynamic_slice_in_dim(gain_sum, lax.axis_index("grp") * own_part, own_part, 1)
     return (
         layer_out,
-        grad_input.reshape(layer_in.shape),
+        grad_x,
         gain_grads[0],
         mixer_grads[0],
         mixer_grads[1],
-        jnp.transpose(rec_grads[:, :, :tap_count], (0, 2, 1)),
-        rec_grads[:, :, tap_count],
-        rec_grads[:, :, at : at + head_dim],
-        rec_grads[:, :, tap_count + 1],
-        rec_grads[:, :, at + head_dim :],
-        rec_grads[:, :, tap_count + 2],
-        rec_grads[:, :, tap_count + 3],
+        jnp.transpose(rec_sum[:, :, :tap_count], (0, 2, 1)),
+        rec_sum[:, :, tap_count],
+        rec_sum[:, :, at : at + head_dim],
+        rec_sum[:, :, tap_count + 1],
+        rec_sum[:, :, at + head_dim :],
+        rec_sum[:, :, tap_count + 2],
+        rec_sum[:, :, tap_count + 3],
         mixer_grads[2],
         gain_grads[1],
         mlp_grads[0],

time: 1370 us -> 758 us (0.55)
  waiting for transfers between devices: 1050 us -> 2.47 us
  Pallas kernels: 32.2 us -> 571 us
  matrix products: 138 us -> 100 us
  other arithmetic: 56 us -> 25.9 us
  local copies, waits for them, and re-layouts: 61 us -> 33 us
    pallas_call x0 -> x4, Pallas kernels: none -> 539 us  [call(): pl.pallas_call(body, in_specs=in_specs, out_specs=out_specs, out_shape=ou...]
    reduce_scatter x8 -> x0, waiting for transfers between devices: 325 us -> none  [scatter_tokens(): lax.psum_scatter(parts[s], 'grp', scatter_dimension=0, tiled=True)]
    all_gather x8 -> x0, waiting for transfers between devices: 249 us -> none  [gather_tokens(): lax.all_gather(values[s], 'grp', axis=0, tiled=True)]
    unnamed x36 -> x12, waiting for transfers between devices: 149 us -> 2.39 us
    reduce_scatter x2, waiting for transfers between devices: 75.8 us -> 0.01 us  [sum_rows(): lax.psum_scatter(low[0], 'seq', scatter_dimension=0, tiled=True)]
    all_gather x2, waiting for transfers between devices: 63.3 us -> 0.02 us  [gather_rows(): lax.all_gather(weights[1], 'seq', axis=0, tiled=True)]
    all_gather x2, waiting for transfers between devices: 61 us -> 0.02 us  [gather_rows(): lax.all_gather(weights[0], 'seq', axis=0, tiled=True)]
    reduce_scatter x2, waiting for transfers between devices: 53.4 us -> 0.01 us  [sum_rows(): lax.psum_scatter(low[1], 'seq', scatter_dimension=0, tiled=True)]
  transfers between devices with their start and end apart: 32 -> 12, of which waited for: 30 -> 0; matrix products, arithmetic and copies ran while one was open for 13% -> 16% of each run, Pallas kernels for 2% -> 58%
where the time goes in v3:
time: 758 us; the launch traced here: 748 us
  Pallas kernels  571 us (75%)
  matrix products  100 us (13%)
  local copies, waits for them, and re-layouts  33 us (4%)
  other arithmetic  25.9 us (3%)
  between operations  15.2 us (2%)
    pallas_call x4, Pallas kernels, call(): pl.pallas_call(body, in_specs=in_specs, out_specs=out_specs, out_shape=ou...  539 us
    dot_general x6, matrix products, matmul_tn(): lax.dot_general(left, right, (((0,), (0,)), ((), ())), preferred_element_...  47.7 us
    dot_general x4, matrix products, matmul(): return jnp.dot(left, right, preferred_element_type=jnp.float32)  36.3 us
    unnamed x96, local copies, waits for them, and re-layouts  22.5 us
    pallas_call x1, Pallas kernels, rec_backward(): pl.pallas_call(rec_backward_body, grid=(blocks,), in_specs=[block, block,...  20.1 us
    dot_general x2, matrix products, matmul_nt(): lax.dot_general(left, right, (((1,), (1,)), ((), ())), preferred_element_...  16.1 us
  transfers between devices with their start and end apart: 12, of which 0 were waited for; matrix products, arithmetic and copies ran while one was open for 16% of the time, Pallas kernels for 58%

profile of v3, /device:TPU:0, one launch (start us, length us, event | category | flops | bytes accessed | tf_op | source)
XLA Modules:
  0.0 748.4 jit_solution(12680722338664359545)
XLA Ops:
  7.3 1.9 copy.87
  9.3 1.9 copy.89
  16.5 63.9 %gather_first.1 = (bf16[2,768,2048]{2,1,0:T(8,128)(2,1)}, f32[4,256,128]{2,1,0:T(8,128)}, f32[8,4,8,128]{3,2,1,0:T(8,128)}) custom-call(bf16[2,96,2048]{2,1,0:T(8,128)(2,1)} %refs_4_.1, f32[256,128]{1,0:T(8,128)} %maximum_convert_fusion.refs_1_), custom_call_target="tpu_custom_call" | custom-call | flops 70000001024 | bytes 210000000 | tf_op jit(solution)/shard_map/gather_first/pallas_call | solution.py:578
  80.4 1.4 copy.116
  83.1 4.1 fusion
  89.1 7.2 fusion.2
  96.5 5.8 convolution_convert_fusion.3
  102.3 0.8 copy.88
  103.1 6.2 fusion.13.branch_ref
  109.3 12.0 %rec_forward.1 = (bf16[2,768,352]{2,1,0:T(8,128)(2,1)S(1)}, f32[2,768,352]{2,1,0:T(8,128)S(1)}, f32[2,768,352]{2,1,0:T(8,128)S(1)}, f32[2,768,352]{2,1,0:T(8,128)S(1)}, bf16[2,768,352]{2,1,0:T(8,128)(2,1)S(1)}) custom-call(bf16[2,768,352]{2,1,0:T(8,128)(2,1)S(1)} %bitcast.99, f32[2,768,352]{2,1,0:T(8,128)S(1)} %fusion.13.branch_ref, f32[8,352]{1,0:T(8,128)S(1)} %bitcast.103, ...), custom_call_target="tpu_custom_call" | custom-call | tf_op jit(solution)/shard_map/rec_forward/pallas_call | solution.py:246
  121.3 1.5 copy-done
  122.8 1.4 copy-done.1
  124.2 1.5 copy-done.7
  125.6 1.4 copy-done.9
  127.1 1.0 copy-done.10
  128.1 1.0 copy-done.25
  129.1 177.6 %mixer_out.1 = (f32[2,96,2048]{2,1,0:T(8,128)}, bf16[2,768,2048]{2,1,0:T(8,128)(2,1)}, bf16[2,768,2048]{2,1,0:T(8,128)(2,1)}) custom-call(bf16[2,768,352]{2,1,0:T(8,128)(2,1)} %copy-done.25, bf16[352,2048]{1,0:T(8,128)(2,1)} %all-gather.11.cloned.1.call-done.refs_1_, bf16[2,96,2048]{2,1,0:T(8,128)(2,1)} %refs_4_.1, bf16[2,96,2048]{2,1,0:T(8,128)(2,1)} %refs_5_.1, ...), custom_call_target="tpu_custom_call" | custom-call | flops 130000003072 | bytes 390000000 | tf_op jit(solution)/shard_map/mixer_out/pallas_call | solution.py:578
  306.7 9.9 %fusion.28 = f32[1536,768]{1,0:T(8,128)} fusion(bf16[1536,2048]{1,0:T(8,128)(2,1)} %bitcast.130, bf16[768,2048]{1,0:T(8,128)(2,1)} %all-gather.13.cloned.1.call-done.refs_10_), kind=kOutput, calls=%fused_computation.71 | convolution fusion | flops 4831838208 | bytes 14155776 | tf_op jit(solution)/shard_map/dot_general | solution.py:27
  316.6 9.5 %fusion.29 = f32[1536,768]{1,0:T(8,128)} fusion(bf16[1536,2048]{1,0:T(8,128)(2,1)} %bitcast.126, bf16[2048,768]{1,0:T(8,128)(2,1)} %all-gather.17.cloned.1.call-done.refs_2_), kind=kOutput, calls=%fused_computation.72 | convolution fusion | flops 4831838208 | bytes 14155776 | tf_op jit(solution)/shard_map/dot_general | solution.py:17
  326.1 14.8 %multiply_convert_fusion = (bf16[1536,768]{1,0:T(8,128)(2,1)}, bf16[1536,768]{1,0:T(8,128)(2,1)}, bf16[1536,768]{1,0:T(8,128)(2,1)}) fusion(f32[1536,768]{1,0:T(8,128)} %fusion.29, f32[1536,768]{1,0:T(8,128)} %fusion.28, bf16[1536,2048]{1,0:T(8,128)(2,1)} %bitcast.127, bf16[2048,768]{1,0:T(8,128)(2,1)} %all-gather.15.cloned.1.call-done.refs_3_), kind=kOutput, calls=%fused_computation.14 | convolution fusion | flops 4862509056 | bytes 25952256 | tf_op jit(solution)/shard_map/dot_general | solution.py:17
  340.9 140.4 %mlp_back.1 = (f32[2,96,2048]{2,1,0:T(8,128)}, f32[8,2048]{1,0:T(8,128)}, bf16[2,768,2048]{2,1,0:T(8,128)(2,1)}) custom-call(bf16[2,768,768]{2,1,0:T(8,128)(2,1)} %bitcast.134, bf16[2,768,768]{2,1,0:T(8,128)(2,1)} %bitcast.133, bf16[2048,768]{1,0:T(8,128)(2,1)} %all-gather.17.cloned.1.call-done.refs_2_, ...), custom_call_target="tpu_custom_call" | custom-call | flops 109999996928 | bytes 330000000 | tf_op jit(solution)/shard_map/mlp_back/pallas_call | solution.py:578
  481.4 6.4 fusion.12
  487.9 6.1 fusion.15.grad_mixed_ref
  494.1 20.1 %rec_backward.1 = (bf16[2,768,352]{2,1,0:T(8,128)(2,1)S(1)}, bf16[2,768,352]{2,1,0:T(8,128)(2,1)S(1)}, f32[352,352]{1,0:T(8,128)S(1)}, f32[352,352]{1,0:T(8,128)S(1)}, f32[8,352]{1,0:T(8,128)S(1)}) custom-call(f32[2,768,352]{2,1,0:T(8,128)S(1)} %fusion.15.grad_mixed_ref, f32[2,768,352]{2,1,0:T(8,128)S(1)} %copy-done.2, bf16[2,768,352]{2,1,0:T(8,128)(2,1)S(1)} %bitcast.100, ...), custom_call_target="tpu_custom_call" | custom-call | tf_op jit(solution)/shard_map/rec_backward/pallas_call | solution.py:276
  514.2 0.8 copy-done.12
  515.0 0.8 copy-done.14
  516.4 1.0 copy-done.22
  517.4 1.0 copy-done.24
  518.4 6.4 fusion.11
  525.0 6.5 fusion.10
  531.6 9.4 %convolution_convert_fusion = bf16[768,2048]{1,0:T(8,128)(2,1)} fusion(bf16[1536,768]{1,0:T(8,128)(2,1)S(1)} %copy-done.40, bf16[1536,2048]{1,0:T(8,128)(2,1)} %bitcast.131), kind=kOutput, calls=%fused_computation.17 | convolution fusion | flops 4833411072 | bytes 11796480 | tf_op jit(solution)/shard_map/dot_general | solution.py:21
  541.5 9.3 %convolution_convert_fusion.2 = bf16[2048,768]{1,0:T(8,128)(2,1)} fusion(bf16[1536,2048]{1,0:T(8,128)(2,1)} %bitcast.128, bf16[1536,768]{1,0:T(8,128)(2,1)} %get-tuple-element.121), kind=kOutput, calls=%fused_computation.19 | convolution fusion | flops 4833411072 | bytes 11796480 | tf_op jit(solution)/shard_map/dot_general | solution.py:21
  553.1 0.8 copy.117
  554.0 9.7 %convolution_convert_fusion.1 = bf16[2048,768]{1,0:T(8,128)(2,1)} fusion(bf16[1536,2048]{1,0:T(8,128)(2,1)} %bitcast.129, bf16[1536,768]{1,0:T(8,128)(2,1)S(1)} %copy-done.41), kind=kOutput, calls=%fused_computation.18 | convolution fusion | flops 4833411072 | bytes 11796480 | tf_op jit(solution)/shard_map/dot_general | solution.py:21
  563.6 157.0 %last.1 = (f32[2,96,2048]{2,1,0:T(8,128)}, f32[248,128]{1,0:T(8,128)}, f32[8,512]{1,0:T(8,128)}, bf16[2,96,2048]{2,1,0:T(8,128)(2,1)}) custom-call(bf16[2,768,352]{2,1,0:T(8,128)(2,1)} %copy-done.22, bf16[2,768,352]{2,1,0:T(8,128)(2,1)} %copy-done.24, bf16[2048,352]{1,0:T(8,128)(2,1)} %all-gather.9.cloned.1.call-done.refs_2_, ...), custom_call_target="tpu_custom_call" | custom-call | flops 109999996928 | bytes 330000000 | tf_op jit(solution)/shard_map/last/pallas_call | solution.py:578
  720.7 1.1 reshape.182
  722.6 0.7 copy.103
  723.3 0.7 copy.102
  724.0 0.7 constant_dynamic-slice_fusion
  724.7 0.8 slice_reduce_fusion
  726.0 1.9 convert_element_type.93
  728.0 2.0 convert_element_type.91
  730.0 2.1 convert_element_type.89
  732.0 2.5 convert_element_type.99
  734.5 2.4 convert_element_type.95
  737.0 2.4 convert_element_type.97
  739.3 0.9 copy.120
  740.2 1.1 copy.121
  (158 shorter events, 13.4 us)
Async XLA Ops:
  7.2 6.6 copy-start.33
  7.2 6.7 copy-start.34
  7.2 6.8 copy-start.35
  7.2 7.0 copy-start.36
  7.2 7.1 copy-start.37
  7.2 7.2 copy-start.32
  7.3 7.2 copy-start.31
  7.3 8.5 %copy-start.38 = (bf16[64]{0:T(256)(128)(2,1)S(1)}, bf16[64]{0:T(256)(128)(2,1)}, u32[]{:S(2)}) copy-start(bf16[64]{0:T(256)(128)(2,1)} %param.29) | copy-start | bytes 388
  7.3 8.5 %copy-start.39 = (bf16[64]{0:T(256)(128)(2,1)S(1)}, bf16[64]{0:T(256)(128)(2,1)}, u32[]{:S(2)}) copy-start(bf16[64]{0:T(256)(128)(2,1)} %param.18) | copy-start | bytes 388
  7.3 89.2 %all-gather.7.cloned.1.call-start = ((), (), s32[]{:S(2)}) async-start(), calls=%async_computation.6 | async-start | bytes 1966080 | tf_op jit(solution)/shard_map/all_gather | solution.py:40
  9.3 93.8 %all-gather.9.cloned.1.call-start = ((), (), s32[]{:S(2)}) async-start(), calls=%async_computation.7 | async-start | bytes 1966080 | tf_op jit(solution)/shard_map/all_gather | solution.py:39
  11.3 117.8 %all-gather.11.cloned.1.call-start = ((), (), s32[]{:S(2)}) async-start(), calls=%async_computation.8 | async-start | bytes 1802240 | tf_op jit(solution)/shard_map/all_gather | solution.py:41
  12.0 294.7 %all-gather.13.cloned.1.call-start = ((), (), s32[]{:S(2)}) async-start(), calls=%async_computation.9 | async-start | bytes 3932160 | tf_op jit(solution)/shard_map/all_gather | solution.py:41
  12.6 304.1 %all-gather.17.cloned.1.call-start = ((), (), s32[]{:S(2)}) async-start(), calls=%async_computation.11 | async-start | bytes 3932160 | tf_op jit(solution)/shard_map/all_gather | solution.py:39
  13.2 313.0 %all-gather.15.cloned.1.call-start = ((), (), s32[]{:S(2)}) async-start(), calls=%async_computation.10 | async-start | bytes 3932160 | tf_op jit(solution)/shard_map/all_gather | solution.py:40
  13.7 712.3 %reduce-scatter.11.cloned.1.call-start = ((), (), s32[]{:S(2)}) async-start(), calls=%async_computation.14 | async-start | bytes 1802240 | tf_op jit(solution)/shard_map/reduce_scatter | solution.py:50
  80.4 2.6 copy-start.29
  88.9 20.4 %copy-start.16 = (f32[352,8]{0,1:T(8,128)}, f32[352,8]{0,1:T(8,128)S(1)}, u32[]{:S(2)}) copy-start(f32[352,8]{0,1:T(8,128)S(1)} %reshape.173) | copy-start | bytes 33796
  88.9 20.4 %copy-start.20 = (f32[1,352]{1,0:T(1,128)}, f32[1,352]{1,0:T(1,128)S(1)}, u32[]{:S(2)}) copy-start(f32[1,352]{1,0:T(1,128)S(1)} %compare_select_fusion.softness_ref) | copy-start | bytes 4228
  96.5 12.9 %copy-start.3 = (bf16[352,352]{1,0:T(8,128)(2,1)}, bf16[352,352]{1,0:T(8,128)(2,1)S(1)}, u32[]{:S(2)}) copy-start(bf16[352,352]{1,0:T(8,128)(2,1)S(1)} %get-tuple-element.136.gate_a_ref) | copy-start | bytes 743428
  96.5 12.9 %copy-start.5 = (bf16[352,352]{1,0:T(8,128)(2,1)}, bf16[352,352]{1,0:T(8,128)(2,1)S(1)}, u32[]{:S(2)}) copy-start(bf16[352,352]{1,0:T(8,128)(2,1)S(1)} %get-tuple-element.137.gate_x_ref) | copy-start | bytes 743428
  121.3 1.5 copy-start
  122.8 1.4 copy-start.1
  124.2 1.5 copy-start.7
  125.6 1.4 copy-start.9
  340.9 140.4 %copy-start.26 = (bf16[2,768,352]{2,1,0:T(8,128)(2,1)S(1)}, bf16[2,768,352]{2,1,0:T(8,128)(2,1)}, u32[]{:S(2)}) copy-start(bf16[2,768,352]{2,1,0:T(8,128)(2,1)} %copy-done.25) | copy-start | bytes 3244036
  487.8 6.3 copy-start.2
  487.8 6.3 copy-start.17
  487.8 6.3 copy-start.21
  487.8 240.2 %reduce-scatter.9.cloned.1.call-start = ((), (), s32[]{:S(2)}) async-start(), calls=%async_computation.13 | async-start | bytes 1802240 | tf_op jit(solution)/shard_map/reduce_scatter | solution.py:49
  487.8 6.2 copy-start.4
  487.9 6.2 copy-start.6
  487.9 6.2 copy-start.8
  487.9 6.2 copy-start.11
  517.4 1.0 copy-start.24
  518.4 6.5 copy-start.23
  524.9 205.1 %reduce-scatter.7.cloned.1.call-start = ((), (), s32[]{:S(2)}) async-start(), calls=%async_computation.12 | async-start | bytes 1802240 | tf_op jit(solution)/shard_map/reduce_scatter | solution.py:48
  525.0 6.6 copy-start.40
  531.5 200.5 %reduce-scatter.17.cloned.1.call-start = ((), (), s32[]{:S(2)}) async-start(), calls=%async_computation.17 | async-start | bytes 3932160 | tf_op jit(solution)/shard_map/reduce_scatter | solution.py:50
  541.0 9.9 %copy-start.30 = (f32[1,4,8,64]{3,0,2,1:T(1,128)S(1)}, f32[1,4,8,64]{3,0,2,1:T(1,128)}, u32[]{:S(2)}) copy-start(f32[1,4,8,64]{3,0,2,1:T(1,128)} %get-tuple-element.133) | copy-start | bytes 24580
  541.0 10.6 %copy-start.15 = (f32[352,352]{1,0:T(8,128)S(1)}, f32[352,352]{1,0:T(8,128)}, u32[]{:S(2)}) copy-start(f32[352,352]{1,0:T(8,128)} %copy-done.14) | copy-start | bytes 1486852
  541.0 10.7 %copy-start.19 = (f32[8,352]{1,0:T(8,128)S(1)}, f32[8,352]{1,0:T(8,128)}, u32[]{:S(2)}) copy-start(f32[8,352]{1,0:T(8,128)} %copy-done.18) | copy-start | bytes 33796
  541.0 193.5 %reduce-scatter.13.cloned.1.call-start = ((), (), s32[]{:S(2)}) async-start(), calls=%async_computation.15 | async-start | bytes 3932160 | tf_op jit(solution)/shard_map/reduce_scatter | solution.py:48
  550.8 1.2 copy-start.13
  550.8 186.1 %reduce-scatter.15.cloned.1.call-start = ((), (), s32[]{:S(2)}) async-start(), calls=%async_computation.16 | async-start | bytes 3932160 | tf_op jit(solution)/shard_map/reduce_scatter | solution.py:49
  552.2 1.8 copy-start.41
  728.0 11.4 %copy-start.28 = (bf16[2,96,2048]{2,1,0:T(8,128)(2,1)S(1)}, bf16[2,96,2048]{2,1,0:T(8,128)(2,1)}, u32[]{:S(2)}) copy-start(bf16[2,96,2048]{2,1,0:T(8,128)(2,1)} %get-tuple-element.155) | copy-start | bytes 2359300
  730.0 10.2 %copy-start.27 = (f32[2,96,2048]{2,1,0:T(8,128)S(1)}, f32[2,96,2048]{2,1,0:T(8,128)}, u32[]{:S(2)}) copy-start(f32[2,96,2048]{2,1,0:T(8,128)} %get-tuple-element.156) | copy-start | bytes 4718596
  (6 other events, 5.2 us)
Sparse Core Ops, SparseCore 0:
  10.5 38.2 all-gather.6
  51.2 30.9 all-gather.8
  84.1 29.7 all-gather.10
  115.5 43.8 all-gather.12
  161.1 43.9 all-gather.16
  206.8 43.9 all-gather.14
  487.9 30.0 reduce-scatter.10
  525.0 30.0 reduce-scatter.8
  558.6 34.5 reduce-scatter.6
  596.3 43.9 reduce-scatter.16
  643.6 44.2 reduce-scatter.12
  691.0 43.9 reduce-scatter.14

commit v4 on v3

--- a/solution.py
+++ b/solution.py
@@ -1,3 +1,4 @@
+import functools
 import math
 
 import jax
@@ -34,21 +35,19 @@
     return inverse * (scaled - normal_part * jnp.mean(scaled * normal_part, axis=-1, keepdims=True))
 
 
-def gather_rows(weights):
-    return (
-        lax.all_gather(weights[0], "seq", axis=0, tiled=True),
-        lax.all_gather(weights[1], "seq", axis=0, tiled=True),
-        lax.all_gather(weights[2], "seq", axis=1, tiled=True),
-    )
-
-
-def sum_rows(grads):
-    low = [grad.astype(jnp.bfloat16) for grad in grads]
-    return (
-        lax.psum_scatter(low[0], "seq", scatter_dimension=0, tiled=True).astype(jnp.float32),
-        lax.psum_scatter(low[1], "seq", scatter_dimension=0, tiled=True).astype(jnp.float32),
-        lax.psum_scatter(low[2], "seq", scatter_dimension=1, tiled=True).astype(jnp.float32),
-    )
+def low_all(grads):
+    return tuple(grad.astype(jnp.bfloat16) for grad in grads)
+
+
+def sum_slots(grads, slots):
+    sums = []
+    for grad, slot, axis in zip(grads, slots, weight_axes):
+        size = slot.shape[1 + axis]
+        own = lax.dynamic_slice_in_dim(grad, lax.axis_index("seq") * size, size, axis)
+        for k in range(slot.shape[0]):
+            own = own.astype(jnp.float32) + slot[k].astype(jnp.float32)
+        sums.append(own)
+    return sums
 
 
 def padded_rows(values):
@@ -494,40 +493,31 @@
         self.swap(p, c).wait_recv()
         return self.part[p, c] + self.swap_in[p, c].astype(jnp.float32)
 
-    def hop(self, p, h):
-        c = self.chips - 1 - h
-
-        @pl.when(c > self.chip)
+    def hop(self, p, t):
+        last = self.chips - 1
+
+        def send(c, first, arrival, onward):
+            self.swap(p, c).wait_send()
+            total = self.own(p, c)
+
+            @pl.when(first)
+            def _():
+                self.out[p, c] = total.astype(jnp.bfloat16)
+
+            @pl.when(jnp.logical_not(first))
+            def _():
+                arrival(p, c).wait_recv()
+                self.out[p, c] = (total + self.line_in[p, c].astype(jnp.float32)).astype(jnp.bfloat16)
+
+            onward(p, c).start()
+
+        @pl.when(self.chip <= t)
         def _():
-            self.swap(p, c).wait_send()
-
-            @pl.when(self.chip == 0)
-            def _():
-                self.out[p, c] = self.own(p, c).astype(jnp.bfloat16)
-
-            @pl.when(self.chip > 0)
-            def _():
-                total = self.own(p, c)
-                self.right(p, c).wait_recv()
-                self.out[p, c] = (total + self.line_in[p, c].astype(jnp.float32)).astype(jnp.bfloat16)
-
-            self.right(p, c).start()
-
-        @pl.when(h < self.chip)
+            send(last - t + self.chip, self.chip == 0, self.right, self.right)
+
+        @pl.when(last - self.chip <= t)
         def _():
-            self.swap(p, h).wait_send()
-
-            @pl.when(self.chip == self.chips - 1)
-            def _():
-                self.out[p, h] = self.own(p, h).astype(jnp.bfloat16)
-
-            @pl.when(self.chip < self.chips - 1)
-            def _():
-                total = self.own(p, h)
-                self.from_right(p, h).wait_recv()
-                self.out[p, h] = (total + self.line_in[p, h].astype(jnp.float32)).astype(jnp.bfloat16)
-
-            self.left(p, h).start()
+            send(t - last + self.chip, self.chip == last, self.from_right, self.left)
 
     def result(self, p):
         chip = self.chip
@@ -591,79 +581,153 @@
     )(*inputs)
 
 
+class Exchange:
+    def __init__(self, axis, source, slot, send_sem, recv_sem, steps=None):
+        self.axis, self.source, self.slot, self.steps = axis, source, slot, steps
+        self.size, self.me = lax.axis_size(axis), lax.axis_index(axis)
+        self.send_sem, self.recv_sem = send_sem, recv_sem
+
+    def copy(self, k, owner):
+        peer = lax.rem(self.me + k, self.size)
+        return pltpu.make_async_remote_copy(
+            src_ref=self.source(peer),
+            dst_ref=self.slot(owner) if self.slot else self.steps.at[k - 1],
+            send_sem=self.send_sem.at[k],
+            recv_sem=self.recv_sem.at[k],
+            device_id={self.axis: peer},
+            device_id_type=MESH,
+        )
+
+    def own(self):
+        return pltpu.make_async_copy(self.source(self.me), self.slot(self.me), self.send_sem.at[0])
+
+    def start(self):
+        self.own().start()
+        self.start_others()
+
+    def start_others(self):
+        for k in range(1, self.size):
+            self.copy(k, self.me).start()
+
+    def finish(self):
+        self.own().wait()
+        self.finish_others()
+
+    def finish_others(self):
+        for k in range(1, self.size):
+            self.copy(k, lax.rem(self.me - k + self.size, self.size)).wait_recv()
+        for k in range(1, self.size):
+            self.copy(k, self.me).wait_send()
+
+
+def sum_of(slots):
+    total = slots[0]
+    for k in range(1, slots.shape[0]):
+        total = total + slots[k]
+    return total
+
+
+def block(ref, axis, parts):
+    size = ref.shape[axis] // parts
+
+    def view(k):
+        at = pl.ds(pl.multiple_of(k * size, size), size)
+        return ref.at[at, :] if axis == 0 else ref.at[:, at]
+
+    return view
+
+
+def weight_gathers(axes, sources, outs, send_sem, recv_sem):
+    parts = lax.axis_size("seq")
+    return [
+        Exchange(
+            "seq", lambda k, ref=source: ref, block(out, axis, parts), send_sem.at[i], recv_sem.at[i]
+        )
+        for i, (axis, source, out) in enumerate(zip(axes, sources, outs))
+    ]
+
+
+def weight_sums(axes, sources, outs, send_sem, recv_sem):
+    parts = lax.axis_size("seq")
+    return [
+        Exchange(
+            "seq", block(source, axis, parts), None, send_sem.at[i], recv_sem.at[i], out
+        )
+        for i, (axis, source, out) in enumerate(zip(axes, sources, outs))
+    ]
+
+
+def seq_sems(count):
+    return [pltpu.SemaphoreType.DMA((count, lax.axis_size("seq")))] * 2
+
+
+def gathered(block_of, axis):
+    shape = list(block_of.shape)
+    shape[axis] *= lax.axis_size("seq")
+    return jax.ShapeDtypeStruct(shape, block_of.dtype)
+
+
+def slots_of(matrix, axis):
+    shape = list(matrix.shape)
+    size = lax.axis_size("seq")
+    shape[axis] //= size
+    return jax.ShapeDtypeStruct((size - 1, *shape), matrix.dtype)
+
+
+weight_axes = (0, 0, 1)
+
+
 def views(ref):
     return [ref.at[s] for s in range(ref.shape[0])]
 
 
-def first_body(seqs, x_ref, pack_ref, *refs):
-    full_ref, params_ref, gains_ref = refs[:3]
-    small_send, small_recv, gain_send, gain_recv = refs[6:]
+def first_body(x_ref, grad_ref, pack_ref, w0, w1, w2, later_ref, full_ref, params_ref, gains_ref, o0, o1, o2, *refs):
+    small_send, small_recv, gain_send, gain_recv, weight_send, weight_recv = refs[3:]
     greet_axes(("seq", "grp"))
-    gather = Gather(views(x_ref), views(full_ref), x_ref.shape[1], *refs[3:6])
+    seqs = x_ref.shape[0]
+    gather = Gather(views(x_ref), views(full_ref), x_ref.shape[1], *refs[:3])
+    weights = weight_gathers(weight_axes, (w0, w1, w2), (o0, o1, o2), weight_send, weight_recv)
+    small = Exchange("seq", lambda k: pack_ref, lambda k: params_ref.at[k], small_send, small_recv)
+    small.start()
     for s in range(seqs):
         gather.start(s)
-    size, me = lax.axis_size("seq"), lax.axis_index("seq")
-
-    def small(k, owner):
-        return pltpu.make_async_remote_copy(
-            src_ref=pack_ref,
-            dst_ref=params_ref.at[owner],
-            send_sem=small_send.at[k],
-            recv_sem=small_recv.at[k],
-            device_id={"seq": lax.rem(me + k, size)},
-            device_id_type=MESH,
-        )
-
-    for k in range(1, size):
-        small(k, me).start()
-    params_ref[me] = pack_ref[...]
-    for k in range(1, size):
-        small(k, lax.rem(me - k + size, size)).wait_recv()
-    n, place = lax.axis_size("grp"), lax.axis_index("grp")
-    for owner in range(size):
+    for weight in weights:
+        weight.start()
+    later_ref[...] = grad_ref[...]
+    small.finish()
+    place = lax.axis_index("grp")
+    for owner in range(small.size):
         gains_ref[place, owner] = params_ref[owner, pl.ds(pack_ref.shape[0] - 8, 8), :]
-
-    def gain(k, owner):
-        return pltpu.make_async_remote_copy(
-            src_ref=gains_ref.at[place],
-            dst_ref=gains_ref.at[owner],
-            send_sem=gain_send.at[k],
-            recv_sem=gain_recv.at[k],
-            device_id={"grp": lax.rem(place + k, n)},
-            device_id_type=MESH,
-        )
-
-    for k in range(1, n):
-        gain(k, place).start()
+    gains = Exchange("grp", lambda k: gains_ref.at[place], lambda k: gains_ref.at[k], gain_send, gain_recv)
+    gains.start_others()
     for h in range(gather.chips - 1):
         for s in range(seqs):
             gather.hop(s, h)
-    for k in range(1, n):
-        gain(k, lax.rem(place - k + n, n)).wait_recv()
-    for k in range(1, size):
-        small(k, me).wait_send()
-    for k in range(1, n):
-        gain(k, place).wait_send()
+    gains.finish_others()
+    for weight in weights:
+        weight.finish()
     for s in range(seqs):
         gather.finish(s)
 
 
-def gather_first(layer_in, pack):
+def gather_first(layer_in, out_grad, pack, weights):
     seqs, rows, width = layer_in.shape
     n, size = lax.axis_size("grp"), lax.axis_size("seq")
-    full = jax.ShapeDtypeStruct((seqs, n * rows, width), jnp.bfloat16)
     return call(
-        lambda *refs: first_body(seqs, *refs), "gather_first", 1,
-        (layer_in, pack), [in_hbm, in_vmem],
+        first_body, "gather_first", 1,
+        (layer_in, out_grad, pack, *weights), [in_vmem] * 6,
         [
-            full,
+            jax.ShapeDtypeStruct(out_grad.shape, out_grad.dtype),
+            jax.ShapeDtypeStruct((seqs, n * rows, width), jnp.bfloat16),
             jax.ShapeDtypeStruct((size,) + pack.shape, jnp.float32),
             jax.ShapeDtypeStruct((n, size, 8, 128), jnp.float32),
-        ],
-        [in_hbm] + [in_vmem] * 2,
+        ]
+        + [gathered(w, axis) for w, axis in zip(weights, weight_axes)],
+        [in_vmem, in_hbm] + [in_vmem] * 2 + [in_hbm] * 3,
         gather_sems(seqs)
         + [pltpu.SemaphoreType.DMA((size,))] * 2
-        + [pltpu.SemaphoreType.DMA((n,))] * 2,
+        + [pltpu.SemaphoreType.DMA((n,))] * 2
+        + seq_sems(3),
         70,
     )
 
@@ -672,73 +736,92 @@
     return jnp.mean(values, axis=-1, keepdims=True)
 
 
-def mixer_out_body(seqs, mixed_ref, out_w_ref, x_ref, grad_ref, gain_ref, *refs):
-    residual_ref, normed_ref, grads_ref, low_ref = refs[:4]
-    greet_line()
-    rows = x_ref.shape[1]
-    gather = Gather(
-        views(low_ref) + views(grad_ref), views(normed_ref) + views(grads_ref), rows, *refs[4:7]
-    )
-    scatter = Scatter(rows, *refs[7:])
-    hops = range(gather.chips - 1)
-    for s in range(seqs):
+def sum_then_gather(scatter, gather, fills, stores):
+    hops = range(1, scatter.chips - 1)
+    fills[0]()
+    scatter.hop(0, 0)
+    for p, store in enumerate(stores):
+        if p + 1 < len(fills):
+            fills[p + 1]()
+        for h in hops:
+            scatter.hop(p, h)
+            if gather and p:
+                gather.hop(p - 1, h - 1)
+        if p + 1 < len(fills):
+            scatter.hop(p + 1, 0)
+        store()
+        if gather:
+            gather.start(p)
+            if p:
+                gather.hop(p - 1, gather.chips - 2)
+    if gather:
+        for h in range(gather.chips - 1):
+            gather.hop(len(stores) - 1, h)
+        for p in range(len(stores)):
+            gather.finish(p)
+    for p in range(len(fills)):
+        scatter.finish(p)
+
+
+def mixer_out_body(mixed_ref, out_w_ref, x_ref, gain_ref, w0, w1, w2, residual_ref, normed_ref, o0, o1, o2, low_ref, *refs):
+    greet_axes(("seq", "grp"))
+    seqs, rows, _ = x_ref.shape
+    weights = weight_gathers(weight_axes, (w0, w1, w2), (o0, o1, o2), *refs[:2])
+    for weight in weights:
+        weight.start()
+    gather = Gather(views(low_ref), views(normed_ref), rows, *refs[2:5])
+    scatter = Scatter(rows, *refs[5:])
+
+    def fill(s):
         scatter.fill(s, s, [mixed_ref], [out_w_ref], False)
-        if s == 0:
-            gather.start(seqs)
-    for s in range(seqs):
-        for h in hops:
-            scatter.hop(s, h)
-            if s == 0:
-                gather.hop(seqs, h)
-            else:
-                gather.hop(s - 1, h)
+
+    def store(s):
         residual = x_ref[s].astype(jnp.float32) + scatter.result(s)[...]
         residual_ref[s] = residual
         normal = residual * lax.rsqrt(mean_of(residual * residual) + epsilon)
         low_ref[s] = (normal * gain_ref[...]).astype(jnp.bfloat16)
-        gather.start(s)
-    for s in range(1, seqs):
-        gather.start(seqs + s)
-    for h in hops:
-        gather.hop(seqs - 1, h)
-        for s in range(1, seqs):
-            gather.hop(seqs + s, h)
-    for s in range(seqs):
-        scatter.finish(s)
-        gather.finish(s)
-        gather.finish(seqs + s)
-
-
-def mixer_out(mixed, out_w, layer_in, out_grad, gain):
+
+    sum_then_gather(
+        scatter, gather, [functools.partial(fill, s) for s in range(seqs)], [functools.partial(store, s) for s in range(seqs)]
+    )
+    for weight in weights:
+        weight.finish()
+
+
+def mixer_out(mixed, out_w, layer_in, gain, weights):
     seqs, rows, width = layer_in.shape
     full = jax.ShapeDtypeStruct((seqs, lax.axis_size("grp") * rows, width), jnp.bfloat16)
     return call(
-        lambda *refs: mixer_out_body(seqs, *refs), "mixer_out", 2,
-        (mixed, out_w, layer_in, out_grad, gain), [in_vmem] * 3 + [in_hbm] + [in_vmem],
-        [jax.ShapeDtypeStruct(layer_in.shape, jnp.float32), full, full],
-        [in_vmem] + [in_hbm] * 2,
+        mixer_out_body, "mixer_out", 2,
+        (mixed, out_w, layer_in, gain, *weights), [in_vmem] * 7,
+        [jax.ShapeDtypeStruct(layer_in.shape, jnp.float32), full]
+        + [gathered(w, axis) for w, axis in zip(weights, weight_axes)],
+        [in_vmem] + [in_hbm] * 4,
         [pltpu.VMEM(layer_in.shape, jnp.bfloat16)]
-        + gather_sems(2 * seqs)
+        + seq_sems(3)
+        + gather_sems(seqs)
         + scatter_scratch(seqs, rows, width),
-        130,
-    )
-
-
-def mlp_back_body(seqs, gate_ref, up_ref, gate_w_ref, up_w_ref, residual_ref, grad_ref, gain_ref, *refs):
-    grad_residual_ref, gain_grad_ref, full_ref, low_ref = refs[:4]
-    greet_line()
-    rows = grad_ref.shape[1]
-    gather = Gather(views(low_ref), views(full_ref), rows, *refs[4:7])
-    scatter = Scatter(rows, *refs[7:])
-    hops = range(gather.chips - 1)
-    for s in range(seqs):
+        100,
+    )
+
+
+def mlp_back_body(
+    gate_ref, up_ref, gate_w_ref, up_w_ref, residual_ref, grad_ref, gain_ref, w0, w1, w2,
+    grad_residual_ref, gain_grad_ref, full_ref, o0, o1, o2, low_ref, *refs,
+):
+    greet_axes(("seq", "grp"))
+    seqs, rows, _ = grad_ref.shape
+    sums = weight_sums(weight_axes, (w0, w1, w2), (o0, o1, o2), *refs[:2])
+    for weight in sums:
+        weight.start_others()
+    gather = Gather(views(low_ref), views(full_ref), rows, *refs[2:5])
+    scatter = Scatter(rows, *refs[5:])
+    gain_grad_ref[...] = jnp.zeros_like(gain_grad_ref)
+
+    def fill(s):
         scatter.fill(s, s, [gate_ref, up_ref], [gate_w_ref, up_w_ref], True)
-    gain_grad_ref[...] = jnp.zeros_like(gain_grad_ref)
-    for s in range(seqs):
-        for h in hops:
-            scatter.hop(s, h)
-            if s:
-                gather.hop(s - 1, h)
+
+    def store(s):
         term = scatter.result(s)[...]
         residual = residual_ref[s]
         inverse = lax.rsqrt(mean_of(residual * residual) + epsilon)
@@ -747,66 +830,35 @@
         grad = grad_ref[s].astype(jnp.float32) + norm_back(term, normal, inverse, gain_ref[...])
         grad_residual_ref[s] = grad
         low_ref[s] = grad.astype(jnp.bfloat16)
-        gather.start(s)
-    for h in hops:
-        gather.hop(seqs - 1, h)
-    for s in range(seqs):
-        scatter.finish(s)
-        gather.finish(s)
-
-
-def mlp_back(grad_gate, grad_up, gate_w, up_w, residual, out_grad, gain):
+
+    sum_then_gather(
+        scatter, gather, [functools.partial(fill, s) for s in range(seqs)], [functools.partial(store, s) for s in range(seqs)]
+    )
+    for weight in sums:
+        weight.finish_others()
+
+
+def mlp_back(grad_gate, grad_up, gate_w, up_w, residual, out_grad, gain, grads):
     seqs, rows, width = residual.shape
-    full = jax.ShapeDtypeStruct((seqs, lax.axis_size("grp") * rows, width), jnp.bfloat16)
     return call(
-        lambda *refs: mlp_back_body(seqs, *refs), "mlp_back", 3,
-        (grad_gate, grad_up, gate_w, up_w, residual, out_grad, gain), [in_vmem] * 7,
+        mlp_back_body, "mlp_back", 3,
+        (grad_gate, grad_up, gate_w, up_w, residual, out_grad, gain, *grads), [in_vmem] * 7 + [in_hbm] * 3,
         [
             jax.ShapeDtypeStruct(residual.shape, jnp.float32),
             jax.ShapeDtypeStruct((8, width), jnp.float32),
-            full,
-        ],
-        [in_vmem] * 2 + [in_hbm],
-        [pltpu.VMEM(residual.shape, jnp.bfloat16)] + gather_sems(seqs) + scatter_scratch(seqs, rows, width),
+            jax.ShapeDtypeStruct((seqs, lax.axis_size("grp") * rows, width), jnp.bfloat16),
+        ]
+        + [slots_of(grad, axis) for grad, axis in zip(grads, weight_axes)],
+        [in_vmem] * 2 + [in_hbm] * 4,
+        [pltpu.VMEM(residual.shape, jnp.bfloat16)]
+        + seq_sems(3)
+        + gather_sems(seqs)
+        + scatter_scratch(seqs, rows, width),
         110,
     )
 
 
-class Exchange:
-    def __init__(self, axis, source, slots, send_sem, recv_sem):
-        self.axis, self.source, self.slots = axis, source, slots
-        self.size, self.me = lax.axis_size(axis), lax.axis_index(axis)
-        self.send_sem, self.recv_sem = send_sem, recv_sem
-
-    def copy(self, k, owner):
-        peer = lax.rem(self.me + k, self.size)
-        return pltpu.make_async_remote_copy(
-            src_ref=self.source(peer),
-            dst_ref=self.slots.at[owner],
-            send_sem=self.send_sem.at[k],
-            recv_sem=self.recv_sem.at[k],
-            device_id={self.axis: peer},
-            device_id_type=MESH,
-        )
-
-    def start(self):
-        for k in range(1, self.size):
-            self.copy(k, self.me).start()
-
-    def finish(self):
-        for k in range(1, self.size):
-            self.copy(k, lax.rem(self.me - k + self.size, self.size)).wait_recv()
-        for k in range(1, self.size):
-            self.copy(k, self.me).wait_send()
-
-    def total(self):
-        total = self.slots[0]
-        for k in range(1, self.size):
-            total = total + self.slots[k]
-        return total
-
-
-def out_body(seqs, hidden_ref, down_w_ref, residual_ref, layer_out_ref, scatter, first):
+def out_body(hidden_ref, down_w_ref, residual_ref, layer_out_ref, scatter, first):
     def fill(s):
         scatter.fill(first + s, s, [hidden_ref], [down_w_ref], False)
 
@@ -817,89 +869,86 @@
 
 
 def last_body(
-    seqs, with_out, branch_ref, feed_ref, branch_w_ref, rec_w_ref, x_ref, grad_ref, gain_ref, gain_two_ref, rec_ref, *refs
+    with_out, branch_ref, feed_ref, branch_w_ref, rec_w_ref, x_ref, grad_ref, gain_ref, gain_two_ref, rec_ref,
+    w0, w1, w2, *refs,
 ):
     if with_out:
         hidden_ref, down_w_ref, residual_ref = refs[:3]
         refs = refs[3:]
-    grad_x_ref, rec_sum_ref, gain_sum_ref = refs[:3]
-    refs = refs[3:]
+    grad_x_ref, rec_sum_ref, gain_sum_ref, o0, o1, o2 = refs[:6]
+    refs = refs[6:]
     if with_out:
         layer_out_ref = refs[0]
         refs = refs[1:]
     rec_slots, gain_local, gain_part, gain_slots, part_slots = refs[:5]
     rec_sems, gain_sems, part_sems = refs[5:7], refs[7:9], refs[9:11]
     greet_axes(("seq", "grp"))
-    rows = x_ref.shape[1]
-    scatter = Scatter(rows, *refs[11:])
-    rec = Exchange("seq", lambda peer: rec_ref.at[peer], rec_slots, *rec_sems)
+    seqs, rows, _ = x_ref.shape
+    sums = weight_sums(weight_axes, (w0, w1, w2), (o0, o1, o2), *refs[11:13])
+    scatter = Scatter(rows, *refs[13:])
+    rec = Exchange("seq", lambda k: rec_ref.at[k], lambda k: rec_slots.at[k], *rec_sems)
     rec.start()
-    rec_slots[rec.me] = rec_ref[rec.me]
-    fills = [lambda s=s: scatter.fill(s, s, [branch_ref, feed_ref], [branch_w_ref, rec_w_ref], True) for s in range(seqs)]
-    stores = []
-    if with_out:
-        fill, store = out_body(seqs, hidden_ref, down_w_ref, residual_ref, layer_out_ref, scatter, seqs)
-        fills += [lambda s=s: fill(s) for s in range(seqs)]
-        stores = [lambda s=s: store(s) for s in range(seqs)]
+    for weight in sums:
+        weight.start_others()
     gain_local[...] = jnp.zeros_like(gain_local)
     gain_local[1:2, :] = gain_two_ref[0:1, :]
 
-    def finish_grad(s):
+    def fill(s):
+        scatter.fill(s, s, [branch_ref, feed_ref], [branch_w_ref, rec_w_ref], True)
+
+    across = Exchange(
+        "seq", block(gain_local, 1, lax.axis_size("seq")), lambda k: gain_slots.at[k], *gain_sems
+    )
+
+    def store(s):
         term = scatter.result(s)[...]
         inputs = x_ref[s].astype(jnp.float32)
         inverse = lax.rsqrt(mean_of(inputs * inputs) + epsilon)
         normal = inputs * inverse
         gain_local[0:1, :] += jnp.sum(term * normal, axis=0, keepdims=True)
+        if s == seqs - 1:
+            across.start()
         grad_x_ref[s] = grad_ref[s] + norm_back(term, normal, inverse, gain_ref[...])
 
-    stores = [lambda s=s: finish_grad(s) for s in range(seqs)] + stores
-    ahead = seqs
-    for p in range(min(ahead, len(fills))):
-        fills[p]()
-    for p in range(len(fills)):
-        for h in range(scatter.chips - 1):
-            scatter.hop(p, h)
-        if p + ahead < len(fills):
-            fills[p + ahead]()
-        stores[p]()
-        if p == seqs - 1:
-            part = gain_part.shape[1]
-
-            def lanes(owner):
-                return gain_local.at[:, pl.ds(pl.multiple_of(owner * part, part), part)]
-
-            across = Exchange("seq", lanes, gain_slots, *gain_sems)
-            across.start()
-            gain_slots[across.me] = lanes(across.me)[...]
+    fills = [functools.partial(fill, s) for s in range(seqs)]
+    stores = [functools.partial(store, s) for s in range(seqs)]
+    if with_out:
+        fill_out, store_out = out_body(hidden_ref, down_w_ref, residual_ref, layer_out_ref, scatter, seqs)
+        fills += [functools.partial(fill_out, s) for s in range(seqs)]
+        stores += [functools.partial(store_out, s) for s in range(seqs)]
+    sum_then_gather(scatter, None, fills, stores)
     across.finish()
-    gain_part[...] = across.total()
-    along = Exchange("grp", lambda peer: gain_part, part_slots, *part_sems)
+    gain_part[...] = sum_of(gain_slots)
+    along = Exchange("grp", lambda k: gain_part, lambda k: part_slots.at[k], *part_sems)
     along.start()
-    part_slots[along.me] = gain_part[...]
     rec.finish()
-    rec_sum_ref[...] = rec.total()
+    rec_sum_ref[...] = sum_of(rec_slots)
+    for weight in sums:
+        weight.finish_others()
     along.finish()
-    gain_sum_ref[...] = along.total()
-    for p in range(len(fills)):
-        scatter.finish(p)
-
-
-def last(grad_branch, grad_feed, branch_w, rec_w, layer_in, grad_residual, gain, gain_two_grad, rec_blocks, out_inputs):
+    gain_sum_ref[...] = sum_of(part_slots)
+
+
+def last(grad_branch, grad_feed, branch_w, rec_w, layer_in, grad_residual, gain, gain_two_grad, rec_blocks, grads, out_inputs):
     seqs, rows, width = layer_in.shape
     size, n = lax.axis_size("seq"), lax.axis_size("grp")
     f32 = jnp.float32
     inputs = (grad_branch, grad_feed, branch_w, rec_w, layer_in, grad_residual, gain, gain_two_grad, rec_blocks)
-    inputs = inputs + tuple(out_inputs)
     outs = [
         jax.ShapeDtypeStruct(layer_in.shape, f32),
         jax.ShapeDtypeStruct(rec_blocks.shape[1:], f32),
         jax.ShapeDtypeStruct((8, width // size), f32),
     ]
+    outs += [slots_of(grad, axis) for grad, axis in zip(grads, weight_axes)]
+    out_specs = [in_vmem] * 3 + [in_hbm] * 3
     if out_inputs:
         outs.append(jax.ShapeDtypeStruct(layer_in.shape, jnp.bfloat16))
+        out_specs.append(in_vmem)
     return call(
-        lambda *refs: last_body(seqs, bool(out_inputs), *refs), "last", 4,
-        inputs, [in_vmem] * len(inputs), outs, [in_vmem] * len(outs),
+        functools.partial(last_body, bool(out_inputs)), "last", 4,
+        inputs + tuple(grads) + tuple(out_inputs),
+        [in_vmem] * len(inputs) + [in_hbm] * 3 + [in_vmem] * len(out_inputs),
+        outs, out_specs,
         [
             pltpu.VMEM(rec_blocks.shape, f32),
             pltpu.VMEM((8, width), f32),
@@ -909,29 +958,26 @@
         ]
         + [pltpu.SemaphoreType.DMA((size,))] * 4
         + [pltpu.SemaphoreType.DMA((n,))] * 2
+        + seq_sems(3)
         + scatter_scratch(seqs * (2 if out_inputs else 1), rows, width),
         110,
     )
 
 
-def out_only_body(seqs, hidden_ref, down_w_ref, residual_ref, layer_out_ref, *scratch):
+def out_only_body(hidden_ref, down_w_ref, residual_ref, layer_out_ref, *scratch):
     greet_line()
     scatter = Scatter(residual_ref.shape[1], *scratch)
-    fill, store = out_body(seqs, hidden_ref, down_w_ref, residual_ref, layer_out_ref, scatter, 0)
-    for s in range(seqs):
-        fill(s)
-    for s in range(seqs):
-        for h in range(scatter.chips - 1):
-            scatter.hop(s, h)
-        store(s)
-    for s in range(seqs):
-        scatter.finish(s)
+    fill, store = out_body(hidden_ref, down_w_ref, residual_ref, layer_out_ref, scatter, 0)
+    seqs = range(residual_ref.shape[0])
+    sum_then_gather(
+        scatter, None, [functools.partial(fill, s) for s in seqs], [functools.partial(store, s) for s in seqs]
+    )
 
 
 def out_only(hidden, down_w, residual):
     seqs, rows, width = residual.shape
     return call(
-        lambda *refs: out_only_body(seqs, *refs), "layer_out", 5,
+        out_only_body, "layer_out", 5,
         (hidden, down_w, residual), [in_vmem] * 3,
         [jax.ShapeDtypeStruct(residual.shape, jnp.bfloat16)], [in_vmem],
         scatter_scratch(seqs, rows, width), 60,
@@ -959,9 +1005,12 @@
     pack = jnp.concatenate(
         [padded_rows(own_params.reshape(1, -1))[0], padded_rows(own_gains.reshape(1, -1))[0]]
     )
-    x_full, params, gains = gather_first(layer_in, pack)
-    branch_w, rec_w, out_w = gather_rows((w_branch, w_rec, w_out))
-    gate_w, up_w, down_w = gather_rows((mlp_gate, mlp_up, mlp_down))
+    late_grad, x_full, params, gains, branch_w, rec_w, out_w = gather_first(
+        layer_in, out_grad, pack, (w_branch, w_rec, w_out)
+    )
+    grad_output = jnp.concatenate(
+        [lax.all_gather(late_grad[s], "grp", axis=0, tiled=True) for s in range(seqs_here)]
+    )
 
     gains = gains.reshape(grp_devices, seq_devices, -1)[:, :, : own_gains.size]
     gains = jnp.transpose(gains.reshape(grp_devices, seq_devices, 2, -1), (2, 1, 0, 3)).reshape(2, 1, -1)
@@ -981,25 +1030,28 @@
     branch_pre = matmul(normed_one, branch_w).reshape(seqs_here, -1, channels)
     feed = matmul(normed_one, rec_w).astype(jnp.bfloat16).reshape(seqs_here, -1, channels)
     conv, rate, gate, state, mixed = rec_forward(feed, branch_pre, vectors, softness, diag_a, diag_x)
-    residual, normed_two, grad_output = mixer_out(mixed, out_w, layer_in, out_grad, gains[1])
+    residual, normed_two, gate_w, up_w, down_w = mixer_out(
+        mixed, out_w, layer_in, gains[1], (mlp_gate, mlp_up, mlp_down)
+    )
     mixed = mixed.reshape(-1, channels)
     normed_two = normed_two.reshape(-1, model_width)
-    grad_output = grad_output.reshape(-1, model_width)
     up_proj = matmul(normed_two, up_w)
     gate_act, gate_pull = jax.vjp(jax.nn.gelu, matmul(normed_two, gate_w))
     hidden = (gate_act * up_proj).astype(jnp.bfloat16)
-    grad_down = matmul_tn(hidden, grad_output)
     grad_hidden = matmul_nt(grad_output, down_w)
     grad_gate = gate_pull(grad_hidden * up_proj)[0].astype(jnp.bfloat16)
     grad_up = (grad_hidden * gate_act).astype(jnp.bfloat16)
-    mlp_grads = sum_rows((matmul_tn(normed_two, grad_gate), matmul_tn(normed_two, grad_up), grad_down))
+    mlp_grads = low_all(
+        (matmul_tn(normed_two, grad_gate), matmul_tn(normed_two, grad_up), matmul_tn(hidden, grad_output))
+    )
 
     def by_seq(values):
         return values.reshape(seqs_here, -1, values.shape[-1])
 
-    grad_residual, gain_two_grad, residual_low = mlp_back(
-        by_seq(grad_gate), by_seq(grad_up), gate_w, up_w, residual, out_grad, gains[1]
-    )
+    grad_residual, gain_two_grad, residual_low, *mlp_slots = mlp_back(
+        by_seq(grad_gate), by_seq(grad_up), gate_w, up_w, residual, out_grad, gains[1], mlp_grads
+    )
+    mlp_grads = sum_slots(mlp_grads, mlp_slots)
     residual_low = residual_low.reshape(-1, model_width)
     out_weight_grad = matmul_tn(mixed, residual_low)
     grad_mixed = by_seq(matmul_nt(residual_low, out_w))
@@ -1019,7 +1071,7 @@
     )
     rec_grads = rec_grads.reshape(heads_here, seq_devices, part_dim, -1)
     rec_blocks = padded_rows(jnp.transpose(rec_grads, (1, 0, 2, 3)))
-    mixer_grads = sum_rows(
+    mixer_grads = low_all(
         (
             matmul_tn(normed_one, grad_branch.reshape(-1, channels)),
             matmul_tn(normed_one, grad_feed.reshape(-1, channels)),
@@ -1027,14 +1079,16 @@
         )
     )
     last_inputs = (
-        grad_branch, grad_feed, branch_w, rec_w, layer_in, grad_residual, gains[0], gain_two_grad, rec_blocks
+        grad_branch, grad_feed, branch_w, rec_w, layer_in, grad_residual, gains[0], gain_two_grad, rec_blocks,
+        mixer_grads,
     )
     out_inputs = (by_seq(hidden), down_w, residual)
     if grp_devices > 8:
         layer_out = out_only(*out_inputs)
-        grad_x, rec_sum, gain_sum = last(*last_inputs, ())
+        grad_x, rec_sum, gain_sum, *mixer_slots = last(*last_inputs, ())
     else:
-        grad_x, rec_sum, gain_sum, layer_out = last(*last_inputs, out_inputs)
+        grad_x, rec_sum, gain_sum, *mixer_slots, layer_out = last(*last_inputs, out_inputs)
+    mixer_grads = sum_slots(mixer_grads, mixer_slots)
     rec_sum = rec_sum.reshape(-1)[: own_params.size].reshape(own_params.shape)
     own_part = gain_one.shape[0]
     gain_grads = lax.dynamic_slice_in_dim(gain_sum, lax.axis_index("grp") * own_part, own_part, 1)

time: 758 us -> 643 us (0.85)
  Pallas kernels: 571 us -> 468 us
  matrix products: 100 us -> 84.8 us
  local copies, waits for them, and re-layouts: 33 us -> 47 us
    pallas_call x4, Pallas kernels: 539 us -> 435 us  [call(): pl.pallas_call(body, in_specs=in_specs, out_specs=out_specs, out_shape=ou...]
    add x0 -> x6, other arithmetic: none -> 13.6 us  [sum_slots(): own = own.astype(jnp.float32) + slot[k].astype(jnp.float32)]
    convert_element_type x6 -> x0, other arithmetic: 13.3 us -> none  [the longest x2 4.46 us: sum_rows(): lax.psum_scatter(low[0], 'seq', scatter_dimension=0, tiled=True)]
    dot_general x4, matrix products: 36.3 us -> 28.6 us  [matmul(): return jnp.dot(left, right, preferred_element_type=jnp.float32)]
    unnamed x96 -> x84, local copies, waits for them, and re-layouts: 22.5 us -> 27.9 us
  transfers between devices with their start and end apart: 12 -> 2, of which waited for: 0 -> 0; matrix products, arithmetic and copies ran while one was open for 16% -> 5% of each run, Pallas kernels for 58% -> 22%
where the time goes in v4:
time: 643 us; the launch traced here: 640 us
  Pallas kernels  468 us (73%)
  matrix products  84.8 us (13%)
  local copies, waits for them, and re-layouts  47 us (7%)
  other arithmetic  25 us (4%)
  between operations  14.8 us (2%)
    pallas_call x4, Pallas kernels, call(): pl.pallas_call(body, in_specs=in_specs, out_specs=out_specs, out_shape=ou...  435 us
    dot_general x6, matrix products, matmul_tn(): lax.dot_general(left, right, (((0,), (0,)), ((), ())), preferred_element_...  41.6 us
    dot_general x4, matrix products, matmul(): return jnp.dot(left, right, preferred_element_type=jnp.float32)  28.6 us
    unnamed x84, local copies, waits for them, and re-layouts  27.9 us
    pallas_call x1, Pallas kernels, rec_backward(): pl.pallas_call(rec_backward_body, grid=(blocks,), in_specs=[block, block,...  20.9 us
    dot_general x2, matrix products, matmul_nt(): lax.dot_general(left, right, (((1,), (1,)), ((), ())), preferred_element_...  14.6 us
    add x6, other arithmetic, sum_slots(): own = own.astype(jnp.float32) + slot[k].astype(jnp.float32)  13.6 us
  transfers between devices with their start and end apart: 2, of which 0 were waited for; matrix products, arithmetic and copies ran while one was open for 5% of the time, Pallas kernels for 22%

profile of v4, /device:TPU:0, one launch (start us, length us, event | category | flops | bytes accessed | tf_op | source)
XLA Modules:
  0.0 640.0 jit_solution(18176547225386764046)
XLA Ops:
  11.2 1.4 concatenate.54
  13.2 1.9 copy.94.w0
  15.1 1.9 copy.95.w1
  18.4 66.6 %gather_first.1 = (bf16[2,96,2048]{2,1,0:T(8,128)(2,1)}, bf16[2,768,2048]{2,1,0:T(8,128)(2,1)}, f32[4,256,128]{2,1,0:T(8,128)}, f32[8,4,8,128]{3,2,1,0:T(8,128)}...) custom-call(bf16[2,96,2048]{2,1,0:T(8,128)(2,1)} %x_ref.5, ...), custom_call_target="tpu_custom_call" | custom-call | flops 70000001024 | bytes 210000000 | tf_op jit(solution)/shard_map/gather_first/pallas_call | solution.py:568
  85.1 2.1 fusion.28
  87.9 1.4 copy.132
  90.5 4.3 fusion
  96.8 4.4 fusion.2
  101.2 2.6 copy-done.17
  103.9 2.5 convolution_convert_fusion.2
  107.1 6.0 fusion.14.branch_ref
  113.3 11.7 %rec_forward.1 = (bf16[2,768,352]{2,1,0:T(8,128)(2,1)S(1)}, f32[2,768,352]{2,1,0:T(8,128)S(1)}, f32[2,768,352]{2,1,0:T(8,128)S(1)}, f32[2,768,352]{2,1,0:T(8,128)S(1)}, bf16[2,768,352]{2,1,0:T(8,128)(2,1)S(1)}) custom-call(bf16[2,768,352]{2,1,0:T(8,128)(2,1)S(1)} %bitcast.148, f32[2,768,352]{2,1,0:T(8,128)S(1)} %fusion.14.branch_ref, ...), custom_call_target="tpu_custom_call" | custom-call | tf_op jit(solution)/shard_map/rec_forward/pallas_call | solution.py:245
  125.0 1.4 copy-done
  126.5 1.4 copy-done.7
  127.9 1.0 copy-done.8
  128.9 1.0 copy-done.12
  129.9 129.4 %mixer_out.1 = (f32[2,96,2048]{2,1,0:T(8,128)}, bf16[2,768,2048]{2,1,0:T(8,128)(2,1)}, bf16[2048,768]{1,0:T(8,128)(2,1)}, bf16[2048,768]{1,0:T(8,128)(2,1)}, bf16[768,2048]{1,0:T(8,128)(2,1)}) custom-call(bf16[2,768,352]{2,1,0:T(8,128)(2,1)} %copy-done.12, bf16[352,2048]{1,0:T(8,128)(2,1)} %get-tuple-element.59.out_w_ref, bf16[2,96,2048]{2,1,0:T(8,128)(2,1)} %x_ref.5, ...), custom_call_target="tpu_custom_call" | custom-call | flops 99999997952 | bytes 300000000 | tf_op jit(solution)/shard_map/mixer_out/pallas_call | solution.py:568
  259.3 1.4 squeeze.68.gain_ref
  260.7 9.4 %fusion.32 = f32[1536,768]{1,0:T(8,128)} fusion(bf16[1536,2048]{1,0:T(8,128)(2,1)} %bitcast.179, bf16[2048,768]{1,0:T(8,128)(2,1)} %get-tuple-element.63.gate_w_ref), kind=kOutput, calls=%fused_computation.93 | convolution fusion | flops 4831838208 | bytes 14155776 | tf_op jit(solution)/shard_map/dot_general | solution.py:18
  270.1 11.2 %fusion.11 = f32[1536,768]{1,0:T(8,128)} fusion(bf16[768,2048]{1,0:T(8,128)(2,1)} %get-tuple-element.60.refs_1_, bf16[768,2048]{1,0:T(8,128)(2,1)} %bitcast.177, bf16[768,2048]{1,0:T(8,128)(2,1)} %bitcast.175), kind=kOutput, calls=%fused_computation.19 | convolution fusion | flops 4844421120 | bytes 14155776 | tf_op jit(solution)/shard_map/dot_general | solution.py:28
  281.3 10.7 %multiply_convert_fusion = (bf16[1536,768]{1,0:T(8,128)(2,1)S(1)}, bf16[1536,768]{1,0:T(8,128)(2,1)S(1)}, bf16[1536,768]{1,0:T(8,128)(2,1)S(1)}) fusion(f32[1536,768]{1,0:T(8,128)} %fusion.32, f32[1536,768]{1,0:T(8,128)} %fusion.11, bf16[1536,2048]{1,0:T(8,128)(2,1)S(1)} %bitcast.180, bf16[2048,768]{1,0:T(8,128)(2,1)S(1)} %copy-done.34), kind=kOutput, calls=%fused_computation.15 | convolution fusion | flops 4862509056 | bytes 25952256 | tf_op jit(solution)/shard_map/dot_general | solution.py:18
  292.1 6.7 %fusion.12.w2 = bf16[768,2048]{1,0:T(8,128)(2,1)} fusion(bf16[1536,768]{1,0:T(8,128)(2,1)S(1)} %get-tuple-element.144, bf16[768,2048]{1,0:T(8,128)(2,1)S(1)} %bitcast.178, bf16[768,2048]{1,0:T(8,128)(2,1)S(1)} %bitcast.176), kind=kOutput, calls=%fused_computation.20 | convolution fusion | flops 4845993984 | bytes 11796480 | tf_op jit(solution)/shard_map/dot_general | solution.py:22
  298.7 6.6 %convolution_convert_fusion.1.w0 = bf16[2048,768]{1,0:T(8,128)(2,1)} fusion(bf16[1536,2048]{1,0:T(8,128)(2,1)S(1)} %bitcast.181, bf16[1536,768]{1,0:T(8,128)(2,1)S(1)} %get-tuple-element.145), kind=kOutput, calls=%fused_computation.22 | convolution fusion | flops 4833411072 | bytes 11796480 | tf_op jit(solution)/shard_map/dot_general | solution.py:22
  305.3 6.6 %convolution_convert_fusion.w1 = bf16[2048,768]{1,0:T(8,128)(2,1)} fusion(bf16[1536,2048]{1,0:T(8,128)(2,1)S(1)} %bitcast.182, bf16[1536,768]{1,0:T(8,128)(2,1)S(1)} %get-tuple-element.146), kind=kOutput, calls=%fused_computation.21 | convolution fusion | flops 4833411072 | bytes 11796480 | tf_op jit(solution)/shard_map/dot_general | solution.py:22
  311.9 115.0 %mlp_back.1 = (f32[2,96,2048]{2,1,0:T(8,128)}, f32[8,2048]{1,0:T(8,128)}, bf16[2,768,2048]{2,1,0:T(8,128)(2,1)}, bf16[3,512,768]{2,1,0:T(8,128)(2,1)}, bf16[3,51...) custom-call(bf16[2,768,768]{2,1,0:T(8,128)(2,1)} %bitcast.184, bf16[2,768,768]{2,1,0:T(8,128)(2,1)} %bitcast.185, ...), custom_call_target="tpu_custom_call" | custom-call | flops 109999996928 | bytes 330000000 | tf_op jit(solution)/shard_map/mlp_back/pallas_call | solution.py:568
  426.9 6.9 %fusion.13.w2 = bf16[352,2048]{1,0:T(8,128)(2,1)} fusion(bf16[2,768,352]{2,1,0:T(8,128)(2,1)} %copy-done.12, bf16[2,768,2048]{2,1,0:T(8,128)(2,1)} %get-tuple-element.65), kind=kOutput, calls=%fused_computation.26 | convolution fusion | flops 2215313408 | bytes 8814592 | tf_op jit(solution)/shard_map/dot_general | solution.py:22
  433.8 3.5 fusion.16.grad_mixed_ref
  437.3 20.9 %rec_backward.1 = (bf16[2,768,352]{2,1,0:T(8,128)(2,1)S(1)}, bf16[2,768,352]{2,1,0:T(8,128)(2,1)S(1)}, f32[352,352]{1,0:T(8,128)S(1)}, f32[352,352]{1,0:T(8,128)S(1)}, f32[8,352]{1,0:T(8,128)S(1)}) custom-call(f32[2,768,352]{2,1,0:T(8,128)S(1)} %fusion.16.grad_mixed_ref, f32[2,768,352]{2,1,0:T(8,128)S(1)} %copy-done.2, bf16[2,768,352]{2,1,0:T(8,128)(2,1)S(1)} %bitcast.149, ...), custom_call_target="tpu_custom_call" | custom-call | tf_op jit(solution)/shard_map/rec_backward/pallas_call | solution.py:275
  458.9 1.0 copy-done.13
  460.0 1.0 copy-done.15
  462.6 1.1 fusion.30
  465.5 7.5 %bitcast_convert_fusion.1.w0 = bf16[2048,352]{1,0:T(8,128)(2,1)} fusion(bf16[2,768,2048]{2,1,0:T(8,128)(2,1)} %copy-done.17, bf16[2,768,352]{2,1,0:T(8,128)(2,1)S(1)} %copy-done.14), kind=kOutput, calls=%fused_computation.24 | convolution fusion | flops 2215313408 | bytes 8814592 | tf_op jit(solution)/shard_map/dot_general | solution.py:22
  473.0 7.4 %bitcast_convert_fusion.w1 = bf16[2048,352]{1,0:T(8,128)(2,1)} fusion(bf16[2,768,2048]{2,1,0:T(8,128)(2,1)} %copy-done.17, bf16[2,768,352]{2,1,0:T(8,128)(2,1)S(1)} %copy-done.16), kind=kOutput, calls=%fused_computation.23 | convolution fusion | flops 2215313408 | bytes 8814592 | tf_op jit(solution)/shard_map/dot_general | solution.py:22
  480.4 124.0 %last.1 = (f32[2,96,2048]{2,1,0:T(8,128)}, f32[248,128]{1,0:T(8,128)}, f32[8,512]{1,0:T(8,128)}, bf16[3,512,352]{2,1,0:T(8,128)(2,1)}, bf16[3,512,352]{2,1,0:T(8...) custom-call(bf16[2,768,352]{2,1,0:T(8,128)(2,1)} %copy-done.13, bf16[2,768,352]{2,1,0:T(8,128)(2,1)} %copy-done.15, ...), custom_call_target="tpu_custom_call" | custom-call | flops 109999996928 | bytes 330000000 | tf_op jit(solution)/shard_map/last/pallas_call | solution.py:568
  604.5 1.2 reshape.214
  607.9 3.4 convert_add_fusion
  611.3 2.8 convert_add_fusion.3
  614.1 2.8 convert_add_fusion.6
  616.9 2.1 convert_add_fusion.15
  619.0 1.2 convert_add_fusion.9
  620.2 1.1 copy.112
  621.3 1.3 convert_add_fusion.12
  622.6 1.1 copy.111
  625.0 1.5 copy.113
  626.5 1.6 copy.115
  628.1 1.6 copy.114
  629.7 2.1 copy.136
  631.8 1.1 copy.137
  (117 shorter events, 18.4 us)
Async XLA Ops:
  7.2 262.9 %all-gather.5.cloned.1.call-start = ((), (), s32[]{:S(2)}) async-start(), calls=%async_computation | async-start | bytes 3538944 | tf_op jit(solution)/shard_map/all_gather | solution.py:1012
  87.2 182.9 %all-gather.7.cloned.1.call-start = ((), (), s32[]{:S(2)}) async-start(), calls=%async_computation.1 | async-start | bytes 3538944 | tf_op jit(solution)/shard_map/all_gather | solution.py:1012
  90.5 4.3 copy-start.24
  96.8 7.1 %copy-start.32 = (bf16[2048,352]{1,0:T(8,128)(2,1)S(1)}, bf16[2048,352]{1,0:T(8,128)(2,1)}, u32[]{:S(2)}) copy-start(bf16[2048,352]{1,0:T(8,128)(2,1)} %get-tuple-element.55.rec_w_ref) | copy-start | bytes 4325380
  101.2 2.6 copy-start.17
  113.1 11.9 %copy-start.1 = (f32[2,768,352]{2,1,0:T(8,128)}, f32[2,768,352]{2,1,0:T(8,128)S(1)}, u32[]{:S(2)}) copy-start(f32[2,768,352]{2,1,0:T(8,128)S(1)} %fusion.14.branch_ref) | copy-start | bytes 6488068
  113.2 16.7 %copy-start.3 = (bf16[352,352]{1,0:T(8,128)(2,1)}, bf16[352,352]{1,0:T(8,128)(2,1)S(1)}, u32[]{:S(2)}) copy-start(bf16[352,352]{1,0:T(8,128)(2,1)S(1)} %get-tuple-element.162.gate_a_ref) | copy-start | bytes 743428
  113.2 16.6 %copy-start.5 = (bf16[352,352]{1,0:T(8,128)(2,1)}, bf16[352,352]{1,0:T(8,128)(2,1)S(1)}, u32[]{:S(2)}) copy-start(bf16[352,352]{1,0:T(8,128)(2,1)S(1)} %get-tuple-element.163.gate_x_ref) | copy-start | bytes 743428
  125.0 1.5 copy-start
  126.5 1.4 copy-start.7
  127.9 1.0 copy-start.8
  128.9 1.0 copy-start.12
  270.1 11.2 %copy-start.27 = (bf16[2,768,2048]{2,1,0:T(8,128)(2,1)S(1)}, bf16[2,768,2048]{2,1,0:T(8,128)(2,1)}, u32[]{:S(2)}) copy-start(bf16[2,768,2048]{2,1,0:T(8,128)(2,1)} %get-tuple-element.61) | copy-start | bytes 18874372
  270.1 11.2 %copy-start.34 = (bf16[2048,768]{1,0:T(8,128)(2,1)S(1)}, bf16[2048,768]{1,0:T(8,128)(2,1)}, u32[]{:S(2)}) copy-start(bf16[2048,768]{1,0:T(8,128)(2,1)} %get-tuple-element.62.up_w_ref) | copy-start | bytes 9437188
  281.3 10.7 %copy-start.25 = (bf16[1,768,2048]{2,1,0:T(8,128)(2,1)S(1)}, bf16[1,768,2048]{2,1,0:T(8,128)(2,1)}, u32[]{:S(2)}) copy-start(bf16[1,768,2048]{2,1,0:T(8,128)(2,1)} %all-gather.5.cloned.1.call-done) | copy-start | bytes 9437188
  281.3 10.7 %copy-start.26 = (bf16[1,768,2048]{2,1,0:T(8,128)(2,1)S(1)}, bf16[1,768,2048]{2,1,0:T(8,128)(2,1)}, u32[]{:S(2)}) copy-start(bf16[1,768,2048]{2,1,0:T(8,128)(2,1)} %all-gather.7.cloned.1.call-done) | copy-start | bytes 9437188
  292.0 6.7 %copy-start.28 = (bf16[1536,768]{1,0:T(8,128)(2,1)}, bf16[1536,768]{1,0:T(8,128)(2,1)S(1)}, u32[]{:S(2)}) copy-start(bf16[1536,768]{1,0:T(8,128)(2,1)S(1)} %get-tuple-element.144) | copy-start | bytes 7077892
  292.0 6.7 %copy-start.29 = (bf16[1536,768]{1,0:T(8,128)(2,1)}, bf16[1536,768]{1,0:T(8,128)(2,1)S(1)}, u32[]{:S(2)}) copy-start(bf16[1536,768]{1,0:T(8,128)(2,1)S(1)} %get-tuple-element.145) | copy-start | bytes 7077892
  292.0 13.3 %copy-start.30 = (bf16[1536,768]{1,0:T(8,128)(2,1)}, bf16[1536,768]{1,0:T(8,128)(2,1)S(1)}, u32[]{:S(2)}) copy-start(bf16[1536,768]{1,0:T(8,128)(2,1)S(1)} %get-tuple-element.146) | copy-start | bytes 7077892
  426.8 6.9 %copy-start.31 = (bf16[2,768,2048]{2,1,0:T(8,128)(2,1)S(1)}, bf16[2,768,2048]{2,1,0:T(8,128)(2,1)}, u32[]{:S(2)}) copy-start(bf16[2,768,2048]{2,1,0:T(8,128)(2,1)} %get-tuple-element.65) | copy-start | bytes 18874372
  426.9 6.9 %copy-start.33 = (bf16[352,2048]{1,0:T(8,128)(2,1)S(1)}, bf16[352,2048]{1,0:T(8,128)(2,1)}, u32[]{:S(2)}) copy-start(bf16[352,2048]{1,0:T(8,128)(2,1)} %get-tuple-element.59.out_w_ref) | copy-start | bytes 4325380
  433.7 3.5 copy-start.2
  433.7 3.5 copy-start.4
  433.8 3.5 copy-start.6
  433.8 3.5 copy-start.9
  458.1 0.8 copy-start.10
  458.9 1.0 copy-start.13
  460.0 1.0 copy-start.15
  461.0 0.6 copy-start.11
  463.7 1.8 copy-start.14
  465.5 7.5 %copy-start.16 = (bf16[2,768,352]{2,1,0:T(8,128)(2,1)S(1)}, bf16[2,768,352]{2,1,0:T(8,128)(2,1)}, u32[]{:S(2)}) copy-start(bf16[2,768,352]{2,1,0:T(8,128)(2,1)} %copy-done.15) | copy-start | bytes 3244036
  604.5 6.8 %copy-start.19 = (bf16[3,512,768]{2,1,0:T(8,128)(2,1)S(1)}, bf16[3,512,768]{2,1,0:T(8,128)(2,1)}, u32[]{:S(2)}) copy-start(bf16[3,512,768]{2,1,0:T(8,128)(2,1)} %get-tuple-element.85) | copy-start | bytes 7077892
  611.3 2.8 copy-start.18
  614.1 2.8 copy-start.23
  614.1 5.0 copy-start.22
  616.9 4.4 copy-start.21
  621.3 10.4 %copy-start.20 = (f32[2,96,2048]{2,1,0:T(8,128)S(1)}, f32[2,96,2048]{2,1,0:T(8,128)}, u32[]{:S(2)}) copy-start(f32[2,96,2048]{2,1,0:T(8,128)} %get-tuple-element.182) | copy-start | bytes 4718596
Sparse Core Ops, SparseCore 0:
  87.3 36.6 all-gather.4
  126.2 51.3 all-gather.6

commit v5 on v4

--- a/solution.py
+++ b/solution.py
@@ -76,8 +76,8 @@
     )
 
 
-def pick_rows(seq_len):
-    for rows in (128, 96, 64, 32, 16):
+def pick_rows(seq_len, choices=(128, 96, 64, 32, 16)):
+    for rows in choices:
         if seq_len % rows == 0:
             return rows
     return seq_len
@@ -128,38 +128,37 @@
     return jnp.exp(log_decay), jnp.sqrt(minus_expm1(2.0 * log_decay))
 
 
+def rec_forward_rows(feed, branch, vectors_ref, softness_ref, gate_a_ref, gate_x_ref, window, carry):
+    rows = feed.shape[0]
+    window[pl.ds(8, rows), :] = feed.astype(jnp.float32)
+    conv = vectors_ref[4:5, :] + vectors_ref[0:1, :] * window[pl.ds(8, rows), :]
+    for k in range(1, 4):
+        conv = conv + vectors_ref[k : k + 1, :] * window[pl.ds(8 - k, rows), :]
+    window[pl.ds(0, 8), :] = window[pl.ds(rows, 8), :]
+    conv_low = conv.astype(jnp.bfloat16)
+    rate = jax.nn.sigmoid(matmul(conv_low, gate_a_ref[...]) + vectors_ref[5:6, :])
+    gate = jax.nn.sigmoid(matmul(conv_low, gate_x_ref[...]) + vectors_ref[6:7, :])
+    decay, scale = decay_parts(rate, softness_ref[...])
+    total, state = scan_block(decay, scale * gate * conv_low.astype(jnp.float32), shift_down)
+    state = state + total * carry[0:1, :]
+    carry[0:1, :] = state[rows - 1 : rows, :]
+    gelu_branch = gelu_parts(branch)[0]
+    mixed = (gelu_branch * state.astype(jnp.bfloat16).astype(jnp.float32)).astype(jnp.bfloat16)
+    return conv_low, rate, gate, state, mixed
+
+
 def rec_forward_body(
     feed_ref, branch_ref, vectors_ref, softness_ref, gate_a_ref, gate_x_ref,
     conv_ref, rate_ref, input_ref, state_ref, mixed_ref, window, carry,
 ):
-    seqs, rows, _ = feed_ref.shape
-
     @pl.when(pl.program_id(0) == 0)
     def _():
         window[...] = jnp.zeros_like(window)
         carry[...] = jnp.zeros_like(carry)
 
-    softness = softness_ref[...]
-    for s in range(seqs):
-        window[s, pl.ds(8, rows), :] = feed_ref[s].astype(jnp.float32)
-        conv = vectors_ref[4:5, :] + vectors_ref[0:1, :] * window[s, pl.ds(8, rows), :]
-        for k in range(1, 4):
-            conv = conv + vectors_ref[k : k + 1, :] * window[s, pl.ds(8 - k, rows), :]
-        window[s, pl.ds(0, 8), :] = window[s, pl.ds(rows, 8), :]
-        conv_low = conv.astype(jnp.bfloat16)
-        conv_ref[s] = conv_low
-        rate = jax.nn.sigmoid(matmul(conv_low, gate_a_ref[...]) + vectors_ref[5:6, :])
-        gate = jax.nn.sigmoid(matmul(conv_low, gate_x_ref[...]) + vectors_ref[6:7, :])
-        rate_ref[s] = rate
-        input_ref[s] = gate
-        decay, scale = decay_parts(rate, softness)
-        total, state = scan_block(decay, scale * gate * conv_low.astype(jnp.float32), shift_down)
-        state = state + total * carry[s, 0:1, :]
-        carry[s, 0:1, :] = state[rows - 1 : rows, :]
-        state_ref[s] = state
-        gelu_branch = gelu_parts(branch_ref[s])[0]
-        mixed_ref[s] = (gelu_branch * state.astype(jnp.bfloat16).astype(jnp.float32)).astype(
-            jnp.bfloat16
+    for s in range(feed_ref.shape[0]):
+        conv_ref[s], rate_ref[s], input_ref[s], state_ref[s], mixed_ref[s] = rec_forward_rows(
+            feed_ref[s], branch_ref[s], vectors_ref, softness_ref, gate_a_ref, gate_x_ref, window.at[s], carry.at[s]
         )
 
 
@@ -484,10 +483,15 @@
         def to_part(c, columns, value):
             self.part[p, c, :, columns] = value
 
-        product(1 - self.core, to_out)
-        for c in range(self.chips):
-            self.swap(p, c).start()
-        product(self.core, to_part)
+        def partners():
+            product(1 - self.core, to_out)
+            for c in range(self.chips):
+                self.swap(p, c).start()
+
+        def own():
+            product(self.core, to_part)
+
+        return partners, own
 
     def own(self, p, c):
         self.swap(p, c).wait_recv()
@@ -736,31 +740,45 @@
     return jnp.mean(values, axis=-1, keepdims=True)
 
 
-def sum_then_gather(scatter, gather, fills, stores):
+def sum_then_gather(scatter, gather, fills, stores, count=0):
     hops = range(1, scatter.chips - 1)
-    fills[0]()
+    for step in fills[0]:
+        step()
     scatter.hop(0, 0)
     for p, store in enumerate(stores):
-        if p + 1 < len(fills):
-            fills[p + 1]()
+        ahead = list(fills[p + 1]) if p + 1 < len(fills) else []
         for h in hops:
+            if ahead:
+                ahead.pop(0)()
             scatter.hop(p, h)
-            if gather and p:
+            if 0 < p <= count:
                 gather.hop(p - 1, h - 1)
+        for step in ahead:
+            step()
         if p + 1 < len(fills):
             scatter.hop(p + 1, 0)
         store()
-        if gather:
+        if p < count:
             gather.start(p)
-            if p:
-                gather.hop(p - 1, gather.chips - 2)
-    if gather:
+        if 0 < p <= count:
+            gather.hop(p - 1, gather.chips - 2)
+    if count == len(stores):
         for h in range(gather.chips - 1):
-            gather.hop(len(stores) - 1, h)
-        for p in range(len(stores)):
-            gather.finish(p)
+            gather.hop(count - 1, h)
+    for p in range(count):
+        gather.finish(p)
     for p in range(len(fills)):
         scatter.finish(p)
+
+
+def out_body(hidden_ref, down_w_ref, residual_ref, layer_out_ref, scatter, first):
+    def fill(s):
+        return scatter.fill(first + s, s, [hidden_ref], [down_w_ref], False)
+
+    def store(s):
+        layer_out_ref[s] = (residual_ref[s] + scatter.result(first + s)[...]).astype(jnp.bfloat16)
+
+    return fill, store
 
 
 def mixer_out_body(mixed_ref, out_w_ref, x_ref, gain_ref, w0, w1, w2, residual_ref, normed_ref, o0, o1, o2, low_ref, *refs):
@@ -773,7 +791,7 @@
     scatter = Scatter(rows, *refs[5:])
 
     def fill(s):
-        scatter.fill(s, s, [mixed_ref], [out_w_ref], False)
+        return scatter.fill(s, s, [mixed_ref], [out_w_ref], False)
 
     def store(s):
         residual = x_ref[s].astype(jnp.float32) + scatter.result(s)[...]
@@ -782,7 +800,7 @@
         low_ref[s] = (normal * gain_ref[...]).astype(jnp.bfloat16)
 
     sum_then_gather(
-        scatter, gather, [functools.partial(fill, s) for s in range(seqs)], [functools.partial(store, s) for s in range(seqs)]
+        scatter, gather, [fill(s) for s in range(seqs)], [functools.partial(store, s) for s in range(seqs)], seqs
     )
     for weight in weights:
         weight.finish()
@@ -805,10 +823,135 @@
     )
 
 
+def mixer_forward_body(
+    x_full_ref, gains_ref, branch_w_ref, rec_w_ref, out_w_ref, vectors_ref, softness_ref, gate_a_ref, gate_x_ref,
+    grad_ref, w0, w1, w2,
+    normed_one_ref, branch_ref, feed_ref, conv_ref, rate_ref, input_ref, state_ref, mixed_ref, residual_ref,
+    normed_ref, grads_ref, o0, o1, o2, low_ref, window, carry, *refs,
+):
+    greet_axes(("seq", "grp"))
+    seqs, seq_len, _ = x_full_ref.shape
+    rows = grad_ref.shape[1]
+    me = lax.axis_index("grp")
+    weights = weight_gathers(weight_axes, (w0, w1, w2), (o0, o1, o2), *refs[:2])
+    gather = Gather(views(low_ref) + views(grad_ref), views(normed_ref) + views(grads_ref), rows, *refs[2:5])
+    scatter = Scatter(rows, *refs[5:])
+    for s in range(seqs):
+        gather.start(seqs + s)
+    for weight in weights:
+        weight.start()
+    tile = pick_rows(seq_len, (256, 192, 128, 96, 64, 32, 16))
+    chunk = window.shape[0] - 8
+    window[...] = jnp.zeros_like(window)
+
+    def project(s):
+        @pl.loop(0, seq_len // tile)
+        def _(i):
+            at = pl.ds(pl.multiple_of(i * tile, tile), tile)
+            inputs = x_full_ref[s, at, :].astype(jnp.float32)
+            normal = inputs * lax.rsqrt(mean_of(inputs * inputs) + epsilon)
+            normed = (normal * gains_ref[0]).astype(jnp.bfloat16)
+            normed_one_ref[s, at, :] = normed
+            branch_ref[s, at, :] = matmul(normed, branch_w_ref[...])
+            feed_ref[s, at, :] = matmul(normed, rec_w_ref[...]).astype(jnp.bfloat16)
+
+    def recur(s):
+        window[pl.ds(0, 8), :] = jnp.zeros((8, window.shape[1]), jnp.float32)
+        carry[...] = jnp.zeros_like(carry)
+
+        @pl.loop(0, seq_len // chunk)
+        def _(i):
+            at = pl.ds(pl.multiple_of(i * chunk, chunk), chunk)
+            conv, rate, gate, state, mixed = rec_forward_rows(
+                feed_ref[s, at, :], branch_ref[s, at, :], vectors_ref, softness_ref, gate_a_ref, gate_x_ref, window, carry
+            )
+            conv_ref[s, at, :] = conv
+            rate_ref[s, at, :] = rate
+            input_ref[s, at, :] = gate
+            state_ref[s, at, :] = state
+            mixed_ref[s, at, :] = mixed
+
+    def late_hop(h):
+        if h < gather.chips - 1:
+            for s in range(seqs):
+                gather.hop(seqs + s, h)
+
+    def steps(s):
+        partners, own = scatter.fill(s, s, [mixed_ref], [out_w_ref], False)
+        late = [functools.partial(late_hop, h) for h in range(gather.chips - 1)]
+
+        def second():
+            if s == 0:
+                late_hop(0)
+            recur(s)
+
+        def third():
+            partners()
+            if s == 0:
+                late_hop(1)
+
+        def fourth():
+            own()
+            if s == seqs - 1:
+                for hop in late[2 if seqs > 1 else 1 :]:
+                    hop()
+
+        return [functools.partial(project, s), second, third, fourth]
+
+    def store(s):
+        own = x_full_ref[s, pl.ds(pl.multiple_of(me * rows, rows), rows), :]
+        residual = own.astype(jnp.float32) + scatter.result(s)[...]
+        residual_ref[s] = residual
+        normal = residual * lax.rsqrt(mean_of(residual * residual) + epsilon)
+        low_ref[s] = (normal * gains_ref[1]).astype(jnp.bfloat16)
+
+    sum_then_gather(
+        scatter, gather, [steps(s) for s in range(seqs)], [functools.partial(store, s) for s in range(seqs)], seqs
+    )
+    for s in range(seqs):
+        gather.finish(seqs + s)
+    for weight in weights:
+        weight.finish()
+
+
+def mixer_forward(x_full, gains, branch_w, rec_w, out_w, vectors, softness, gate_a, gate_x, out_grad, weights):
+    seqs, seq_len, width = x_full.shape
+    rows, channels = out_grad.shape[1], vectors.shape[1]
+    low = jax.ShapeDtypeStruct((seqs, seq_len, channels), jnp.bfloat16)
+    full = jax.ShapeDtypeStruct((seqs, seq_len, channels), jnp.float32)
+    outs = [x_full, full, low, low, full, full, full, low]
+    outs += [jax.ShapeDtypeStruct(out_grad.shape, jnp.float32), x_full, x_full]
+    outs = [jax.ShapeDtypeStruct(out.shape, out.dtype) for out in outs]
+    outs += [gathered(w, axis) for w, axis in zip(weights, weight_axes)]
+    return call(
+        mixer_forward_body, "mixer_forward", 2,
+        (x_full, gains, branch_w, rec_w, out_w, vectors, softness, gate_a, gate_x, out_grad, *weights),
+        [in_vmem] * 13,
+        outs, [in_vmem] * 9 + [in_hbm] * 5,
+        [
+            pltpu.VMEM(out_grad.shape, jnp.bfloat16),
+            pltpu.VMEM((pick_rows(seq_len) + 8, channels), jnp.float32),
+            pltpu.VMEM((8, channels), jnp.float32),
+        ]
+        + seq_sems(3)
+        + gather_sems(2 * seqs)
+        + scatter_scratch(seqs, rows, width),
+        130,
+    )
+
+
 def mlp_back_body(
-    gate_ref, up_ref, gate_w_ref, up_w_ref, residual_ref, grad_ref, gain_ref, w0, w1, w2,
-    grad_residual_ref, gain_grad_ref, full_ref, o0, o1, o2, low_ref, *refs,
+    with_out, gate_ref, up_ref, gate_w_ref, up_w_ref, residual_ref, grad_ref, gain_ref, w0, w1, w2, *refs
 ):
+    if with_out:
+        hidden_ref, down_w_ref = refs[:2]
+        refs = refs[2:]
+    grad_residual_ref, gain_grad_ref, full_ref, o0, o1, o2 = refs[:6]
+    refs = refs[6:]
+    if with_out:
+        layer_out_ref = refs[0]
+        refs = refs[1:]
+    low_ref, *refs = refs
     greet_axes(("seq", "grp"))
     seqs, rows, _ = grad_ref.shape
     sums = weight_sums(weight_axes, (w0, w1, w2), (o0, o1, o2), *refs[:2])
@@ -819,7 +962,7 @@
     gain_grad_ref[...] = jnp.zeros_like(gain_grad_ref)
 
     def fill(s):
-        scatter.fill(s, s, [gate_ref, up_ref], [gate_w_ref, up_w_ref], True)
+        return scatter.fill(s, s, [gate_ref, up_ref], [gate_w_ref, up_w_ref], True)
 
     def store(s):
         term = scatter.result(s)[...]
@@ -831,55 +974,48 @@
         grad_residual_ref[s] = grad
         low_ref[s] = grad.astype(jnp.bfloat16)
 
-    sum_then_gather(
-        scatter, gather, [functools.partial(fill, s) for s in range(seqs)], [functools.partial(store, s) for s in range(seqs)]
-    )
+    fills = [fill(s) for s in range(seqs)]
+    stores = [functools.partial(store, s) for s in range(seqs)]
+    if with_out:
+        fill_out, store_out = out_body(hidden_ref, down_w_ref, residual_ref, layer_out_ref, scatter, seqs)
+        fills += [fill_out(s) for s in range(seqs)]
+        stores += [functools.partial(store_out, s) for s in range(seqs)]
+    sum_then_gather(scatter, gather, fills, stores, seqs)
     for weight in sums:
         weight.finish_others()
 
 
-def mlp_back(grad_gate, grad_up, gate_w, up_w, residual, out_grad, gain, grads):
+def mlp_back(grad_gate, grad_up, gate_w, up_w, residual, out_grad, gain, grads, out_inputs):
     seqs, rows, width = residual.shape
+    outs = [
+        jax.ShapeDtypeStruct(residual.shape, jnp.float32),
+        jax.ShapeDtypeStruct((8, width), jnp.float32),
+        jax.ShapeDtypeStruct((seqs, lax.axis_size("grp") * rows, width), jnp.bfloat16),
+    ]
+    outs += [slots_of(grad, axis) for grad, axis in zip(grads, weight_axes)]
+    out_specs = [in_vmem] * 2 + [in_hbm] * 4
+    if out_inputs:
+        outs.append(jax.ShapeDtypeStruct(residual.shape, jnp.bfloat16))
+        out_specs.append(in_vmem)
     return call(
-        mlp_back_body, "mlp_back", 3,
-        (grad_gate, grad_up, gate_w, up_w, residual, out_grad, gain, *grads), [in_vmem] * 7 + [in_hbm] * 3,
-        [
-            jax.ShapeDtypeStruct(residual.shape, jnp.float32),
-            jax.ShapeDtypeStruct((8, width), jnp.float32),
-            jax.ShapeDtypeStruct((seqs, lax.axis_size("grp") * rows, width), jnp.bfloat16),
-        ]
-        + [slots_of(grad, axis) for grad, axis in zip(grads, weight_axes)],
-        [in_vmem] * 2 + [in_hbm] * 4,
+        functools.partial(mlp_back_body, bool(out_inputs)), "mlp_back", 3,
+        (grad_gate, grad_up, gate_w, up_w, residual, out_grad, gain, *grads, *out_inputs),
+        [in_vmem] * 7 + [in_hbm] * 3 + [in_vmem] * len(out_inputs),
+        outs, out_specs,
         [pltpu.VMEM(residual.shape, jnp.bfloat16)]
         + seq_sems(3)
         + gather_sems(seqs)
-        + scatter_scratch(seqs, rows, width),
-        110,
-    )
-
-
-def out_body(hidden_ref, down_w_ref, residual_ref, layer_out_ref, scatter, first):
-    def fill(s):
-        scatter.fill(first + s, s, [hidden_ref], [down_w_ref], False)
-
-    def store(s):
-        layer_out_ref[s] = (residual_ref[s] + scatter.result(first + s)[...]).astype(jnp.bfloat16)
-
-    return fill, store
+        + scatter_scratch(seqs * (2 if out_inputs else 1), rows, width),
+        130,
+    )
 
 
 def last_body(
-    with_out, branch_ref, feed_ref, branch_w_ref, rec_w_ref, x_ref, grad_ref, gain_ref, gain_two_ref, rec_ref,
+    branch_ref, feed_ref, branch_w_ref, rec_w_ref, x_ref, grad_ref, gain_ref, gain_two_ref, rec_ref,
     w0, w1, w2, *refs,
 ):
-    if with_out:
-        hidden_ref, down_w_ref, residual_ref = refs[:3]
-        refs = refs[3:]
     grad_x_ref, rec_sum_ref, gain_sum_ref, o0, o1, o2 = refs[:6]
     refs = refs[6:]
-    if with_out:
-        layer_out_ref = refs[0]
-        refs = refs[1:]
     rec_slots, gain_local, gain_part, gain_slots, part_slots = refs[:5]
     rec_sems, gain_sems, part_sems = refs[5:7], refs[7:9], refs[9:11]
     greet_axes(("seq", "grp"))
@@ -894,7 +1030,7 @@
     gain_local[1:2, :] = gain_two_ref[0:1, :]
 
     def fill(s):
-        scatter.fill(s, s, [branch_ref, feed_ref], [branch_w_ref, rec_w_ref], True)
+        return scatter.fill(s, s, [branch_ref, feed_ref], [branch_w_ref, rec_w_ref], True)
 
     across = Exchange(
         "seq", block(gain_local, 1, lax.axis_size("seq")), lambda k: gain_slots.at[k], *gain_sems
@@ -910,13 +1046,9 @@
             across.start()
         grad_x_ref[s] = grad_ref[s] + norm_back(term, normal, inverse, gain_ref[...])
 
-    fills = [functools.partial(fill, s) for s in range(seqs)]
-    stores = [functools.partial(store, s) for s in range(seqs)]
-    if with_out:
-        fill_out, store_out = out_body(hidden_ref, down_w_ref, residual_ref, layer_out_ref, scatter, seqs)
-        fills += [functools.partial(fill_out, s) for s in range(seqs)]
-        stores += [functools.partial(store_out, s) for s in range(seqs)]
-    sum_then_gather(scatter, None, fills, stores)
+    sum_then_gather(
+        scatter, None, [fill(s) for s in range(seqs)], [functools.partial(store, s) for s in range(seqs)]
+    )
     across.finish()
     gain_part[...] = sum_of(gain_slots)
     along = Exchange("grp", lambda k: gain_part, lambda k: part_slots.at[k], *part_sems)
@@ -929,7 +1061,7 @@
     gain_sum_ref[...] = sum_of(part_slots)
 
 
-def last(grad_branch, grad_feed, branch_w, rec_w, layer_in, grad_residual, gain, gain_two_grad, rec_blocks, grads, out_inputs):
+def last(grad_branch, grad_feed, branch_w, rec_w, layer_in, grad_residual, gain, gain_two_grad, rec_blocks, grads):
     seqs, rows, width = layer_in.shape
     size, n = lax.axis_size("seq"), lax.axis_size("grp")
     f32 = jnp.float32
@@ -941,13 +1073,9 @@
     ]
     outs += [slots_of(grad, axis) for grad, axis in zip(grads, weight_axes)]
     out_specs = [in_vmem] * 3 + [in_hbm] * 3
-    if out_inputs:
-        outs.append(jax.ShapeDtypeStruct(layer_in.shape, jnp.bfloat16))
-        out_specs.append(in_vmem)
     return call(
-        functools.partial(last_body, bool(out_inputs)), "last", 4,
-        inputs + tuple(grads) + tuple(out_inputs),
-        [in_vmem] * len(inputs) + [in_hbm] * 3 + [in_vmem] * len(out_inputs),
+        last_body, "last", 4,
+        inputs + tuple(grads), [in_vmem] * len(inputs) + [in_hbm] * 3,
         outs, out_specs,
         [
             pltpu.VMEM(rec_blocks.shape, f32),
@@ -959,8 +1087,8 @@
         + [pltpu.SemaphoreType.DMA((size,))] * 4
         + [pltpu.SemaphoreType.DMA((n,))] * 2
         + seq_sems(3)
-        + scatter_scratch(seqs * (2 if out_inputs else 1), rows, width),
-        110,
+        + scatter_scratch(seqs, rows, width),
+        80,
     )
 
 
@@ -970,7 +1098,7 @@
     fill, store = out_body(hidden_ref, down_w_ref, residual_ref, layer_out_ref, scatter, 0)
     seqs = range(residual_ref.shape[0])
     sum_then_gather(
-        scatter, None, [functools.partial(fill, s) for s in seqs], [functools.partial(store, s) for s in seqs]
+        scatter, None, [fill(s) for s in seqs], [functools.partial(store, s) for s in seqs]
     )
 
 
@@ -1007,9 +1135,6 @@
     )
     late_grad, x_full, params, gains, branch_w, rec_w, out_w = gather_first(
         layer_in, out_grad, pack, (w_branch, w_rec, w_out)
-    )
-    grad_output = jnp.concatenate(
-        [lax.all_gather(late_grad[s], "grp", axis=0, tiled=True) for s in range(seqs_here)]
     )
 
     gains = gains.reshape(grp_devices, seq_devices, -1)[:, :, : own_gains.size]
@@ -1024,15 +1149,30 @@
     logit = vectors[tap_count + 3 :]
     softness = jax.nn.softplus(-logit)
 
-    inputs = x_full.astype(f32)
-    normal_one = inputs * lax.rsqrt(mean_of(inputs * inputs) + epsilon)
-    normed_one = (normal_one * gains[0]).astype(jnp.bfloat16).reshape(-1, model_width)
-    branch_pre = matmul(normed_one, branch_w).reshape(seqs_here, -1, channels)
-    feed = matmul(normed_one, rec_w).astype(jnp.bfloat16).reshape(seqs_here, -1, channels)
-    conv, rate, gate, state, mixed = rec_forward(feed, branch_pre, vectors, softness, diag_a, diag_x)
-    residual, normed_two, gate_w, up_w, down_w = mixer_out(
-        mixed, out_w, layer_in, gains[1], (mlp_gate, mlp_up, mlp_down)
-    )
+    short_line = seqs_here * positions * grp_devices <= 2048
+    mlp_weights = (mlp_gate, mlp_up, mlp_down)
+    if short_line:
+        (
+            normed_one, branch_pre, feed, conv, rate, gate, state, mixed, residual, normed_two, grad_output,
+            gate_w, up_w, down_w,
+        ) = mixer_forward(
+            x_full, gains, branch_w, rec_w, out_w, vectors, softness, diag_a, diag_x, late_grad, mlp_weights
+        )
+        normed_one = normed_one.reshape(-1, model_width)
+        grad_output = grad_output.reshape(-1, model_width)
+    else:
+        grad_output = jnp.concatenate(
+            [lax.all_gather(late_grad[s], "grp", axis=0, tiled=True) for s in range(seqs_here)]
+        )
+        inputs = x_full.astype(f32)
+        normal_one = inputs * lax.rsqrt(mean_of(inputs * inputs) + epsilon)
+        normed_one = (normal_one * gains[0]).astype(jnp.bfloat16).reshape(-1, model_width)
+        branch_pre = matmul(normed_one, branch_w).reshape(seqs_here, -1, channels)
+        feed = matmul(normed_one, rec_w).astype(jnp.bfloat16).reshape(seqs_here, -1, channels)
+        conv, rate, gate, state, mixed = rec_forward(feed, branch_pre, vectors, softness, diag_a, diag_x)
+        residual, normed_two, gate_w, up_w, down_w = mixer_out(
+            mixed, out_w, layer_in, gains[1], mlp_weights
+        )
     mixed = mixed.reshape(-1, channels)
     normed_two = normed_two.reshape(-1, model_width)
     up_proj = matmul(normed_two, up_w)
@@ -1048,9 +1188,16 @@
     def by_seq(values):
         return values.reshape(seqs_here, -1, values.shape[-1])
 
-    grad_residual, gain_two_grad, residual_low, *mlp_slots = mlp_back(
+    back_inputs = (
         by_seq(grad_gate), by_seq(grad_up), gate_w, up_w, residual, out_grad, gains[1], mlp_grads
     )
+    if not short_line:
+        layer_out = out_only(by_seq(hidden), down_w, residual)
+        grad_residual, gain_two_grad, residual_low, *mlp_slots = mlp_back(*back_inputs, ())
+    else:
+        grad_residual, gain_two_grad, residual_low, *mlp_slots, layer_out = mlp_back(
+            *back_inputs, (by_seq(hidden), down_w)
+        )
     mlp_grads = sum_slots(mlp_grads, mlp_slots)
     residual_low = residual_low.reshape(-1, model_width)
     out_weight_grad = matmul_tn(mixed, residual_low)
@@ -1078,16 +1225,10 @@
             out_weight_grad,
         )
     )
-    last_inputs = (
+    grad_x, rec_sum, gain_sum, *mixer_slots = last(
         grad_branch, grad_feed, branch_w, rec_w, layer_in, grad_residual, gains[0], gain_two_grad, rec_blocks,
         mixer_grads,
     )
-    out_inputs = (by_seq(hidden), down_w, residual)
-    if grp_devices > 8:
-        layer_out = out_only(*out_inputs)
-        grad_x, rec_sum, gain_sum, *mixer_slots = last(*last_inputs, ())
-    else:
-        grad_x, rec_sum, gain_sum, *mixer_slots, layer_out = last(*last_inputs, out_inputs)
     mixer_grads = sum_slots(mixer_grads, mixer_slots)
     rec_sum = rec_sum.reshape(-1)[: own_params.size].reshape(own_params.shape)
     own_part = gain_one.shape[0]

time: 643 us -> 581 us (0.904)
  matrix products: 84.8 us -> 65.3 us
  local copies, waits for them, and re-layouts: 47 us -> 32.9 us
  Pallas kernels: 468 us -> 454 us
  between operations: 14.8 us -> 1.36 us
  other arithmetic: 25 us -> 18.1 us
    unnamed x84 -> x68, local copies, waits for them, and re-layouts: 27.9 us -> 14.5 us
    pallas_call x1 -> x0, Pallas kernels: 11.7 us -> none  [rec_forward(): pl.pallas_call(rec_forward_body, grid=(seq_len // rows,), in_specs=[block...]
    dot_general x4 -> x2, matrix products: 28.6 us -> 17.4 us  [matmul(): return jnp.dot(left, right, preferred_element_type=jnp.float32)]
  transfers between devices with their start and end apart: 2 -> 0, of which waited for: 0 -> 0; matrix products, arithmetic and copies ran while one was open for 5% -> 0% of each run, Pallas kernels for 22% -> 0%
where the time goes in v5:
time: 581 us; the launch traced here: 572 us
  Pallas kernels  454 us (78%)
  matrix products  65.3 us (11%)
  local copies, waits for them, and re-layouts  32.9 us (6%)
  other arithmetic  18.1 us (3%)
    pallas_call x4, Pallas kernels, call(): pl.pallas_call(body, in_specs=in_specs, out_specs=out_specs, out_shape=ou...  433 us
    dot_general x6, matrix products, matmul_tn(): lax.dot_general(left, right, (((0,), (0,)), ((), ())), preferred_element_...  36 us
    pallas_call x1, Pallas kernels, rec_backward(): pl.pallas_call(rec_backward_body, grid=(blocks,), in_specs=[block, block,...  20.7 us
    dot_general x2, matrix products, matmul(): return jnp.dot(left, right, preferred_element_type=jnp.float32)  17.4 us
    add x6, other arithmetic, sum_slots(): own = own.astype(jnp.float32) + slot[k].astype(jnp.float32)  14.8 us
    unnamed x68, local copies, waits for them, and re-layouts  14.5 us
    dot_general x2, matrix products, matmul_nt(): lax.dot_general(left, right, (((1,), (1,)), ((), ())), preferred_element_...  11.9 us

profile of v5, /device:TPU:0, one launch (start us, length us, event | category | flops | bytes accessed | tf_op | source)
XLA Modules:
  0.0 571.9 jit_solution(11063150876525059337)
XLA Ops:
  0.7 0.8 fusion.17
  1.4 0.8 copy.83
  2.2 0.8 copy.84
  3.0 0.8 copy.85
  3.8 0.8 copy.86
  4.6 0.8 copy.87
  5.4 1.4 concatenate.51
  8.0 1.9 copy.89.w0
  9.9 1.9 copy.90.w1
  11.8 66.6 %gather_first.1 = (bf16[2,96,2048]{2,1,0:T(8,128)(2,1)}, bf16[2,768,2048]{2,1,0:T(8,128)(2,1)}, f32[4,256,128]{2,1,0:T(8,128)}, f32[8,4,8,128]{3,2,1,0:T(8,128)}...) custom-call(bf16[2,96,2048]{2,1,0:T(8,128)(2,1)} %x_ref.3, ...), custom_call_target="tpu_custom_call" | custom-call | flops 70000001024 | bytes 210000000 | tf_op jit(solution)/shard_map/gather_first/pallas_call | solution.py:572
  78.5 0.9 reshape.187
  81.7 1.4 copy.124
  85.2 0.9 fusion.14
  86.1 149.2 %mixer_forward.1 = (bf16[2,768,2048]{2,1,0:T(8,128)(2,1)}, f32[2,768,352]{2,1,0:T(8,128)}, bf16[2,768,352]{2,1,0:T(8,128)(2,1)}, bf16[2,768,352]{2,1,0:T(8,128)(...) custom-call(bf16[2,768,2048]{2,1,0:T(8,128)(2,1)} %get-tuple-element, ...), custom_call_target="tpu_custom_call" | custom-call | flops 130000003072 | bytes 390000000 | tf_op jit(solution)/shard_map/mixer_forward/pallas_call | solution.py:572
  235.4 8.3 %fusion.21 = f32[1536,768]{1,0:T(8,128)S(1)} fusion(bf16[1536,2048]{1,0:T(8,128)(2,1)} %bitcast.169, bf16[768,2048]{1,0:T(8,128)(2,1)} %get-tuple-element.64.refs_1_), kind=kOutput, calls=%fused_computation.78 | convolution fusion | flops 4831838208 | bytes 14155776 | tf_op jit(solution)/shard_map/dot_general | solution.py:28
  243.7 6.7 %fusion.22 = f32[1536,768]{1,0:T(8,128)} fusion(bf16[1536,2048]{1,0:T(8,128)(2,1)S(1)} %bitcast.165, bf16[2048,768]{1,0:T(8,128)(2,1)S(1)} %copy-done.22), kind=kOutput, calls=%fused_computation.79 | convolution fusion | flops 4831838208 | bytes 14155776 | tf_op jit(solution)/shard_map/dot_general | solution.py:18
  250.4 10.7 %multiply_convert_fusion = (bf16[1536,768]{1,0:T(8,128)(2,1)S(1)}, bf16[1536,768]{1,0:T(8,128)(2,1)S(1)}, bf16[1536,768]{1,0:T(8,128)(2,1)S(1)}) fusion(f32[1536,768]{1,0:T(8,128)} %fusion.22, f32[1536,768]{1,0:T(8,128)S(1)} %fusion.21, bf16[1536,2048]{1,0:T(8,128)(2,1)S(1)} %bitcast.166, bf16[2048,768]{1,0:T(8,128)(2,1)} %get-tuple-element.66.up_w_ref), kind=kOutput, calls=%fused_computation.9 | convolution fusion | flops 4862509056 | bytes 25952256 | tf_op jit(solution)/shard_map/dot_general | solution.py:18
  261.2 6.5 %convolution_convert_fusion.w2 = bf16[768,2048]{1,0:T(8,128)(2,1)} fusion(bf16[1536,768]{1,0:T(8,128)(2,1)S(1)} %get-tuple-element.152, bf16[1536,2048]{1,0:T(8,128)(2,1)S(1)} %bitcast.172), kind=kOutput, calls=%fused_computation.12 | convolution fusion | flops 4833411072 | bytes 11796480 | tf_op jit(solution)/shard_map/dot_general | solution.py:22
  267.7 6.5 %convolution_convert_fusion.2.w0 = bf16[2048,768]{1,0:T(8,128)(2,1)} fusion(bf16[1536,2048]{1,0:T(8,128)(2,1)S(1)} %bitcast.167, bf16[1536,768]{1,0:T(8,128)(2,1)S(1)} %get-tuple-element.153), kind=kOutput, calls=%fused_computation.14 | convolution fusion | flops 4833411072 | bytes 11796480 | tf_op jit(solution)/shard_map/dot_general | solution.py:22
  274.2 6.7 %convolution_convert_fusion.1.w1 = bf16[2048,768]{1,0:T(8,128)(2,1)} fusion(bf16[1536,2048]{1,0:T(8,128)(2,1)S(1)} %bitcast.168, bf16[1536,768]{1,0:T(8,128)(2,1)S(1)} %get-tuple-element.154), kind=kOutput, calls=%fused_computation.13 | convolution fusion | flops 4833411072 | bytes 11796480 | tf_op jit(solution)/shard_map/dot_general | solution.py:22
  280.9 141.9 %mlp_back.1 = (f32[2,96,2048]{2,1,0:T(8,128)}, f32[8,2048]{1,0:T(8,128)}, bf16[2,768,2048]{2,1,0:T(8,128)(2,1)}, bf16[3,512,768]{2,1,0:T(8,128)(2,1)}, bf16[3,51...) custom-call(bf16[2,768,768]{2,1,0:T(8,128)(2,1)} %bitcast.174, ...), custom_call_target="tpu_custom_call" | custom-call | flops 130000003072 | bytes 390000000 | tf_op jit(solution)/shard_map/mlp_back/pallas_call | solution.py:572
  422.9 3.6 convert_add_fusion
  426.5 2.8 convert_add_fusion.3
  429.3 3.2 convert_add_fusion.6
  432.5 3.6 fusion.7.w2
  436.2 3.6 fusion.8.grad_mixed_ref
  439.8 20.7 %rec_backward.1 = (bf16[2,768,352]{2,1,0:T(8,128)(2,1)S(1)}, bf16[2,768,352]{2,1,0:T(8,128)(2,1)S(1)}, f32[352,352]{1,0:T(8,128)S(1)}, f32[352,352]{1,0:T(8,128)S(1)}, f32[8,352]{1,0:T(8,128)S(1)}) custom-call(f32[2,768,352]{2,1,0:T(8,128)S(1)} %fusion.8.grad_mixed_ref, f32[2,768,352]{2,1,0:T(8,128)S(1)} %copy-done.1, bf16[2,768,352]{2,1,0:T(8,128)(2,1)S(1)} %copy-done, ...), custom_call_target="tpu_custom_call" | custom-call | tf_op jit(solution)/shard_map/rec_backward/pallas_call | solution.py:274
  460.6 1.0 fusion.18
  461.8 1.0 stack.19
  462.8 0.8 fusion.19
  463.6 0.9 stack.21
  464.5 0.9 stack.22
  466.4 0.8 copy.125
  467.2 8.0 %bitcast_convert_fusion.1.w0 = bf16[2048,352]{1,0:T(8,128)(2,1)} fusion(bf16[2,768,2048]{2,1,0:T(8,128)(2,1)} %get-tuple-element.84, bf16[2,768,352]{2,1,0:T(8,128)(2,1)S(1)} %get-tuple-element.77.branch_ref), kind=kOutput, calls=%fused_computation.16 | convolution fusion | flops 2215313408 | bytes 8814592 | tf_op jit(solution)/shard_map/dot_general | solution.py:22
  475.2 4.7 bitcast_convert_fusion.w1
  479.9 75.7 %last.1 = (f32[2,96,2048]{2,1,0:T(8,128)}, f32[248,128]{1,0:T(8,128)}, f32[8,512]{1,0:T(8,128)}, bf16[3,512,352]{2,1,0:T(8,128)(2,1)}, bf16[3,512,352]{2,1,0:T(8,128)(2,1)}, /*index=5*/bf16[3,352,512]{2,1,0:T(8,128)(2,1)}) custom-call(bf16[2,768,352]{2,1,0:T(8,128)(2,1)} %copy-done.9, bf16[2,768,352]{2,1,0:T(8,128)(2,1)} %copy-done.10, ...), custom_call_target="tpu_custom_call" | custom-call | flops 80000000000 | bytes 240000000 | tf_op jit(solution)/shard_map/last/pallas_call | solution.py:572
  555.6 2.4 convert_add_fusion.15
  558.0 1.5 convert_add_fusion.9
  559.6 1.1 copy.105
  560.7 1.3 convert_add_fusion.12
  562.0 1.1 copy.104
  563.1 0.8 constant_dynamic-slice_fusion
  564.4 1.1 reshape.202
  565.4 0.8 slice_reduce_fusion
  567.0 0.7 copy.108
  567.7 0.7 copy.107
  568.4 2.1 copy.128
  570.5 1.1 copy.129
  (90 shorter events, 8.2 us)
Async XLA Ops:
  84.4 1.7 copy-start.6
  235.3 8.3 %copy-start.15 = (bf16[2,768,2048]{2,1,0:T(8,128)(2,1)S(1)}, bf16[2,768,2048]{2,1,0:T(8,128)(2,1)}, u32[]{:S(2)}) copy-start(bf16[2,768,2048]{2,1,0:T(8,128)(2,1)} %get-tuple-element.65) | copy-start | bytes 18874372
  235.3 8.3 %copy-start.22 = (bf16[2048,768]{1,0:T(8,128)(2,1)S(1)}, bf16[2048,768]{1,0:T(8,128)(2,1)}, u32[]{:S(2)}) copy-start(bf16[2048,768]{1,0:T(8,128)(2,1)} %get-tuple-element.67.gate_w_ref) | copy-start | bytes 9437188
  243.7 17.4 %slice-start = ((s8[6291456]{0:T(1024)(128)(4,1)}), s8[4194304]{0:T(1024)(128)(4,1)S(1)}, s32[]{:S(2)}) async-start(s8[6291456]{0:T(1024)(128)(4,1)} %bitcast.170), calls=%async_computation | async-start | bytes 8388608
  250.4 10.8 %slice-start.1 = ((s8[6291456]{0:T(1024)(128)(4,1)}), s8[2097152]{0:T(1024)(128)(4,1)S(1)}, s32[]{:S(2)}) async-start(s8[6291456]{0:T(1024)(128)(4,1)} %bitcast.170), calls=%async_computation.1 | async-start | bytes 4194304
  261.1 6.6 %copy-start.16 = (bf16[1536,768]{1,0:T(8,128)(2,1)}, bf16[1536,768]{1,0:T(8,128)(2,1)S(1)}, u32[]{:S(2)}) copy-start(bf16[1536,768]{1,0:T(8,128)(2,1)S(1)} %get-tuple-element.152) | copy-start | bytes 7077892
  261.1 6.6 %copy-start.17 = (bf16[1536,768]{1,0:T(8,128)(2,1)}, bf16[1536,768]{1,0:T(8,128)(2,1)S(1)}, u32[]{:S(2)}) copy-start(bf16[1536,768]{1,0:T(8,128)(2,1)S(1)} %get-tuple-element.153) | copy-start | bytes 7077892
  261.1 13.1 %copy-start.18 = (bf16[1536,768]{1,0:T(8,128)(2,1)}, bf16[1536,768]{1,0:T(8,128)(2,1)S(1)}, u32[]{:S(2)}) copy-start(bf16[1536,768]{1,0:T(8,128)(2,1)S(1)} %get-tuple-element.154) | copy-start | bytes 7077892
  280.9 151.5 %copy-start.20 = (bf16[2,768,352]{2,1,0:T(8,128)(2,1)S(1)}, bf16[2,768,352]{2,1,0:T(8,128)(2,1)}, u32[]{:S(2)}) copy-start(bf16[2,768,352]{2,1,0:T(8,128)(2,1)} %get-tuple-element.85) | copy-start | bytes 3244036
  422.9 3.6 copy-start.12
  426.4 2.8 copy-start.11
  426.4 6.0 %copy-start.19 = (bf16[2,768,2048]{2,1,0:T(8,128)(2,1)S(1)}, bf16[2,768,2048]{2,1,0:T(8,128)(2,1)}, u32[]{:S(2)}) copy-start(bf16[2,768,2048]{2,1,0:T(8,128)(2,1)} %get-tuple-element.70) | copy-start | bytes 18874372
  432.5 3.6 copy-start.21
  436.1 3.6 copy-start
  436.1 3.6 copy-start.1
  436.1 3.7 copy-start.2
  436.1 3.7 copy-start.3
  436.1 3.7 copy-start.4
  436.1 3.7 copy-start.5
  436.1 3.7 copy-start.7
  436.1 3.7 copy-start.8
  460.5 6.7 %copy-start.9 = (bf16[2,768,352]{2,1,0:T(8,128)(2,1)}, bf16[2,768,352]{2,1,0:T(8,128)(2,1)S(1)}, u32[]{:S(2)}) copy-start(bf16[2,768,352]{2,1,0:T(8,128)(2,1)S(1)} %get-tuple-element.77.branch_ref) | copy-start | bytes 3244036
  460.6 14.6 %copy-start.10 = (bf16[2,768,352]{2,1,0:T(8,128)(2,1)}, bf16[2,768,352]{2,1,0:T(8,128)(2,1)S(1)}, u32[]{:S(2)}) copy-start(bf16[2,768,352]{2,1,0:T(8,128)(2,1)S(1)} %get-tuple-element.78.feed_ref) | copy-start | bytes 3244036
  466.3 8.9 %slice-start.2 = ((s8[6291456]{0:T(1024)(128)(4,1)}), s8[4194304]{0:T(1024)(128)(4,1)S(1)}, s32[]{:S(2)}) async-start(s8[6291456]{0:T(1024)(128)(4,1)} %bitcast.176), calls=%async_computation.2 | async-start | bytes 8388608
  467.2 8.0 %slice-start.3 = ((s8[6291456]{0:T(1024)(128)(4,1)}), s8[2097152]{0:T(1024)(128)(4,1)S(1)}, s32[]{:S(2)}) async-start(s8[6291456]{0:T(1024)(128)(4,1)} %bitcast.176), calls=%async_computation.3 | async-start | bytes 4194304
  555.6 5.1 copy-start.14
  560.7 9.8 %copy-start.13 = (f32[2,96,2048]{2,1,0:T(8,128)S(1)}, f32[2,96,2048]{2,1,0:T(8,128)}, u32[]{:S(2)}) copy-start(f32[2,96,2048]{2,1,0:T(8,128)} %get-tuple-element.187) | copy-start | bytes 4718596

commit v6 on v5

--- a/solution.py
+++ b/solution.py
@@ -39,15 +39,22 @@
     return tuple(grad.astype(jnp.bfloat16) for grad in grads)
 
 
-def sum_slots(grads, slots):
+def sum_slots(grads, slots, axes):
     sums = []
-    for grad, slot, axis in zip(grads, slots, weight_axes):
+    for grad, slot, axis in zip(grads, slots, axes):
         size = slot.shape[1 + axis]
         own = lax.dynamic_slice_in_dim(grad, lax.axis_index("seq") * size, size, axis)
         for k in range(slot.shape[0]):
             own = own.astype(jnp.float32) + slot[k].astype(jnp.float32)
         sums.append(own)
     return sums
+
+
+def sum_all(slots):
+    total = slots[0].astype(jnp.float32)
+    for k in range(1, slots.shape[0]):
+        total = total + slots[k].astype(jnp.float32)
+    return total
 
 
 def padded_rows(values):
@@ -162,73 +169,75 @@
         )
 
 
+def rec_backward_rows(
+    grad_mixed, branch, feed, feed_before, conv_low, rate, gate, state, state_before,
+    vectors_ref, softness_ref, gate_a_ref, gate_x_ref, grad_a_ref, grad_x_ref, sums_ref, window, later, carry,
+):
+    rows = feed.shape[0]
+    softness = softness_ref[...]
+    gelu_branch, slope = gelu_parts(branch)
+    state_low = state.astype(jnp.bfloat16).astype(jnp.float32)
+    grad_state = (grad_mixed * gelu_branch).astype(jnp.bfloat16).astype(jnp.float32)
+    grad_branch = (slope * grad_mixed * state_low).astype(jnp.bfloat16)
+    decay, scale = decay_parts(rate, softness)
+    total, carried = scan_block(shift_up(decay, 1, 1.0), grad_state, shift_up)
+    carried = carried + total * carry[0:1, :]
+    carry[0:1, :] = decay[0:1, :] * carried[0:1, :]
+    index = lax.broadcasted_iota(jnp.int32, state.shape, 0)
+    previous = jnp.where(index >= 1, pltpu.roll(state, 1, 0), state_before[7:8, :])
+    conv = conv_low.astype(jnp.float32)
+    grad_log = carried * previous * decay - carried * gate * conv * decay * decay / scale
+    log_rate = grad_log * rate
+    pre_a = -8.0 * softness * log_rate * (1.0 - rate)
+    pre_x = carried * scale * conv * gate * (1.0 - gate)
+    low_a = pre_a.astype(jnp.bfloat16)
+    low_x = pre_x.astype(jnp.bfloat16)
+    grad_a_ref[...] += matmul_tn(conv_low, low_a)
+    grad_x_ref[...] += matmul_tn(conv_low, low_x)
+    grad_conv = (
+        carried * scale * gate
+        + matmul_nt(low_a, gate_a_ref[...])
+        + matmul_nt(low_x, gate_x_ref[...])
+    )
+    window[pl.ds(0, 8), :] = feed_before
+    window[pl.ds(8, rows), :] = feed.astype(jnp.float32)
+    later[pl.ds(rows, 8), :] = later[pl.ds(0, 8), :]
+    later[pl.ds(0, rows), :] = grad_conv
+    grad_feed = vectors_ref[0:1, :] * grad_conv
+    sums_ref[0:1, :] += jnp.sum(grad_conv * window[pl.ds(8, rows), :], axis=0, keepdims=True)
+    for k in range(1, 4):
+        grad_feed = grad_feed + vectors_ref[k : k + 1, :] * later[pl.ds(k, rows), :]
+        sums_ref[k : k + 1, :] += jnp.sum(
+            grad_conv * window[pl.ds(8 - k, rows), :], axis=0, keepdims=True
+        )
+    sums_ref[4:5, :] += jnp.sum(grad_conv, axis=0, keepdims=True)
+    sums_ref[5:6, :] += jnp.sum(pre_a, axis=0, keepdims=True)
+    sums_ref[6:7, :] += jnp.sum(pre_x, axis=0, keepdims=True)
+    sums_ref[7:8, :] += jnp.sum(log_rate, axis=0, keepdims=True)
+    return grad_branch, grad_feed.astype(jnp.bfloat16)
+
+
 def rec_backward_body(
     grad_mixed_ref, branch_ref, feed_ref, feed_before_ref, conv_ref, rate_ref, input_ref,
     state_ref, state_before_ref, vectors_ref, softness_ref, gate_a_ref, gate_x_ref,
     grad_branch_ref, grad_feed_ref, grad_a_ref, grad_x_ref, sums_ref, window, later, carry,
 ):
-    seqs, rows, channels = feed_ref.shape
     step = pl.program_id(0)
-    first_block = step == pl.num_programs(0) - 1
-    before = feed_before_ref.shape[1]
 
     @pl.when(step == 0)
     def _():
-        later[...] = jnp.zeros_like(later)
-        carry[...] = jnp.zeros_like(carry)
-        grad_a_ref[...] = jnp.zeros_like(grad_a_ref)
-        grad_x_ref[...] = jnp.zeros_like(grad_x_ref)
-        sums_ref[...] = jnp.zeros_like(sums_ref)
-
-    softness = softness_ref[...]
-    keep = jnp.where(first_block, 0.0, 1.0)
-    for s in range(seqs):
-        gelu_branch, slope = gelu_parts(branch_ref[s])
-        grad_mixed = grad_mixed_ref[s]
-        state = state_ref[s]
-        state_low = state.astype(jnp.bfloat16).astype(jnp.float32)
-        grad_state = (grad_mixed * gelu_branch).astype(jnp.bfloat16).astype(jnp.float32)
-        grad_branch_ref[s] = (slope * grad_mixed * state_low).astype(jnp.bfloat16)
-        rate = rate_ref[s]
-        gate = input_ref[s]
-        decay, scale = decay_parts(rate, softness)
-        total, carried = scan_block(shift_up(decay, 1, 1.0), grad_state, shift_up)
-        carried = carried + total * carry[s, 0:1, :]
-        carry[s, 0:1, :] = decay[0:1, :] * carried[0:1, :]
-        index = lax.broadcasted_iota(jnp.int32, state.shape, 0)
-        last = state_before_ref[s][7:8, :] * keep
-        previous = jnp.where(index >= 1, pltpu.roll(state, 1, 0), last)
-        conv_low = conv_ref[s]
-        conv = conv_low.astype(jnp.float32)
-        grad_log = carried * previous * decay - carried * gate * conv * decay * decay / scale
-        log_rate = grad_log * rate
-        pre_a = -8.0 * softness * log_rate * (1.0 - rate)
-        pre_x = carried * scale * conv * gate * (1.0 - gate)
-        low_a = pre_a.astype(jnp.bfloat16)
-        low_x = pre_x.astype(jnp.bfloat16)
-        grad_a_ref[...] += matmul_tn(conv_low, low_a)
-        grad_x_ref[...] += matmul_tn(conv_low, low_x)
-        grad_conv = (
-            carried * scale * gate
-            + matmul_nt(low_a, gate_a_ref[...])
-            + matmul_nt(low_x, gate_x_ref[...])
-        )
-        window[s, pl.ds(0, 8), :] = feed_before_ref[s].astype(jnp.float32)[before - 8 :, :] * keep
-        window[s, pl.ds(8, rows), :] = feed_ref[s].astype(jnp.float32)
-        later[s, pl.ds(rows, 8), :] = later[s, pl.ds(0, 8), :]
-        later[s, pl.ds(0, rows), :] = grad_conv
-        grad_feed = vectors_ref[0:1, :] * grad_conv
-        sums_ref[0:1, :] += jnp.sum(grad_conv * window[s, pl.ds(8, rows), :], axis=0, keepdims=True)
-        for k in range(1, 4):
-            grad_feed = grad_feed + vectors_ref[k : k + 1, :] * later[s, pl.ds(k, rows), :]
-            sums_ref[k : k + 1, :] += jnp.sum(
-                grad_conv * window[s, pl.ds(8 - k, rows), :], axis=0, keepdims=True
-            )
-        grad_feed_ref[s] = grad_feed.astype(jnp.bfloat16)
-        sums_ref[4:5, :] += jnp.sum(grad_conv, axis=0, keepdims=True)
-        sums_ref[5:6, :] += jnp.sum(pre_a, axis=0, keepdims=True)
-        sums_ref[6:7, :] += jnp.sum(pre_x, axis=0, keepdims=True)
-        sums_ref[7:8, :] += jnp.sum(log_rate, axis=0, keepdims=True)
+        for ref in (later, carry, grad_a_ref, grad_x_ref, sums_ref):
+            ref[...] = jnp.zeros_like(ref)
+
+    keep = jnp.where(step == pl.num_programs(0) - 1, 0.0, 1.0)
+    for s in range(feed_ref.shape[0]):
+        before = feed_before_ref[s].astype(jnp.float32)
+        grad_branch_ref[s], grad_feed_ref[s] = rec_backward_rows(
+            grad_mixed_ref[s], branch_ref[s], feed_ref[s], before[before.shape[0] - 8 :] * keep, conv_ref[s],
+            rate_ref[s], input_ref[s], state_ref[s], state_before_ref[s] * keep,
+            vectors_ref, softness_ref, gate_a_ref, gate_x_ref, grad_a_ref, grad_x_ref, sums_ref,
+            window.at[s], later.at[s], carry.at[s],
+        )
 
 
 def whole(shape):
@@ -580,14 +589,14 @@
             flops=us * 1000000000, bytes_accessed=us * 3000000, transcendentals=0
         ),
         compiler_params=pltpu.CompilerParams(
-            collective_id=number, has_side_effects=True, vmem_limit_bytes=60 << 20
+            collective_id=number, has_side_effects=True, vmem_limit_bytes=62 << 20
         ),
     )(*inputs)
 
 
 class Exchange:
-    def __init__(self, axis, source, slot, send_sem, recv_sem, steps=None):
-        self.axis, self.source, self.slot, self.steps = axis, source, slot, steps
+    def __init__(self, axis, source, slot, send_sem, recv_sem, steps=None, first=1):
+        self.axis, self.source, self.slot, self.steps, self.first = axis, source, slot, steps, first
         self.size, self.me = lax.axis_size(axis), lax.axis_index(axis)
         self.send_sem, self.recv_sem = send_sem, recv_sem
 
@@ -595,7 +604,7 @@
         peer = lax.rem(self.me + k, self.size)
         return pltpu.make_async_remote_copy(
             src_ref=self.source(peer),
-            dst_ref=self.slot(owner) if self.slot else self.steps.at[k - 1],
+            dst_ref=self.slot(owner) if self.slot else self.steps.at[k - self.first],
             send_sem=self.send_sem.at[k],
             recv_sem=self.recv_sem.at[k],
             device_id={self.axis: peer},
@@ -603,7 +612,8 @@
         )
 
     def own(self):
-        return pltpu.make_async_copy(self.source(self.me), self.slot(self.me), self.send_sem.at[0])
+        slot = self.slot(self.me) if self.slot else self.steps.at[0]
+        return pltpu.make_async_copy(self.source(self.me), slot, self.send_sem.at[0])
 
     def start(self):
         self.own().start()
@@ -651,11 +661,11 @@
     ]
 
 
-def weight_sums(axes, sources, outs, send_sem, recv_sem):
+def weight_sums(axes, sources, outs, send_sem, recv_sem, first=1):
     parts = lax.axis_size("seq")
     return [
         Exchange(
-            "seq", block(source, axis, parts), None, send_sem.at[i], recv_sem.at[i], out
+            "seq", block(source, axis, parts), None, send_sem.at[i], recv_sem.at[i], out, first
         )
         for i, (axis, source, out) in enumerate(zip(axes, sources, outs))
     ]
@@ -671,14 +681,15 @@
     return jax.ShapeDtypeStruct(shape, block_of.dtype)
 
 
-def slots_of(matrix, axis):
+def slots_of(matrix, axis, first=1):
     shape = list(matrix.shape)
     size = lax.axis_size("seq")
     shape[axis] //= size
-    return jax.ShapeDtypeStruct((size - 1, *shape), matrix.dtype)
+    return jax.ShapeDtypeStruct((size - first, *shape), matrix.dtype)
 
 
 weight_axes = (0, 0, 1)
+mixer_axes = (1, 1, 1)
 
 
 def views(ref):
@@ -690,7 +701,7 @@
     greet_axes(("seq", "grp"))
     seqs = x_ref.shape[0]
     gather = Gather(views(x_ref), views(full_ref), x_ref.shape[1], *refs[:3])
-    weights = weight_gathers(weight_axes, (w0, w1, w2), (o0, o1, o2), weight_send, weight_recv)
+    weights = weight_gathers(mixer_axes, (w0, w1, w2), (o0, o1, o2), weight_send, weight_recv)
     small = Exchange("seq", lambda k: pack_ref, lambda k: params_ref.at[k], small_send, small_recv)
     small.start()
     for s in range(seqs):
@@ -726,7 +737,7 @@
             jax.ShapeDtypeStruct((size,) + pack.shape, jnp.float32),
             jax.ShapeDtypeStruct((n, size, 8, 128), jnp.float32),
         ]
-        + [gathered(w, axis) for w, axis in zip(weights, weight_axes)],
+        + [gathered(w, axis) for w, axis in zip(weights, mixer_axes)],
         [in_vmem, in_hbm] + [in_vmem] * 2 + [in_hbm] * 3,
         gather_sems(seqs)
         + [pltpu.SemaphoreType.DMA((size,))] * 2
@@ -740,13 +751,13 @@
     return jnp.mean(values, axis=-1, keepdims=True)
 
 
-def sum_then_gather(scatter, gather, fills, stores, count=0):
+def sum_then_gather(scatter, gather, fills, stores, count=0, between=None, after=()):
     hops = range(1, scatter.chips - 1)
     for step in fills[0]:
         step()
     scatter.hop(0, 0)
     for p, store in enumerate(stores):
-        ahead = list(fills[p + 1]) if p + 1 < len(fills) else []
+        ahead = list(fills[p + 1] if p + 1 < len(fills) else after)
         for h in hops:
             if ahead:
                 ahead.pop(0)()
@@ -757,6 +768,8 @@
             step()
         if p + 1 < len(fills):
             scatter.hop(p + 1, 0)
+        if between and p == 0:
+            between()
         store()
         if p < count:
             gather.start(p)
@@ -852,8 +865,8 @@
             normal = inputs * lax.rsqrt(mean_of(inputs * inputs) + epsilon)
             normed = (normal * gains_ref[0]).astype(jnp.bfloat16)
             normed_one_ref[s, at, :] = normed
-            branch_ref[s, at, :] = matmul(normed, branch_w_ref[...])
-            feed_ref[s, at, :] = matmul(normed, rec_w_ref[...]).astype(jnp.bfloat16)
+            branch_ref[s, at, :] = matmul_nt(normed, branch_w_ref[...])
+            feed_ref[s, at, :] = matmul_nt(normed, rec_w_ref[...]).astype(jnp.bfloat16)
 
     def recur(s):
         window[pl.ds(0, 8), :] = jnp.zeros((8, window.shape[1]), jnp.float32)
@@ -949,8 +962,8 @@
     grad_residual_ref, gain_grad_ref, full_ref, o0, o1, o2 = refs[:6]
     refs = refs[6:]
     if with_out:
-        layer_out_ref = refs[0]
-        refs = refs[1:]
+        layer_out_ref, late_ref = refs[:2]
+        refs = refs[2:]
     low_ref, *refs = refs
     greet_axes(("seq", "grp"))
     seqs, rows, _ = grad_ref.shape
@@ -978,9 +991,18 @@
     stores = [functools.partial(store, s) for s in range(seqs)]
     if with_out:
         fill_out, store_out = out_body(hidden_ref, down_w_ref, residual_ref, layer_out_ref, scatter, seqs)
-        fills += [fill_out(s) for s in range(seqs)]
-        stores += [functools.partial(store_out, s) for s in range(seqs)]
-    sum_then_gather(scatter, gather, fills, stores, seqs)
+        fills += [fill_out(s) for s in range(seqs - 1)]
+        stores += [functools.partial(store_out, s) for s in range(seqs - 1)]
+
+    def late():
+        step = 256
+
+        @pl.loop(0, late_ref.shape[0] // step)
+        def _(i):
+            at = pl.ds(pl.multiple_of(i * step, step), step)
+            late_ref[at, :] = matmul(hidden_ref[seqs - 1, at, :], down_w_ref[...]).astype(jnp.bfloat16)
+
+    sum_then_gather(scatter, gather, fills, stores, seqs, after=(late,) if with_out else ())
     for weight in sums:
         weight.finish_others()
 
@@ -995,8 +1017,9 @@
     outs += [slots_of(grad, axis) for grad, axis in zip(grads, weight_axes)]
     out_specs = [in_vmem] * 2 + [in_hbm] * 4
     if out_inputs:
-        outs.append(jax.ShapeDtypeStruct(residual.shape, jnp.bfloat16))
-        out_specs.append(in_vmem)
+        outs.append(jax.ShapeDtypeStruct((seqs - 1, rows, width), jnp.bfloat16))
+        outs.append(jax.ShapeDtypeStruct((lax.axis_size("grp") * rows, width), jnp.bfloat16))
+        out_specs += [in_vmem] * 2
     return call(
         functools.partial(mlp_back_body, bool(out_inputs)), "mlp_back", 3,
         (grad_gate, grad_up, gate_w, up_w, residual, out_grad, gain, *grads, *out_inputs),
@@ -1005,8 +1028,8 @@
         [pltpu.VMEM(residual.shape, jnp.bfloat16)]
         + seq_sems(3)
         + gather_sems(seqs)
-        + scatter_scratch(seqs * (2 if out_inputs else 1), rows, width),
-        130,
+        + scatter_scratch(seqs * 2 - 1 if out_inputs else seqs, rows, width),
+        120,
     )
 
 
@@ -1020,7 +1043,7 @@
     rec_sems, gain_sems, part_sems = refs[5:7], refs[7:9], refs[9:11]
     greet_axes(("seq", "grp"))
     seqs, rows, _ = x_ref.shape
-    sums = weight_sums(weight_axes, (w0, w1, w2), (o0, o1, o2), *refs[11:13])
+    sums = weight_sums(mixer_axes, (w0, w1, w2), (o0, o1, o2), *refs[11:13])
     scatter = Scatter(rows, *refs[13:])
     rec = Exchange("seq", lambda k: rec_ref.at[k], lambda k: rec_slots.at[k], *rec_sems)
     rec.start()
@@ -1030,7 +1053,7 @@
     gain_local[1:2, :] = gain_two_ref[0:1, :]
 
     def fill(s):
-        return scatter.fill(s, s, [branch_ref, feed_ref], [branch_w_ref, rec_w_ref], True)
+        return scatter.fill(s, s, [branch_ref, feed_ref], [branch_w_ref, rec_w_ref], False)
 
     across = Exchange(
         "seq", block(gain_local, 1, lax.axis_size("seq")), lambda k: gain_slots.at[k], *gain_sems
@@ -1071,7 +1094,7 @@
         jax.ShapeDtypeStruct(rec_blocks.shape[1:], f32),
         jax.ShapeDtypeStruct((8, width // size), f32),
     ]
-    outs += [slots_of(grad, axis) for grad, axis in zip(grads, weight_axes)]
+    outs += [slots_of(grad, axis) for grad, axis in zip(grads, mixer_axes)]
     out_specs = [in_vmem] * 3 + [in_hbm] * 3
     return call(
         last_body, "last", 4,
@@ -1092,6 +1115,264 @@
     )
 
 
+def copies(pairs, sem):
+    return [pltpu.make_async_copy(source, buffer, sem.at[i]) for i, (source, buffer) in enumerate(pairs)]
+
+
+def head_windows(heads, head_dim, parts):
+    part = head_dim // parts
+    rows = max(-(-(k + 1) * part // 8) * 8 - k * part // 8 * 8 for k in range(parts))
+
+    def start(h, k):
+        return pl.multiple_of(h * head_dim + k * part // 8 * 8, 8)
+
+    return rows, start
+
+
+def mixer_back_body(
+    heads, low_in, out_w_in, branch_in, feed_in, conv_in, rate_in, input_in, state_in, mixed_in, branch_w_in, rec_w_in,
+    normed_in, vectors_ref, softness_ref, gate_a_ref, gate_x_ref, x_ref, grad_ref, gain_ref, gain_two_ref,
+    grad_x_ref, squares_out_ref, sums_out_ref, gain_sum_ref, o0, o1, o2,
+    low_ref, out_w_ref, branch_ref, feed_ref, conv_ref, rate_ref, input_ref, state_ref, mixed_ref, branch_w_ref,
+    rec_w_ref, grad_mixed, grad_branch, grad_feed, squares, sums, window, later, carry, tiles, d0, d1, d2,
+    square_slots, sum_slots_ref, gain_local, gain_part, gain_slots, part_slots, load_sem, tile_sem,
+    square_send, square_recv, sum_send, sum_recv, gain_send, gain_recv, part_send, part_recv, weight_send, weight_recv,
+    *refs,
+):
+    seqs, rows, width = x_ref.shape
+    seq_len, channels = feed_ref.shape[1:]
+    per_seq = (
+        (low_in, low_ref), (branch_in, branch_ref), (feed_in, feed_ref), (conv_in, conv_ref), (rate_in, rate_ref),
+        (input_in, input_ref), (state_in, state_ref),
+    )
+    pairs = [(out_w_in, out_w_ref)]
+    for s in range(seqs):
+        pairs += [(source.at[s], buffer.at[s]) for source, buffer in per_seq]
+        if s == 0:
+            pairs += [(branch_w_in, branch_w_ref), (rec_w_in, rec_w_ref)]
+    pairs += [(mixed_in, mixed_ref)]
+    loads = copies(pairs, load_sem)
+    for load in loads:
+        load.start()
+    greet_axes(("seq", "grp"))
+    scatter = Scatter(rows, *refs)
+    parts = lax.axis_size("seq")
+    for ref in (squares, sums, gain_local):
+        ref[...] = jnp.zeros_like(ref)
+    gain_local[1:2, :] = gain_two_ref[0:1, :]
+    window_rows, start_of = head_windows(heads, channels // heads, parts)
+    square_moves = [
+        Exchange(
+            "seq",
+            lambda k, h=h: squares.at[:, pl.ds(start_of(h, k), window_rows), :],
+            lambda k, h=h: square_slots.at[k, h],
+            square_send.at[h],
+            square_recv.at[h],
+        )
+        for h in range(heads)
+    ]
+    sum_move = Exchange("seq", lambda k: sums, lambda k: sum_slots_ref.at[k], sum_send, sum_recv)
+    across = Exchange("seq", block(gain_local, 1, parts), lambda k: gain_slots.at[k], gain_send, gain_recv)
+    moves = weight_sums(mixer_axes, (d0, d1, d2), (o0, o1, o2), weight_send, weight_recv, 0)
+    tile_rows = pick_rows(seq_len, (256, 192, 128, 96, 64, 32, 16))
+    chunk = window.shape[0] - 8
+
+    def mix(s):
+        if s == 0:
+            for load in loads[: 1 + len(per_seq)]:
+                load.wait()
+        else:
+            first = 3 + s * len(per_seq)
+            for load in loads[first : first + len(per_seq)]:
+                load.wait()
+
+        @pl.loop(0, seq_len // tile_rows)
+        def _(i):
+            at = pl.ds(pl.multiple_of(i * tile_rows, tile_rows), tile_rows)
+            grad_mixed[at, :] = matmul_nt(low_ref[s, at, :], out_w_ref[...])
+
+    def recur(s):
+        carry[...] = jnp.zeros_like(carry)
+        later[...] = jnp.zeros_like(later)
+        blocks = seq_len // chunk
+
+        @pl.loop(0, blocks)
+        def _(i):
+            first = (blocks - 1 - i) * chunk
+            at = pl.ds(pl.multiple_of(first, chunk), chunk)
+            keep = jnp.where(i == blocks - 1, 0.0, 1.0)
+            before8 = pl.ds(pl.multiple_of(jnp.maximum(first - 8, 0), 8), 8)
+            before16 = pl.ds(pl.multiple_of(jnp.maximum(first - 16, 0), 16), 16)
+            grad_branch[s, at, :], grad_feed[s, at, :] = rec_backward_rows(
+                grad_mixed[at, :], branch_ref[s, at, :], feed_ref[s, at, :],
+                feed_ref[s, before16, :].astype(jnp.float32)[8:] * keep, conv_ref[s, at, :], rate_ref[s, at, :],
+                input_ref[s, at, :], state_ref[s, at, :], state_ref[s, before8, :] * keep,
+                vectors_ref, softness_ref, gate_a_ref, gate_x_ref, squares.at[0], squares.at[1], sums,
+                window, later, carry,
+            )
+
+        if s == seqs - 1:
+            for move in square_moves:
+                move.start()
+            sum_move.start()
+
+    def steps(s):
+        partners, own = scatter.fill(s, s, [grad_branch, grad_feed], [branch_w_ref, rec_w_ref], False)
+
+        def third():
+            if s == 0:
+                for load in loads[1 + len(per_seq) : 3 + len(per_seq)]:
+                    load.wait()
+            partners()
+
+        def first():
+            mix(s)
+            if s == seqs - 1:
+                out_grads()
+
+        return [first, functools.partial(recur, s), third, own]
+
+    def out_grads():
+        loads[-1].wait()
+        step = width // parts
+
+        @pl.loop(0, parts)
+        def _(k):
+            at = pl.ds(pl.multiple_of(k * step, step), step)
+            total = matmul_tn(mixed_ref[0], low_ref[0, :, at])
+            for s in range(1, seqs):
+                total = total + matmul_tn(mixed_ref[s], low_ref[s, :, at])
+            d2[:, at] = total.astype(jnp.bfloat16)
+
+        moves[2].start()
+
+    step = tiles.shape[-1]
+    count = width // parts // step
+
+    def columns_of(i):
+        peer = lax.rem(lax.axis_index("seq") + 1 + i // count, parts)
+        return pl.ds(pl.multiple_of((peer * count + lax.rem(i, count)) * step, step), step)
+
+    def tile_load(i, slot):
+        return pltpu.make_async_copy(normed_in.at[:, :, columns_of(i)], tiles.at[slot], tile_sem.at[slot])
+
+    def in_grads(part):
+        if part == 0:
+            tile_load(0, 0).start()
+
+        @pl.loop(part * count, (part + 1) * count)
+        def _(i):
+            slot = lax.rem(i, 2)
+            tile_load(i, slot).wait()
+
+            @pl.when(i + 1 < parts * count)
+            def _():
+                tile_load(i + 1, 1 - slot).start()
+
+            for to, grads in ((d0, grad_branch), (d1, grad_feed)):
+                total = matmul_tn(grads[0], tiles[slot, 0])
+                for s in range(1, seqs):
+                    total = total + matmul_tn(grads[s], tiles[slot, s])
+                to[:, columns_of(i)] = total.astype(jnp.bfloat16)
+
+        for move in moves[:2]:
+            if part < parts - 1:
+                move.copy(part + 1, move.me).start()
+            else:
+                move.own().start()
+
+    def grads_from(first, end):
+        for part in range(first, end):
+            in_grads(part)
+
+    def store(s):
+        term = scatter.result(s)[...]
+        inputs = x_ref[s].astype(jnp.float32)
+        inverse = lax.rsqrt(mean_of(inputs * inputs) + epsilon)
+        normal = inputs * inverse
+        gain_local[0:1, :] += jnp.sum(term * normal, axis=0, keepdims=True)
+        if s == seqs - 1:
+            across.start()
+        grad_x_ref[s] = grad_ref[s] + norm_back(term, normal, inverse, gain_ref[...])
+
+    sum_then_gather(
+        scatter, None, [steps(s) for s in range(seqs)], [functools.partial(store, s) for s in range(seqs)],
+        between=functools.partial(grads_from, 0, parts // 2),
+        after=(functools.partial(grads_from, parts // 2, parts - 1), functools.partial(grads_from, parts - 1, parts)),
+    )
+    across.finish()
+    gain_part[...] = sum_of(gain_slots)
+    along = Exchange("grp", lambda k: gain_part, lambda k: part_slots.at[k], part_send, part_recv)
+    along.start()
+    for move in square_moves:
+        move.finish()
+    squares_out_ref[...] = sum_of(square_slots)
+    sum_move.finish()
+    sums_out_ref[...] = sum_of(sum_slots_ref)
+    for move in moves:
+        move.finish()
+    along.finish()
+    gain_sum_ref[...] = sum_of(part_slots)
+
+
+def mixer_back(
+    heads, low, out_w, branch, feed, conv, rate, gate, state, mixed, branch_w, rec_w, normed,
+    vectors, softness, gate_a, gate_x, layer_in, grad_residual, gain, gain_two_grad,
+):
+    seqs, rows, width = layer_in.shape
+    seq_len, channels = feed.shape[1:]
+    size, n = lax.axis_size("seq"), lax.axis_size("grp")
+    f32, bf16 = jnp.float32, jnp.bfloat16
+    large = (low, out_w, branch, feed, conv, rate, gate, state, mixed, branch_w, rec_w)
+    small = (vectors, softness, gate_a, gate_x, layer_in, grad_residual, gain, gain_two_grad)
+    window_rows = head_windows(heads, channels // heads, size)[0]
+    grads = [jax.ShapeDtypeStruct(w.shape, bf16) for w in (branch_w, rec_w, out_w)]
+    squares = (heads, 2, window_rows, channels)
+    part = width // size
+    return call(
+        functools.partial(mixer_back_body, heads), "mixer_back", 6,
+        large + (normed,) + small,
+        [in_hbm] * 12 + [in_vmem] * 8,
+        [
+            jax.ShapeDtypeStruct(layer_in.shape, f32),
+            jax.ShapeDtypeStruct(squares, f32),
+            jax.ShapeDtypeStruct((8, channels), f32),
+            jax.ShapeDtypeStruct((8, part), f32),
+        ]
+        + [slots_of(grad, axis, 0) for grad, axis in zip(grads, mixer_axes)],
+        [in_vmem] * 4 + [in_hbm] * 3,
+        [pltpu.VMEM(v.shape, v.dtype) for v in large]
+        + [
+            pltpu.VMEM((seq_len, channels), f32),
+            pltpu.VMEM(feed.shape, bf16),
+            pltpu.VMEM(feed.shape, bf16),
+            pltpu.VMEM((2, channels, channels), f32),
+            pltpu.VMEM((8, channels), f32),
+            pltpu.VMEM((pick_rows(seq_len) + 8, channels), f32),
+            pltpu.VMEM((pick_rows(seq_len) + 8, channels), f32),
+            pltpu.VMEM((8, channels), f32),
+            pltpu.VMEM((2, seqs, seq_len, 256), bf16),
+        ]
+        + [pltpu.VMEM(grad.shape, bf16) for grad in grads]
+        + [
+            pltpu.VMEM((size,) + squares, f32),
+            pltpu.VMEM((size, 8, channels), f32),
+            pltpu.VMEM((8, width), f32),
+            pltpu.VMEM((8, part), f32),
+            pltpu.VMEM((size, 8, part), f32),
+            pltpu.VMEM((n, 8, part), f32),
+            pltpu.SemaphoreType.DMA((4 + 7 * seqs,)),
+            pltpu.SemaphoreType.DMA((2,)),
+        ]
+        + [pltpu.SemaphoreType.DMA((heads, size))] * 2
+        + [pltpu.SemaphoreType.DMA((size,))] * 4
+        + [pltpu.SemaphoreType.DMA((n,))] * 2
+        + seq_sems(3)
+        + scatter_scratch(seqs, rows, width),
+        100,
+    )
+
+
 def out_only_body(hidden_ref, down_w_ref, residual_ref, layer_out_ref, *scratch):
     greet_line()
     scatter = Scatter(residual_ref.shape[1], *scratch)
@@ -1134,7 +1415,7 @@
         [padded_rows(own_params.reshape(1, -1))[0], padded_rows(own_gains.reshape(1, -1))[0]]
     )
     late_grad, x_full, params, gains, branch_w, rec_w, out_w = gather_first(
-        layer_in, out_grad, pack, (w_branch, w_rec, w_out)
+        layer_in, out_grad, pack, (w_branch.T, w_rec.T, w_out)
     )
 
     gains = gains.reshape(grp_devices, seq_devices, -1)[:, :, : own_gains.size]
@@ -1167,8 +1448,8 @@
         inputs = x_full.astype(f32)
         normal_one = inputs * lax.rsqrt(mean_of(inputs * inputs) + epsilon)
         normed_one = (normal_one * gains[0]).astype(jnp.bfloat16).reshape(-1, model_width)
-        branch_pre = matmul(normed_one, branch_w).reshape(seqs_here, -1, channels)
-        feed = matmul(normed_one, rec_w).astype(jnp.bfloat16).reshape(seqs_here, -1, channels)
+        branch_pre = matmul_nt(normed_one, branch_w).reshape(seqs_here, -1, channels)
+        feed = matmul_nt(normed_one, rec_w).astype(jnp.bfloat16).reshape(seqs_here, -1, channels)
         conv, rate, gate, state, mixed = rec_forward(feed, branch_pre, vectors, softness, diag_a, diag_x)
         residual, normed_two, gate_w, up_w, down_w = mixer_out(
             mixed, out_w, layer_in, gains[1], mlp_weights
@@ -1195,10 +1476,35 @@
         layer_out = out_only(by_seq(hidden), down_w, residual)
         grad_residual, gain_two_grad, residual_low, *mlp_slots = mlp_back(*back_inputs, ())
     else:
-        grad_residual, gain_two_grad, residual_low, *mlp_slots, layer_out = mlp_back(
+        grad_residual, gain_two_grad, residual_low, *mlp_slots, layer_out, late = mlp_back(
             *back_inputs, (by_seq(hidden), down_w)
         )
-    mlp_grads = sum_slots(mlp_grads, mlp_slots)
+        late = lax.psum_scatter(late, "grp", scatter_dimension=0, tiled=True)
+        late = (residual[seqs_here - 1] + late.astype(f32)).astype(jnp.bfloat16)
+        layer_out = jnp.concatenate([layer_out, late[None]])
+    mlp_grads = sum_slots(mlp_grads, mlp_slots, weight_axes)
+    if short_line:
+        grad_x, squares, sums, gain_sum, *mixer_slots = mixer_back(
+            heads_here, residual_low, out_w, branch_pre, feed, conv, rate, gate, state, by_seq(mixed), branch_w, rec_w,
+            by_seq(normed_one), vectors, softness, diag_a, diag_x, layer_in, grad_residual, gains[0], gain_two_grad,
+        )
+        mixer_grads = [sum_all(slot) for slot in mixer_slots]
+        place = lax.axis_index("seq")
+        first = place * part_dim % 8
+        square_parts = [
+            lax.dynamic_slice_in_dim(squares[h], first, part_dim, 1)[:, :, h * head_dim : (h + 1) * head_dim]
+            for h in range(heads_here)
+        ]
+        grad_a, grad_x_gate = (jnp.stack([part[i] for part in square_parts]) for i in range(2))
+        own_sums = lax.dynamic_slice_in_dim(
+            sums.reshape(at, heads_here, head_dim), place * part_dim, part_dim, 2
+        )
+        logit_grad = 8.0 * jax.nn.sigmoid(-decay_logit.astype(f32)) * own_sums[tap_count + 3]
+        rec_outs = (
+            jnp.transpose(own_sums[:tap_count], (1, 0, 2)), own_sums[tap_count], grad_a, own_sums[tap_count + 1],
+            grad_x_gate, own_sums[tap_count + 2], logit_grad,
+        )
+        return finish(layer_out, grad_x, gain_sum, mixer_grads, rec_outs, mlp_grads)
     residual_low = residual_low.reshape(-1, model_width)
     out_weight_grad = matmul_tn(mixed, residual_low)
     grad_mixed = by_seq(matmul_nt(residual_low, out_w))
@@ -1220,8 +1526,8 @@
     rec_blocks = padded_rows(jnp.transpose(rec_grads, (1, 0, 2, 3)))
     mixer_grads = low_all(
         (
-            matmul_tn(normed_one, grad_branch.reshape(-1, channels)),
-            matmul_tn(normed_one, grad_feed.reshape(-1, channels)),
+            matmul_tn(grad_branch.reshape(-1, channels), normed_one),
+            matmul_tn(grad_feed.reshape(-1, channels), normed_one),
             out_weight_grad,
         )
     )
@@ -1229,16 +1535,9 @@
         grad_branch, grad_feed, branch_w, rec_w, layer_in, grad_residual, gains[0], gain_two_grad, rec_blocks,
         mixer_grads,
     )
-    mixer_grads = sum_slots(mixer_grads, mixer_slots)
+    mixer_grads = sum_slots(mixer_grads, mixer_slots, mixer_axes)
     rec_sum = rec_sum.reshape(-1)[: own_params.size].reshape(own_params.shape)
-    own_part = gain_one.shape[0]
-    gain_grads = lax.dynamic_slice_in_dim(gain_sum, lax.axis_index("grp") * own_part, own_part, 1)
-    return (
-        layer_out,
-        grad_x,
-        gain_grads[0],
-        mixer_grads[0],
-        mixer_grads[1],
+    rec_outs = (
         jnp.transpose(rec_sum[:, :, :tap_count], (0, 2, 1)),
         rec_sum[:, :, tap_count],
         rec_sum[:, :, at : at + head_dim],
@@ -1246,11 +1545,16 @@
         rec_sum[:, :, at + head_dim :],
         rec_sum[:, :, tap_count + 2],
         rec_sum[:, :, tap_count + 3],
-        mixer_grads[2],
-        gain_grads[1],
-        mlp_grads[0],
-        mlp_grads[1],
-        mlp_grads[2],
+    )
+    return finish(layer_out, grad_x, gain_sum, mixer_grads, rec_outs, mlp_grads)
+
+
+def finish(layer_out, grad_x, gain_sum, mixer_grads, rec_outs, mlp_grads):
+    part = gain_sum.shape[1] // lax.axis_size("grp")
+    gain_grads = lax.dynamic_slice_in_dim(gain_sum, lax.axis_index("grp") * part, part, 1)
+    return (
+        layer_out, grad_x, gain_grads[0], mixer_grads[0].T, mixer_grads[1].T, *rec_outs, mixer_grads[2], gain_grads[1],
+        *mlp_grads,
     )
 
 

time: 581 us -> 553 us (0.952)
  matrix products: 65.3 us -> 45.9 us
  between operations: 1.36 us -> 14.9 us
  local copies, waits for them, and re-layouts: 32.9 us -> 19.4 us
  Pallas kernels: 454 us -> 444 us
    pallas_call x1 -> x0, Pallas kernels: 20.7 us -> none  [rec_backward(): pl.pallas_call(rec_backward_body, grid=(blocks,), in_specs=[block, block,...]
    dot_general x6 -> x3, matrix products: 36 us -> 19.8 us  [matmul_tn(): lax.dot_general(left, right, (((0,), (0,)), ((), ())), preferred_element_...]
    pallas_call x4, Pallas kernels: 433 us -> 444 us  [call(): pl.pallas_call(body, in_specs=in_specs, out_specs=out_specs, out_shape=ou...]
    unnamed x68 -> x41, local copies, waits for them, and re-layouts: 14.5 us -> 4.69 us
    add x6 -> x3, other arithmetic: 14.8 us -> 8.35 us  [sum_slots(): own = own.astype(jnp.float32) + slot[k].astype(jnp.float32)]
    dot_general x2 -> x1, matrix products: 11.9 us -> 8.73 us  [matmul_nt(): lax.dot_general(left, right, (((1,), (1,)), ((), ())), preferred_element_...]
  transfers between devices with their start and end apart: 0 -> 1, of which waited for: 0 -> 0; matrix products, arithmetic and copies ran while one was open for 0% -> 4% of each run, Pallas kernels for 0% -> 19%
where the time goes in v6:
time: 553 us; the launch traced here: 544 us
  Pallas kernels  444 us (80%)
  matrix products  45.9 us (8%)
  other arithmetic  20 us (4%)
  local copies, waits for them, and re-layouts  19.4 us (4%)
  between operations  14.9 us (3%)
    pallas_call x4, Pallas kernels, call(): pl.pallas_call(body, in_specs=in_specs, out_specs=out_specs, out_shape=ou...  444 us
    dot_general x3, matrix products, matmul_tn(): lax.dot_general(left, right, (((0,), (0,)), ((), ())), preferred_element_...  19.8 us
    dot_general x2, matrix products, matmul(): return jnp.dot(left, right, preferred_element_type=jnp.float32)  17.4 us
  transfers between devices with their start and end apart: 1, of which 0 were waited for; matrix products, arithmetic and copies ran while one was open for 4% of the time, Pallas kernels for 19%

profile of v6, /device:TPU:0, one launch (start us, length us, event | category | flops | bytes accessed | tf_op | source)
XLA Modules:
  0.0 544.1 jit_solution(12187954927422932046)
XLA Ops:
  7.2 0.8 copy.41
  8.0 0.8 copy.42
  8.8 0.8 copy.43
  9.6 0.8 copy.44
  10.4 0.8 copy.45
  11.2 1.4 concatenate.43
  12.8 0.4 pad_reduce_fusion
  13.2 0.8 fusion.16
  13.9 0.7 maximum_convert_fusion.pack_ref
  14.6 65.1 %gather_first.1 = (bf16[2,96,2048]{2,1,0:T(8,128)(2,1)}, bf16[2,768,2048]{2,1,0:T(8,128)(2,1)}, f32[4,256,128]{2,1,0:T(8,128)}, f32[8,4,8,128]{3,2,1,0:T(8,128)}...) custom-call(bf16[2,96,2048]{2,1,0:T(8,128)(2,1)} %x_ref.3, ...), custom_call_target="tpu_custom_call" | custom-call | flops 70000001024 | bytes 210000000 | tf_op jit(solution)/shard_map/gather_first/pallas_call | solution.py:581
  79.7 0.9 reshape.161
  80.8 0.7 slice_reduce_fusion
  81.4 1.4 copy.69
  82.9 0.7 reshape.165
  83.6 0.3 copy.49
  84.0 0.7 reshape.163.gains_ref
  84.7 0.7 squeeze.30.gain_ref
  85.6 0.6 compare_select_fusion.softness_ref
  86.3 0.9 fusion.13
  87.3 149.8 %mixer_forward.1 = (bf16[2,768,2048]{2,1,0:T(8,128)(2,1)}, f32[2,768,352]{2,1,0:T(8,128)}, bf16[2,768,352]{2,1,0:T(8,128)(2,1)}, bf16[2,768,352]{2,1,0:T(8,128)(...) custom-call(bf16[2,768,2048]{2,1,0:T(8,128)(2,1)} %get-tuple-element, ...), custom_call_target="tpu_custom_call" | custom-call | flops 130000003072 | bytes 390000000 | tf_op jit(solution)/shard_map/mixer_forward/pallas_call | solution.py:581
  237.1 8.7 %fusion.25 = f32[1536,768]{1,0:T(8,128)S(1)} fusion(bf16[1536,2048]{1,0:T(8,128)(2,1)} %bitcast.156, bf16[768,2048]{1,0:T(8,128)(2,1)} %get-tuple-element.61.refs_1_), kind=kOutput, calls=%fused_computation.78 | convolution fusion | flops 4831838208 | bytes 14155776 | tf_op jit(solution)/shard_map/dot_general | solution.py:28
  245.9 6.7 %fusion.26 = f32[1536,768]{1,0:T(8,128)} fusion(bf16[1536,2048]{1,0:T(8,128)(2,1)S(1)} %bitcast.152, bf16[2048,768]{1,0:T(8,128)(2,1)S(1)} %copy-done.15), kind=kOutput, calls=%fused_computation.79 | convolution fusion | flops 4831838208 | bytes 14155776 | tf_op jit(solution)/shard_map/dot_general | solution.py:18
  252.6 10.7 %multiply_convert_fusion = (bf16[1536,768]{1,0:T(8,128)(2,1)S(1)}, bf16[1536,768]{1,0:T(8,128)(2,1)S(1)}, bf16[1536,768]{1,0:T(8,128)(2,1)S(1)}) fusion(f32[1536,768]{1,0:T(8,128)} %fusion.26, f32[1536,768]{1,0:T(8,128)S(1)} %fusion.25, bf16[1536,2048]{1,0:T(8,128)(2,1)S(1)} %bitcast.153, bf16[2048,768]{1,0:T(8,128)(2,1)} %get-tuple-element.63.up_w_ref), kind=kOutput, calls=%fused_computation.9 | convolution fusion | flops 4862509056 | bytes 25952256 | tf_op jit(solution)/shard_map/dot_general | solution.py:18
  263.4 6.5 %convolution_convert_fusion.w2 = bf16[768,2048]{1,0:T(8,128)(2,1)} fusion(bf16[1536,768]{1,0:T(8,128)(2,1)S(1)} %get-tuple-element.91, bf16[1536,2048]{1,0:T(8,128)(2,1)S(1)} %bitcast.159), kind=kOutput, calls=%fused_computation.12 | convolution fusion | flops 4833411072 | bytes 11796480 | tf_op jit(solution)/shard_map/dot_general | solution.py:22
  269.9 6.5 %convolution_convert_fusion.2.w0 = bf16[2048,768]{1,0:T(8,128)(2,1)} fusion(bf16[1536,2048]{1,0:T(8,128)(2,1)S(1)} %bitcast.154, bf16[1536,768]{1,0:T(8,128)(2,1)S(1)} %get-tuple-element.92), kind=kOutput, calls=%fused_computation.14 | convolution fusion | flops 4833411072 | bytes 11796480 | tf_op jit(solution)/shard_map/dot_general | solution.py:22
  276.4 6.7 %convolution_convert_fusion.1.w1 = bf16[2048,768]{1,0:T(8,128)(2,1)} fusion(bf16[1536,2048]{1,0:T(8,128)(2,1)S(1)} %bitcast.155, bf16[1536,768]{1,0:T(8,128)(2,1)S(1)} %get-tuple-element.93), kind=kOutput, calls=%fused_computation.13 | convolution fusion | flops 4833411072 | bytes 11796480 | tf_op jit(solution)/shard_map/dot_general | solution.py:22
  283.1 126.1 %mlp_back.1 = (f32[2,96,2048]{2,1,0:T(8,128)}, f32[8,2048]{1,0:T(8,128)}, bf16[2,768,2048]{2,1,0:T(8,128)(2,1)}, bf16[3,512,768]{2,1,0:T(8,128)(2,1)}, bf16[3,51...) custom-call(bf16[2,768,768]{2,1,0:T(8,128)(2,1)} %bitcast.161, ...), custom_call_target="tpu_custom_call" | custom-call | flops 120000004096 | bytes 360000000 | tf_op jit(solution)/shard_map/mlp_back/pallas_call | solution.py:581
  409.2 0.7 copy-done.8
  409.9 0.7 squeeze.32.gain_ref
  410.6 102.9 %mixer_back.1 = (f32[2,96,2048]{2,1,0:T(8,128)}, f32[2,2,48,352]{3,2,1,0:T(8,128)}, f32[8,352]{1,0:T(8,128)}, f32[8,512]{1,0:T(8,128)}, bf16[4,352,512]{2,1,0:T(...) custom-call(bf16[2,768,2048]{2,1,0:T(8,128)(2,1)} %get-tuple-element.68.low_in, ...), custom_call_target="tpu_custom_call" | custom-call | flops 99999997952 | bytes 300000000 | tf_op jit(solution)/shard_map/mixer_back/pallas_call | solution.py:581
  513.5 0.9 reshape.173
  514.5 0.6 copy.72
  515.1 1.0 fusion.22
  516.3 0.7 fusion.21
  517.0 0.7 constant_dynamic-slice_fusion.7
  518.1 0.7 pad_maximum_fusion.2
  518.8 0.7 pad_maximum_fusion.1
  519.5 0.6 fusion.18
  520.2 0.5 slice_bitcast_fusion.4
  520.7 2.5 add_bitcast_fusion.2
  523.2 1.0 add_bitcast_fusion.1
  524.2 1.0 add_bitcast_fusion
  525.3 2.7 convert_add_fusion
  528.0 2.8 convert_add_fusion.3
  530.8 2.8 convert_add_fusion.6
  533.6 1.1 fusion.12
  534.7 0.9 pad_maximum_fusion
  535.7 1.1 copy.74
  (58 shorter events, 1.5 us)
Async XLA Ops:
  7.2 526.4 %reduce-scatter.2.cloned.1.call-start = ((), (), s32[]{:S(2)}) async-start(), calls=%async_computation.1 | async-start | bytes 3538944 | tf_op jit(solution)/shard_map/reduce_scatter | solution.py:1482
  85.6 1.7 copy-start.9
  237.1 8.8 %copy-start.11 = (bf16[2,768,2048]{2,1,0:T(8,128)(2,1)S(1)}, bf16[2,768,2048]{2,1,0:T(8,128)(2,1)}, u32[]{:S(2)}) copy-start(bf16[2,768,2048]{2,1,0:T(8,128)(2,1)} %get-tuple-element.62) | copy-start | bytes 18874372
  237.1 8.8 %copy-start.15 = (bf16[2048,768]{1,0:T(8,128)(2,1)S(1)}, bf16[2048,768]{1,0:T(8,128)(2,1)}, u32[]{:S(2)}) copy-start(bf16[2048,768]{1,0:T(8,128)(2,1)} %get-tuple-element.64.gate_w_ref) | copy-start | bytes 9437188
  245.9 17.5 %slice-start = ((s8[6291456]{0:T(1024)(128)(4,1)}), s8[4194304]{0:T(1024)(128)(4,1)S(1)}, s32[]{:S(2)}) async-start(s8[6291456]{0:T(1024)(128)(4,1)} %bitcast.157), calls=%async_computation.2 | async-start | bytes 8388608
  252.6 10.8 %slice-start.1 = ((s8[6291456]{0:T(1024)(128)(4,1)}), s8[2097152]{0:T(1024)(128)(4,1)S(1)}, s32[]{:S(2)}) async-start(s8[6291456]{0:T(1024)(128)(4,1)} %bitcast.157), calls=%async_computation.3 | async-start | bytes 4194304
  263.3 6.6 %copy-start.12 = (bf16[1536,768]{1,0:T(8,128)(2,1)}, bf16[1536,768]{1,0:T(8,128)(2,1)S(1)}, u32[]{:S(2)}) copy-start(bf16[1536,768]{1,0:T(8,128)(2,1)S(1)} %get-tuple-element.91) | copy-start | bytes 7077892
  263.3 6.6 %copy-start.13 = (bf16[1536,768]{1,0:T(8,128)(2,1)}, bf16[1536,768]{1,0:T(8,128)(2,1)S(1)}, u32[]{:S(2)}) copy-start(bf16[1536,768]{1,0:T(8,128)(2,1)S(1)} %get-tuple-element.92) | copy-start | bytes 7077892
  263.3 13.1 %copy-start.14 = (bf16[1536,768]{1,0:T(8,128)(2,1)}, bf16[1536,768]{1,0:T(8,128)(2,1)S(1)}, u32[]{:S(2)}) copy-start(bf16[1536,768]{1,0:T(8,128)(2,1)S(1)} %get-tuple-element.93) | copy-start | bytes 7077892
  409.2 0.7 copy-start.8
  410.6 108.9 %copy-start.10 = (bf16[2,44]{1,0:T(2,128)(2,1)S(1)}, bf16[2,44]{1,0:T(2,128)(2,1)}, u32[]{:S(2)}) copy-start(bf16[2,44]{1,0:T(2,128)(2,1)} %param.27) | copy-start | bytes 532
  513.5 9.7 %copy-start.5 = (bf16[4,352,512]{2,1,0:T(8,128)(2,1)S(1)}, bf16[4,352,512]{2,1,0:T(8,128)(2,1)}, u32[]{:S(2)}) copy-start(bf16[4,352,512]{2,1,0:T(8,128)(2,1)} %get-tuple-element.82) | copy-start | bytes 4325380
  516.1 8.1 %copy-start.4 = (bf16[4,352,512]{2,1,0:T(8,128)(2,1)S(1)}, bf16[4,352,512]{2,1,0:T(8,128)(2,1)}, u32[]{:S(2)}) copy-start(bf16[4,352,512]{2,1,0:T(8,128)(2,1)} %get-tuple-element.85) | copy-start | bytes 4325380
  520.7 4.6 copy-start.2
  524.2 3.7 copy-start.1
  528.0 2.8 copy-start
  530.8 2.9 copy-start.6
  530.8 3.9 copy-start.7
  530.8 4.9 copy-start.3
Sparse Core Ops, SparseCore 0:
  409.4 48.4 reduce-scatter.1

commit v7 on v6

--- a/solution.py
+++ b/solution.py
@@ -690,6 +690,10 @@
 
 weight_axes = (0, 0, 1)
 mixer_axes = (1, 1, 1)
+
+
+def copies(pairs, sem):
+    return [pltpu.make_async_copy(source, buffer, sem.at[i]) for i, (source, buffer) in enumerate(pairs)]
 
 
 def views(ref):
@@ -837,11 +841,27 @@
 
 
 def mixer_forward_body(
-    x_full_ref, gains_ref, branch_w_ref, rec_w_ref, out_w_ref, vectors_ref, softness_ref, gate_a_ref, gate_x_ref,
+    x_full_in, branch_w_in, rec_w_in, out_w_in, gains_ref, vectors_ref, softness_ref, gate_a_ref, gate_x_ref,
     grad_ref, w0, w1, w2,
-    normed_one_ref, branch_ref, feed_ref, conv_ref, rate_ref, input_ref, state_ref, mixed_ref, residual_ref,
-    normed_ref, grads_ref, o0, o1, o2, low_ref, window, carry, *refs,
+    residual_ref, normed_one_out, branch_out, feed_out, conv_out, rate_out, input_out, state_out, mixed_out,
+    normed_ref, grads_ref, o0, o1, o2,
+    x_full_ref, branch_w_ref, rec_w_ref, out_w_ref, normed_one_ref, branch_ref, feed_ref, conv_ref, rate_ref, input_ref,
+    state_ref, mixed_ref, load_sem, store_sem, low_ref, window, carry, *refs,
 ):
+    pairs = [(branch_w_in, branch_w_ref), (rec_w_in, rec_w_ref), (out_w_in, out_w_ref)]
+    pairs[:0] = [(x_full_in.at[0], x_full_ref.at[0])]
+    pairs += [(x_full_in.at[s], x_full_ref.at[s]) for s in range(1, x_full_ref.shape[0])]
+    loads = copies(pairs, load_sem)
+    for load in loads:
+        load.start()
+    kept = (
+        (normed_one_ref, normed_one_out), (branch_ref, branch_out), (feed_ref, feed_out), (conv_ref, conv_out),
+        (rate_ref, rate_out), (input_ref, input_out), (state_ref, state_out), (mixed_ref, mixed_out),
+    )
+    keeps = [
+        copies([(buffer.at[s], out.at[s]) for buffer, out in kept], store_sem.at[s])
+        for s in range(x_full_ref.shape[0])
+    ]
     greet_axes(("seq", "grp"))
     seqs, seq_len, _ = x_full_ref.shape
     rows = grad_ref.shape[1]
@@ -858,6 +878,9 @@
     window[...] = jnp.zeros_like(window)
 
     def project(s):
+        for load in loads[:3] if s == 0 else loads[3 + s : 4 + s]:
+            load.wait()
+
         @pl.loop(0, seq_len // tile)
         def _(i):
             at = pl.ds(pl.multiple_of(i * tile, tile), tile)
@@ -891,25 +914,26 @@
 
     def steps(s):
         partners, own = scatter.fill(s, s, [mixed_ref], [out_w_ref], False)
-        late = [functools.partial(late_hop, h) for h in range(gather.chips - 1)]
+
+        def first():
+            if s == 1:
+                late_hop(0)
+            project(s)
 
         def second():
+            recur(s)
+            for keep in keeps[s]:
+                keep.start()
+            if s == 1:
+                late_hop(1)
             if s == 0:
-                late_hop(0)
-            recur(s)
-
-        def third():
-            partners()
-            if s == 0:
-                late_hop(1)
-
-        def fourth():
-            own()
-            if s == seqs - 1:
-                for hop in late[2 if seqs > 1 else 1 :]:
-                    hop()
-
-        return [functools.partial(project, s), second, third, fourth]
+                loads[3].wait()
+
+        return [first, second, partners, own]
+
+    def last_late_hops():
+        for h in range(2 if seqs > 1 else 0, gather.chips - 1):
+            late_hop(h)
 
     def store(s):
         own = x_full_ref[s, pl.ds(pl.multiple_of(me * rows, rows), rows), :]
@@ -919,10 +943,13 @@
         low_ref[s] = (normal * gains_ref[1]).astype(jnp.bfloat16)
 
     sum_then_gather(
-        scatter, gather, [steps(s) for s in range(seqs)], [functools.partial(store, s) for s in range(seqs)], seqs
+        scatter, gather, [steps(s) for s in range(seqs)], [functools.partial(store, s) for s in range(seqs)], seqs,
+        after=(last_late_hops,),
     )
     for s in range(seqs):
         gather.finish(seqs + s)
+        for keep in keeps[s]:
+            keep.wait()
     for weight in weights:
         weight.finish()
 
@@ -932,16 +959,19 @@
     rows, channels = out_grad.shape[1], vectors.shape[1]
     low = jax.ShapeDtypeStruct((seqs, seq_len, channels), jnp.bfloat16)
     full = jax.ShapeDtypeStruct((seqs, seq_len, channels), jnp.float32)
-    outs = [x_full, full, low, low, full, full, full, low]
-    outs += [jax.ShapeDtypeStruct(out_grad.shape, jnp.float32), x_full, x_full]
-    outs = [jax.ShapeDtypeStruct(out.shape, out.dtype) for out in outs]
+    kept = [x_full, full, low, low, full, full, full, low]
+    kept = [jax.ShapeDtypeStruct(out.shape, out.dtype) for out in kept]
+    outs = [jax.ShapeDtypeStruct(out_grad.shape, jnp.float32)] + kept + [kept[0]] * 2
     outs += [gathered(w, axis) for w, axis in zip(weights, weight_axes)]
     return call(
         mixer_forward_body, "mixer_forward", 2,
-        (x_full, gains, branch_w, rec_w, out_w, vectors, softness, gate_a, gate_x, out_grad, *weights),
-        [in_vmem] * 13,
-        outs, [in_vmem] * 9 + [in_hbm] * 5,
-        [
+        (x_full, branch_w, rec_w, out_w, gains, vectors, softness, gate_a, gate_x, out_grad, *weights),
+        [in_hbm] * 4 + [in_vmem] * 9,
+        outs, [in_vmem] + [in_hbm] * 13,
+        [pltpu.VMEM(v.shape, v.dtype) for v in [x_full, branch_w, rec_w, out_w] + kept]
+        + [
+            pltpu.SemaphoreType.DMA((3 + seqs,)),
+            pltpu.SemaphoreType.DMA((seqs, len(kept))),
             pltpu.VMEM(out_grad.shape, jnp.bfloat16),
             pltpu.VMEM((pick_rows(seq_len) + 8, channels), jnp.float32),
             pltpu.VMEM((8, channels), jnp.float32),
@@ -954,17 +984,24 @@
 
 
 def mlp_back_body(
-    with_out, gate_ref, up_ref, gate_w_ref, up_w_ref, residual_ref, grad_ref, gain_ref, w0, w1, w2, *refs
+    with_out, gate_in, up_in, gate_w_in, up_w_in, residual_ref, grad_ref, gain_ref, w0, w1, w2, *refs
 ):
     if with_out:
-        hidden_ref, down_w_ref = refs[:2]
+        hidden_in, down_w_in = refs[:2]
         refs = refs[2:]
     grad_residual_ref, gain_grad_ref, full_ref, o0, o1, o2 = refs[:6]
     refs = refs[6:]
     if with_out:
         layer_out_ref, late_ref = refs[:2]
         refs = refs[2:]
-    low_ref, *refs = refs
+    low_ref, load_sem, gate_ref, up_ref, gate_w_ref, up_w_ref, *refs = refs
+    pairs = [(gate_in, gate_ref), (up_in, up_ref), (gate_w_in, gate_w_ref), (up_w_in, up_w_ref)]
+    if with_out:
+        hidden_ref, down_w_ref, *refs = refs
+        pairs += [(hidden_in, hidden_ref), (down_w_in, down_w_ref)]
+    loads = copies(pairs, load_sem)
+    for load in loads:
+        load.start()
     greet_axes(("seq", "grp"))
     seqs, rows, _ = grad_ref.shape
     sums = weight_sums(weight_axes, (w0, w1, w2), (o0, o1, o2), *refs[:2])
@@ -987,11 +1024,21 @@
         grad_residual_ref[s] = grad
         low_ref[s] = grad.astype(jnp.bfloat16)
 
+    def wait_first():
+        for load in loads[:4]:
+            load.wait()
+
+    def wait_later():
+        for load in loads[4:]:
+            load.wait()
+
     fills = [fill(s) for s in range(seqs)]
+    fills[0] = (wait_first, *fills[0])
     stores = [functools.partial(store, s) for s in range(seqs)]
     if with_out:
         fill_out, store_out = out_body(hidden_ref, down_w_ref, residual_ref, layer_out_ref, scatter, seqs)
         fills += [fill_out(s) for s in range(seqs - 1)]
+        fills[seqs - 1] = (*fills[seqs - 1], wait_later)
         stores += [functools.partial(store_out, s) for s in range(seqs - 1)]
 
     def late():
@@ -1023,9 +1070,10 @@
     return call(
         functools.partial(mlp_back_body, bool(out_inputs)), "mlp_back", 3,
         (grad_gate, grad_up, gate_w, up_w, residual, out_grad, gain, *grads, *out_inputs),
-        [in_vmem] * 7 + [in_hbm] * 3 + [in_vmem] * len(out_inputs),
+        [in_hbm] * 4 + [in_vmem] * 3 + [in_hbm] * (3 + len(out_inputs)),
         outs, out_specs,
-        [pltpu.VMEM(residual.shape, jnp.bfloat16)]
+        [pltpu.VMEM(residual.shape, jnp.bfloat16), pltpu.SemaphoreType.DMA((6,))]
+        + [pltpu.VMEM(v.shape, v.dtype) for v in (grad_gate, grad_up, gate_w, up_w, *out_inputs)]
         + seq_sems(3)
         + gather_sems(seqs)
         + scatter_scratch(seqs * 2 - 1 if out_inputs else seqs, rows, width),
@@ -1113,10 +1161,6 @@
         + scatter_scratch(seqs, rows, width),
         80,
     )
-
-
-def copies(pairs, sem):
-    return [pltpu.make_async_copy(source, buffer, sem.at[i]) for i, (source, buffer) in enumerate(pairs)]
 
 
 def head_windows(heads, head_dim, parts):
@@ -1434,7 +1478,7 @@
     mlp_weights = (mlp_gate, mlp_up, mlp_down)
     if short_line:
         (
-            normed_one, branch_pre, feed, conv, rate, gate, state, mixed, residual, normed_two, grad_output,
+            residual, normed_one, branch_pre, feed, conv, rate, gate, state, mixed, normed_two, grad_output,
             gate_w, up_w, down_w,
         ) = mixer_forward(
             x_full, gains, branch_w, rec_w, out_w, vectors, softness, diag_a, diag_x, late_grad, mlp_weights

time: 553 us -> 535 us (0.967)
  Pallas kernels: 444 us -> 425 us
    pallas_call x4, Pallas kernels: 444 us -> 425 us  [call(): pl.pallas_call(body, in_specs=in_specs, out_specs=out_specs, out_shape=ou...]
  transfers between devices with their start and end apart: 1 -> 1, of which waited for: 0 -> 0; matrix products, arithmetic and copies ran while one was open for 4% -> 4% of each run, Pallas kernels for 19% -> 20%
where the time goes in v7:
time: 535 us; the launch traced here: 525 us
  Pallas kernels  425 us (79%)
  matrix products  45.9 us (9%)
  other arithmetic  20 us (4%)
  local copies, waits for them, and re-layouts  19.4 us (4%)
  between operations  14.9 us (3%)
    pallas_call x4, Pallas kernels, call(): pl.pallas_call(body, in_specs=in_specs, out_specs=out_specs, out_shape=ou...  425 us
    dot_general x3, matrix products, matmul_tn(): lax.dot_general(left, right, (((0,), (0,)), ((), ())), preferred_element_...  19.8 us
    dot_general x2, matrix products, matmul(): return jnp.dot(left, right, preferred_element_type=jnp.float32)  17.4 us
  transfers between devices with their start and end apart: 1, of which 0 were waited for; matrix products, arithmetic and copies ran while one was open for 4% of the time, Pallas kernels for 20%

profile of v7, /device:TPU:0, one launch (start us, length us, event | category | flops | bytes accessed | tf_op | source)
XLA Modules:
  0.0 525.3 jit_solution(16653337155092066199)
XLA Ops:
  7.2 0.8 copy.41
  8.0 0.8 copy.42
  8.8 0.8 copy.43
  9.6 0.8 copy.44
  10.4 0.8 copy.45
  11.2 1.4 concatenate.43
  12.8 0.4 pad_reduce_fusion
  13.2 0.8 fusion.16
  13.9 0.7 maximum_convert_fusion.pack_ref
  14.6 65.1 %gather_first.1 = (bf16[2,96,2048]{2,1,0:T(8,128)(2,1)}, bf16[2,768,2048]{2,1,0:T(8,128)(2,1)}, f32[4,256,128]{2,1,0:T(8,128)}, f32[8,4,8,128]{3,2,1,0:T(8,128)}...) custom-call(bf16[2,96,2048]{2,1,0:T(8,128)(2,1)} %x_ref.3, ...), custom_call_target="tpu_custom_call" | custom-call | flops 70000001024 | bytes 210000000 | tf_op jit(solution)/shard_map/gather_first/pallas_call | solution.py:581
  79.7 0.9 reshape.161
  80.8 0.7 slice_reduce_fusion
  81.4 1.4 copy.69
  82.9 0.7 reshape.165
  83.6 0.3 copy.49
  84.0 0.7 reshape.163.gains_ref
  84.7 0.7 squeeze.30.gain_ref
  85.6 0.6 compare_select_fusion.softness_ref
  86.3 0.9 fusion.13
  87.3 132.0 %mixer_forward.1 = (f32[2,96,2048]{2,1,0:T(8,128)}, bf16[2,768,2048]{2,1,0:T(8,128)(2,1)}, f32[2,768,352]{2,1,0:T(8,128)}, bf16[2,768,352]{2,1,0:T(8,128)(2,1)},...) custom-call(bf16[2,768,2048]{2,1,0:T(8,128)(2,1)} %get-tuple-element, ...), custom_call_target="tpu_custom_call" | custom-call | flops 130000003072 | bytes 390000000 | tf_op jit(solution)/shard_map/mixer_forward/pallas_call | solution.py:581
  219.3 8.7 %fusion.25 = f32[1536,768]{1,0:T(8,128)S(1)} fusion(bf16[1536,2048]{1,0:T(8,128)(2,1)} %bitcast.156, bf16[768,2048]{1,0:T(8,128)(2,1)} %get-tuple-element.61.refs_1_), kind=kOutput, calls=%fused_computation.78 | convolution fusion | flops 4831838208 | bytes 14155776 | tf_op jit(solution)/shard_map/dot_general | solution.py:28
  228.1 6.7 %fusion.26 = f32[1536,768]{1,0:T(8,128)} fusion(bf16[1536,2048]{1,0:T(8,128)(2,1)S(1)} %bitcast.152, bf16[2048,768]{1,0:T(8,128)(2,1)S(1)} %copy-done.15), kind=kOutput, calls=%fused_computation.79 | convolution fusion | flops 4831838208 | bytes 14155776 | tf_op jit(solution)/shard_map/dot_general | solution.py:18
  234.8 10.7 %multiply_convert_fusion = (bf16[1536,768]{1,0:T(8,128)(2,1)S(1)}, bf16[1536,768]{1,0:T(8,128)(2,1)S(1)}, bf16[1536,768]{1,0:T(8,128)(2,1)S(1)}) fusion(f32[1536,768]{1,0:T(8,128)} %fusion.26, f32[1536,768]{1,0:T(8,128)S(1)} %fusion.25, bf16[1536,2048]{1,0:T(8,128)(2,1)S(1)} %bitcast.153, bf16[2048,768]{1,0:T(8,128)(2,1)} %get-tuple-element.63.up_w_in), kind=kOutput, calls=%fused_computation.9 | convolution fusion | flops 4862509056 | bytes 25952256 | tf_op jit(solution)/shard_map/dot_general | solution.py:18
  245.6 6.5 %convolution_convert_fusion.w2 = bf16[768,2048]{1,0:T(8,128)(2,1)} fusion(bf16[1536,768]{1,0:T(8,128)(2,1)S(1)} %get-tuple-element.91, bf16[1536,2048]{1,0:T(8,128)(2,1)S(1)} %bitcast.159), kind=kOutput, calls=%fused_computation.12 | convolution fusion | flops 4833411072 | bytes 11796480 | tf_op jit(solution)/shard_map/dot_general | solution.py:22
  252.1 6.5 %convolution_convert_fusion.2.w0 = bf16[2048,768]{1,0:T(8,128)(2,1)} fusion(bf16[1536,2048]{1,0:T(8,128)(2,1)S(1)} %bitcast.154, bf16[1536,768]{1,0:T(8,128)(2,1)S(1)} %get-tuple-element.92), kind=kOutput, calls=%fused_computation.14 | convolution fusion | flops 4833411072 | bytes 11796480 | tf_op jit(solution)/shard_map/dot_general | solution.py:22
  258.6 6.7 %convolution_convert_fusion.1.w1 = bf16[2048,768]{1,0:T(8,128)(2,1)} fusion(bf16[1536,2048]{1,0:T(8,128)(2,1)S(1)} %bitcast.155, bf16[1536,768]{1,0:T(8,128)(2,1)S(1)} %get-tuple-element.93), kind=kOutput, calls=%fused_computation.13 | convolution fusion | flops 4833411072 | bytes 11796480 | tf_op jit(solution)/shard_map/dot_general | solution.py:22
  265.3 123.7 %mlp_back.1 = (f32[2,96,2048]{2,1,0:T(8,128)}, f32[8,2048]{1,0:T(8,128)}, bf16[2,768,2048]{2,1,0:T(8,128)(2,1)}, bf16[3,512,768]{2,1,0:T(8,128)(2,1)}, bf16[3,51...) custom-call(bf16[2,768,768]{2,1,0:T(8,128)(2,1)} %bitcast.161, ...), custom_call_target="tpu_custom_call" | custom-call | flops 120000004096 | bytes 360000000 | tf_op jit(solution)/shard_map/mlp_back/pallas_call | solution.py:581
  389.1 0.7 copy-done.8
  389.7 0.7 squeeze.32.gain_ref
  390.4 104.3 %mixer_back.1 = (f32[2,96,2048]{2,1,0:T(8,128)}, f32[2,2,48,352]{3,2,1,0:T(8,128)}, f32[8,352]{1,0:T(8,128)}, f32[8,512]{1,0:T(8,128)}, bf16[4,352,512]{2,1,0:T(...) custom-call(bf16[2,768,2048]{2,1,0:T(8,128)(2,1)} %get-tuple-element.68.low_in, ...), custom_call_target="tpu_custom_call" | custom-call | flops 99999997952 | bytes 300000000 | tf_op jit(solution)/shard_map/mixer_back/pallas_call | solution.py:581
  494.7 0.9 reshape.173
  495.7 0.6 copy.72
  496.3 1.0 fusion.22
  497.5 0.7 fusion.21
  498.2 0.7 constant_dynamic-slice_fusion.7
  499.3 0.7 pad_maximum_fusion.2
  500.0 0.7 pad_maximum_fusion.1
  500.7 0.6 fusion.18
  501.4 0.5 slice_bitcast_fusion.4
  501.9 2.5 add_bitcast_fusion.2
  504.4 1.0 add_bitcast_fusion.1
  505.4 1.0 add_bitcast_fusion
  506.5 2.7 convert_add_fusion
  509.2 2.8 convert_add_fusion.3
  512.0 2.8 convert_add_fusion.6
  514.8 1.1 fusion.12
  515.9 0.9 pad_maximum_fusion
  516.9 1.1 copy.74
  (58 shorter events, 1.5 us)
Async XLA Ops:
  7.2 507.7 %reduce-scatter.2.cloned.1.call-start = ((), (), s32[]{:S(2)}) async-start(), calls=%async_computation.1 | async-start | bytes 3538944 | tf_op jit(solution)/shard_map/reduce_scatter | solution.py:1526
  85.6 1.7 copy-start.9
  219.3 8.8 %copy-start.11 = (bf16[2,768,2048]{2,1,0:T(8,128)(2,1)S(1)}, bf16[2,768,2048]{2,1,0:T(8,128)(2,1)}, u32[]{:S(2)}) copy-start(bf16[2,768,2048]{2,1,0:T(8,128)(2,1)} %get-tuple-element.62) | copy-start | bytes 18874372
  219.3 8.8 %copy-start.15 = (bf16[2048,768]{1,0:T(8,128)(2,1)S(1)}, bf16[2048,768]{1,0:T(8,128)(2,1)}, u32[]{:S(2)}) copy-start(bf16[2048,768]{1,0:T(8,128)(2,1)} %get-tuple-element.64.gate_w_in) | copy-start | bytes 9437188
  228.0 17.5 %slice-start = ((s8[6291456]{0:T(1024)(128)(4,1)}), s8[4194304]{0:T(1024)(128)(4,1)S(1)}, s32[]{:S(2)}) async-start(s8[6291456]{0:T(1024)(128)(4,1)} %bitcast.157), calls=%async_computation.2 | async-start | bytes 8388608
  234.8 10.8 %slice-start.1 = ((s8[6291456]{0:T(1024)(128)(4,1)}), s8[2097152]{0:T(1024)(128)(4,1)S(1)}, s32[]{:S(2)}) async-start(s8[6291456]{0:T(1024)(128)(4,1)} %bitcast.157), calls=%async_computation.3 | async-start | bytes 4194304
  245.5 6.6 %copy-start.12 = (bf16[1536,768]{1,0:T(8,128)(2,1)}, bf16[1536,768]{1,0:T(8,128)(2,1)S(1)}, u32[]{:S(2)}) copy-start(bf16[1536,768]{1,0:T(8,128)(2,1)S(1)} %get-tuple-element.91) | copy-start | bytes 7077892
  245.5 6.6 %copy-start.13 = (bf16[1536,768]{1,0:T(8,128)(2,1)}, bf16[1536,768]{1,0:T(8,128)(2,1)S(1)}, u32[]{:S(2)}) copy-start(bf16[1536,768]{1,0:T(8,128)(2,1)S(1)} %get-tuple-element.92) | copy-start | bytes 7077892
  245.5 13.1 %copy-start.14 = (bf16[1536,768]{1,0:T(8,128)(2,1)}, bf16[1536,768]{1,0:T(8,128)(2,1)S(1)}, u32[]{:S(2)}) copy-start(bf16[1536,768]{1,0:T(8,128)(2,1)S(1)} %get-tuple-element.93) | copy-start | bytes 7077892
  389.0 0.7 copy-start.8
  390.4 110.3 %copy-start.10 = (bf16[2,44]{1,0:T(2,128)(2,1)S(1)}, bf16[2,44]{1,0:T(2,128)(2,1)}, u32[]{:S(2)}) copy-start(bf16[2,44]{1,0:T(2,128)(2,1)} %param.27) | copy-start | bytes 532
  494.7 9.7 %copy-start.5 = (bf16[4,352,512]{2,1,0:T(8,128)(2,1)S(1)}, bf16[4,352,512]{2,1,0:T(8,128)(2,1)}, u32[]{:S(2)}) copy-start(bf16[4,352,512]{2,1,0:T(8,128)(2,1)} %get-tuple-element.82) | copy-start | bytes 4325380
  497.3 8.1 %copy-start.4 = (bf16[4,352,512]{2,1,0:T(8,128)(2,1)S(1)}, bf16[4,352,512]{2,1,0:T(8,128)(2,1)}, u32[]{:S(2)}) copy-start(bf16[4,352,512]{2,1,0:T(8,128)(2,1)} %get-tuple-element.85) | copy-start | bytes 4325380
  501.9 4.6 copy-start.2
  505.4 3.7 copy-start.1
  509.2 2.8 copy-start
  512.0 2.9 copy-start.6
  512.0 3.9 copy-start.7
  512.0 4.9 copy-start.3
Sparse Core Ops, SparseCore 0:
  389.2 51.4 reduce-scatter.1

commit v8 on v7

--- a/solution.py
+++ b/solution.py
@@ -408,11 +408,17 @@
 
             self.to_partner(p, here, right_origin).start()
 
-    def finish(self, p):
+    def arrive(self, p):
         for c in range(self.chips):
             origin = c * 2 + 1 - self.core
             self.to_partner(p, self.slot(p, origin), origin).wait_recv()
         self.own(p).wait()
+
+    def finish(self, p):
+        self.arrive(p)
+        self.sent(p)
+
+    def sent(self, p):
         for c in range(self.chips):
             origin = c * 2 + self.core
             here = self.slot(p, origin)
@@ -841,47 +847,90 @@
 
 
 def mixer_forward_body(
-    x_full_in, branch_w_in, rec_w_in, out_w_in, gains_ref, vectors_ref, softness_ref, gate_a_ref, gate_x_ref,
-    grad_ref, w0, w1, w2,
-    residual_ref, normed_one_out, branch_out, feed_out, conv_out, rate_out, input_out, state_out, mixed_out,
+    x_ref, grad_ref, gain_pack_ref, vector_pack_ref, gate_pack_ref, v0, v1, v2, w0, w1, w2,
+    residual_ref, gains_ref, vectors_ref, gate_a_ref, gate_x_ref,
+    normed_one_out, branch_out, feed_out, conv_out, rate_out, input_out, state_out, mixed_out, u0, u1, u2,
     normed_ref, grads_ref, o0, o1, o2,
-    x_full_ref, branch_w_ref, rec_w_ref, out_w_ref, normed_one_ref, branch_ref, feed_ref, conv_ref, rate_ref, input_ref,
-    state_ref, mixed_ref, load_sem, store_sem, low_ref, window, carry, *refs,
+    normed_one_ref, branch_ref, feed_ref, conv_ref, rate_ref, input_ref, state_ref, mixed_ref,
+    branch_w_ref, rec_w_ref, out_w_ref, x_full_ref, low_ref, window, carry, gates, gain_slots, vector_slots, gate_slots,
+    store_sem, weight_store_sem, gain_send, gain_recv, small_send, small_recv,
+    mixer_send, mixer_recv, weight_send, weight_recv, *refs,
 ):
-    pairs = [(branch_w_in, branch_w_ref), (rec_w_in, rec_w_ref), (out_w_in, out_w_ref)]
-    pairs[:0] = [(x_full_in.at[0], x_full_ref.at[0])]
-    pairs += [(x_full_in.at[s], x_full_ref.at[s]) for s in range(1, x_full_ref.shape[0])]
-    loads = copies(pairs, load_sem)
-    for load in loads:
-        load.start()
+    seqs, rows, width = x_ref.shape
+    seq_len = x_full_ref.shape[1]
+    me = lax.axis_index("grp")
     kept = (
         (normed_one_ref, normed_one_out), (branch_ref, branch_out), (feed_ref, feed_out), (conv_ref, conv_out),
         (rate_ref, rate_out), (input_ref, input_out), (state_ref, state_out), (mixed_ref, mixed_out),
     )
     keeps = [
-        copies([(buffer.at[s], out.at[s]) for buffer, out in kept], store_sem.at[s])
-        for s in range(x_full_ref.shape[0])
+        copies([(buffer.at[s], out.at[s]) for buffer, out in kept], store_sem.at[s]) for s in range(seqs)
     ]
+    weight_keeps = copies([(branch_w_ref, u0), (rec_w_ref, u1), (out_w_ref, u2)], weight_store_sem)
     greet_axes(("seq", "grp"))
-    seqs, seq_len, _ = x_full_ref.shape
-    rows = grad_ref.shape[1]
-    me = lax.axis_index("grp")
-    weights = weight_gathers(weight_axes, (w0, w1, w2), (o0, o1, o2), *refs[:2])
-    gather = Gather(views(low_ref) + views(grad_ref), views(normed_ref) + views(grads_ref), rows, *refs[2:5])
-    scatter = Scatter(rows, *refs[5:])
-    for s in range(seqs):
-        gather.start(seqs + s)
-    for weight in weights:
+    mixer_weights = weight_gathers(
+        mixer_axes, (v0, v1, v2), (branch_w_ref, rec_w_ref, out_w_ref), mixer_send, mixer_recv
+    )
+    weights = weight_gathers(weight_axes, (w0, w1, w2), (o0, o1, o2), weight_send, weight_recv)
+    gather = Gather(
+        views(low_ref) + views(grad_ref) + views(x_ref),
+        views(normed_ref) + views(grads_ref) + views(x_full_ref),
+        rows, *refs[:3],
+    )
+    scatter = Scatter(rows, *refs[3:])
+    place = lax.axis_index("grp")
+    small = [
+        Exchange("seq", lambda k, ref=pack: ref, lambda k, ref=slots: ref.at[k], small_send.at[i], small_recv.at[i])
+        for i, (pack, slots) in enumerate(
+            ((gain_pack_ref, gain_slots.at[place]), (vector_pack_ref, vector_slots), (gate_pack_ref, gate_slots))
+        )
+    ]
+    along = Exchange("grp", lambda k: gain_slots.at[place], lambda k: gain_slots.at[k], gain_send, gain_recv)
+    first_x = 2 * seqs
+    small[0].start()
+    gather.start(first_x)
+    for move in small[1:]:
+        move.start()
+    for weight in mixer_weights[:2]:
         weight.start()
-    tile = pick_rows(seq_len, (256, 192, 128, 96, 64, 32, 16))
+    small[0].finish()
+    along.start_others()
+    last_hop = gather.chips - 2
+    for h in range(gather.chips - 1):
+        gather.hop(first_x, h)
+        if h == max(last_hop - 1, 0):
+            for s in range(1, seqs):
+                gather.start(first_x + s)
+    gates[...] = jnp.zeros_like(gates)
+    window[...] = jnp.zeros_like(window)
+    along.finish_others()
+    parts = lax.axis_size("seq")
+    gain_part = width // (parts * along.size)
+    for k in range(parts):
+        for g in range(along.size):
+            at = (k * along.size + g) * gain_part
+            for i in range(2):
+                gains_ref[i, :, at : at + gain_part] = gain_slots[g, k, 0:1, i * gain_part : (i + 1) * gain_part]
+    for move in small[1:]:
+        move.finish()
+    heads = gate_pack_ref.shape[0] // 2
+    part, head_dim = gate_pack_ref.shape[1:]
+    for k in range(parts):
+        for h in range(heads):
+            at = h * head_dim + k * part
+            vectors_ref[:, at : at + part] = vector_slots[k, :, h * part : (h + 1) * part]
+            for i in range(2):
+                gates[i, at : at + part, h * head_dim : (h + 1) * head_dim] = gate_slots[k, i * heads + h]
+    gate_a_ref[...] = gates[0].astype(jnp.bfloat16)
+    gate_x_ref[...] = gates[1].astype(jnp.bfloat16)
+    softness_ref = vectors_ref.at[pl.ds(7, 1), :]
+    tile = pick_rows(seq_len // 2, (192, 128, 96, 64, 32, 16))
     chunk = window.shape[0] - 8
-    window[...] = jnp.zeros_like(window)
-
-    def project(s):
-        for load in loads[:3] if s == 0 else loads[3 + s : 4 + s]:
-            load.wait()
-
-        @pl.loop(0, seq_len // tile)
+
+    def project(s, half):
+        count = seq_len // tile // 2
+
+        @pl.loop(half * count, (half + 1) * count)
         def _(i):
             at = pl.ds(pl.multiple_of(i * tile, tile), tile)
             inputs = x_full_ref[s, at, :].astype(jnp.float32)
@@ -907,36 +956,56 @@
             state_ref[s, at, :] = state
             mixed_ref[s, at, :] = mixed
 
-    def late_hop(h):
-        if h < gather.chips - 1:
+        for keep in keeps[s]:
+            keep.start()
+
+    def late_hops(first, end):
+        for h in range(first, min(end, gather.chips - 1)):
             for s in range(seqs):
                 gather.hop(seqs + s, h)
 
+    def next_x(h):
+        for s in range(1, seqs):
+            if h <= last_hop:
+                gather.hop(first_x + s, h)
+
     def steps(s):
         partners, own = scatter.fill(s, s, [mixed_ref], [out_w_ref], False)
 
         def first():
-            if s == 1:
-                late_hop(0)
-            project(s)
+            gather.arrive(first_x + s)
+            if s == 0:
+                for weight in mixer_weights[:2]:
+                    weight.finish()
+                mixer_weights[2].start()
+            project(s, 0)
+            if s == 0:
+                next_x(0)
+            project(s, 1)
+            if s == 0:
+                next_x(1)
+            else:
+                late_hops(0, 1)
 
         def second():
             recur(s)
-            for keep in keeps[s]:
-                keep.start()
-            if s == 1:
-                late_hop(1)
             if s == 0:
-                loads[3].wait()
+                for h in range(2, gather.chips - 1):
+                    next_x(h)
+                mixer_weights[2].finish()
+                for weight in weights:
+                    weight.start()
+                for t in range(seqs):
+                    gather.start(seqs + t)
+                for keep in weight_keeps:
+                    keep.start()
+            else:
+                late_hops(1, 2)
 
         return [first, second, partners, own]
 
-    def last_late_hops():
-        for h in range(2 if seqs > 1 else 0, gather.chips - 1):
-            late_hop(h)
-
     def store(s):
-        own = x_full_ref[s, pl.ds(pl.multiple_of(me * rows, rows), rows), :]
+        own = x_ref[s]
         residual = own.astype(jnp.float32) + scatter.result(s)[...]
         residual_ref[s] = residual
         normal = residual * lax.rsqrt(mean_of(residual * residual) + epsilon)
@@ -944,42 +1013,57 @@
 
     sum_then_gather(
         scatter, gather, [steps(s) for s in range(seqs)], [functools.partial(store, s) for s in range(seqs)], seqs,
-        after=(last_late_hops,),
+        after=(lambda: None, functools.partial(late_hops, 2, gather.chips)),
     )
     for s in range(seqs):
         gather.finish(seqs + s)
+        gather.sent(first_x + s)
         for keep in keeps[s]:
             keep.wait()
+    for keep in weight_keeps:
+        keep.wait()
     for weight in weights:
         weight.finish()
 
 
-def mixer_forward(x_full, gains, branch_w, rec_w, out_w, vectors, softness, gate_a, gate_x, out_grad, weights):
-    seqs, seq_len, width = x_full.shape
-    rows, channels = out_grad.shape[1], vectors.shape[1]
-    low = jax.ShapeDtypeStruct((seqs, seq_len, channels), jnp.bfloat16)
-    full = jax.ShapeDtypeStruct((seqs, seq_len, channels), jnp.float32)
-    kept = [x_full, full, low, low, full, full, full, low]
-    kept = [jax.ShapeDtypeStruct(out.shape, out.dtype) for out in kept]
-    outs = [jax.ShapeDtypeStruct(out_grad.shape, jnp.float32)] + kept + [kept[0]] * 2
+def mixer_forward(layer_in, out_grad, gain_pack, vector_pack, gate_pack, mixer_weights, weights):
+    seqs, rows, width = layer_in.shape
+    size, n = lax.axis_size("seq"), lax.axis_size("grp")
+    seq_len, channels = n * rows, mixer_weights[0].shape[0]
+    f32, bf16 = jnp.float32, jnp.bfloat16
+    shape = jax.ShapeDtypeStruct
+    low, full = shape((seqs, seq_len, channels), bf16), shape((seqs, seq_len, channels), f32)
+    tokens = shape((seqs, seq_len, width), bf16)
+    kept = [tokens, full, low, low, full, full, full, low]
+    mixer_full = [gathered(w, axis) for w, axis in zip(mixer_weights, mixer_axes)]
+    outs = [
+        shape(layer_in.shape, f32), shape((2, 1, width), f32), shape((8, channels), f32),
+        shape((channels, channels), bf16), shape((channels, channels), bf16),
+    ]
+    outs += kept + mixer_full + [tokens] * 2
     outs += [gathered(w, axis) for w, axis in zip(weights, weight_axes)]
     return call(
-        mixer_forward_body, "mixer_forward", 2,
-        (x_full, branch_w, rec_w, out_w, gains, vectors, softness, gate_a, gate_x, out_grad, *weights),
-        [in_hbm] * 4 + [in_vmem] * 9,
-        outs, [in_vmem] + [in_hbm] * 13,
-        [pltpu.VMEM(v.shape, v.dtype) for v in [x_full, branch_w, rec_w, out_w] + kept]
+        mixer_forward_body, "mixer_forward", 7,
+        (layer_in, out_grad, gain_pack, vector_pack, gate_pack, *mixer_weights, *weights),
+        [in_vmem] * 11,
+        outs, [in_vmem] * 5 + [in_hbm] * 16,
+        [pltpu.VMEM(v.shape, v.dtype) for v in kept + mixer_full + [tokens]]
         + [
-            pltpu.SemaphoreType.DMA((3 + seqs,)),
+            pltpu.VMEM(layer_in.shape, bf16),
+            pltpu.VMEM((pick_rows(seq_len) + 8, channels), f32),
+            pltpu.VMEM((8, channels), f32),
+            pltpu.VMEM((2, channels, channels), f32),
+            pltpu.VMEM((n, size) + gain_pack.shape, f32),
+            pltpu.VMEM((size,) + vector_pack.shape, f32),
+            pltpu.VMEM((size,) + gate_pack.shape, f32),
             pltpu.SemaphoreType.DMA((seqs, len(kept))),
-            pltpu.VMEM(out_grad.shape, jnp.bfloat16),
-            pltpu.VMEM((pick_rows(seq_len) + 8, channels), jnp.float32),
-            pltpu.VMEM((8, channels), jnp.float32),
+            pltpu.SemaphoreType.DMA((3,)),
         ]
-        + seq_sems(3)
-        + gather_sems(2 * seqs)
+        + [pltpu.SemaphoreType.DMA((n,))] * 2
+        + seq_sems(3) * 3
+        + gather_sems(3 * seqs)
         + scatter_scratch(seqs, rows, width),
-        130,
+        180,
     )
 
 
@@ -1175,7 +1259,7 @@
 
 def mixer_back_body(
     heads, low_in, out_w_in, branch_in, feed_in, conv_in, rate_in, input_in, state_in, mixed_in, branch_w_in, rec_w_in,
-    normed_in, vectors_ref, softness_ref, gate_a_ref, gate_x_ref, x_ref, grad_ref, gain_ref, gain_two_ref,
+    normed_in, vectors_ref, gate_a_ref, gate_x_ref, x_ref, grad_ref, gain_ref, gain_two_ref,
     grad_x_ref, squares_out_ref, sums_out_ref, gain_sum_ref, o0, o1, o2,
     low_ref, out_w_ref, branch_ref, feed_ref, conv_ref, rate_ref, input_ref, state_ref, mixed_ref, branch_w_ref,
     rec_w_ref, grad_mixed, grad_branch, grad_feed, squares, sums, window, later, carry, tiles, d0, d1, d2,
@@ -1185,6 +1269,7 @@
 ):
     seqs, rows, width = x_ref.shape
     seq_len, channels = feed_ref.shape[1:]
+    softness_ref = vectors_ref.at[pl.ds(7, 1), :]
     per_seq = (
         (low_in, low_ref), (branch_in, branch_ref), (feed_in, feed_ref), (conv_in, conv_ref), (rate_in, rate_ref),
         (input_in, input_ref), (state_in, state_ref),
@@ -1361,14 +1446,14 @@
 
 def mixer_back(
     heads, low, out_w, branch, feed, conv, rate, gate, state, mixed, branch_w, rec_w, normed,
-    vectors, softness, gate_a, gate_x, layer_in, grad_residual, gain, gain_two_grad,
+    vectors, gate_a, gate_x, layer_in, grad_residual, gain, gain_two_grad,
 ):
     seqs, rows, width = layer_in.shape
     seq_len, channels = feed.shape[1:]
     size, n = lax.axis_size("seq"), lax.axis_size("grp")
     f32, bf16 = jnp.float32, jnp.bfloat16
     large = (low, out_w, branch, feed, conv, rate, gate, state, mixed, branch_w, rec_w)
-    small = (vectors, softness, gate_a, gate_x, layer_in, grad_residual, gain, gain_two_grad)
+    small = (vectors, gate_a, gate_x, layer_in, grad_residual, gain, gain_two_grad)
     window_rows = head_windows(heads, channels // heads, size)[0]
     grads = [jax.ShapeDtypeStruct(w.shape, bf16) for w in (branch_w, rec_w, out_w)]
     squares = (heads, 2, window_rows, channels)
@@ -1376,7 +1461,7 @@
     return call(
         functools.partial(mixer_back_body, heads), "mixer_back", 6,
         large + (normed,) + small,
-        [in_hbm] * 12 + [in_vmem] * 8,
+        [in_hbm] * 12 + [in_vmem] * 7,
         [
             jax.ShapeDtypeStruct(layer_in.shape, f32),
             jax.ShapeDtypeStruct(squares, f32),
@@ -1448,44 +1533,51 @@
     channels = heads_here * head_dim
     f32 = jnp.float32
 
-    own_params = jnp.concatenate(
-        [jnp.transpose(conv_w, (0, 2, 1))]
-        + [v[:, :, None] for v in (conv_b, gate_a_b, gate_x_b, decay_logit)]
-        + [gate_a_w, gate_x_w],
-        axis=2,
-    ).astype(f32)
-    own_gains = jnp.concatenate([gain_one, gain_two]).astype(f32)
-    pack = jnp.concatenate(
-        [padded_rows(own_params.reshape(1, -1))[0], padded_rows(own_gains.reshape(1, -1))[0]]
-    )
-    late_grad, x_full, params, gains, branch_w, rec_w, out_w = gather_first(
-        layer_in, out_grad, pack, (w_branch.T, w_rec.T, w_out)
-    )
-
-    gains = gains.reshape(grp_devices, seq_devices, -1)[:, :, : own_gains.size]
-    gains = jnp.transpose(gains.reshape(grp_devices, seq_devices, 2, -1), (2, 1, 0, 3)).reshape(2, 1, -1)
-    params = params.reshape(seq_devices, -1)[:, : own_params.size]
-    params = params.reshape((seq_devices,) + own_params.shape)
-    params = jnp.transpose(params, (1, 0, 2, 3)).reshape(heads_here, head_dim, -1)
-    vectors = params[:, :, : tap_count + 4].reshape(channels, -1).T
+    short_line = seqs_here * positions * grp_devices <= 2048
+    mixer_weights = (w_branch.T, w_rec.T, w_out)
+    mlp_weights = (mlp_gate, mlp_up, mlp_down)
     at = tap_count + 4
-    diag_a = head_diagonal(params[:, :, at : at + head_dim].astype(jnp.bfloat16))
-    diag_x = head_diagonal(params[:, :, at + head_dim :].astype(jnp.bfloat16))
-    logit = vectors[tap_count + 3 :]
-    softness = jax.nn.softplus(-logit)
-
-    short_line = seqs_here * positions * grp_devices <= 2048
-    mlp_weights = (mlp_gate, mlp_up, mlp_down)
     if short_line:
+        softness = jax.nn.softplus(-decay_logit.astype(f32))
+        vector_rows = [jnp.transpose(conv_w, (1, 0, 2)).reshape(tap_count, -1)]
+        vector_rows += [v.reshape(1, -1) for v in (conv_b, gate_a_b, gate_x_b)]
+        vector_pack = jnp.concatenate([v.astype(f32) for v in vector_rows] + [softness.reshape(1, -1)])
+        vector_pack = jnp.pad(vector_pack, ((0, 0), (0, -vector_pack.shape[1] % 128)))
+        gain_pack = jnp.concatenate([gain_one, gain_two]).astype(f32)[None]
+        gain_pack = jnp.pad(gain_pack, ((0, 7), (0, -gain_pack.shape[1] % 128)))
+        gate_pack = jnp.concatenate([gate_a_w, gate_x_w]).astype(f32)
         (
-            residual, normed_one, branch_pre, feed, conv, rate, gate, state, mixed, normed_two, grad_output,
-            gate_w, up_w, down_w,
-        ) = mixer_forward(
-            x_full, gains, branch_w, rec_w, out_w, vectors, softness, diag_a, diag_x, late_grad, mlp_weights
-        )
+            residual, gains, vectors, diag_a, diag_x,
+            normed_one, branch_pre, feed, conv, rate, gate, state, mixed, branch_w, rec_w, out_w,
+            normed_two, grad_output, gate_w, up_w, down_w,
+        ) = mixer_forward(layer_in, out_grad, gain_pack, vector_pack, gate_pack, mixer_weights, mlp_weights)
         normed_one = normed_one.reshape(-1, model_width)
         grad_output = grad_output.reshape(-1, model_width)
     else:
+        own_params = jnp.concatenate(
+            [jnp.transpose(conv_w, (0, 2, 1))]
+            + [v[:, :, None] for v in (conv_b, gate_a_b, gate_x_b, decay_logit)]
+            + [gate_a_w, gate_x_w],
+            axis=2,
+        ).astype(f32)
+        own_gains = jnp.concatenate([gain_one, gain_two]).astype(f32)
+        pack = jnp.concatenate(
+            [padded_rows(own_params.reshape(1, -1))[0], padded_rows(own_gains.reshape(1, -1))[0]]
+        )
+        late_grad, x_full, params, gains, branch_w, rec_w, out_w = gather_first(
+            layer_in, out_grad, pack, mixer_weights
+        )
+
+        gains = gains.reshape(grp_devices, seq_devices, -1)[:, :, : own_gains.size]
+        gains = jnp.transpose(gains.reshape(grp_devices, seq_devices, 2, -1), (2, 1, 0, 3)).reshape(2, 1, -1)
+        params = params.reshape(seq_devices, -1)[:, : own_params.size]
+        params = params.reshape((seq_devices,) + own_params.shape)
+        params = jnp.transpose(params, (1, 0, 2, 3)).reshape(heads_here, head_dim, -1)
+        vectors = params[:, :, : tap_count + 4].reshape(channels, -1).T
+        diag_a = head_diagonal(params[:, :, at : at + head_dim].astype(jnp.bfloat16))
+        diag_x = head_diagonal(params[:, :, at + head_dim :].astype(jnp.bfloat16))
+        logit = vectors[tap_count + 3 :]
+        softness = jax.nn.softplus(-logit)
         grad_output = jnp.concatenate(
             [lax.all_gather(late_grad[s], "grp", axis=0, tiled=True) for s in range(seqs_here)]
         )
@@ -1530,7 +1622,7 @@
     if short_line:
         grad_x, squares, sums, gain_sum, *mixer_slots = mixer_back(
             heads_here, residual_low, out_w, branch_pre, feed, conv, rate, gate, state, by_seq(mixed), branch_w, rec_w,
-            by_seq(normed_one), vectors, softness, diag_a, diag_x, layer_in, grad_residual, gains[0], gain_two_grad,
+            by_seq(normed_one), vectors, diag_a, diag_x, layer_in, grad_residual, gains[0], gain_two_grad,
         )
         mixer_grads = [sum_all(slot) for slot in mixer_slots]
         place = lax.axis_index("seq")

time: 535 us -> 525 us (0.981)
  local copies, waits for them, and re-layouts: 19.4 us -> 11.4 us
    pallas_call x4 -> x3, Pallas kernels: 425 us -> 424 us  [call(): pl.pallas_call(body, in_specs=in_specs, out_specs=out_specs, out_shape=ou...]
  transfers between devices with their start and end apart: 1 -> 1, of which waited for: 0 -> 0; matrix products, arithmetic and copies ran while one was open for 4% -> 3% of each run, Pallas kernels for 20% -> 20%
where the time goes in v8:
time: 525 us; the launch traced here: 514 us
  Pallas kernels  424 us (81%)
  matrix products  45.9 us (9%)
  other arithmetic  18.3 us (3%)
  between operations  14.7 us (3%)
  local copies, waits for them, and re-layouts  11.4 us (2%)
    pallas_call x3, Pallas kernels, call(): pl.pallas_call(body, in_specs=in_specs, out_specs=out_specs, out_shape=ou...  424 us
    dot_general x3, matrix products, matmul_tn(): lax.dot_general(left, right, (((0,), (0,)), ((), ())), preferred_element_...  19.8 us
    dot_general x2, matrix products, matmul(): return jnp.dot(left, right, preferred_element_type=jnp.float32)  19.1 us
  transfers between devices with their start and end apart: 1, of which 0 were waited for; matrix products, arithmetic and copies ran while one was open for 3% of the time, Pallas kernels for 20%

profile of v8, /device:TPU:0, one launch (start us, length us, event | category | flops | bytes accessed | tf_op | source)
XLA Modules:
  0.0 514.2 jit_solution(13028013576610037128)
XLA Ops:
  7.2 0.0 reduce-scatter.2.cloned.1.call-start
  7.2 0.8 copy.39
  8.0 0.8 copy.40
  8.8 0.7 convert_bitcast_fusion
  9.5 0.1 reshape.180
  9.6 0.7 compare_select_fusion
  10.3 0.1 reshape.173
  10.4 0.7 reshape.181
  11.1 0.7 reshape.182
  11.8 0.7 reshape.183
  12.6 0.7 maximum_convert_fusion.gate_pack_ref
  13.3 0.6 pad.12.vector_pack_ref
  13.9 1.3 fusion.12.gain_pack_ref
  15.2 196.0 %mixer_forward.1 = (f32[2,96,2048]{2,1,0:T(8,128)}, f32[2,1,2048]{2,1,0:T(1,128)}, f32[8,352]{1,0:T(8,128)}, bf16[352,352]{1,0:T(8,128)(2,1)}, bf16[352,352]{1,0...) custom-call(bf16[2,96,2048]{2,1,0:T(8,128)(2,1)} %x_ref.3, ...), custom_call_target="tpu_custom_call" | custom-call | flops 179999997952 | bytes 540000000 | tf_op jit(solution)/shard_map/mixer_forward/pallas_call | solution.py:587
  211.3 0.0 slice-start
  211.3 8.6 %fusion.31 = f32[1536,768]{1,0:T(8,128)S(1)} fusion(bf16[1536,2048]{1,0:T(8,128)(2,1)} %bitcast.112, bf16[2048,768]{1,0:T(8,128)(2,1)} %get-tuple-element.57.gate_w_in), kind=kOutput, calls=%fused_computation.76 | convolution fusion | flops 4831838208 | bytes 14155776 | tf_op jit(solution)/shard_map/dot_general | solution.py:18
  219.9 0.0 slice-start.1
  219.9 6.9 %fusion.30 = f32[1536,768]{1,0:T(8,128)} fusion(bf16[1536,2048]{1,0:T(8,128)(2,1)S(1)} %bitcast.110, bf16[768,2048]{1,0:T(8,128)(2,1)S(1)} %copy-done.14), kind=kOutput, calls=%fused_computation.75 | convolution fusion | flops 4831838208 | bytes 14155776 | tf_op jit(solution)/shard_map/dot_general | solution.py:28
  226.8 10.6 %multiply_convert_fusion = (bf16[1536,768]{1,0:T(8,128)(2,1)S(1)}, bf16[1536,768]{1,0:T(8,128)(2,1)S(1)}, bf16[1536,768]{1,0:T(8,128)(2,1)S(1)}) fusion(f32[1536,768]{1,0:T(8,128)S(1)} %fusion.31, f32[1536,768]{1,0:T(8,128)} %fusion.30, bf16[1536,2048]{1,0:T(8,128)(2,1)S(1)} %bitcast.115, bf16[2048,768]{1,0:T(8,128)(2,1)} %get-tuple-element.56.up_w_in), kind=kOutput, calls=%fused_computation.9 | convolution fusion | flops 4862509056 | bytes 25952256 | tf_op jit(solution)/shard_map/dot_general | solution.py:18
  237.4 6.6 %convolution_convert_fusion.1.w1 = bf16[2048,768]{1,0:T(8,128)(2,1)} fusion(bf16[1536,2048]{1,0:T(8,128)(2,1)S(1)} %bitcast.116, bf16[1536,768]{1,0:T(8,128)(2,1)S(1)} %get-tuple-element.91), kind=kOutput, calls=%fused_computation.13 | convolution fusion | flops 4833411072 | bytes 11796480 | tf_op jit(solution)/shard_map/dot_general | solution.py:22
  244.0 6.6 %convolution_convert_fusion.2.w0 = bf16[2048,768]{1,0:T(8,128)(2,1)} fusion(bf16[1536,2048]{1,0:T(8,128)(2,1)S(1)} %bitcast.117, bf16[1536,768]{1,0:T(8,128)(2,1)S(1)} %get-tuple-element.90), kind=kOutput, calls=%fused_computation.14 | convolution fusion | flops 4833411072 | bytes 11796480 | tf_op jit(solution)/shard_map/dot_general | solution.py:22
  250.6 6.7 %convolution_convert_fusion.w2 = bf16[768,2048]{1,0:T(8,128)(2,1)} fusion(bf16[1536,768]{1,0:T(8,128)(2,1)S(1)} %get-tuple-element.89, bf16[1536,2048]{1,0:T(8,128)(2,1)S(1)} %bitcast.111), kind=kOutput, calls=%fused_computation.12 | convolution fusion | flops 4833411072 | bytes 11796480 | tf_op jit(solution)/shard_map/dot_general | solution.py:22
  257.3 0.6 slice_bitcast_fusion
  257.9 123.6 %mlp_back.1 = (f32[2,96,2048]{2,1,0:T(8,128)}, f32[8,2048]{1,0:T(8,128)}, bf16[2,768,2048]{2,1,0:T(8,128)(2,1)}, bf16[3,512,768]{2,1,0:T(8,128)(2,1)}, bf16[3,51...) custom-call(bf16[2,768,768]{2,1,0:T(8,128)(2,1)} %bitcast.119, ...), custom_call_target="tpu_custom_call" | custom-call | flops 120000004096 | bytes 360000000 | tf_op jit(solution)/shard_map/mlp_back/pallas_call | solution.py:587
  381.5 0.0 reduce-scatter.2.cloned.1.call-update
  381.5 0.0 copy-start.9
  381.6 104.1 %mixer_back.1 = (f32[2,96,2048]{2,1,0:T(8,128)}, f32[2,2,48,352]{3,2,1,0:T(8,128)}, f32[8,352]{1,0:T(8,128)}, f32[8,512]{1,0:T(8,128)}, bf16[4,352,512]{2,1,0:T(...) custom-call(bf16[2,768,2048]{2,1,0:T(8,128)(2,1)} %get-tuple-element.62.low_in, ...), custom_call_target="tpu_custom_call" | custom-call | flops 99999997952 | bytes 300000000 | tf_op jit(solution)/shard_map/mixer_back/pallas_call | solution.py:587
  485.7 1.2 fusion.27
  486.9 0.1 copy.54
  487.0 0.1 copy.53
  487.0 0.8 reshape.179
  487.8 0.1 constant_dynamic-slice_fusion.3
  487.9 0.6 copy.55
  488.5 0.6 fusion.26
  489.1 0.7 constant_dynamic-slice_fusion.7
  489.9 0.1 fusion.28
  490.0 0.3 fusion.29
  490.2 0.7 pad_maximum_fusion.2
  491.0 0.7 pad_maximum_fusion.1
  491.7 0.6 fusion.22
  492.3 0.5 slice_bitcast_fusion.2
  492.8 2.5 add_bitcast_fusion.2
  495.3 1.5 add_bitcast_fusion
  496.8 2.8 convert_add_fusion
  499.7 3.9 convert_add_fusion.3
  503.6 1.2 fusion.8
  504.8 0.9 pad_maximum_fusion
  505.7 1.1 copy.57
  (36 shorter events, 0.1 us)
Async XLA Ops:
  7.2 496.4 %reduce-scatter.2.cloned.1.call-start = ((), (), s32[]{:S(2)}) async-start(), calls=%async_computation.1 | async-start | bytes 3538944 | tf_op jit(solution)/shard_map/reduce_scatter | solution.py:1618
  211.3 8.6 %copy-start.10 = (bf16[2,768,2048]{2,1,0:T(8,128)(2,1)S(1)}, bf16[2,768,2048]{2,1,0:T(8,128)(2,1)}, u32[]{:S(2)}) copy-start(bf16[2,768,2048]{2,1,0:T(8,128)(2,1)} %get-tuple-element.53) | copy-start | bytes 18874372
  211.3 8.6 %copy-start.14 = (bf16[768,2048]{1,0:T(8,128)(2,1)S(1)}, bf16[768,2048]{1,0:T(8,128)(2,1)}, u32[]{:S(2)}) copy-start(bf16[768,2048]{1,0:T(8,128)(2,1)} %get-tuple-element.54.refs_1_) | copy-start | bytes 9437188
  211.3 15.5 %slice-start = ((s8[6291456]{0:T(1024)(128)(4,1)}), s8[4194304]{0:T(1024)(128)(4,1)S(1)}, s32[]{:S(2)}) async-start(s8[6291456]{0:T(1024)(128)(4,1)} %bitcast.113), calls=%async_computation.2 | async-start | bytes 8388608
  219.9 6.9 %slice-start.1 = ((s8[6291456]{0:T(1024)(128)(4,1)}), s8[2097152]{0:T(1024)(128)(4,1)S(1)}, s32[]{:S(2)}) async-start(s8[6291456]{0:T(1024)(128)(4,1)} %bitcast.113), calls=%async_computation.3 | async-start | bytes 4194304
  237.4 6.6 %copy-start.13 = (bf16[1536,768]{1,0:T(8,128)(2,1)}, bf16[1536,768]{1,0:T(8,128)(2,1)S(1)}, u32[]{:S(2)}) copy-start(bf16[1536,768]{1,0:T(8,128)(2,1)S(1)} %get-tuple-element.91) | copy-start | bytes 7077892
  237.4 6.6 %copy-start.12 = (bf16[1536,768]{1,0:T(8,128)(2,1)}, bf16[1536,768]{1,0:T(8,128)(2,1)S(1)}, u32[]{:S(2)}) copy-start(bf16[1536,768]{1,0:T(8,128)(2,1)S(1)} %get-tuple-element.90) | copy-start | bytes 7077892
  237.4 13.2 %copy-start.11 = (bf16[1536,768]{1,0:T(8,128)(2,1)}, bf16[1536,768]{1,0:T(8,128)(2,1)S(1)}, u32[]{:S(2)}) copy-start(bf16[1536,768]{1,0:T(8,128)(2,1)S(1)} %get-tuple-element.89) | copy-start | bytes 7077892
  250.6 6.7 %copy-start.8 = (f32[2,1,2048]{2,1,0:T(1,128)S(1)}, f32[2,1,2048]{2,1,0:T(1,128)}, u32[]{:S(2)}) copy-start(f32[2,1,2048]{2,1,0:T(1,128)} %get-tuple-element.59) | copy-start | bytes 49156
  381.5 110.1 %copy-start.9 = (bf16[2,44]{1,0:T(2,128)(2,1)S(1)}, bf16[2,44]{1,0:T(2,128)(2,1)}, u32[]{:S(2)}) copy-start(bf16[2,44]{1,0:T(2,128)(2,1)} %param.27) | copy-start | bytes 532
  485.6 9.7 %copy-start.4 = (bf16[4,352,512]{2,1,0:T(8,128)(2,1)S(1)}, bf16[4,352,512]{2,1,0:T(8,128)(2,1)}, u32[]{:S(2)}) copy-start(bf16[4,352,512]{2,1,0:T(8,128)(2,1)} %get-tuple-element.82) | copy-start | bytes 4325380
  485.6 9.7 %copy-start.5 = (bf16[4,352,512]{2,1,0:T(8,128)(2,1)S(1)}, bf16[4,352,512]{2,1,0:T(8,128)(2,1)}, u32[]{:S(2)}) copy-start(bf16[4,352,512]{2,1,0:T(8,128)(2,1)} %get-tuple-element.85) | copy-start | bytes 4325380
  492.8 4.0 copy-start
  496.8 2.8 copy-start.1
  496.8 2.8 copy-start.2
  499.7 3.9 copy-start.6
  499.7 5.1 copy-start.7
  503.6 2.2 copy-start.3
Sparse Core Ops, SparseCore 0:
  381.7 51.0 reduce-scatter.1

commit v9 on v8

--- a/solution.py
+++ b/solution.py
@@ -1081,14 +1081,26 @@
     low_ref, load_sem, gate_ref, up_ref, gate_w_ref, up_w_ref, *refs = refs
     pairs = [(gate_in, gate_ref), (up_in, up_ref), (gate_w_in, gate_w_ref), (up_w_in, up_w_ref)]
     if with_out:
-        hidden_ref, down_w_ref, *refs = refs
+        hidden_ref, down_w_ref, tiles, made_up, made_down, tile_sem, *refs = refs
         pairs += [(hidden_in, hidden_ref), (down_w_in, down_w_ref)]
     loads = copies(pairs, load_sem)
     for load in loads:
         load.start()
     greet_axes(("seq", "grp"))
     seqs, rows, _ = grad_ref.shape
-    sums = weight_sums(weight_axes, (w0, w1, w2), (o0, o1, o2), *refs[:2])
+    if with_out:
+        sums = weight_sums(weight_axes[:1], (w0,), (o0,), *refs[:2])
+        parts, me = lax.axis_size("seq"), lax.axis_index("seq")
+        moves = [
+            Exchange(
+                "seq", lambda k, ref=made: ref.at[lax.rem(k - me + parts, parts)], None,
+                refs[0].at[i], refs[1].at[i], out, 0,
+            )
+            for i, made, out in ((1, made_up, o1), (2, made_down, o2))
+        ]
+        order = [(kind, k) for kind in range(2) for k in range(1, parts)] + [(0, 0), (1, 0)]
+    else:
+        sums = weight_sums(weight_axes, (w0, w1, w2), (o0, o1, o2), *refs[:2])
     for weight in sums:
         weight.start_others()
     gather = Gather(views(low_ref), views(full_ref), rows, *refs[2:5])
@@ -1108,6 +1120,44 @@
         grad_residual_ref[s] = grad
         low_ref[s] = grad.astype(jnp.bfloat16)
 
+    def tile_load(i, j):
+        kind, k = order[i]
+        step = tiles.shape[-1]
+        first = lax.rem(me + k, parts) * 2 * step + j * step
+        source = (w1, w2)[kind].at[:, :, pl.ds(pl.multiple_of(first, step), step)]
+        return pltpu.make_async_copy(source, tiles.at[j], tile_sem.at[j])
+
+    def make(i):
+        kind, k = order[i]
+        step = tiles.shape[-1]
+
+        @pl.loop(0, 2)
+        def _(j):
+            tile_load(i, j).wait()
+            at = pl.ds(pl.multiple_of(j * step, step), step)
+            total = None
+            for s in range(seqs):
+                if kind == 0:
+                    term = matmul_tn(tiles[j, s], up_ref[s])
+                else:
+                    term = matmul_tn(hidden_ref[s], tiles[j, s])
+                total = term if total is None else total + term
+            if kind == 0:
+                made_up[k, at, :] = total.astype(jnp.bfloat16)
+            else:
+                made_down[k, :, at] = total.astype(jnp.bfloat16)
+            if i + 1 < len(order):
+                tile_load(i + 1, j).start()
+
+        if k:
+            moves[kind].copy(k, me).start()
+        else:
+            moves[kind].own().start()
+
+    def make_all(first, end):
+        for i in range(first, end):
+            make(i)
+
     def wait_first():
         for load in loads[:4]:
             load.wait()
@@ -1123,6 +1173,24 @@
         fill_out, store_out = out_body(hidden_ref, down_w_ref, residual_ref, layer_out_ref, scatter, seqs)
         fills += [fill_out(s) for s in range(seqs - 1)]
         fills[seqs - 1] = (*fills[seqs - 1], wait_later)
+        third = parts - 1
+
+        def partners_then(step):
+            step()
+            make_all(2, third)
+
+        def own_then(step):
+            step()
+            make_all(third, third + 1)
+
+        if len(fills) > seqs:
+            fills[seqs] = (
+                functools.partial(partners_then, fills[seqs][0]),
+                functools.partial(own_then, fills[seqs][1]),
+                functools.partial(make_all, third + 1, 2 * third),
+            )
+        for j in range(2):
+            tile_load(0, j).start()
         stores += [functools.partial(store_out, s) for s in range(seqs - 1)]
 
     def late():
@@ -1133,9 +1201,18 @@
             at = pl.ds(pl.multiple_of(i * step, step), step)
             late_ref[at, :] = matmul(hidden_ref[seqs - 1, at, :], down_w_ref[...]).astype(jnp.bfloat16)
 
-    sum_then_gather(scatter, gather, fills, stores, seqs, after=(late,) if with_out else ())
+    def rest():
+        make_all(2 * third if len(fills) > seqs else 2, len(order))
+
+    sum_then_gather(
+        scatter, gather, fills, stores, seqs,
+        between=functools.partial(make_all, 0, 2) if with_out else None, after=(late, rest) if with_out else (),
+    )
     for weight in sums:
         weight.finish_others()
+    if with_out:
+        for move in moves:
+            move.finish()
 
 
 def mlp_back(grad_gate, grad_up, gate_w, up_w, residual, out_grad, gain, grads, out_inputs):
@@ -1145,7 +1222,20 @@
         jax.ShapeDtypeStruct((8, width), jnp.float32),
         jax.ShapeDtypeStruct((seqs, lax.axis_size("grp") * rows, width), jnp.bfloat16),
     ]
-    outs += [slots_of(grad, axis) for grad, axis in zip(grads, weight_axes)]
+    if out_inputs:
+        size = lax.axis_size("seq")
+        hidden_width, part = grad_gate.shape[-1], width // size
+        outs.append(slots_of(grads[0], 0))
+        outs.append(jax.ShapeDtypeStruct((size, part, hidden_width), jnp.bfloat16))
+        outs.append(jax.ShapeDtypeStruct((size, hidden_width, part), jnp.bfloat16))
+        makers = [
+            pltpu.VMEM((2, *grad_gate.shape[:2], part // 2), jnp.bfloat16),
+            *(pltpu.VMEM(out.shape, out.dtype) for out in outs[-2:]),
+            pltpu.SemaphoreType.DMA((2,)),
+        ]
+    else:
+        outs += [slots_of(grad, axis) for grad, axis in zip(grads, weight_axes)]
+        makers = []
     out_specs = [in_vmem] * 2 + [in_hbm] * 4
     if out_inputs:
         outs.append(jax.ShapeDtypeStruct((seqs - 1, rows, width), jnp.bfloat16))
@@ -1158,6 +1248,7 @@
         outs, out_specs,
         [pltpu.VMEM(residual.shape, jnp.bfloat16), pltpu.SemaphoreType.DMA((6,))]
         + [pltpu.VMEM(v.shape, v.dtype) for v in (grad_gate, grad_up, gate_w, up_w, *out_inputs)]
+        + makers
         + seq_sems(3)
         + gather_sems(seqs)
         + scatter_scratch(seqs * 2 - 1 if out_inputs else seqs, rows, width),
@@ -1533,7 +1624,7 @@
     channels = heads_here * head_dim
     f32 = jnp.float32
 
-    short_line = seqs_here * positions * grp_devices <= 2048
+    short_line = seqs_here * positions * grp_devices <= 2048 and model_width // seq_devices == 512
     mixer_weights = (w_branch.T, w_rec.T, w_out)
     mlp_weights = (mlp_gate, mlp_up, mlp_down)
     at = tap_count + 4
@@ -1598,12 +1689,16 @@
     grad_hidden = matmul_nt(grad_output, down_w)
     grad_gate = gate_pull(grad_hidden * up_proj)[0].astype(jnp.bfloat16)
     grad_up = (grad_hidden * gate_act).astype(jnp.bfloat16)
-    mlp_grads = low_all(
-        (matmul_tn(normed_two, grad_gate), matmul_tn(normed_two, grad_up), matmul_tn(hidden, grad_output))
-    )
-
     def by_seq(values):
         return values.reshape(seqs_here, -1, values.shape[-1])
+
+    if short_line:
+        first_grad = matmul_tn(normed_two, grad_gate).astype(jnp.bfloat16)
+        mlp_grads = (first_grad, by_seq(normed_two), by_seq(grad_output))
+    else:
+        mlp_grads = low_all(
+            (matmul_tn(normed_two, grad_gate), matmul_tn(normed_two, grad_up), matmul_tn(hidden, grad_output))
+        )
 
     back_inputs = (
         by_seq(grad_gate), by_seq(grad_up), gate_w, up_w, residual, out_grad, gains[1], mlp_grads
@@ -1618,7 +1713,10 @@
         late = lax.psum_scatter(late, "grp", scatter_dimension=0, tiled=True)
         late = (residual[seqs_here - 1] + late.astype(f32)).astype(jnp.bfloat16)
         layer_out = jnp.concatenate([layer_out, late[None]])
-    mlp_grads = sum_slots(mlp_grads, mlp_slots, weight_axes)
+    if short_line:
+        mlp_grads = sum_slots(mlp_grads[:1], mlp_slots[:1], weight_axes) + [sum_all(slot) for slot in mlp_slots[1:]]
+    else:
+        mlp_grads = sum_slots(mlp_grads, mlp_slots, weight_axes)
     if short_line:
         grad_x, squares, sums, gain_sum, *mixer_slots = mixer_back(
             heads_here, residual_low, out_w, branch_pre, feed, conv, rate, gate, state, by_seq(mixed), branch_w, rec_w,

time: 525 us -> 507 us (0.966)
  matrix products: 45.9 us -> 29.3 us
    dot_general x3 -> x1, matrix products: 19.8 us -> 6.53 us  [matmul_tn(): lax.dot_general(left, right, (((0,), (0,)), ((), ())), preferred_element_...]
  transfers between devices with their start and end apart: 1 -> 1, of which waited for: 0 -> 0; matrix products, arithmetic and copies ran while one was open for 3% -> 3% of each run, Pallas kernels for 20% -> 21%
where the time goes in v9:
time: 507 us; the launch traced here: 498 us
  Pallas kernels  424 us (84%)
  matrix products  29.3 us (6%)
  other arithmetic  17.4 us (3%)
  between operations  14.7 us (3%)
  local copies, waits for them, and re-layouts  12.3 us (2%)
    pallas_call x3, Pallas kernels, call(): pl.pallas_call(body, in_specs=in_specs, out_specs=out_specs, out_shape=ou...  424 us
    dot_general x2, matrix products, matmul(): return jnp.dot(left, right, preferred_element_type=jnp.float32)  17.6 us
  transfers between devices with their start and end apart: 1, of which 0 were waited for; matrix products, arithmetic and copies ran while one was open for 3% of the time, Pallas kernels for 21%

profile of v9, /device:TPU:0, one launch (start us, length us, event | category | flops | bytes accessed | tf_op | source)
XLA Modules:
  0.0 497.7 jit_solution(14057359815811563187)
XLA Ops:
  7.2 0.0 reduce-scatter.2.cloned.1.call-start
  7.2 0.8 copy.39
  8.0 0.8 copy.40
  8.8 0.7 convert_bitcast_fusion
  9.5 0.1 reshape.182
  9.6 0.7 compare_select_fusion
  10.3 0.1 reshape.175
  10.4 0.7 reshape.183
  11.1 0.7 reshape.184
  11.8 0.7 reshape.185
  12.6 0.7 maximum_convert_fusion.gate_pack_ref
  13.3 0.6 pad.12.vector_pack_ref
  13.9 1.3 fusion.12.gain_pack_ref
  15.2 196.0 %mixer_forward.1 = (f32[2,96,2048]{2,1,0:T(8,128)}, f32[2,1,2048]{2,1,0:T(1,128)}, f32[8,352]{1,0:T(8,128)}, bf16[352,352]{1,0:T(8,128)(2,1)}, bf16[352,352]{1,0...) custom-call(bf16[2,96,2048]{2,1,0:T(8,128)(2,1)} %x_ref.3, ...), custom_call_target="tpu_custom_call" | custom-call | flops 179999997952 | bytes 540000000 | tf_op jit(solution)/shard_map/mixer_forward/pallas_call | solution.py:587
  211.3 0.0 slice-start
  211.3 8.2 %fusion.31 = f32[1536,768]{1,0:T(8,128)S(1)} fusion(bf16[1536,2048]{1,0:T(8,128)(2,1)} %bitcast.92, bf16[2048,768]{1,0:T(8,128)(2,1)} %get-tuple-element.57.gate_w_in), kind=kOutput, calls=%fused_computation.70 | convolution fusion | flops 4831838208 | bytes 14155776 | tf_op jit(solution)/shard_map/dot_general | solution.py:18
  219.5 0.0 slice-start.1
  219.6 5.1 %fusion.30 = f32[1536,768]{1,0:T(8,128)S(1)} fusion(bf16[1536,2048]{1,0:T(8,128)(2,1)S(1)} %bitcast.97, bf16[768,2048]{1,0:T(8,128)(2,1)S(1)} %copy-done.12), kind=kOutput, calls=%fused_computation.69 | convolution fusion | flops 4831838208 | bytes 14155776 | tf_op jit(solution)/shard_map/dot_general | solution.py:28
  224.8 9.4 %multiply_convert_fusion = (bf16[1536,768]{1,0:T(8,128)(2,1)}, bf16[1536,768]{1,0:T(8,128)(2,1)S(1)}, bf16[1536,768]{1,0:T(8,128)(2,1)}) fusion(f32[1536,768]{1,0:T(8,128)S(1)} %fusion.31, f32[1536,768]{1,0:T(8,128)S(1)} %fusion.30, bf16[1536,2048]{1,0:T(8,128)(2,1)S(1)} %bitcast.95, bf16[2048,768]{1,0:T(8,128)(2,1)S(1)} %copy-done.13), kind=kOutput, calls=%fused_computation.9 | convolution fusion | flops 4862509056 | bytes 25952256 | tf_op jit(solution)/shard_map/dot_general | solution.py:18
  234.1 6.5 %convolution_convert_fusion.w0 = bf16[2048,768]{1,0:T(8,128)(2,1)} fusion(bf16[1536,2048]{1,0:T(8,128)(2,1)S(1)} %bitcast.96, bf16[1536,768]{1,0:T(8,128)(2,1)S(1)} %get-tuple-element.90), kind=kOutput, calls=%fused_computation.12 | convolution fusion | flops 4833411072 | bytes 11796480 | tf_op jit(solution)/shard_map/dot_general | solution.py:22
  240.7 0.6 slice_bitcast_fusion
  241.3 123.8 %mlp_back.1 = (f32[2,96,2048]{2,1,0:T(8,128)}, f32[8,2048]{1,0:T(8,128)}, bf16[2,768,2048]{2,1,0:T(8,128)(2,1)}, bf16[3,512,768]{2,1,0:T(8,128)(2,1)}, bf16[4,51...) custom-call(bf16[2,768,768]{2,1,0:T(8,128)(2,1)} %bitcast.99, ...), custom_call_target="tpu_custom_call" | custom-call | flops 120000004096 | bytes 360000000 | tf_op jit(solution)/shard_map/mlp_back/pallas_call | solution.py:587
  365.1 0.0 reduce-scatter.2.cloned.1.call-update
  365.1 0.0 copy-start.9
  365.1 104.0 %mixer_back.1 = (f32[2,96,2048]{2,1,0:T(8,128)}, f32[2,2,48,352]{3,2,1,0:T(8,128)}, f32[8,352]{1,0:T(8,128)}, f32[8,512]{1,0:T(8,128)}, bf16[4,352,512]{2,1,0:T(...) custom-call(bf16[2,768,2048]{2,1,0:T(8,128)(2,1)} %get-tuple-element.62.low_in, ...), custom_call_target="tpu_custom_call" | custom-call | flops 99999997952 | bytes 300000000 | tf_op jit(solution)/shard_map/mixer_back/pallas_call | solution.py:587
  469.2 1.2 fusion.27
  470.4 0.1 copy.54
  470.5 0.1 copy.53
  470.6 0.8 reshape.181
  471.4 0.1 constant_dynamic-slice_fusion.3
  471.5 0.6 copy.55
  472.1 0.6 fusion.26
  472.7 0.8 constant_dynamic-slice_fusion.7
  473.5 0.1 fusion.28
  473.5 0.3 fusion.29
  473.8 0.7 pad_maximum_fusion.2
  474.5 0.7 pad_maximum_fusion.1
  475.3 0.6 fusion.22
  475.9 0.5 slice_bitcast_fusion.2
  476.4 2.5 add_bitcast_fusion.4
  478.9 1.5 add_bitcast_fusion.2
  480.4 1.6 add_bitcast_fusion
  481.9 0.9 copy-done
  482.8 1.5 add_bitcast_fusion.1
  484.4 2.8 convert_add_fusion
  487.2 1.1 fusion.8
  488.3 0.9 pad_maximum_fusion
  489.2 1.1 copy.57
  (33 shorter events, 0.1 us)
Async XLA Ops:
  7.2 480.0 %reduce-scatter.2.cloned.1.call-start = ((), (), s32[]{:S(2)}) async-start(), calls=%async_computation.1 | async-start | bytes 3538944 | tf_op jit(solution)/shard_map/reduce_scatter | solution.py:1713
  211.3 8.3 %copy-start.10 = (bf16[2,768,2048]{2,1,0:T(8,128)(2,1)S(1)}, bf16[2,768,2048]{2,1,0:T(8,128)(2,1)}, u32[]{:S(2)}) copy-start(bf16[2,768,2048]{2,1,0:T(8,128)(2,1)} %get-tuple-element.53.w2) | copy-start | bytes 18874372
  211.3 8.3 %copy-start.12 = (bf16[768,2048]{1,0:T(8,128)(2,1)S(1)}, bf16[768,2048]{1,0:T(8,128)(2,1)}, u32[]{:S(2)}) copy-start(bf16[768,2048]{1,0:T(8,128)(2,1)} %get-tuple-element.54.refs_1_) | copy-start | bytes 9437188
  211.3 13.4 %slice-start = ((s8[6291456]{0:T(1024)(128)(4,1)}), s8[4194304]{0:T(1024)(128)(4,1)S(1)}, s32[]{:S(2)}) async-start(s8[6291456]{0:T(1024)(128)(4,1)} %bitcast.93), calls=%async_computation.2 | async-start | bytes 8388608
  219.5 5.2 %slice-start.1 = ((s8[6291456]{0:T(1024)(128)(4,1)}), s8[2097152]{0:T(1024)(128)(4,1)S(1)}, s32[]{:S(2)}) async-start(s8[6291456]{0:T(1024)(128)(4,1)} %bitcast.93), calls=%async_computation.3 | async-start | bytes 4194304
  219.6 5.2 %copy-start.13 = (bf16[2048,768]{1,0:T(8,128)(2,1)S(1)}, bf16[2048,768]{1,0:T(8,128)(2,1)}, u32[]{:S(2)}) copy-start(bf16[2048,768]{1,0:T(8,128)(2,1)} %get-tuple-element.56.up_w_in) | copy-start | bytes 9437188
  234.1 6.5 %copy-start.11 = (bf16[1536,768]{1,0:T(8,128)(2,1)}, bf16[1536,768]{1,0:T(8,128)(2,1)S(1)}, u32[]{:S(2)}) copy-start(bf16[1536,768]{1,0:T(8,128)(2,1)S(1)} %get-tuple-element.90) | copy-start | bytes 7077892
  234.1 6.5 %copy-start.8 = (f32[2,1,2048]{2,1,0:T(1,128)S(1)}, f32[2,1,2048]{2,1,0:T(1,128)}, u32[]{:S(2)}) copy-start(f32[2,1,2048]{2,1,0:T(1,128)} %get-tuple-element.59) | copy-start | bytes 49156
  365.1 110.1 %copy-start.9 = (bf16[2,44]{1,0:T(2,128)(2,1)S(1)}, bf16[2,44]{1,0:T(2,128)(2,1)}, u32[]{:S(2)}) copy-start(bf16[2,44]{1,0:T(2,128)(2,1)} %param.27) | copy-start | bytes 532
  469.2 9.7 %copy-start.4 = (bf16[4,352,512]{2,1,0:T(8,128)(2,1)S(1)}, bf16[4,352,512]{2,1,0:T(8,128)(2,1)}, u32[]{:S(2)}) copy-start(bf16[4,352,512]{2,1,0:T(8,128)(2,1)} %get-tuple-element.82) | copy-start | bytes 4325380
  469.2 9.7 %copy-start.5 = (bf16[4,352,512]{2,1,0:T(8,128)(2,1)S(1)}, bf16[4,352,512]{2,1,0:T(8,128)(2,1)}, u32[]{:S(2)}) copy-start(bf16[4,352,512]{2,1,0:T(8,128)(2,1)} %get-tuple-element.85) | copy-start | bytes 4325380
  476.4 4.0 copy-start.1
  480.4 2.5 copy-start
  481.9 2.4 copy-start.2
  484.3 2.9 copy-start.6
  484.3 3.9 copy-start.7
  484.4 4.9 copy-start.3
Sparse Core Ops, SparseCore 0:
  365.3 51.0 reduce-scatter.1

commit v10 on v9

--- a/solution.py
+++ b/solution.py
@@ -847,12 +847,14 @@
 
 
 def mixer_forward_body(
-    x_ref, grad_ref, gain_pack_ref, vector_pack_ref, gate_pack_ref, v0, v1, v2, w0, w1, w2,
+    x_ref, grad_ref, gain_one_ref, gain_two_ref, taps_ref, taps_bias_ref, bias_a_ref, bias_x_ref, softness_own_ref,
+    weight_a_ref, weight_x_ref, v0, v1, v2, w0, w1, w2,
     residual_ref, gains_ref, vectors_ref, gate_a_ref, gate_x_ref,
     normed_one_out, branch_out, feed_out, conv_out, rate_out, input_out, state_out, mixed_out, u0, u1, u2,
     normed_ref, grads_ref, o0, o1, o2,
     normed_one_ref, branch_ref, feed_ref, conv_ref, rate_ref, input_ref, state_ref, mixed_ref,
     branch_w_ref, rec_w_ref, out_w_ref, x_full_ref, low_ref, window, carry, gates, gain_slots, vector_slots, gate_slots,
+    gain_pack_ref, vector_pack_ref, gate_pack_ref,
     store_sem, weight_store_sem, gain_send, gain_recv, small_send, small_recv,
     mixer_send, mixer_recv, weight_send, weight_recv, *refs,
 ):
@@ -866,6 +868,19 @@
     keeps = [
         copies([(buffer.at[s], out.at[s]) for buffer, out in kept], store_sem.at[s]) for s in range(seqs)
     ]
+    gain_pack_ref[...] = jnp.zeros_like(gain_pack_ref)
+    vector_pack_ref[...] = jnp.zeros_like(vector_pack_ref)
+    gain_part = gain_one_ref.shape[1]
+    gain_pack_ref[0:1, :gain_part] = gain_one_ref[...].astype(jnp.float32)
+    gain_pack_ref[0:1, gain_part : 2 * gain_part] = gain_two_ref[...].astype(jnp.float32)
+    heads, part, head_dim = weight_a_ref.shape
+    for h in range(heads):
+        columns = slice(h * part, (h + 1) * part)
+        vector_pack_ref[0:4, columns] = taps_ref[h].astype(jnp.float32)
+        for row, ref in enumerate((taps_bias_ref, bias_a_ref, bias_x_ref, softness_own_ref)):
+            vector_pack_ref[4 + row : 5 + row, columns] = ref[...].astype(jnp.float32)[h : h + 1]
+        gate_pack_ref[h] = weight_a_ref[h].astype(jnp.float32)
+        gate_pack_ref[heads + h] = weight_x_ref[h].astype(jnp.float32)
     weight_keeps = copies([(branch_w_ref, u0), (rec_w_ref, u1), (out_w_ref, u2)], weight_store_sem)
     greet_axes(("seq", "grp"))
     mixer_weights = weight_gathers(
@@ -905,7 +920,6 @@
     window[...] = jnp.zeros_like(window)
     along.finish_others()
     parts = lax.axis_size("seq")
-    gain_part = width // (parts * along.size)
     for k in range(parts):
         for g in range(along.size):
             at = (k * along.size + g) * gain_part
@@ -913,8 +927,6 @@
                 gains_ref[i, :, at : at + gain_part] = gain_slots[g, k, 0:1, i * gain_part : (i + 1) * gain_part]
     for move in small[1:]:
         move.finish()
-    heads = gate_pack_ref.shape[0] // 2
-    part, head_dim = gate_pack_ref.shape[1:]
     for k in range(parts):
         for h in range(heads):
             at = h * head_dim + k * part
@@ -1026,7 +1038,7 @@
         weight.finish()
 
 
-def mixer_forward(layer_in, out_grad, gain_pack, vector_pack, gate_pack, mixer_weights, weights):
+def mixer_forward(layer_in, out_grad, small, mixer_weights, weights):
     seqs, rows, width = layer_in.shape
     size, n = lax.axis_size("seq"), lax.axis_size("grp")
     seq_len, channels = n * rows, mixer_weights[0].shape[0]
@@ -1036,6 +1048,10 @@
     tokens = shape((seqs, seq_len, width), bf16)
     kept = [tokens, full, low, low, full, full, full, low]
     mixer_full = [gathered(w, axis) for w, axis in zip(mixer_weights, mixer_axes)]
+    heads, part, head_dim = small[-1].shape
+    packs = [
+        (8, -(-2 * small[0].shape[1] // 128) * 128), (8, -(-heads * part // 128) * 128), (2 * heads, part, head_dim)
+    ]
     outs = [
         shape(layer_in.shape, f32), shape((2, 1, width), f32), shape((8, channels), f32),
         shape((channels, channels), bf16), shape((channels, channels), bf16),
@@ -1044,8 +1060,8 @@
     outs += [gathered(w, axis) for w, axis in zip(weights, weight_axes)]
     return call(
         mixer_forward_body, "mixer_forward", 7,
-        (layer_in, out_grad, gain_pack, vector_pack, gate_pack, *mixer_weights, *weights),
-        [in_vmem] * 11,
+        (layer_in, out_grad, *small, *mixer_weights, *weights),
+        [in_vmem] * (8 + len(small)),
         outs, [in_vmem] * 5 + [in_hbm] * 16,
         [pltpu.VMEM(v.shape, v.dtype) for v in kept + mixer_full + [tokens]]
         + [
@@ -1053,9 +1069,10 @@
             pltpu.VMEM((pick_rows(seq_len) + 8, channels), f32),
             pltpu.VMEM((8, channels), f32),
             pltpu.VMEM((2, channels, channels), f32),
-            pltpu.VMEM((n, size) + gain_pack.shape, f32),
-            pltpu.VMEM((size,) + vector_pack.shape, f32),
-            pltpu.VMEM((size,) + gate_pack.shape, f32),
+            pltpu.VMEM((n, size) + packs[0], f32),
+            pltpu.VMEM((size,) + packs[1], f32),
+            pltpu.VMEM((size,) + packs[2], f32),
+            *(pltpu.VMEM(pack, f32) for pack in packs),
             pltpu.SemaphoreType.DMA((seqs, len(kept))),
             pltpu.SemaphoreType.DMA((3,)),
         ]
@@ -1630,18 +1647,14 @@
     at = tap_count + 4
     if short_line:
         softness = jax.nn.softplus(-decay_logit.astype(f32))
-        vector_rows = [jnp.transpose(conv_w, (1, 0, 2)).reshape(tap_count, -1)]
-        vector_rows += [v.reshape(1, -1) for v in (conv_b, gate_a_b, gate_x_b)]
-        vector_pack = jnp.concatenate([v.astype(f32) for v in vector_rows] + [softness.reshape(1, -1)])
-        vector_pack = jnp.pad(vector_pack, ((0, 0), (0, -vector_pack.shape[1] % 128)))
-        gain_pack = jnp.concatenate([gain_one, gain_two]).astype(f32)[None]
-        gain_pack = jnp.pad(gain_pack, ((0, 7), (0, -gain_pack.shape[1] % 128)))
-        gate_pack = jnp.concatenate([gate_a_w, gate_x_w]).astype(f32)
+        small = (
+            gain_one[None], gain_two[None], conv_w, conv_b, gate_a_b, gate_x_b, softness, gate_a_w, gate_x_w
+        )
         (
             residual, gains, vectors, diag_a, diag_x,
             normed_one, branch_pre, feed, conv, rate, gate, state, mixed, branch_w, rec_w, out_w,
             normed_two, grad_output, gate_w, up_w, down_w,
-        ) = mixer_forward(layer_in, out_grad, gain_pack, vector_pack, gate_pack, mixer_weights, mlp_weights)
+        ) = mixer_forward(layer_in, out_grad, small, mixer_weights, mlp_weights)
         normed_one = normed_one.reshape(-1, model_width)
         grad_output = grad_output.reshape(-1, model_width)
     else:

time: 507 us -> 503 us (level)
  no operation moved by 1% of the time
where the time goes in v10:
time: 503 us; the launch traced here: 494 us
  Pallas kernels  424 us (84%)
  matrix products  29.3 us (6%)
  other arithmetic  15.2 us (3%)
  between operations  14.7 us (3%)
  local copies, waits for them, and re-layouts  10.6 us (2%)
    pallas_call x3, Pallas kernels, call(): pl.pallas_call(body, in_specs=in_specs, out_specs=out_specs, out_shape=ou...  424 us
    dot_general x2, matrix products, matmul(): return jnp.dot(left, right, preferred_element_type=jnp.float32)  17.6 us
  transfers between devices with their start and end apart: 1, of which 0 were waited for; matrix products, arithmetic and copies ran while one was open for 3% of the time, Pallas kernels for 21%

profile of v10, /device:TPU:0, one launch (start us, length us, event | category | flops | bytes accessed | tf_op | source)
XLA Modules:
  0.0 493.8 jit_solution(8188256698319452031)
XLA Ops:
  7.2 0.0 reduce-scatter.2.cloned.1.call-start
  7.2 1.4 copy.37.weight_a_ref
  8.7 1.4 copy.38.weight_x_ref
  10.1 1.2 compare_select_fusion.softness_own_ref
  11.3 196.1 %mixer_forward.1 = (f32[2,96,2048]{2,1,0:T(8,128)}, f32[2,1,2048]{2,1,0:T(1,128)}, f32[8,352]{1,0:T(8,128)}, bf16[352,352]{1,0:T(8,128)(2,1)}, bf16[352,352]{1,0...) custom-call(bf16[2,96,2048]{2,1,0:T(8,128)(2,1)} %x_ref.3, ...), custom_call_target="tpu_custom_call" | custom-call | flops 179999997952 | bytes 540000000 | tf_op jit(solution)/shard_map/mixer_forward/pallas_call | solution.py:587
  207.4 0.0 copy-start.10
  207.4 0.0 copy-start.12
  207.5 0.0 slice-start
  207.5 8.2 %fusion.27 = f32[1536,768]{1,0:T(8,128)S(1)} fusion(bf16[1536,2048]{1,0:T(8,128)(2,1)} %bitcast.90, bf16[2048,768]{1,0:T(8,128)(2,1)} %get-tuple-element.57.gate_w_in), kind=kOutput, calls=%fused_computation.63 | convolution fusion | flops 4831838208 | bytes 14155776 | tf_op jit(solution)/shard_map/dot_general | solution.py:18
  215.7 0.0 slice-start.1
  215.7 0.0 copy-done.10
  215.7 0.0 copy-done.12
  215.7 0.0 copy-start.13
  215.7 5.1 %fusion.26 = f32[1536,768]{1,0:T(8,128)S(1)} fusion(bf16[1536,2048]{1,0:T(8,128)(2,1)S(1)} %bitcast.95, bf16[768,2048]{1,0:T(8,128)(2,1)S(1)} %copy-done.12), kind=kOutput, calls=%fused_computation.62 | convolution fusion | flops 4831838208 | bytes 14155776 | tf_op jit(solution)/shard_map/dot_general | solution.py:28
  220.9 0.0 slice-done
  220.9 0.0 slice-done.1
  220.9 0.0 copy-done.13
  220.9 9.4 %multiply_convert_fusion = (bf16[1536,768]{1,0:T(8,128)(2,1)}, bf16[1536,768]{1,0:T(8,128)(2,1)S(1)}, bf16[1536,768]{1,0:T(8,128)(2,1)}) fusion(f32[1536,768]{1,0:T(8,128)S(1)} %fusion.27, f32[1536,768]{1,0:T(8,128)S(1)} %fusion.26, bf16[1536,2048]{1,0:T(8,128)(2,1)S(1)} %bitcast.93, bf16[2048,768]{1,0:T(8,128)(2,1)S(1)} %copy-done.13), kind=kOutput, calls=%fused_computation.9 | convolution fusion | flops 4862509056 | bytes 25952256 | tf_op jit(solution)/shard_map/dot_general | solution.py:18
  230.3 6.5 %convolution_convert_fusion.w0 = bf16[2048,768]{1,0:T(8,128)(2,1)} fusion(bf16[1536,2048]{1,0:T(8,128)(2,1)S(1)} %bitcast.94, bf16[1536,768]{1,0:T(8,128)(2,1)S(1)} %get-tuple-element.90), kind=kOutput, calls=%fused_computation.12 | convolution fusion | flops 4833411072 | bytes 11796480 | tf_op jit(solution)/shard_map/dot_general | solution.py:22
  236.8 0.6 slice_bitcast_fusion
  237.5 123.8 %mlp_back.1 = (f32[2,96,2048]{2,1,0:T(8,128)}, f32[8,2048]{1,0:T(8,128)}, bf16[2,768,2048]{2,1,0:T(8,128)(2,1)}, bf16[3,512,768]{2,1,0:T(8,128)(2,1)}, bf16[4,51...) custom-call(bf16[2,768,768]{2,1,0:T(8,128)(2,1)} %bitcast.97, ...), custom_call_target="tpu_custom_call" | custom-call | flops 120000004096 | bytes 360000000 | tf_op jit(solution)/shard_map/mlp_back/pallas_call | solution.py:587
  361.3 0.0 reduce-scatter.2.cloned.1.call-update
  361.3 0.0 copy-start.9
  361.3 104.0 %mixer_back.1 = (f32[2,96,2048]{2,1,0:T(8,128)}, f32[2,2,48,352]{3,2,1,0:T(8,128)}, f32[8,352]{1,0:T(8,128)}, f32[8,512]{1,0:T(8,128)}, bf16[4,352,512]{2,1,0:T(...) custom-call(bf16[2,768,2048]{2,1,0:T(8,128)(2,1)} %get-tuple-element.62.low_in, ...), custom_call_target="tpu_custom_call" | custom-call | flops 99999997952 | bytes 300000000 | tf_op jit(solution)/shard_map/mixer_back/pallas_call | solution.py:587
  465.3 1.2 fusion.23
  466.5 0.1 copy.52
  466.6 0.1 copy.51
  466.7 0.8 reshape.100
  467.5 0.1 constant_dynamic-slice_fusion.3
  467.6 0.6 copy.53
  468.2 0.6 fusion.22
  468.8 0.8 constant_dynamic-slice_fusion.7
  469.6 0.1 fusion.24
  469.6 0.3 fusion.25
  469.9 0.7 pad_maximum_fusion.2
  470.6 0.7 pad_maximum_fusion.1
  471.4 0.6 fusion.18
  472.0 0.5 slice_bitcast_fusion.2
  472.5 2.5 add_bitcast_fusion.4
  475.0 0.0 copy-done.4
  475.0 1.5 add_bitcast_fusion.2
  476.5 1.6 add_bitcast_fusion
  478.0 0.9 copy-done
  478.9 1.5 add_bitcast_fusion.1
  480.5 2.8 convert_add_fusion
  483.3 1.1 fusion.8
  484.4 0.9 pad_maximum_fusion
  485.3 1.1 copy.55
  (22 shorter events, 0.1 us)
Async XLA Ops:
  7.2 476.1 %reduce-scatter.2.cloned.1.call-start = ((), (), s32[]{:S(2)}) async-start(), calls=%async_computation.1 | async-start | bytes 3538944 | tf_op jit(solution)/shard_map/reduce_scatter | solution.py:1726
  207.4 8.3 %copy-start.10 = (bf16[2,768,2048]{2,1,0:T(8,128)(2,1)S(1)}, bf16[2,768,2048]{2,1,0:T(8,128)(2,1)}, u32[]{:S(2)}) copy-start(bf16[2,768,2048]{2,1,0:T(8,128)(2,1)} %get-tuple-element.53.w2) | copy-start | bytes 18874372
  207.4 8.3 %copy-start.12 = (bf16[768,2048]{1,0:T(8,128)(2,1)S(1)}, bf16[768,2048]{1,0:T(8,128)(2,1)}, u32[]{:S(2)}) copy-start(bf16[768,2048]{1,0:T(8,128)(2,1)} %get-tuple-element.54.refs_1_) | copy-start | bytes 9437188
  207.5 13.4 %slice-start = ((s8[6291456]{0:T(1024)(128)(4,1)}), s8[4194304]{0:T(1024)(128)(4,1)S(1)}, s32[]{:S(2)}) async-start(s8[6291456]{0:T(1024)(128)(4,1)} %bitcast.91), calls=%async_computation.2 | async-start | bytes 8388608
  215.7 5.2 %slice-start.1 = ((s8[6291456]{0:T(1024)(128)(4,1)}), s8[2097152]{0:T(1024)(128)(4,1)S(1)}, s32[]{:S(2)}) async-start(s8[6291456]{0:T(1024)(128)(4,1)} %bitcast.91), calls=%async_computation.3 | async-start | bytes 4194304
  215.7 5.2 %copy-start.13 = (bf16[2048,768]{1,0:T(8,128)(2,1)S(1)}, bf16[2048,768]{1,0:T(8,128)(2,1)}, u32[]{:S(2)}) copy-start(bf16[2048,768]{1,0:T(8,128)(2,1)} %get-tuple-element.56.up_w_in) | copy-start | bytes 9437188
  230.3 6.5 %copy-start.11 = (bf16[1536,768]{1,0:T(8,128)(2,1)}, bf16[1536,768]{1,0:T(8,128)(2,1)S(1)}, u32[]{:S(2)}) copy-start(bf16[1536,768]{1,0:T(8,128)(2,1)S(1)} %get-tuple-element.90) | copy-start | bytes 7077892
  230.3 6.5 %copy-start.8 = (f32[2,1,2048]{2,1,0:T(1,128)S(1)}, f32[2,1,2048]{2,1,0:T(1,128)}, u32[]{:S(2)}) copy-start(f32[2,1,2048]{2,1,0:T(1,128)} %get-tuple-element.59) | copy-start | bytes 49156
  361.3 110.1 %copy-start.9 = (bf16[2,44]{1,0:T(2,128)(2,1)S(1)}, bf16[2,44]{1,0:T(2,128)(2,1)}, u32[]{:S(2)}) copy-start(bf16[2,44]{1,0:T(2,128)(2,1)} %param.27) | copy-start | bytes 532
  465.3 9.7 %copy-start.4 = (bf16[4,352,512]{2,1,0:T(8,128)(2,1)S(1)}, bf16[4,352,512]{2,1,0:T(8,128)(2,1)}, u32[]{:S(2)}) copy-start(bf16[4,352,512]{2,1,0:T(8,128)(2,1)} %get-tuple-element.82) | copy-start | bytes 4325380
  465.3 9.7 %copy-start.5 = (bf16[4,352,512]{2,1,0:T(8,128)(2,1)S(1)}, bf16[4,352,512]{2,1,0:T(8,128)(2,1)}, u32[]{:S(2)}) copy-start(bf16[4,352,512]{2,1,0:T(8,128)(2,1)} %get-tuple-element.85) | copy-start | bytes 4325380
  472.5 4.0 copy-start.1
  476.5 2.5 copy-start
  478.0 2.4 copy-start.2
  480.4 2.9 copy-start.6
  480.4 3.9 copy-start.7
  480.5 4.9 copy-start.3
Sparse Core Ops, SparseCore 0:
  361.4 51.1 reduce-scatter.1

commit v11 on v10

--- a/solution.py
+++ b/solution.py
@@ -83,7 +83,7 @@
     )
 
 
-def pick_rows(seq_len, choices=(128, 96, 64, 32, 16)):
+def pick_rows(seq_len, choices=(192, 128, 96, 64, 32, 16)):
     for rows in choices:
         if seq_len % rows == 0:
             return rows

time: 503 us -> 502 us (level)
  no operation moved by 1% of the time
where the time goes in v11:
time: 502 us; the launch traced here: 493 us
  Pallas kernels  423 us (84%)
  matrix products  29.3 us (6%)
  other arithmetic  15.2 us (3%)
  between operations  14.7 us (3%)
  local copies, waits for them, and re-layouts  10.6 us (2%)
    pallas_call x3, Pallas kernels, call(): pl.pallas_call(body, in_specs=in_specs, out_specs=out_specs, out_shape=ou...  423 us
    dot_general x2, matrix products, matmul(): return jnp.dot(left, right, preferred_element_type=jnp.float32)  17.6 us
  transfers between devices with their start and end apart: 1, of which 0 were waited for; matrix products, arithmetic and copies ran while one was open for 3% of the time, Pallas kernels for 21%

profile of v11, /device:TPU:0, one launch (start us, length us, event | category | flops | bytes accessed | tf_op | source)
XLA Modules:
  0.0 493.2 jit_solution(7991373063746629488)
XLA Ops:
  7.2 0.0 reduce-scatter.2.cloned.1.call-start
  7.2 1.4 copy.37.weight_a_ref
  8.7 1.4 copy.38.weight_x_ref
  10.1 1.2 compare_select_fusion.softness_own_ref
  11.3 196.1 %mixer_forward.1 = (f32[2,96,2048]{2,1,0:T(8,128)}, f32[2,1,2048]{2,1,0:T(1,128)}, f32[8,352]{1,0:T(8,128)}, bf16[352,352]{1,0:T(8,128)(2,1)}, bf16[352,352]{1,0...) custom-call(bf16[2,96,2048]{2,1,0:T(8,128)(2,1)} %x_ref.3, ...), custom_call_target="tpu_custom_call" | custom-call | flops 179999997952 | bytes 540000000 | tf_op jit(solution)/shard_map/mixer_forward/pallas_call | solution.py:587
  207.4 0.0 copy-start.10
  207.4 0.0 copy-start.12
  207.5 0.0 slice-start
  207.5 8.2 %fusion.27 = f32[1536,768]{1,0:T(8,128)S(1)} fusion(bf16[1536,2048]{1,0:T(8,128)(2,1)} %bitcast.90, bf16[2048,768]{1,0:T(8,128)(2,1)} %get-tuple-element.57.gate_w_in), kind=kOutput, calls=%fused_computation.63 | convolution fusion | flops 4831838208 | bytes 14155776 | tf_op jit(solution)/shard_map/dot_general | solution.py:18
  215.7 0.0 slice-start.1
  215.7 0.0 copy-done.10
  215.7 0.0 copy-done.12
  215.7 0.0 copy-start.13
  215.7 5.1 %fusion.26 = f32[1536,768]{1,0:T(8,128)S(1)} fusion(bf16[1536,2048]{1,0:T(8,128)(2,1)S(1)} %bitcast.95, bf16[768,2048]{1,0:T(8,128)(2,1)S(1)} %copy-done.12), kind=kOutput, calls=%fused_computation.62 | convolution fusion | flops 4831838208 | bytes 14155776 | tf_op jit(solution)/shard_map/dot_general | solution.py:28
  220.9 0.0 slice-done
  220.9 9.4 %multiply_convert_fusion = (bf16[1536,768]{1,0:T(8,128)(2,1)}, bf16[1536,768]{1,0:T(8,128)(2,1)S(1)}, bf16[1536,768]{1,0:T(8,128)(2,1)}) fusion(f32[1536,768]{1,0:T(8,128)S(1)} %fusion.27, f32[1536,768]{1,0:T(8,128)S(1)} %fusion.26, bf16[1536,2048]{1,0:T(8,128)(2,1)S(1)} %bitcast.93, bf16[2048,768]{1,0:T(8,128)(2,1)S(1)} %copy-done.13), kind=kOutput, calls=%fused_computation.9 | convolution fusion | flops 4862509056 | bytes 25952256 | tf_op jit(solution)/shard_map/dot_general | solution.py:18
  230.3 6.5 %convolution_convert_fusion.w0 = bf16[2048,768]{1,0:T(8,128)(2,1)} fusion(bf16[1536,2048]{1,0:T(8,128)(2,1)S(1)} %bitcast.94, bf16[1536,768]{1,0:T(8,128)(2,1)S(1)} %get-tuple-element.90), kind=kOutput, calls=%fused_computation.12 | convolution fusion | flops 4833411072 | bytes 11796480 | tf_op jit(solution)/shard_map/dot_general | solution.py:22
  236.8 0.0 copy-done.11
  236.8 0.6 slice_bitcast_fusion
  237.5 123.8 %mlp_back.1 = (f32[2,96,2048]{2,1,0:T(8,128)}, f32[8,2048]{1,0:T(8,128)}, bf16[2,768,2048]{2,1,0:T(8,128)(2,1)}, bf16[3,512,768]{2,1,0:T(8,128)(2,1)}, bf16[4,51...) custom-call(bf16[2,768,768]{2,1,0:T(8,128)(2,1)} %bitcast.97, ...), custom_call_target="tpu_custom_call" | custom-call | flops 120000004096 | bytes 360000000 | tf_op jit(solution)/shard_map/mlp_back/pallas_call | solution.py:587
  361.3 0.0 reduce-scatter.2.cloned.1.call-update
  361.3 0.0 copy-start.9
  361.3 103.4 %mixer_back.1 = (f32[2,96,2048]{2,1,0:T(8,128)}, f32[2,2,48,352]{3,2,1,0:T(8,128)}, f32[8,352]{1,0:T(8,128)}, f32[8,512]{1,0:T(8,128)}, bf16[4,352,512]{2,1,0:T(...) custom-call(bf16[2,768,2048]{2,1,0:T(8,128)(2,1)} %get-tuple-element.62.low_in, ...), custom_call_target="tpu_custom_call" | custom-call | flops 99999997952 | bytes 300000000 | tf_op jit(solution)/shard_map/mixer_back/pallas_call | solution.py:587
  464.8 1.2 fusion.23
  466.0 0.1 copy.52
  466.0 0.1 copy.51
  466.1 0.8 reshape.100
  466.9 0.1 constant_dynamic-slice_fusion.3
  467.0 0.6 copy.53
  467.6 0.6 fusion.22
  468.2 0.8 constant_dynamic-slice_fusion.7
  469.0 0.1 fusion.24
  469.1 0.3 fusion.25
  469.3 0.7 pad_maximum_fusion.2
  470.1 0.7 pad_maximum_fusion.1
  470.8 0.6 fusion.18
  471.4 0.5 slice_bitcast_fusion.2
  471.9 2.5 add_bitcast_fusion.4
  474.4 0.0 copy-done.4
  474.4 1.5 add_bitcast_fusion.2
  475.9 1.6 add_bitcast_fusion
  477.5 0.9 copy-done
  478.4 1.5 add_bitcast_fusion.1
  479.9 0.0 copy-done.2
  479.9 2.8 convert_add_fusion
  482.7 1.1 fusion.8
  483.8 0.9 pad_maximum_fusion
  484.8 1.1 copy.55
  (22 shorter events, 0.1 us)
Async XLA Ops:
  7.2 475.5 %reduce-scatter.2.cloned.1.call-start = ((), (), s32[]{:S(2)}) async-start(), calls=%async_computation.1 | async-start | bytes 3538944 | tf_op jit(solution)/shard_map/reduce_scatter | solution.py:1726
  207.4 8.3 %copy-start.10 = (bf16[2,768,2048]{2,1,0:T(8,128)(2,1)S(1)}, bf16[2,768,2048]{2,1,0:T(8,128)(2,1)}, u32[]{:S(2)}) copy-start(bf16[2,768,2048]{2,1,0:T(8,128)(2,1)} %get-tuple-element.53.w2) | copy-start | bytes 18874372
  207.4 8.3 %copy-start.12 = (bf16[768,2048]{1,0:T(8,128)(2,1)S(1)}, bf16[768,2048]{1,0:T(8,128)(2,1)}, u32[]{:S(2)}) copy-start(bf16[768,2048]{1,0:T(8,128)(2,1)} %get-tuple-element.54.refs_1_) | copy-start | bytes 9437188
  207.5 13.4 %slice-start = ((s8[6291456]{0:T(1024)(128)(4,1)}), s8[4194304]{0:T(1024)(128)(4,1)S(1)}, s32[]{:S(2)}) async-start(s8[6291456]{0:T(1024)(128)(4,1)} %bitcast.91), calls=%async_computation.2 | async-start | bytes 8388608
  215.7 5.2 %slice-start.1 = ((s8[6291456]{0:T(1024)(128)(4,1)}), s8[2097152]{0:T(1024)(128)(4,1)S(1)}, s32[]{:S(2)}) async-start(s8[6291456]{0:T(1024)(128)(4,1)} %bitcast.91), calls=%async_computation.3 | async-start | bytes 4194304
  215.7 5.2 %copy-start.13 = (bf16[2048,768]{1,0:T(8,128)(2,1)S(1)}, bf16[2048,768]{1,0:T(8,128)(2,1)}, u32[]{:S(2)}) copy-start(bf16[2048,768]{1,0:T(8,128)(2,1)} %get-tuple-element.56.up_w_in) | copy-start | bytes 9437188
  230.3 6.5 %copy-start.11 = (bf16[1536,768]{1,0:T(8,128)(2,1)}, bf16[1536,768]{1,0:T(8,128)(2,1)S(1)}, u32[]{:S(2)}) copy-start(bf16[1536,768]{1,0:T(8,128)(2,1)S(1)} %get-tuple-element.90) | copy-start | bytes 7077892
  230.3 6.5 %copy-start.8 = (f32[2,1,2048]{2,1,0:T(1,128)S(1)}, f32[2,1,2048]{2,1,0:T(1,128)}, u32[]{:S(2)}) copy-start(f32[2,1,2048]{2,1,0:T(1,128)} %get-tuple-element.59) | copy-start | bytes 49156
  361.3 109.5 %copy-start.9 = (bf16[2,44]{1,0:T(2,128)(2,1)S(1)}, bf16[2,44]{1,0:T(2,128)(2,1)}, u32[]{:S(2)}) copy-start(bf16[2,44]{1,0:T(2,128)(2,1)} %param.27) | copy-start | bytes 532
  464.7 9.7 %copy-start.4 = (bf16[4,352,512]{2,1,0:T(8,128)(2,1)S(1)}, bf16[4,352,512]{2,1,0:T(8,128)(2,1)}, u32[]{:S(2)}) copy-start(bf16[4,352,512]{2,1,0:T(8,128)(2,1)} %get-tuple-element.82) | copy-start | bytes 4325380
  464.7 9.7 %copy-start.5 = (bf16[4,352,512]{2,1,0:T(8,128)(2,1)S(1)}, bf16[4,352,512]{2,1,0:T(8,128)(2,1)}, u32[]{:S(2)}) copy-start(bf16[4,352,512]{2,1,0:T(8,128)(2,1)} %get-tuple-element.85) | copy-start | bytes 4325380
  471.9 4.0 copy-start.1
  475.9 2.5 copy-start
  477.5 2.4 copy-start.2
  479.9 2.9 copy-start.6
  479.9 3.9 copy-start.7
  479.9 4.9 copy-start.3
Sparse Core Ops, SparseCore 0:
  361.4 51.5 reduce-scatter.1
